TPU v7x, 256 devices: a whole 4x4x8 slice. The times are simulated.
256 devices in a mesh: wide: 64 (over y, z, x_hi), narrow: 4 (over x_lo, core).
Axes of the slice: x: 4 (x_hi: 2, x_lo: 2; x = x_hi * 2 + x_lo), y: 4, z: 8, core: 2. Of those that a mesh axis runs over, the one named last changes fastest.
Arguments:
- prior_lt: float32 [4096, 49152], P('narrow', 'wide'), may hold values from -2 to 2
- prior_d: float32 [4096], P('narrow'), may hold values from -4 to 4
- prior_e: float32 [4096], P('narrow'), may hold values from -4 to 4
- prior_pairs: int32 [4096], P('narrow'), may hold values from 0 to 1, as said below
- pivots: int32 [2, 256], replicated, may hold values from 0 to 49151, as said below
- a_first: float32 [256, 49152], P('narrow', 'wide'), may hold values from -6 to 6
- a_second: float32 [256, 49152], P('narrow', 'wide'), may hold values from -6 to 6
- inv_d: float32 [2, 256], P(None, 'narrow'), may hold values from -4 to 4
- inv_e: float32 [2, 256], P(None, 'narrow'), may hold values from -4 to 4
- panel_pairs: int32 [2, 256], P(None, 'narrow'), may hold values from 0 to 1, as said below
Outputs:
- l_first: float32 [256, 49152], P('narrow', 'wide')
- l_second: float32 [256, 49152], P('narrow', 'wide')
Inputs may be any that keep to these rules, and one draw needn't show every extreme that they name: `pivots`: all 512 pivot rows are distinct; at most 16 of them lie in one tile of 768 consecutive rows, and some tile holds exactly 16. `prior_pairs`: 1 only at even positions; a 1 at position k joins k and k + 1 into a 2 x 2 pivot block. `panel_pairs`: 1 only at even positions along the last dimension; a 1 at position k joins k and k + 1 into a 2 x 2 pivot block.
All inputs are finite; a program needn't handle non-finite values.
Results may differ from a plain program's by a relative error of at most 0.000098.
Values sent between devices are 32-bit elements; how exact they have to be, the bound alone decides.
No kernel may reach another device: no remote copies, remote signals or barrier semaphores. Data moves between devices by JAX's collectives and lax.ppermute only.
A program may use at most 64 MiB of HBM per device.

v0:
```python
import jax
import jax.numpy as jnp
from jax import lax
from jax.sharding import PartitionSpec as P

P_SIZE = 256


def couple(block, diag, off, pairs):
    joined = off * pairs.astype(jnp.float32)
    zero_row = jnp.zeros_like(block[:1])
    after = jnp.concatenate([block[1:], zero_row], 0)
    before = jnp.concatenate([zero_row, block[:-1]], 0)
    lower = jnp.concatenate([jnp.zeros_like(joined[:1]), joined[:-1]], 0)
    return diag[:, None] * block + joined[:, None] * after + lower[:, None] * before


def shards(
    prior_lt, prior_d, prior_e, prior_pairs, pivots, a_first, a_second, inv_d, inv_e, panel_pairs
):
    k_local, tile_rows = prior_lt.shape
    blocks = a_first.shape[0]
    narrow_count = lax.axis_size("narrow")
    here = lax.axis_index("wide")
    flat = pivots.reshape(-1)
    second = pivots[1]
    mine = flat // tile_rows == here
    taken = jnp.take(prior_lt, flat % tile_rows, axis=1)
    chosen = lax.psum(jnp.where(mine[None, :], taken, 0.0), "wide")
    coupled = couple(chosen, prior_d, prior_e, prior_pairs)
    arranged = (
        coupled.reshape(k_local, 2, narrow_count, blocks)
        .transpose(0, 2, 1, 3)
        .reshape(k_local, 2 * P_SIZE)
    )
    columns = arranged
    update = lax.psum_scatter(
        lax.dot_general(
            columns, prior_lt, (((0,), (0,)), ((), ())), precision=lax.Precision.HIGHEST
        ),
        "narrow",
        scatter_dimension=0,
        tiled=True,
    )
    w_first = a_first - update[:blocks]
    l_first = couple(w_first, inv_d[0], inv_e[0], panel_pairs[0])
    mine_second = second // tile_rows == here
    taken_second = jnp.take(l_first, second % tile_rows, axis=1)
    crossed = lax.psum(jnp.where(mine_second[None, :], taken_second, 0.0), "wide")
    columns = crossed
    correction = lax.psum_scatter(
        lax.dot_general(
            columns, w_first, (((0,), (0,)), ((), ())), precision=lax.Precision.HIGHEST
        ),
        "narrow",
        scatter_dimension=0,
        tiled=True,
    )
    w_second = a_second - update[blocks:] - correction
    l_second = couple(w_second, inv_d[1], inv_e[1], panel_pairs[1])
    return (l_first, l_second)


def solution(mesh):
    in_specs = (
        P("narrow", "wide"),
        P("narrow"),
        P("narrow"),
        P("narrow"),
        P(),
        P("narrow", "wide"),
        P("narrow", "wide"),
        P(None, "narrow"),
        P(None, "narrow"),
        P(None, "narrow"),
    )
    out_specs = (P("narrow", "wide"), P("narrow", "wide"))
    return jax.shard_map(shards, mesh=mesh, in_specs=in_specs, out_specs=out_specs, check_vma=False)
```

profile of v0, /device:TPU:1, one launch (start us, length us, event | category | flops | bytes accessed | tf_op | source)
XLA Modules:
  0.0 1413.8 jit_solution(1788546036238899778)
XLA Ops:
  7.2 0.0 all-reduce.9.cloned.1.call-start
  7.2 0.7 remainder_bitcast_fusion.1
  7.9 0.7 sign_compare_fusion
  8.7 2.4 copy.14
  11.0 2.7 gather_fusion
  13.8 3.2 select_bitcast_fusion
  17.0 0.0 all-reduce.9.cloned.1.call-update
  17.0 0.0 reduce-scatter.3.cloned.1.call-start
  17.0 0.6 copy-done.8
  17.6 0.0 copy-done.9
  17.7 0.1 pad_maximum_fusion
  17.7 656.7 %all-reduce.9.cloned.1.call-done = f32[1024,512]{0,1:T(8,128)} async-done(((f32[1024,512]{0,1:T(8,128)}), f32[1024,512]{0,1:T(8,128)}) %all-reduce.9.cloned.1.call-update) | async-done | bytes 2097168 | tf_op jit(solution)/shard_map/psum | solution.py:29
  674.5 3.1 fusion.2
  677.6 0.0 copy-done.7
  677.6 0.0 copy-done
  677.6 0.9 multiply_add_fusion
  678.5 0.0 copy-start.1
  678.5 0.1 copy.15
  678.7 1.7 copy-done.1
  680.4 0.0 copy-start.4
  680.4 6.4 fusion.5
  686.9 0.0 reduce-scatter.3.cloned.1.call-update
  686.9 0.0 all-reduce.11.cloned.1.call-start
  687.0 0.0 copy-done.10
  687.0 0.0 copy-done.11
  687.0 0.1 pad_maximum_fusion.2
  687.1 0.0 copy-done.6
  687.2 0.0 copy-done.12
  687.2 68.4 %reduce-scatter.3.cloned.1.call-done = f32[128,768]{1,0:T(8,128)} async-done(((f32[512,768]{1,0:T(8,128)}), f32[128,768]{1,0:T(8,128)}) %reduce-scatter.3.cloned.1.call-update) | async-done | bytes 393232 | tf_op jit(solution)/shard_map/reduce_scatter | solution.py:37
  755.6 0.0 copy-done.4
  755.6 0.9 slice_subtract_fusion.1
  756.6 0.0 copy-start.3
  756.6 0.0 copy-start.5
  756.6 0.1 multiply_add_fusion.2
  756.8 0.0 copy-start.2
  756.8 0.2 copy.16
  756.9 0.7 gather_fusion.1
  757.7 0.8 select_bitcast_fusion.1
  758.5 0.0 all-reduce.11.cloned.1.call-update
  758.5 0.0 reduce-scatter.5.cloned.1.call-start
  758.5 594.9 %all-reduce.11.cloned.1.call-done = f32[64,256]{0,1:T(8,128)} async-done(((f32[64,256]{0,1:T(8,128)}), f32[64,256]{0,1:T(8,128)}) %all-reduce.11.cloned.1.call-update) | async-done | bytes 65552 | tf_op jit(solution)/shard_map/psum | solution.py:49
  1353.4 2.6 fusion.6
  1356.0 0.0 reduce-scatter.5.cloned.1.call-update
  1356.0 0.1 pad_maximum_fusion.1
  1356.1 49.3 %reduce-scatter.5.cloned.1.call-done = f32[64,768]{1,0:T(8,128)} async-done(((f32[256,768]{1,0:T(8,128)}), f32[64,768]{1,0:T(8,128)}) %reduce-scatter.5.cloned.1.call-update) | async-done | bytes 196624 | tf_op jit(solution)/shard_map/reduce_scatter | solution.py:51
  1405.4 0.0 copy-done.3
  1405.4 1.0 fusion
  1406.4 0.8 multiply_add_fusion.1
  (29 shorter events, 0.2 us)
Async XLA Ops:
  7.2 667.3 %all-reduce.9.cloned.1.call-start = ((), (), s32[]{:S(2)}) async-start(), calls=%async_computation.2 | async-start | bytes 4194304 | tf_op jit(solution)/shard_map/psum | solution.py:29
  17.0 0.7 copy-start.8
  17.0 0.7 copy-start.9
  17.0 738.6 %reduce-scatter.3.cloned.1.call-start = ((), (), s32[]{:S(2)}) async-start(), calls=%async_computation.3 | async-start | bytes 1966080 | tf_op jit(solution)/shard_map/reduce_scatter | solution.py:37
  17.7 659.9 %copy-start.7 = (f32[1024]{0:T(1024)S(1)}, f32[1024]{0:T(1024)}, u32[]{:S(2)}) copy-start(f32[1024]{0:T(1024)} %param.11) | copy-start | bytes 12292
  674.5 3.1 copy-start
  678.5 1.9 copy-start.1
  680.4 6.5 copy-start.10
  680.4 6.5 copy-start.11
  680.4 6.7 copy-start.6
  680.4 6.7 copy-start.12
  680.4 75.2 %copy-start.4 = (f32[64,768]{1,0:T(8,128)S(1)}, f32[64,768]{1,0:T(8,128)}, u32[]{:S(2)}) copy-start(f32[64,768]{1,0:T(8,128)} %param.15) | copy-start | bytes 589828
  686.9 666.5 %all-reduce.11.cloned.1.call-start = ((), (), s32[]{:S(2)}) async-start(), calls=%async_computation.4 | async-start | bytes 262144 | tf_op jit(solution)/shard_map/psum | solution.py:49
  756.6 648.8 %copy-start.3 = (f32[128,768]{1,0:T(8,128)S(1)}, f32[128,768]{1,0:T(8,128)}, u32[]{:S(2)}) copy-start(f32[128,768]{1,0:T(8,128)} %reduce-scatter.3.cloned.1.call-done) | copy-start | bytes 1179652
  756.6 648.8 %copy-start.5 = (f32[64,768]{1,0:T(8,128)S(1)}, f32[64,768]{1,0:T(8,128)}, u32[]{:S(2)}) copy-start(f32[64,768]{1,0:T(8,128)} %param.16) | copy-start | bytes 589828
  756.8 649.6 %copy-start.2 = (f32[64,768]{1,0:T(8,128)}, f32[64,768]{1,0:T(8,128)S(1)}, u32[]{:S(2)}) copy-start(f32[64,768]{1,0:T(8,128)S(1)} %multiply_add_fusion.2) | copy-start | bytes 589828
  758.5 646.9 %reduce-scatter.5.cloned.1.call-start = ((), (), s32[]{:S(2)}) async-start(), calls=%async_computation.5 | async-start | bytes 983040 | tf_op jit(solution)/shard_map/reduce_scatter | solution.py:51
Sparse Core Ops, SparseCore 0:
  17.1 657.3 all-reduce.8
  687.0 68.5 reduce-scatter.2
  759.0 594.3 all-reduce.10
  1356.1 49.2 reduce-scatter.4
where the time goes:
time: 1410 us
  waiting for transfers between devices  1370 us (97%)
    psum x1, waiting for transfers between devices, shards(): chosen = lax.psum(jnp.where(mine[None, :], taken, 0.0), 'wide')  657 us
    psum x1, waiting for transfers between devices, shards(): lax.psum(jnp.where(mine_second[None, :], taken_second, 0.0), 'wide')  595 us
    reduce_scatter x1, waiting for transfers between devices, shards(): lax.psum_scatter(lax.dot_general(columns, prior_lt, (((0,), (0,)), ((), (...  68.4 us
    reduce_scatter x1, waiting for transfers between devices, shards(): lax.psum_scatter(lax.dot_general(columns, w_first, (((0,), (0,)), ((), ()...  49.3 us
  transfers between devices with their start and end apart: 4, of which 4 were waited for; matrix products, arithmetic and copies ran while one was open for 0% of the time, Pallas kernels for 0%

commit v1 on v0

v1 whole, which is shorter than its diff:
```python
import jax
import jax.numpy as jnp
from jax import lax
from jax.sharding import PartitionSpec as P

P_SIZE = 256
CAP = 16
NY, NZ, NH = 4, 8, 2
CORE = [(0, 1), (1, 0), (2, 3), (3, 2)]
CHIP = [(0, 2), (1, 3), (2, 0), (3, 1)]
HIGH = lax.Precision.HIGH
EXACT = lax.Precision.HIGHEST


def couple(block, diag, off, pairs):
    joined = off * pairs.astype(jnp.float32)
    zero_row = jnp.zeros_like(block[:1])
    after = jnp.concatenate([block[1:], zero_row], 0)
    before = jnp.concatenate([zero_row, block[:-1]], 0)
    lower = jnp.concatenate([jnp.zeros_like(joined[:1]), joined[:-1]], 0)
    return diag[:, None] * block + joined[:, None] * after + lower[:, None] * before


def couple_lanes(block, diag, off, pairs):
    joined = off * pairs.astype(jnp.float32)
    zero = jnp.zeros_like(block[:, :1])
    after = jnp.concatenate([block[:, 1:], zero], 1)
    before = jnp.concatenate([zero, block[:, :-1]], 1)
    lower = jnp.concatenate([jnp.zeros_like(joined[:1]), joined[:-1]], 0)
    return diag[None, :] * block + joined[None, :] * after + lower[None, :] * before


def shift(dy, dz, dh):
    pairs = []
    for y in range(NY):
        for z in range(NZ):
            for h in range(NH):
                to = ((y + dy) % NY * NZ + (z + dz) % NZ) * NH + (h + dh) % NH
                pairs.append(((y * NZ + z) * NH + h, to))
    return pairs


def moved(block, offsets, step):
    got = lax.ppermute(block, "wide", shift(*step))
    return got, [
        ((y - step[0]) % NY, (z - step[1]) % NZ, (h - step[2]) % NH) for y, z, h in offsets
    ]


def gather_tiles(block):
    held, at = block, [(0, 0, 0)]
    for step in ((0, 0, 1), (0, 4, 0)):
        got, its = moved(held, at, step)
        held, at = jnp.concatenate([held, got], 0), at + its
    parts = [moved(held, at, step) for step in ((2, 1, 0), (2, -1, 0), (0, 2, 0))]
    held = jnp.concatenate([held] + [p[0] for p in parts], 0)
    at = at + parts[0][1] + parts[1][1] + parts[2][1]
    half = len(at) // 2
    cut = half * block.shape[0]
    last = [moved(held, at, step) for step in ((1, 0, 0), (-1, 0, 0))]
    up, up_at = moved(held[:cut], at[:half], (0, 1, 0))
    have = set(at) | {o for p in last for o in p[1]} | set(up_at)
    low = [(y, (z + 1) % NZ, h) for y, z, h in at]
    keep = [i for i, o in enumerate(low) if o not in have]
    if keep == list(range(half)):
        down, down_at = moved(held[:cut], at[:half], (0, -1, 0))
    else:
        down, down_at = moved(held[cut:], at[half:], (0, -1, 0))
    arrays = [held] + [p[0] for p in last] + [up, down]
    offsets = at + last[0][1] + last[1][1] + up_at + down_at
    return arrays, offsets


def scatter_sum(block):
    me = lax.axis_index("narrow")
    core, chip = me % 2, me // 2
    rows = block.shape[0] // 4
    block = block.reshape(2, 2, rows, block.shape[1])
    mine = jnp.where(core == 0, block[:, 0], block[:, 1])
    other = jnp.where(core == 0, block[:, 1], block[:, 0])
    block = mine + lax.ppermute(other, "narrow", CORE)
    mine = jnp.where(chip == 0, block[0], block[1])
    other = jnp.where(chip == 0, block[1], block[0])
    return mine + lax.ppermute(other, "narrow", CHIP)


def shards(
    prior_lt, prior_d, prior_e, prior_pairs, pivots, a_first, a_second, inv_d, inv_e, panel_pairs
):
    k_local, tile_rows = prior_lt.shape
    blocks = a_first.shape[0]
    here = lax.axis_index("wide")
    flat = pivots.reshape(-1)
    tile = flat // tile_rows
    within = flat % tile_rows
    count = flat.shape[0]
    order = jnp.arange(count)
    rank = jnp.sum((tile[:, None] == tile[None, :]) & (order[None, :] < order[:, None]), 1)
    slot_hit = (rank[None, :] == jnp.arange(CAP)[:, None]) & (tile == here)[None, :]
    column = jnp.sum(jnp.where(slot_hit, within[None, :] + 1, 0), 1) - 1
    pick = (column[:, None] == jnp.arange(tile_rows)[None, :]).astype(jnp.float32)
    dims = (((1,), (1,)), ((), ()))
    slots_l = lax.dot_general(pick, prior_lt, dims, precision=EXACT)
    slots_a = lax.dot_general(pick, a_first, dims, precision=EXACT)
    block = jnp.concatenate([slots_l, jnp.pad(slots_a, ((0, 0), (0, 64)))], 1)
    arrays, offsets = gather_tiles(block)
    ty, tz, th = tile // (NZ * NH), tile // NH % NZ, tile % NH
    hy, hz, hh = here // (NZ * NH), here // NH % NZ, here % NH
    rel = ((ty - hy) % NY * NZ + (tz - hz) % NZ) * NH + (th - hh) % NH
    place_of = [0] * (NY * NZ * NH)
    for i, (y, z, h) in enumerate(offsets):
        place_of[(y * NZ + z) * NH + h] = i
    place = jnp.sum(
        jnp.where(rel[:, None] == jnp.arange(NY * NZ * NH)[None, :], jnp.array(place_of)[None, :], 0), 1
    )
    chosen = jnp.take(jnp.concatenate(arrays, 0), place * CAP + rank, axis=0, mode="clip")
    coupled_lt = couple(prior_lt, prior_d, prior_e, prior_pairs)
    first, second = chosen[:P_SIZE, :k_local], chosen[P_SIZE:, :k_local]
    plain = (((1,), (0,)), ((), ()))
    update_first = lax.dot_general(first, coupled_lt, plain, precision=HIGH)
    update_second = lax.dot_general(second, coupled_lt, plain, precision=HIGH)
    coupled_second = couple_lanes(second, prior_d, prior_e, prior_pairs)
    inner = lax.dot_general(first, coupled_second, dims, precision=HIGH)
    summed = scatter_sum(jnp.concatenate([update_first, inner], 1))
    a_crossed = chosen[P_SIZE:, k_local : k_local + blocks].T
    w_first = a_first - summed[:, :tile_rows]
    l_first = couple(w_first, inv_d[0], inv_e[0], panel_pairs[0])
    crossed = couple(a_crossed - summed[:, tile_rows:], inv_d[0], inv_e[0], panel_pairs[0])
    correction = lax.dot_general(crossed, w_first, (((0,), (0,)), ((), ())), precision=HIGH)
    w_second = a_second - scatter_sum(update_second + correction)
    l_second = couple(w_second, inv_d[1], inv_e[1], panel_pairs[1])
    return (l_first, l_second)


def solution(mesh):
    in_specs = (
        P("narrow", "wide"),
        P("narrow"),
        P("narrow"),
        P("narrow"),
        P(),
        P("narrow", "wide"),
        P("narrow", "wide"),
        P(None, "narrow"),
        P(None, "narrow"),
        P(None, "narrow"),
    )
    out_specs = (P("narrow", "wide"), P("narrow", "wide"))
    return jax.shard_map(shards, mesh=mesh, in_specs=in_specs, out_specs=out_specs, check_vma=False)
```

time: 1410 us -> 140 us (0.10)
  waiting for transfers between devices: 1370 us -> 39.7 us
  starting transfers between devices: 0.16 us -> 46.6 us
  local copies, waits for them, and re-layouts: 11.7 us -> 31 us
    psum x2 -> x0, waiting for transfers between devices: 1250 us -> none  [the longest x1 657 us: shards(): chosen = lax.psum(jnp.where(mine[None, :], taken, 0.0), 'wide')]
    reduce_scatter x2 -> x0, waiting for transfers between devices: 118 us -> none  [the longest x1 68.4 us: shards(): lax.psum_scatter(lax.dot_general(columns, prior_lt, (((0,), (0,)), ((), (...]
    ppermute x0 -> x13, starting transfers between devices: none -> 46.6 us  [the longest x9 33.3 us: moved(): got = lax.ppermute(block, 'wide', shift(*step))]
    ppermute x0 -> x13, waiting for transfers between devices: none -> 39.7 us  [the longest x9 21.6 us: moved(): got = lax.ppermute(block, 'wide', shift(*step))]
  transfers between devices with their start and end apart: 4 -> 13, of which waited for: 4 -> 10; matrix products, arithmetic and copies ran while one was open for 0% -> 10% of each run, Pallas kernels for 0% -> 0%
where the time goes in v1:
time: 140 us; the launch traced here: 139 us
  starting transfers between devices  46.6 us (33%)
  waiting for transfers between devices  39.7 us (28%)
  local copies, waits for them, and re-layouts  31 us (22%)
  other arithmetic  11.8 us (8%)
  matrix products  8.57 us (6%)
    ppermute x9, starting transfers between devices, moved(): got = lax.ppermute(block, 'wide', shift(*step))  33.3 us
    ppermute x9, waiting for transfers between devices, moved(): got = lax.ppermute(block, 'wide', shift(*step))  21.6 us
    unnamed x39, local copies, waits for them, and re-layouts  16.9 us
    ppermute x2, waiting for transfers between devices, scatter_sum(): return mine + lax.ppermute(other, 'narrow', CHIP)  15.2 us
    ppermute x2, starting transfers between devices, scatter_sum(): block = mine + lax.ppermute(other, 'narrow', CORE)  10.7 us
    gather x1, local copies, waits for them, and re-layouts, shards(): jnp.take(jnp.concatenate(arrays, 0), place * CAP + rank, axis=0, mode='cl...  5.39 us
    dot_general x1, matrix products, shards(): slots_l = lax.dot_general(pick, prior_lt, dims, precision=EXACT)  3.4 us
    add x3, other arithmetic, couple(): diag[:, None] * block + joined[:, None] * after + lower[:, None] * before  3.34 us
  transfers between devices with their start and end apart: 13, of which 10 were waited for; matrix products, arithmetic and copies ran while one was open for 10% of the time, Pallas kernels for 0%

profile of v1, /device:TPU:1, one launch (start us, length us, event | category | flops | bytes accessed | tf_op | source)
XLA Modules:
  0.0 138.7 jit_solution(1162767628770242473)
XLA Ops:
  0.7 0.9 divide_bitcast_fusion
  2.9 3.4 %fusion.30 = f32[16,1024]{1,0:T(8,128)S(1)} fusion(f32[1024,768]{1,0:T(8,128)} %param.11, s32[16]{0:T(128)S(1)} %broadcast_add_fusion), kind=kOutput, calls=%fused_computation.58 | convolution fusion | flops 151007232 | bytes 3211328 | tf_op jit(solution)/shard_map/dot_general | solution.py:103
  7.2 3.6 %collective-permute-start = (f32[16,1152]{1,0:T(8,128)S(1)}, f32[16,1152]{1,0:T(8,128)S(1)}, u32[]{:S(2)}, u32[]{:S(2)}) collective-permute-start(f32[16,1152]{1,0:T(8,128)S(1)} %get-tuple-element.34), channel_id=1, source_target_pairs={{0,4},{4,0},{8,12},{12,8},{16,20},{20,16},{24,28},{28,24},{32,36},... | collective-permute-start | bytes 221192 | tf_op jit(solution)/shard_map/ppermute | solution.py:44
  11.3 1.2 collective-permute-done
  12.6 7.2 %collective-permute-start.1 = (f32[32,1152]{1,0:T(8,128)S(1)}, f32[32,1152]{1,0:T(8,128)S(1)}, u32[]{:S(2)}, u32[]{:S(2)}) collective-permute-start(f32[32,1152]{1,0:T(8,128)S(1)} %pad_maximum_fusion.3), channel_id=1, source_target_pairs={{0,32},{4,36},{8,40},{12,44},{16,48},{20,52},{24,56},{28,60},{32,0... | collective-permute-start | bytes 442376 | tf_op jit(solution)/shard_map/ppermute | solution.py:44
  19.8 2.6 %collective-permute-done.1 = f32[32,1152]{1,0:T(8,128)S(1)} collective-permute-done((f32[32,1152]{1,0:T(8,128)S(1)}, f32[32,1152]{1,0:T(8,128)S(1)}, u32[]{:S(2)}, u32[]{:S(2)}) %collective-permute-start.1) | collective-permute-done | bytes 147488 | tf_op jit(solution)/shard_map/ppermute | solution.py:44
  22.4 3.4 %collective-permute-start.2 = (f32[64,1152]{1,0:T(8,128)S(1)}, f32[64,1152]{1,0:T(8,128)S(1)}, u32[]{:S(2)}, u32[]{:S(2)}) collective-permute-start(f32[64,1152]{1,0:T(8,128)S(1)} %pad_maximum_fusion.2), channel_id=1, source_target_pairs={{0,136},{4,140},{8,144},{12,148},{16,152},{20,156},{24,160},{28,16... | collective-permute-start | bytes 884744 | tf_op jit(solution)/shard_map/ppermute | solution.py:44
  26.5 3.8 %collective-permute-start.3 = (f32[64,1152]{1,0:T(8,128)S(1)}, f32[64,1152]{1,0:T(8,128)S(1)}, u32[]{:S(2)}, u32[]{:S(2)}) collective-permute-start(f32[64,1152]{1,0:T(8,128)S(1)} %pad_maximum_fusion.2), channel_id=1, source_target_pairs={{0,184},{4,188},{8,128},{12,132},{16,136},{20,140},{24,144},{28,14... | collective-permute-start | bytes 884744 | tf_op jit(solution)/shard_map/ppermute | solution.py:44
  30.3 2.3 %collective-permute-start.4 = (f32[64,1152]{1,0:T(8,128)S(1)}, f32[64,1152]{1,0:T(8,128)S(1)}, u32[]{:S(2)}, u32[]{:S(2)}) collective-permute-start(f32[64,1152]{1,0:T(8,128)S(1)} %pad_maximum_fusion.2), channel_id=1, source_target_pairs={{0,16},{4,20},{8,24},{12,28},{16,32},{20,36},{24,40},{28,44},{32,4... | collective-permute-start | bytes 884744 | tf_op jit(solution)/shard_map/ppermute | solution.py:44
  33.4 1.6 %collective-permute-done.2 = f32[64,1152]{1,0:T(8,128)S(1)} collective-permute-done((f32[64,1152]{1,0:T(8,128)S(1)}, f32[64,1152]{1,0:T(8,128)S(1)}, u32[]{:S(2)}, u32[]{:S(2)}) %collective-permute-start.2) | collective-permute-done | bytes 294944 | tf_op jit(solution)/shard_map/ppermute | solution.py:44
  34.9 0.9 constant_dynamic-update-slice_fusion.2
  35.8 2.9 %collective-permute-done.3 = f32[64,1152]{1,0:T(8,128)S(1)} collective-permute-done((f32[64,1152]{1,0:T(8,128)S(1)}, f32[64,1152]{1,0:T(8,128)S(1)}, u32[]{:S(2)}, u32[]{:S(2)}) %collective-permute-start.3) | collective-permute-done | bytes 294944 | tf_op jit(solution)/shard_map/ppermute | solution.py:44
  38.7 0.9 constant_dynamic-update-slice_fusion.1
  39.6 4.6 %collective-permute-done.4 = f32[64,1152]{1,0:T(8,128)S(1)} collective-permute-done((f32[64,1152]{1,0:T(8,128)S(1)}, f32[64,1152]{1,0:T(8,128)S(1)}, u32[]{:S(2)}, u32[]{:S(2)}) %collective-permute-start.4) | collective-permute-done | bytes 294944 | tf_op jit(solution)/shard_map/ppermute | solution.py:44
  44.2 0.9 constant_dynamic-update-slice_fusion
  45.0 1.7 %collective-permute-start.5 = (f32[256,1152]{1,0:T(8,128)}, f32[256,1152]{1,0:T(8,128)}, u32[]{:S(2)}, u32[]{:S(2)}) collective-permute-start(f32[256,1152]{1,0:T(8,128)} %get-tuple-element.18), channel_id=1, source_target_pairs={{0,64},{4,68},{8,72},{12,76},{16,80},{20,84},{24,88},{28,92},{32,9... | collective-permute-start | bytes 3538952 | tf_op jit(solution)/shard_map/ppermute | solution.py:44
  46.8 4.1 %collective-permute-start.6 = (f32[256,1152]{1,0:T(8,128)}, f32[256,1152]{1,0:T(8,128)}, u32[]{:S(2)}, u32[]{:S(2)}) collective-permute-start(f32[256,1152]{1,0:T(8,128)} %get-tuple-element.18), channel_id=1, source_target_pairs={{0,192},{4,196},{8,200},{12,204},{16,208},{20,212},{24,216},{28,22... | collective-permute-start | bytes 3538952 | tf_op jit(solution)/shard_map/ppermute | solution.py:44
  51.0 2.4 %multiply_add_fusion = f32[1024,768]{1,0:T(8,128)} fusion(f32[1023,768]{1,0:T(8,128)S(1)} %get-tuple-element.11, f32[1023,768]{1,0:T(8,128)S(1)} %get-tuple-element.10, f32[1024,768]{1,0:T(8,128)S(1)} %copy-done, f32[1024]{0:T(1024)S(1)} %pad_maximum_fusion.5, f32[1024]{0:T(1024)S(1)} %convert_multiply_fusion, f32[1024]{0:T(1024)S(1)} %copy-done.6), kind=kLoop, calls=%fused_computation.1 | loop fusion | flops 3932160 | bytes 12589056 | tf_op jit(solution)/shard_map/add | solution.py:21
  53.4 2.8 %collective-permute-start.7 = (f32[128,1152]{1,0:T(8,128)S(1)}, f32[128,1152]{1,0:T(8,128)S(1)}, u32[]{:S(2)}, u32[]{:S(2)}) collective-permute-start(f32[128,1152]{1,0:T(8,128)S(1)} %pad_maximum_fusion.1), channel_id=1, source_target_pairs={{0,8},{4,12},{8,16},{12,20},{16,24},{20,28},{24,32},{28,36},{32,40... | collective-permute-start | bytes 1769480 | tf_op jit(solution)/shard_map/ppermute | solution.py:44
  56.2 4.5 %collective-permute-start.8 = (f32[128,1152]{1,0:T(8,128)S(1)}, f32[128,1152]{1,0:T(8,128)S(1)}, u32[]{:S(2)}, u32[]{:S(2)}) collective-permute-start(f32[128,1152]{1,0:T(8,128)S(1)} %pad_maximum_fusion.1), channel_id=1, source_target_pairs={{0,56},{4,60},{8,0},{12,4},{16,8},{20,12},{24,16},{28,20},{32,24},... | collective-permute-start | bytes 1769480 | tf_op jit(solution)/shard_map/ppermute | solution.py:44
  60.7 8.7 %collective-permute-done.5 = f32[256,1152]{1,0:T(8,128)} collective-permute-done((f32[256,1152]{1,0:T(8,128)}, f32[256,1152]{1,0:T(8,128)}, u32[]{:S(2)}, u32[]{:S(2)}) %collective-permute-start.5) | collective-permute-done | bytes 1179680 | tf_op jit(solution)/shard_map/ppermute | solution.py:44
  69.3 2.4 %constant_dynamic-update-slice_fusion.9 = f32[1024,1152]{1,0:T(8,128)} fusion(f32[1024,1152]{1,0:T(8,128)} %get-tuple-element.19, f32[256,1152]{1,0:T(8,128)} %collective-permute-done.5), kind=kLoop, calls=%fused_computation.68 | loop fusion | bytes 2359296
  71.7 2.4 %constant_dynamic-update-slice_fusion.8 = f32[1024,1152]{1,0:T(8,128)} fusion(f32[1024,1152]{1,0:T(8,128)} %constant_dynamic-update-slice_fusion.9, f32[256,1152]{1,0:T(8,128)} %collective-permute-done.6), kind=kLoop, calls=%fused_computation.67 | loop fusion | bytes 2359296
  75.0 0.9 constant_dynamic-update-slice_fusion.6
  75.8 5.4 %gather_fusion = f32[512,1152]{1,0:T(8,128)S(1)} fusion(f32[1024,1152]{1,0:T(8,128)} %constant_dynamic-update-slice_fusion.6, s32[1024]{0:T(1024)S(1)} %pad_clamp_fusion), kind=kCustom, calls=%fused_computation | custom fusion | bytes 4720640 | tf_op jit(solution)/shard_map/jit(_take)/gather | solution.py:116
  81.6 1.5 %copy-done.1 = f32[1024,768]{1,0:T(8,128)S(1)} copy-done((f32[1024,768]{1,0:T(8,128)S(1)}, f32[1024,768]{1,0:T(8,128)}, u32[]{:S(2)}) %copy-start.1) | copy-done | bytes 3145752
  83.1 1.8 %fusion.12 = f32[256,768]{1,0:T(8,128)S(1)} fusion(f32[1024,768]{1,0:T(8,128)S(1)} %copy-done.1, f32[512,1152]{1,0:T(8,128)S(1)} %gather_fusion), kind=kOutput, calls=%fused_computation.20 | convolution fusion | flops 1207959552 | bytes 4980736 | tf_op jit(solution)/shard_map/dot_general | solution.py:120
  84.9 0.9 fusion
  85.9 1.0 fusion.51
  87.0 1.4 copy.39
  88.4 2.4 %copy.40 = f32[2,1,64,1024]{2,3,0,1:T(8,128)} copy(f32[2,1,64,1024]{3,2,1,0:T(8,128)} %get-tuple-element.15) | data formatting | bytes 1048576
  90.7 1.1 select_bitcast_fusion
  91.8 2.3 %copy.32 = f32[2,64,1024]{2,1,0:T(8,128)} copy(f32[2,64,1024]{1,2,0:T(8,128)} %select_bitcast_fusion) | data formatting | bytes 1048576 | tf_op jit(solution)/shard_map/jit(_where)/select_n | solution.py:80
  94.2 9.8 %collective-permute-start.9 = (f32[2,64,1024]{2,1,0:T(8,128)}, f32[2,64,1024]{2,1,0:T(8,128)}, u32[]{:S(2)}, u32[]{:S(2)}) collective-permute-start(f32[2,64,1024]{2,1,0:T(8,128)} %copy.32), channel_id=1, source_target_pairs={{0,1},{1,0},{2,3},{3,2},{4,5},{5,4},{6,7},{7,6},{8,9},{9,8},{10,11... | collective-permute-start | bytes 1572872 | tf_op jit(solution)/shard_map/ppermute | solution.py:81
  104.0 1.9 %collective-permute-done.9 = f32[2,64,1024]{2,1,0:T(8,128)} collective-permute-done((f32[2,64,1024]{2,1,0:T(8,128)}, f32[2,64,1024]{2,1,0:T(8,128)}, u32[]{:S(2)}, u32[]{:S(2)}) %collective-permute-start.9) | collective-permute-done | bytes 524320 | tf_op jit(solution)/shard_map/ppermute | solution.py:81
  105.8 2.4 %copy.33 = f32[2,64,1024]{1,2,0:T(8,128)} copy(f32[2,64,1024]{2,1,0:T(8,128)} %collective-permute-done.9) | data formatting | bytes 1048576 | tf_op jit(solution)/shard_map/ppermute | solution.py:81
  108.2 1.7 %bitcast_add_fusion = f32[2,64,1024]{1,2,0:T(8,128)S(1)} fusion(f32[2,64,1024]{1,2,0:T(8,128)} %copy.33, f32[2,1,64,1024]{2,3,0,1:T(8,128)S(1)} %copy.39, f32[2,1,64,1024]{2,3,0,1:T(8,128)} %copy.40, pred[]{:T(512)S(6)} %eq.87), kind=kLoop, calls=%fused_computation.4 | loop fusion | flops 262144 | bytes 2097153 | tf_op jit(solution)/shard_map/add | solution.py:81
  109.9 1.0 copy-done.3
  110.9 0.9 select_bitcast_fusion.1
  111.7 1.2 collective-permute-start.10
  113.0 1.1 copy.34
  114.1 11.3 %collective-permute-done.10 = f32[64,1024]{0,1:T(8,128)S(1)} collective-permute-done((f32[64,1024]{0,1:T(8,128)}, f32[64,1024]{0,1:T(8,128)S(1)}, u32[]{:S(2)}, u32[]{:S(2)}) %collective-permute-start.10) | collective-permute-done | bytes 262176 | tf_op jit(solution)/shard_map/ppermute | solution.py:84
  125.4 1.3 bitcast_add_fusion.1
  127.4 1.8 %convolution_add_fusion = f32[256,768]{1,0:T(8,128)S(1)} fusion(f32[256,768]{1,0:T(8,128)S(1)} %fusion.18, f32[1024,768]{1,0:T(8,128)S(1)} %copy-done.2, f32[512,1152]{1,0:T(8,128)S(1)} %gather_fusion), kind=kOutput, calls=%fused_computation.2 | convolution fusion | flops 1208156160 | bytes 5767168 | tf_op jit(solution)/shard_map/dot_general | solution.py:121
  129.3 0.9 collective-permute-start.11
  130.5 1.1 collective-permute-done.11
  131.7 1.3 collective-permute-start.12
  134.0 3.9 %collective-permute-done.12 = f32[64,768]{1,0:T(8,128)S(1)} collective-permute-done((f32[64,768]{1,0:T(8,128)S(1)}, f32[64,768]{1,0:T(8,128)S(1)}, u32[]{:S(2)}, u32[]{:S(2)}) %collective-permute-start.12) | collective-permute-done | bytes 196640 | tf_op jit(solution)/shard_map/ppermute | solution.py:84
  (72 shorter events, 8.7 us)
Async XLA Ops:
  0.6 10.2 %copy-start = (f32[1024,768]{1,0:T(8,128)S(1)}, f32[1024,768]{1,0:T(8,128)}, u32[]{:S(2)}) copy-start(f32[1024,768]{1,0:T(8,128)} %param.11) | copy-start | bytes 9437188
  0.6 5.6 %copy-start.4 = (f32[64,768]{1,0:T(8,128)S(1)}, f32[64,768]{1,0:T(8,128)}, u32[]{:S(2)}) copy-start(f32[64,768]{1,0:T(8,128)} %param.16) | copy-start | bytes 589828
  7.2 12.6 %copy-start.7 = (f32[1024]{0:T(1024)S(1)}, f32[1024]{0:T(1024)}, u32[]{:S(2)}) copy-start(f32[1024]{0:T(1024)} %param.13) | copy-start | bytes 12292
  7.2 12.6 %copy-start.8 = (s32[1024]{0:T(1024)S(1)}, s32[1024]{0:T(1024)}, u32[]{:S(2)}) copy-start(s32[1024]{0:T(1024)} %param.14) | copy-start | bytes 12292
  7.2 5.3 %collective-permute-start = (f32[16,1152]{1,0:T(8,128)S(1)}, f32[16,1152]{1,0:T(8,128)S(1)}, u32[]{:S(2)}, u32[]{:S(2)}) collective-permute-start(f32[16,1152]{1,0:T(8,128)S(1)} %get-tuple-element.34), channel_id=1, source_target_pairs={{0,4},{4,0},{8,12},{12,8},{16,20},{20,16},{24,28},{28,24},{32,36},... | collective-permute-start | bytes 221192 | tf_op jit(solution)/shard_map/ppermute | solution.py:44
  11.3 35.4 %copy-start.12 = (s32[64]{0:T(128)S(1)}, s32[64]{0:T(128)}, u32[]{:S(2)}) copy-start(s32[64]{0:T(128)} %constant.147.clone) | copy-start | bytes 772
  11.3 39.7 %copy-start.6 = (f32[1024]{0:T(1024)S(1)}, f32[1024]{0:T(1024)}, u32[]{:S(2)}) copy-start(f32[1024]{0:T(1024)} %param.12) | copy-start | bytes 12292
  12.6 9.9 %collective-permute-start.1 = (f32[32,1152]{1,0:T(8,128)S(1)}, f32[32,1152]{1,0:T(8,128)S(1)}, u32[]{:S(2)}, u32[]{:S(2)}) collective-permute-start(f32[32,1152]{1,0:T(8,128)S(1)} %pad_maximum_fusion.3), channel_id=1, source_target_pairs={{0,32},{4,36},{8,40},{12,44},{16,48},{20,52},{24,56},{28,60},{32,0... | collective-permute-start | bytes 442376 | tf_op jit(solution)/shard_map/ppermute | solution.py:44
  22.4 12.5 %collective-permute-start.2 = (f32[64,1152]{1,0:T(8,128)S(1)}, f32[64,1152]{1,0:T(8,128)S(1)}, u32[]{:S(2)}, u32[]{:S(2)}) collective-permute-start(f32[64,1152]{1,0:T(8,128)S(1)} %pad_maximum_fusion.2), channel_id=1, source_target_pairs={{0,136},{4,140},{8,144},{12,148},{16,152},{20,156},{24,160},{28,16... | collective-permute-start | bytes 884744 | tf_op jit(solution)/shard_map/ppermute | solution.py:44
  26.5 12.2 %collective-permute-start.3 = (f32[64,1152]{1,0:T(8,128)S(1)}, f32[64,1152]{1,0:T(8,128)S(1)}, u32[]{:S(2)}, u32[]{:S(2)}) collective-permute-start(f32[64,1152]{1,0:T(8,128)S(1)} %pad_maximum_fusion.2), channel_id=1, source_target_pairs={{0,184},{4,188},{8,128},{12,132},{16,136},{20,140},{24,144},{28,14... | collective-permute-start | bytes 884744 | tf_op jit(solution)/shard_map/ppermute | solution.py:44
  30.3 13.8 %collective-permute-start.4 = (f32[64,1152]{1,0:T(8,128)S(1)}, f32[64,1152]{1,0:T(8,128)S(1)}, u32[]{:S(2)}, u32[]{:S(2)}) collective-permute-start(f32[64,1152]{1,0:T(8,128)S(1)} %pad_maximum_fusion.2), channel_id=1, source_target_pairs={{0,16},{4,20},{8,24},{12,28},{16,32},{20,36},{24,40},{28,44},{32,4... | collective-permute-start | bytes 884744 | tf_op jit(solution)/shard_map/ppermute | solution.py:44
  45.0 24.3 %collective-permute-start.5 = (f32[256,1152]{1,0:T(8,128)}, f32[256,1152]{1,0:T(8,128)}, u32[]{:S(2)}, u32[]{:S(2)}) collective-permute-start(f32[256,1152]{1,0:T(8,128)} %get-tuple-element.18), channel_id=1, source_target_pairs={{0,64},{4,68},{8,72},{12,76},{16,80},{20,84},{24,88},{28,92},{32,9... | collective-permute-start | bytes 3538952 | tf_op jit(solution)/shard_map/ppermute | solution.py:44
  46.8 24.9 %collective-permute-start.6 = (f32[256,1152]{1,0:T(8,128)}, f32[256,1152]{1,0:T(8,128)}, u32[]{:S(2)}, u32[]{:S(2)}) collective-permute-start(f32[256,1152]{1,0:T(8,128)} %get-tuple-element.18), channel_id=1, source_target_pairs={{0,192},{4,196},{8,200},{12,204},{16,208},{20,212},{24,216},{28,22... | collective-permute-start | bytes 3538952 | tf_op jit(solution)/shard_map/ppermute | solution.py:44
  53.4 20.7 %collective-permute-start.7 = (f32[128,1152]{1,0:T(8,128)S(1)}, f32[128,1152]{1,0:T(8,128)S(1)}, u32[]{:S(2)}, u32[]{:S(2)}) collective-permute-start(f32[128,1152]{1,0:T(8,128)S(1)} %pad_maximum_fusion.1), channel_id=1, source_target_pairs={{0,8},{4,12},{8,16},{12,20},{16,24},{20,28},{24,32},{28,36},{32,40... | collective-permute-start | bytes 1769480 | tf_op jit(solution)/shard_map/ppermute | solution.py:44
  56.2 18.8 %collective-permute-start.8 = (f32[128,1152]{1,0:T(8,128)S(1)}, f32[128,1152]{1,0:T(8,128)S(1)}, u32[]{:S(2)}, u32[]{:S(2)}) collective-permute-start(f32[128,1152]{1,0:T(8,128)S(1)} %pad_maximum_fusion.1), channel_id=1, source_target_pairs={{0,56},{4,60},{8,0},{12,4},{16,8},{20,12},{24,16},{28,20},{32,24},... | collective-permute-start | bytes 1769480 | tf_op jit(solution)/shard_map/ppermute | solution.py:44
  81.2 1.9 %copy-start.1 = (f32[1024,768]{1,0:T(8,128)S(1)}, f32[1024,768]{1,0:T(8,128)}, u32[]{:S(2)}) copy-start(f32[1024,768]{1,0:T(8,128)} %multiply_add_fusion) | copy-start | bytes 9437188
  88.3 15.6 %copy-start.9 = (s32[2,64]{1,0:T(2,128)S(1)}, s32[2,64]{1,0:T(2,128)}, u32[]{:S(2)}) copy-start(s32[2,64]{1,0:T(2,128)} %param.20) | copy-start | bytes 1540
  88.4 15.6 %copy-start.10 = (f32[2,64]{1,0:T(2,128)S(1)}, f32[2,64]{1,0:T(2,128)}, u32[]{:S(2)}) copy-start(f32[2,64]{1,0:T(2,128)} %param.19) | copy-start | bytes 1540
  94.2 11.7 %collective-permute-start.9 = (f32[2,64,1024]{2,1,0:T(8,128)}, f32[2,64,1024]{2,1,0:T(8,128)}, u32[]{:S(2)}, u32[]{:S(2)}) collective-permute-start(f32[2,64,1024]{2,1,0:T(8,128)} %copy.32), channel_id=1, source_target_pairs={{0,1},{1,0},{2,3},{3,2},{4,5},{5,4},{6,7},{7,6},{8,9},{9,8},{10,11... | collective-permute-start | bytes 1572872 | tf_op jit(solution)/shard_map/ppermute | solution.py:81
  108.2 5.9 %copy-start.11 = (f32[2,64]{1,0:T(2,128)S(1)}, f32[2,64]{1,0:T(2,128)}, u32[]{:S(2)}) copy-start(f32[2,64]{1,0:T(2,128)} %param.18) | copy-start | bytes 1540
  109.9 1.0 copy-start.3
  111.7 13.7 %collective-permute-start.10 = (f32[64,1024]{0,1:T(8,128)}, f32[64,1024]{0,1:T(8,128)S(1)}, u32[]{:S(2)}, u32[]{:S(2)}) collective-permute-start(f32[64,1024]{0,1:T(8,128)} %select_bitcast_fusion.1), channel_id=1, source_target_pairs={{0,2},{1,3},{2,0},{3,1},{4,6},{5,7},{6,4},{7,5},{8,10},{9,11},{10,... | collective-permute-start | bytes 786440 | tf_op jit(solution)/shard_map/ppermute | solution.py:84
  114.1 13.3 %copy-start.2 = (f32[1024,768]{1,0:T(8,128)S(1)}, f32[1024,768]{1,0:T(8,128)}, u32[]{:S(2)}) copy-start(f32[1024,768]{1,0:T(8,128)} %multiply_add_fusion) | copy-start | bytes 9437188
  129.3 8.6 %copy-start.5 = (f32[64,768]{1,0:T(8,128)S(1)}, f32[64,768]{1,0:T(8,128)}, u32[]{:S(2)}) copy-start(f32[64,768]{1,0:T(8,128)} %param.17) | copy-start | bytes 589828
  129.3 2.3 %collective-permute-start.11 = (f32[2,64,768]{2,1,0:T(8,128)S(1)}, f32[2,64,768]{2,1,0:T(8,128)S(1)}, u32[]{:S(2)}, u32[]{:S(2)}) collective-permute-start(f32[2,64,768]{2,1,0:T(8,128)S(1)} %select_bitcast_fusion.2), channel_id=1, source_target_pairs={{0,1},{1,0},{2,3},{3,2},{4,5},{5,4},{6,7},{7,6},{8,9},{9,8},{10,11... | collective-permute-start | bytes 1179656 | tf_op jit(solution)/shard_map/ppermute | solution.py:81
  131.7 6.2 %collective-permute-start.12 = (f32[64,768]{1,0:T(8,128)S(1)}, f32[64,768]{1,0:T(8,128)S(1)}, u32[]{:S(2)}, u32[]{:S(2)}) collective-permute-start(f32[64,768]{1,0:T(8,128)S(1)} %select_bitcast_fusion.3), channel_id=1, source_target_pairs={{0,2},{1,3},{2,0},{3,1},{4,6},{5,7},{6,4},{7,5},{8,10},{9,11},{10,... | collective-permute-start | bytes 589832 | tf_op jit(solution)/shard_map/ppermute | solution.py:84

commit v2 on v1

--- a/solution.py
+++ b/solution.py
@@ -1,6 +1,10 @@
+import functools
+
 import jax
 import jax.numpy as jnp
 from jax import lax
+from jax.experimental import pallas as pl
+from jax.experimental.pallas import tpu as pltpu
 from jax.sharding import PartitionSpec as P
 
 P_SIZE = 256
@@ -48,40 +52,83 @@
 
 
 def gather_tiles(block):
+    rows = block.shape[0]
     held, at = block, [(0, 0, 0)]
-    for step in ((0, 0, 1), (0, 4, 0)):
-        got, its = moved(held, at, step)
-        held, at = jnp.concatenate([held, got], 0), at + its
+    got, its = moved(held, at, (0, 4, 0))
+    held, at = jnp.concatenate([held, got], 0), at + its
     parts = [moved(held, at, step) for step in ((2, 1, 0), (2, -1, 0), (0, 2, 0))]
     held = jnp.concatenate([held] + [p[0] for p in parts], 0)
     at = at + parts[0][1] + parts[1][1] + parts[2][1]
     half = len(at) // 2
-    cut = half * block.shape[0]
-    last = [moved(held, at, step) for step in ((1, 0, 0), (-1, 0, 0))]
-    up, up_at = moved(held[:cut], at[:half], (0, 1, 0))
-    have = set(at) | {o for p in last for o in p[1]} | set(up_at)
-    low = [(y, (z + 1) % NZ, h) for y, z, h in at]
-    keep = [i for i, o in enumerate(low) if o not in have]
-    if keep == list(range(half)):
-        down, down_at = moved(held[:cut], at[:half], (0, -1, 0))
-    else:
-        down, down_at = moved(held[cut:], at[half:], (0, -1, 0))
-    arrays = [held] + [p[0] for p in last] + [up, down]
-    offsets = at + last[0][1] + last[1][1] + up_at + down_at
-    return arrays, offsets
-
-
-def scatter_sum(block):
-    me = lax.axis_index("narrow")
+    over = moved(held, at, (0, 0, 1))
+    ahead = moved(held, at, (1, 0, 0))
+    behind = moved(held, at, (-1, 0, 0))
+    up = moved(held[: half * rows], at[:half], (0, 1, 0))
+    down = moved(held[: half * rows], at[:half], (0, -1, 0))
+    early = [(held, at), over, ahead, behind, up, down]
+    cut, cut_at = over[0][: half * rows], over[1][:half]
+    late = [
+        moved(ahead[0], ahead[1], (0, 0, 1)),
+        moved(over[0], over[1], (-1, 0, 0)),
+        moved(cut, cut_at, (0, 1, 0)),
+        moved(cut, cut_at, (0, -1, 0)),
+    ]
+    return early, late
+
+
+def pick_kernel(index_ref, *refs, base, sizes, carried):
+    out_ref = refs[-1]
+    pieces = refs[: len(sizes)]
+    width = out_ref.shape[1]
+    step = 128
+    for low in range(0, width, 2 * step):
+        cols = slice(low, min(low + 2 * step, width))
+        total = refs[len(sizes)][:, cols] if carried else None
+        start = base
+        for ref, size in zip(pieces, sizes):
+            slot = start + lax.broadcasted_iota(jnp.int32, (index_ref.shape[0], size), 1)
+            hit = jnp.where(index_ref[...] == slot, 1.0, 0.0).astype(jnp.bfloat16)
+            value = ref[:, cols]
+            big = value.astype(jnp.bfloat16)
+            small = (value - big.astype(jnp.float32)).astype(jnp.bfloat16)
+            part = jnp.dot(hit, big, preferred_element_type=jnp.float32)
+            part = part + jnp.dot(hit, small, preferred_element_type=jnp.float32)
+            total = part if total is None else total + part
+            start += size
+        out_ref[:, cols] = total
+
+
+def pick_rows(index, pieces, base, carry):
+    sizes = [p.shape[0] for p in pieces]
+    width = pieces[0].shape[1]
+    count = index.shape[0]
+    args = [index.reshape(count, 1)] + list(pieces) + ([] if carry is None else [carry])
+    return pl.pallas_call(
+        functools.partial(pick_kernel, base=base, sizes=sizes, carried=carry is not None),
+        out_shape=jax.ShapeDtypeStruct((count, width), jnp.float32),
+        compiler_params=pltpu.CompilerParams(vmem_limit_bytes=48 * 2**20),
+        cost_estimate=pl.CostEstimate(
+            flops=4 * count * sum(sizes) * width,
+            bytes_accessed=4 * width * (sum(sizes) + 2 * count),
+            transcendentals=0,
+        ),
+    )(*args)
+
+
+def quarter_order(me):
     core, chip = me % 2, me // 2
-    rows = block.shape[0] // 4
-    block = block.reshape(2, 2, rows, block.shape[1])
-    mine = jnp.where(core == 0, block[:, 0], block[:, 1])
-    other = jnp.where(core == 0, block[:, 1], block[:, 0])
-    block = mine + lax.ppermute(other, "narrow", CORE)
-    mine = jnp.where(chip == 0, block[0], block[1])
-    other = jnp.where(chip == 0, block[1], block[0])
-    return mine + lax.ppermute(other, "narrow", CHIP)
+    return [(1 - chip) * 2 + 1 - core, chip * 2 + 1 - core, (1 - chip) * 2 + core, me]
+
+
+def in_quarters(rows, quarters, blocks):
+    return jnp.concatenate([lax.dynamic_slice_in_dim(rows, q * blocks, blocks) for q in quarters], 0)
+
+
+def finish_sum(send, keep):
+    half = keep.shape[0] // 2
+    got = lax.ppermute(send, "narrow", CORE)
+    away = lax.ppermute(keep[:half] + got[:half], "narrow", CHIP)
+    return keep[half:] + got[half:] + away
 
 
 def shards(
@@ -103,7 +150,8 @@
     slots_l = lax.dot_general(pick, prior_lt, dims, precision=EXACT)
     slots_a = lax.dot_general(pick, a_first, dims, precision=EXACT)
     block = jnp.concatenate([slots_l, jnp.pad(slots_a, ((0, 0), (0, 64)))], 1)
-    arrays, offsets = gather_tiles(block)
+    early, late = gather_tiles(block)
+    offsets = [o for piece in early + late for o in piece[1]]
     ty, tz, th = tile // (NZ * NH), tile // NH % NZ, tile % NH
     hy, hz, hh = here // (NZ * NH), here // NH % NZ, here % NH
     rel = ((ty - hy) % NY * NZ + (tz - hz) % NZ) * NH + (th - hh) % NH
@@ -113,21 +161,40 @@
     place = jnp.sum(
         jnp.where(rel[:, None] == jnp.arange(NY * NZ * NH)[None, :], jnp.array(place_of)[None, :], 0), 1
     )
-    chosen = jnp.take(jnp.concatenate(arrays, 0), place * CAP + rank, axis=0, mode="clip")
+    where = place * CAP + rank
+    quarters = quarter_order(lax.axis_index("narrow"))
+    where = jnp.concatenate([in_quarters(where[:P_SIZE], quarters, blocks), where[P_SIZE:]])
+    early_rows = CAP * sum(len(piece[1]) for piece in early)
+    chosen = pick_rows(where, [p[0] for p in early], 0, None)
+    chosen = pick_rows(where, [p[0] for p in late], early_rows, chosen)
     coupled_lt = couple(prior_lt, prior_d, prior_e, prior_pairs)
-    first, second = chosen[:P_SIZE, :k_local], chosen[P_SIZE:, :k_local]
     plain = (((1,), (0,)), ((), ()))
-    update_first = lax.dot_general(first, coupled_lt, plain, precision=HIGH)
-    update_second = lax.dot_general(second, coupled_lt, plain, precision=HIGH)
+    second = chosen[P_SIZE:, :k_local]
     coupled_second = couple_lanes(second, prior_d, prior_e, prior_pairs)
-    inner = lax.dot_general(first, coupled_second, dims, precision=HIGH)
-    summed = scatter_sum(jnp.concatenate([update_first, inner], 1))
-    a_crossed = chosen[P_SIZE:, k_local : k_local + blocks].T
+    halves = []
+    for low in (0, P_SIZE // 2):
+        part = chosen[low : low + P_SIZE // 2, :k_local]
+        halves.append(
+            jnp.concatenate(
+                [
+                    lax.dot_general(part, coupled_lt, plain, precision=HIGH),
+                    lax.dot_general(part, coupled_second, dims, precision=HIGH),
+                ],
+                1,
+            )
+        )
+    summed = finish_sum(*halves)
     w_first = a_first - summed[:, :tile_rows]
     l_first = couple(w_first, inv_d[0], inv_e[0], panel_pairs[0])
-    crossed = couple(a_crossed - summed[:, tile_rows:], inv_d[0], inv_e[0], panel_pairs[0])
-    correction = lax.dot_general(crossed, w_first, (((0,), (0,)), ((), ())), precision=HIGH)
-    w_second = a_second - scatter_sum(update_second + correction)
+    w_crossed = chosen[P_SIZE:, k_local : k_local + blocks] - summed[:, tile_rows:].T
+    crossed = couple_lanes(w_crossed, inv_d[0], inv_e[0], panel_pairs[0])
+    halves = []
+    for pair in (quarters[:2], quarters[2:]):
+        halves.append(
+            lax.dot_general(in_quarters(second, pair, blocks), coupled_lt, plain, precision=HIGH)
+            + lax.dot_general(in_quarters(crossed, pair, blocks), w_first, plain, precision=HIGH)
+        )
+    w_second = a_second - finish_sum(*halves)
     l_second = couple(w_second, inv_d[1], inv_e[1], panel_pairs[1])
     return (l_first, l_second)
 

time: 140 us -> 108 us (0.77)
  local copies, waits for them, and re-layouts: 31 us -> 8.44 us
  starting transfers between devices: 46.6 us -> 30.9 us
  Pallas kernels: 0 us -> 9.6 us
  matrix products: 8.57 us -> 14.3 us
  other arithmetic: 11.8 us -> 6.71 us
  waiting for transfers between devices: 39.7 us -> 36.6 us
    unnamed x39 -> x37, local copies, waits for them, and re-layouts: 16.9 us -> 6.09 us
    pallas_call x0 -> x2, Pallas kernels: none -> 9.6 us  [pick_rows(): pl.pallas_call(functools.partial(pick_kernel, base=base, sizes=sizes, car...]
    ppermute x9 -> x13, starting transfers between devices: 33.3 us -> 25.4 us  [moved(): got = lax.ppermute(block, 'wide', shift(*step))]
    ppermute x4, starting transfers between devices: 13.2 us -> 5.54 us  [the longest x2 4.75 us: finish_sum(): got = lax.ppermute(send, 'narrow', CORE)]
    gather x1 -> x0, local copies, waits for them, and re-layouts: 5.39 us -> none  [shards(): jnp.take(jnp.concatenate(arrays, 0), place * CAP + rank, axis=0, mode='cl...]
    dot_general x4 -> x8, matrix products: 4.98 us -> 9.6 us  [the longest x2 5.3 us: shards(): lax.dot_general(part, coupled_lt, plain, precision=HIGH)]
    ppermute x9 -> x13, waiting for transfers between devices: 21.6 us -> 18.9 us  [moved(): got = lax.ppermute(block, 'wide', shift(*step))]
    add x4 -> x5, other arithmetic: 3.03 us -> 0.53 us  [the longest x1 0.34 us: finish_sum(): return keep[half:] + got[half:] + away]
  transfers between devices with their start and end apart: 13 -> 17, of which waited for: 10 -> 7; matrix products, arithmetic and copies ran while one was open for 10% -> 12% of each run, Pallas kernels for 0% -> 5%
where the time goes in v2:
time: 108 us
  waiting for transfers between devices  36.6 us (34%)
  starting transfers between devices  30.9 us (29%)
  matrix products  14.3 us (13%)
  Pallas kernels  9.6 us (9%)
  local copies, waits for them, and re-layouts  8.44 us (8%)
  other arithmetic  6.71 us (6%)
  between operations  1.15 us (1%)
    ppermute x13, starting transfers between devices, moved(): got = lax.ppermute(block, 'wide', shift(*step))  25.4 us
    ppermute x13, waiting for transfers between devices, moved(): got = lax.ppermute(block, 'wide', shift(*step))  18.9 us
    ppermute x2, waiting for transfers between devices, finish_sum(): away = lax.ppermute(keep[:half] + got[:half], 'narrow', CHIP)  16.8 us
    pallas_call x2, Pallas kernels, pick_rows(): pl.pallas_call(functools.partial(pick_kernel, base=base, sizes=sizes, car...  9.6 us
    unnamed x37, local copies, waits for them, and re-layouts  6.09 us
    dot_general x2, matrix products, shards(): lax.dot_general(part, coupled_lt, plain, precision=HIGH)  5.3 us
    ppermute x2, starting transfers between devices, finish_sum(): got = lax.ppermute(send, 'narrow', CORE)  4.75 us
    dot_general x1, matrix products, shards(): slots_l = lax.dot_general(pick, prior_lt, dims, precision=EXACT)  3.47 us
  transfers between devices with their start and end apart: 17, of which 7 were waited for; matrix products, arithmetic and copies ran while one was open for 12% of the time, Pallas kernels for 5%

profile of v2, /device:TPU:1, one launch (start us, length us, event | category | flops | bytes accessed | tf_op | source)
XLA Modules:
  0.0 107.7 jit_solution(13380739369364763795)
XLA Ops:
  0.7 0.7 sign_compare_fusion.1
  1.4 0.7 remainder_bitcast_fusion
  2.1 0.2 convert_reduce_fusion
  2.5 1.3 %fusion.27 = f32[16,64]{1,0:T(8,128)S(1)} fusion(f32[64,768]{1,0:T(8,128)} %param.16, s32[16]{0:T(128)S(1)} %broadcast_add_fusion), kind=kOutput, calls=%fused_computation.50 | convolution fusion | flops 9449472 | bytes 200768 | tf_op jit(solution)/shard_map/dot_general | solution.py:151
  3.8 3.5 %fusion.28 = f32[16,1024]{1,0:T(8,128)S(1)} fusion(f32[1024,768]{1,0:T(8,128)} %param.11, s32[16]{0:T(128)S(1)} %broadcast_add_fusion), kind=kOutput, calls=%fused_computation.51 | convolution fusion | flops 151007232 | bytes 3211328 | tf_op jit(solution)/shard_map/dot_general | solution.py:150
  7.4 7.8 %collective-permute-start = (f32[16,1152]{1,0:T(8,128)S(1)}, f32[16,1152]{1,0:T(8,128)S(1)}, u32[]{:S(2)}, u32[]{:S(2)}) collective-permute-start(f32[16,1152]{1,0:T(8,128)S(1)} %get-tuple-element.30), channel_id=1, source_target_pairs={{0,32},{4,36},{8,40},{12,44},{16,48},{20,52},{24,56},{28,60},{32,0... | collective-permute-start | bytes 221192 | tf_op jit(solution)/shard_map/ppermute | solution.py:48
  15.2 0.5 fusion.49
  15.9 2.4 %multiply_add_fusion = f32[1024,768]{1,0:T(8,128)} fusion(f32[1023,768]{1,0:T(8,128)S(1)} %get-tuple-element.11, f32[1023,768]{1,0:T(8,128)S(1)} %get-tuple-element.10, f32[1024,768]{1,0:T(8,128)S(1)} %copy-done.4, f32[1024]{0:T(1024)S(1)} %pad_maximum_fusion.5, f32[1024]{0:T(1024)S(1)} %convert_multiply_fusion, f32[1024]{0:T(1024)S(1)} %copy-done.8), kind=kLoop, calls=%fused_computation | loop fusion | flops 3932160 | bytes 12589056 | tf_op jit(solution)/shard_map/add | solution.py:25
  18.4 1.3 %collective-permute-start.3 = (f32[32,1152]{1,0:T(8,128)S(1)}, f32[32,1152]{1,0:T(8,128)S(1)}, u32[]{:S(2)}, u32[]{:S(2)}) collective-permute-start(f32[32,1152]{1,0:T(8,128)S(1)} %pad_maximum_fusion.3), channel_id=1, source_target_pairs={{0,16},{4,20},{8,24},{12,28},{16,32},{20,36},{24,40},{28,44},{32,4... | collective-permute-start | bytes 442376 | tf_op jit(solution)/shard_map/ppermute | solution.py:48
  19.7 5.0 %collective-permute-start.2 = (f32[32,1152]{1,0:T(8,128)S(1)}, f32[32,1152]{1,0:T(8,128)S(1)}, u32[]{:S(2)}, u32[]{:S(2)}) collective-permute-start(f32[32,1152]{1,0:T(8,128)S(1)} %pad_maximum_fusion.3), channel_id=1, source_target_pairs={{0,184},{4,188},{8,128},{12,132},{16,136},{20,140},{24,144},{28,14... | collective-permute-start | bytes 442376 | tf_op jit(solution)/shard_map/ppermute | solution.py:48
  24.7 9.6 %collective-permute-done.1 = f32[32,1152]{1,0:T(8,128)S(1)} collective-permute-done((f32[32,1152]{1,0:T(8,128)S(1)}, f32[32,1152]{1,0:T(8,128)S(1)}, u32[]{:S(2)}, u32[]{:S(2)}) %collective-permute-start.1) | collective-permute-done | bytes 147488 | tf_op jit(solution)/shard_map/ppermute | solution.py:48
  34.3 2.8 %collective-permute-start.6 = (f32[128,1152]{1,0:T(8,128)S(1)}, f32[128,1152]{1,0:T(8,128)S(1)}, u32[]{:S(2)}, u32[]{:S(2)}) collective-permute-start(f32[128,1152]{1,0:T(8,128)S(1)} %constant_dynamic-update-slice_fusion.refs_0_), channel_id=1, source_target_pairs={{0,4},{4,0},{8,12},{12,8},{16,20},{20,16},{24,28},{28,24},{32,36},... | collective-permute-start | bytes 1769480 | tf_op jit(solution)/shard_map/ppermute | solution.py:48
  37.2 0.4 collective-permute-start.4
  37.6 2.3 %collective-permute-start.10 = (f32[128,1152]{1,0:T(8,128)S(1)}, f32[128,1152]{1,0:T(8,128)}, u32[]{:S(2)}, u32[]{:S(2)}) collective-permute-start(f32[128,1152]{1,0:T(8,128)S(1)} %constant_dynamic-update-slice_fusion.refs_0_), channel_id=1, source_target_pairs={{0,192},{4,196},{8,200},{12,204},{16,208},{20,212},{24,216},{28,22... | collective-permute-start | bytes 1769480 | tf_op jit(solution)/shard_map/ppermute | solution.py:48
  39.9 1.7 %collective-permute-start.12 = (f32[64,1152]{1,0:T(8,128)S(1)}, f32[64,1152]{1,0:T(8,128)S(1)}, u32[]{:S(2)}, u32[]{:S(2)}) collective-permute-start(f32[64,1152]{1,0:T(8,128)S(1)} %pad_maximum_fusion.2), channel_id=1, source_target_pairs={{0,56},{4,60},{8,0},{12,4},{16,8},{20,12},{24,16},{28,20},{32,24},... | collective-permute-start | bytes 884744 | tf_op jit(solution)/shard_map/ppermute | solution.py:48
  41.6 7.7 %collective-permute-done.6.refs_1_ = f32[128,1152]{1,0:T(8,128)S(1)} collective-permute-done((f32[128,1152]{1,0:T(8,128)S(1)}, f32[128,1152]{1,0:T(8,128)S(1)}, u32[]{:S(2)}, u32[]{:S(2)}) %collective-permute-start.6) | collective-permute-done | bytes 589856 | tf_op jit(solution)/shard_map/ppermute | solution.py:48
  49.3 0.8 collective-permute-start.7
  50.1 1.5 %collective-permute-done.4.refs_2_ = f32[128,1152]{1,0:T(8,128)} collective-permute-done((f32[128,1152]{1,0:T(8,128)S(1)}, f32[128,1152]{1,0:T(8,128)}, u32[]{:S(2)}, u32[]{:S(2)}) %collective-permute-start.4) | collective-permute-done | bytes 589856 | tf_op jit(solution)/shard_map/ppermute | solution.py:48
  51.6 1.4 %collective-permute-start.5 = (f32[128,1152]{1,0:T(8,128)}, f32[128,1152]{1,0:T(8,128)S(1)}, u32[]{:S(2)}, u32[]{:S(2)}) collective-permute-start(f32[128,1152]{1,0:T(8,128)} %collective-permute-done.4.refs_2_), channel_id=1, source_target_pairs={{0,4},{4,0},{8,12},{12,8},{16,20},{20,16},{24,28},{28,24},{32,36},... | collective-permute-start | bytes 1769480 | tf_op jit(solution)/shard_map/ppermute | solution.py:48
  52.9 0.7 slice.162
  53.7 2.0 %collective-permute-start.9 = (f32[64,1152]{1,0:T(8,128)}, f32[64,1152]{1,0:T(8,128)S(1)}, u32[]{:S(2)}, u32[]{:S(2)}) collective-permute-start(f32[64,1152]{1,0:T(8,128)} %slice.162), channel_id=1, source_target_pairs={{0,56},{4,60},{8,0},{12,4},{16,8},{20,12},{24,16},{28,20},{32,24},... | collective-permute-start | bytes 884744 | tf_op jit(solution)/shard_map/ppermute | solution.py:48
  55.7 0.7 copy-done.1
  56.5 0.9 copy.33
  57.7 1.0 copy-done.2
  58.7 5.2 %shard_map.122.refs_4_ = f32[512,1152]{1,0:T(8,128)S(1)} custom-call(s32[512,1]{1,0:T(8,128)S(1)} %copy.28.index_ref, f32[128,1152]{1,0:T(8,128)S(1)} %constant_dynamic-update-slice_fusion.refs_0_, f32[128,1152]{1,0:T(8,128)S(1)} %collective-permute-done.6.refs_1_, f32[128,1152]{1,0:T(8,128)} %collective-permute-done.4.refs_2_, ...), custom_call_target="tpu_custom_call" | custom-call | flops 1509949440 | bytes 7667712 | tf_op jit(solution)/shard_map/pallas_call | solution.py:106
  63.9 1.4 %copy-done = f32[512,1152]{1,0:T(8,128)} copy-done((f32[512,1152]{1,0:T(8,128)}, f32[512,1152]{1,0:T(8,128)S(1)}, u32[]{:S(2)}) %copy-start) | copy-done | bytes 2359320
  65.5 4.4 %shard_map.123 = f32[512,1152]{1,0:T(8,128)S(1)} custom-call(s32[512,1]{1,0:T(8,128)S(1)} %copy.28.index_ref, f32[128,1152]{1,0:T(8,128)S(1)} %collective-permute-done.5.refs_0_, f32[128,1152]{1,0:T(8,128)S(1)} %collective-permute-done.7.refs_1_, f32[64,1152]{1,0:T(8,128)S(1)} %collective-permute-done.8.refs_2_, ...), custom_call_target="tpu_custom_call" | custom-call | flops 905969664 | bytes 6488064 | tf_op jit(solution)/shard_map/pallas_call | solution.py:106
  69.9 0.4 fusion.51
  70.2 0.5 fusion.50
  70.8 0.6 fusion.10
  71.4 1.1 %copy-done.3 = f32[1024,768]{1,0:T(8,128)S(1)} copy-done((f32[1024,768]{1,0:T(8,128)S(1)}, f32[1024,768]{1,0:T(8,128)}, u32[]{:S(2)}) %copy-start.3) | copy-done | bytes 3145752
  72.6 2.6 %fusion.12 = f32[128,768]{0,1:T(8,128)S(1)} fusion(f32[1024,768]{1,0:T(8,128)S(1)} %copy-done.3, f32[512,1152]{1,0:T(8,128)S(1)} %shard_map.123), kind=kOutput, calls=%fused_computation.22 | convolution fusion | flops 603979776 | bytes 4063232 | tf_op jit(solution)/shard_map/dot_general | solution.py:180
  75.3 3.9 %collective-permute-start.13 = (f32[128,1024]{0,1:T(8,128)S(1)}, f32[128,1024]{0,1:T(8,128)S(1)}, u32[]{:S(2)}, u32[]{:S(2)}) collective-permute-start(f32[128,1024]{0,1:T(8,128)S(1)} %pad_maximum_fusion.1), channel_id=1, source_target_pairs={{0,1},{1,0},{2,3},{3,2},{4,5},{5,4},{6,7},{7,6},{8,9},{9,8},{10,11... | collective-permute-start | bytes 1572872 | tf_op jit(solution)/shard_map/ppermute | solution.py:129
  79.1 1.2 %fusion.6 = f32[128,768]{1,0:T(8,128)S(1)} fusion(f32[1024,768]{1,0:T(8,128)S(1)} %copy-done.3, f32[64,1024]{1,0:T(8,128)S(1)} %get-tuple-element.19, f32[64,1024]{1,0:T(8,128)S(1)} %get-tuple-element.17), kind=kOutput, calls=%fused_computation.16 | convolution fusion | flops 604110848 | bytes 4063232 | tf_op jit(solution)/shard_map/dot_general | solution.py:194
  80.4 0.6 fusion.14
  81.0 2.7 %fusion.16 = f32[128,768]{0,1:T(8,128)S(1)} fusion(f32[1024,768]{1,0:T(8,128)S(1)} %copy-done.3, f32[512,1152]{1,0:T(8,128)S(1)} %shard_map.123), kind=kOutput, calls=%fused_computation.26 | convolution fusion | flops 603979776 | bytes 4063232 | tf_op jit(solution)/shard_map/dot_general | solution.py:180
  83.7 0.4 collective-permute-start.14
  84.1 1.2 %fusion.2 = f32[128,768]{1,0:T(8,128)S(1)} fusion(f32[1024,768]{1,0:T(8,128)S(1)} %copy-done.3, f32[64,1024]{1,0:T(8,128)S(1)} %get-tuple-element.18, f32[64,1024]{1,0:T(8,128)S(1)} %get-tuple-element.16), kind=kOutput, calls=%fused_computation.12 | convolution fusion | flops 604110848 | bytes 4063232 | tf_op jit(solution)/shard_map/dot_general | solution.py:194
  85.3 12.0 %collective-permute-done.14 = f32[64,1024]{0,1:T(8,128)S(1)} collective-permute-done((f32[64,1024]{0,1:T(8,128)S(1)}, f32[64,1024]{0,1:T(8,128)S(1)}, u32[]{:S(2)}, u32[]{:S(2)}) %collective-permute-start.14) | collective-permute-done | bytes 262176 | tf_op jit(solution)/shard_map/ppermute | solution.py:130
  97.4 0.3 fusion.1
  98.0 0.3 convolution_add_fusion
  98.4 0.9 collective-permute-start.15
  99.4 0.3 convolution_add_fusion.1
  99.8 0.8 collective-permute-done.15
  100.6 0.4 collective-permute-start.16
  101.2 0.8 copy.34
  102.0 4.8 %collective-permute-done.16 = f32[64,768]{1,0:T(8,128)S(1)} collective-permute-done((f32[64,768]{1,0:T(8,128)S(1)}, f32[64,768]{1,0:T(8,128)S(1)}, u32[]{:S(2)}, u32[]{:S(2)}) %collective-permute-start.16) | collective-permute-done | bytes 196640 | tf_op jit(solution)/shard_map/ppermute | solution.py:130
  106.9 0.8 multiply_add_fusion.3
  (82 shorter events, 2.1 us)
Async XLA Ops:
  2.4 12.9 %copy-start.4 = (f32[1024,768]{1,0:T(8,128)S(1)}, f32[1024,768]{1,0:T(8,128)}, u32[]{:S(2)}) copy-start(f32[1024,768]{1,0:T(8,128)} %param.11) | copy-start | bytes 9437188
  7.3 8.4 %copy-start.14 = (s32[64]{0:T(128)S(1)}, s32[64]{0:T(128)}, u32[]{:S(2)}) copy-start(s32[64]{0:T(128)} %constant.147.clone) | copy-start | bytes 772
  7.3 8.5 %copy-start.11 = (s32[2,64]{1,0:T(2,128)S(1)}, s32[2,64]{1,0:T(2,128)}, u32[]{:S(2)}) copy-start(s32[2,64]{1,0:T(2,128)} %param.20) | copy-start | bytes 1540
  7.3 8.5 %copy-start.12 = (f32[2,64]{1,0:T(2,128)S(1)}, f32[2,64]{1,0:T(2,128)}, u32[]{:S(2)}) copy-start(f32[2,64]{1,0:T(2,128)} %param.19) | copy-start | bytes 1540
  7.3 8.5 %copy-start.9 = (f32[1024]{0:T(1024)S(1)}, f32[1024]{0:T(1024)}, u32[]{:S(2)}) copy-start(f32[1024]{0:T(1024)} %param.13) | copy-start | bytes 12292
  7.4 8.5 %copy-start.10 = (s32[1024]{0:T(1024)S(1)}, s32[1024]{0:T(1024)}, u32[]{:S(2)}) copy-start(s32[1024]{0:T(1024)} %param.14) | copy-start | bytes 12292
  7.4 8.6 %copy-start.8 = (f32[1024]{0:T(1024)S(1)}, f32[1024]{0:T(1024)}, u32[]{:S(2)}) copy-start(f32[1024]{0:T(1024)} %param.12) | copy-start | bytes 12292
  7.4 11.0 %collective-permute-start = (f32[16,1152]{1,0:T(8,128)S(1)}, f32[16,1152]{1,0:T(8,128)S(1)}, u32[]{:S(2)}, u32[]{:S(2)}) collective-permute-start(f32[16,1152]{1,0:T(8,128)S(1)} %get-tuple-element.30), channel_id=1, source_target_pairs={{0,32},{4,36},{8,40},{12,44},{16,48},{20,52},{24,56},{28,60},{32,0... | collective-permute-start | bytes 221192 | tf_op jit(solution)/shard_map/ppermute | solution.py:48
  15.9 2.4 %copy-start.13 = (f32[2,64]{1,0:T(2,128)S(1)}, f32[2,64]{1,0:T(2,128)}, u32[]{:S(2)}) copy-start(f32[2,64]{1,0:T(2,128)} %param.18) | copy-start | bytes 1540
  15.9 40.5 %copy-start.6 = (f32[64,768]{1,0:T(8,128)S(1)}, f32[64,768]{1,0:T(8,128)}, u32[]{:S(2)}) copy-start(f32[64,768]{1,0:T(8,128)} %param.16) | copy-start | bytes 589828
  18.4 15.9 %collective-permute-start.3 = (f32[32,1152]{1,0:T(8,128)S(1)}, f32[32,1152]{1,0:T(8,128)S(1)}, u32[]{:S(2)}, u32[]{:S(2)}) collective-permute-start(f32[32,1152]{1,0:T(8,128)S(1)} %pad_maximum_fusion.3), channel_id=1, source_target_pairs={{0,16},{4,20},{8,24},{12,28},{16,32},{20,36},{24,40},{28,44},{32,4... | collective-permute-start | bytes 442376 | tf_op jit(solution)/shard_map/ppermute | solution.py:48
  19.7 14.6 %collective-permute-start.2 = (f32[32,1152]{1,0:T(8,128)S(1)}, f32[32,1152]{1,0:T(8,128)S(1)}, u32[]{:S(2)}, u32[]{:S(2)}) collective-permute-start(f32[32,1152]{1,0:T(8,128)S(1)} %pad_maximum_fusion.3), channel_id=1, source_target_pairs={{0,184},{4,188},{8,128},{12,132},{16,136},{20,140},{24,144},{28,14... | collective-permute-start | bytes 442376 | tf_op jit(solution)/shard_map/ppermute | solution.py:48
  24.6 9.6 %collective-permute-start.1 = (f32[32,1152]{1,0:T(8,128)S(1)}, f32[32,1152]{1,0:T(8,128)S(1)}, u32[]{:S(2)}, u32[]{:S(2)}) collective-permute-start(f32[32,1152]{1,0:T(8,128)S(1)} %pad_maximum_fusion.3), channel_id=1, source_target_pairs={{0,136},{4,140},{8,144},{12,148},{16,152},{20,156},{24,160},{28,16... | collective-permute-start | bytes 442376 | tf_op jit(solution)/shard_map/ppermute | solution.py:48
  34.3 15.0 %collective-permute-start.6 = (f32[128,1152]{1,0:T(8,128)S(1)}, f32[128,1152]{1,0:T(8,128)S(1)}, u32[]{:S(2)}, u32[]{:S(2)}) collective-permute-start(f32[128,1152]{1,0:T(8,128)S(1)} %constant_dynamic-update-slice_fusion.refs_0_), channel_id=1, source_target_pairs={{0,4},{4,0},{8,12},{12,8},{16,20},{20,16},{24,28},{28,24},{32,36},... | collective-permute-start | bytes 1769480 | tf_op jit(solution)/shard_map/ppermute | solution.py:48
  37.2 14.4 %collective-permute-start.4 = (f32[128,1152]{1,0:T(8,128)S(1)}, f32[128,1152]{1,0:T(8,128)}, u32[]{:S(2)}, u32[]{:S(2)}) collective-permute-start(f32[128,1152]{1,0:T(8,128)S(1)} %constant_dynamic-update-slice_fusion.refs_0_), channel_id=1, source_target_pairs={{0,64},{4,68},{8,72},{12,76},{16,80},{20,84},{24,88},{28,92},{32,9... | collective-permute-start | bytes 1769480 | tf_op jit(solution)/shard_map/ppermute | solution.py:48
  37.6 20.2 %collective-permute-start.10 = (f32[128,1152]{1,0:T(8,128)S(1)}, f32[128,1152]{1,0:T(8,128)}, u32[]{:S(2)}, u32[]{:S(2)}) collective-permute-start(f32[128,1152]{1,0:T(8,128)S(1)} %constant_dynamic-update-slice_fusion.refs_0_), channel_id=1, source_target_pairs={{0,192},{4,196},{8,200},{12,204},{16,208},{20,212},{24,216},{28,22... | collective-permute-start | bytes 1769480 | tf_op jit(solution)/shard_map/ppermute | solution.py:48
  39.9 13.8 %collective-permute-start.12 = (f32[64,1152]{1,0:T(8,128)S(1)}, f32[64,1152]{1,0:T(8,128)S(1)}, u32[]{:S(2)}, u32[]{:S(2)}) collective-permute-start(f32[64,1152]{1,0:T(8,128)S(1)} %pad_maximum_fusion.2), channel_id=1, source_target_pairs={{0,56},{4,60},{8,0},{12,4},{16,8},{20,12},{24,16},{28,20},{32,24},... | collective-permute-start | bytes 884744 | tf_op jit(solution)/shard_map/ppermute | solution.py:48
  41.5 14.2 %collective-permute-start.11 = (f32[64,1152]{1,0:T(8,128)S(1)}, f32[64,1152]{1,0:T(8,128)S(1)}, u32[]{:S(2)}, u32[]{:S(2)}) collective-permute-start(f32[64,1152]{1,0:T(8,128)S(1)} %pad_maximum_fusion.2), channel_id=1, source_target_pairs={{0,8},{4,12},{8,16},{12,20},{16,24},{20,28},{24,32},{28,36},{32,40... | collective-permute-start | bytes 884744 | tf_op jit(solution)/shard_map/ppermute | solution.py:48
  49.3 16.0 %collective-permute-start.7 = (f32[128,1152]{1,0:T(8,128)S(1)}, f32[128,1152]{1,0:T(8,128)S(1)}, u32[]{:S(2)}, u32[]{:S(2)}) collective-permute-start(f32[128,1152]{1,0:T(8,128)S(1)} %collective-permute-done.6.refs_1_), channel_id=1, source_target_pairs={{0,192},{4,196},{8,200},{12,204},{16,208},{20,212},{24,216},{28,22... | collective-permute-start | bytes 1769480 | tf_op jit(solution)/shard_map/ppermute | solution.py:48
  51.6 13.9 %collective-permute-start.5 = (f32[128,1152]{1,0:T(8,128)}, f32[128,1152]{1,0:T(8,128)S(1)}, u32[]{:S(2)}, u32[]{:S(2)}) collective-permute-start(f32[128,1152]{1,0:T(8,128)} %collective-permute-done.4.refs_2_), channel_id=1, source_target_pairs={{0,4},{4,0},{8,12},{12,8},{16,20},{20,16},{24,28},{28,24},{32,36},... | collective-permute-start | bytes 1769480 | tf_op jit(solution)/shard_map/ppermute | solution.py:48
  53.7 11.6 %collective-permute-start.9 = (f32[64,1152]{1,0:T(8,128)}, f32[64,1152]{1,0:T(8,128)S(1)}, u32[]{:S(2)}, u32[]{:S(2)}) collective-permute-start(f32[64,1152]{1,0:T(8,128)} %slice.162), channel_id=1, source_target_pairs={{0,56},{4,60},{8,0},{12,4},{16,8},{20,12},{24,16},{28,20},{32,24},... | collective-permute-start | bytes 884744 | tf_op jit(solution)/shard_map/ppermute | solution.py:48
  55.7 0.7 copy-start.1
  56.4 8.9 %collective-permute-start.8 = (f32[64,1152]{1,0:T(8,128)}, f32[64,1152]{1,0:T(8,128)S(1)}, u32[]{:S(2)}, u32[]{:S(2)}) collective-permute-start(f32[64,1152]{1,0:T(8,128)} %slice.162), channel_id=1, source_target_pairs={{0,8},{4,12},{8,16},{12,20},{16,24},{20,28},{24,32},{28,36},{32,40... | collective-permute-start | bytes 884744 | tf_op jit(solution)/shard_map/ppermute | solution.py:48
  57.7 1.0 copy-start.2
  63.9 1.4 %copy-start = (f32[512,1152]{1,0:T(8,128)}, f32[512,1152]{1,0:T(8,128)S(1)}, u32[]{:S(2)}) copy-start(f32[512,1152]{1,0:T(8,128)S(1)} %shard_map.122.refs_4_) | copy-start | bytes 7077892
  70.7 1.9 %copy-start.3 = (f32[1024,768]{1,0:T(8,128)S(1)}, f32[1024,768]{1,0:T(8,128)}, u32[]{:S(2)}) copy-start(f32[1024,768]{1,0:T(8,128)} %multiply_add_fusion) | copy-start | bytes 9437188
  75.3 8.4 %collective-permute-start.13 = (f32[128,1024]{0,1:T(8,128)S(1)}, f32[128,1024]{0,1:T(8,128)S(1)}, u32[]{:S(2)}, u32[]{:S(2)}) collective-permute-start(f32[128,1024]{0,1:T(8,128)S(1)} %pad_maximum_fusion.1), channel_id=1, source_target_pairs={{0,1},{1,0},{2,3},{3,2},{4,5},{5,4},{6,7},{7,6},{8,9},{9,8},{10,11... | collective-permute-start | bytes 1572872 | tf_op jit(solution)/shard_map/ppermute | solution.py:129
  83.7 13.6 %collective-permute-start.14 = (f32[64,1024]{0,1:T(8,128)S(1)}, f32[64,1024]{0,1:T(8,128)S(1)}, u32[]{:S(2)}, u32[]{:S(2)}) collective-permute-start(f32[64,1024]{0,1:T(8,128)S(1)} %slice_add_fusion), channel_id=1, source_target_pairs={{0,2},{1,3},{2,0},{3,1},{4,6},{5,7},{6,4},{7,5},{8,10},{9,11},{10,... | collective-permute-start | bytes 786440 | tf_op jit(solution)/shard_map/ppermute | solution.py:130
  84.1 13.6 %copy-start.5 = (f32[64,768]{0,1:T(8,128)S(1)}, f32[64,768]{0,1:T(8,128)}, u32[]{:S(2)}) copy-start(f32[64,768]{0,1:T(8,128)} %copy.33) | copy-start | bytes 589828
  98.0 8.8 %copy-start.7 = (f32[64,768]{1,0:T(8,128)S(1)}, f32[64,768]{1,0:T(8,128)}, u32[]{:S(2)}) copy-start(f32[64,768]{1,0:T(8,128)} %param.17) | copy-start | bytes 589828
  98.4 2.2 %collective-permute-start.15 = (f32[128,768]{1,0:T(8,128)S(1)}, f32[128,768]{1,0:T(8,128)S(1)}, u32[]{:S(2)}, u32[]{:S(2)}) collective-permute-start(f32[128,768]{1,0:T(8,128)S(1)} %convolution_add_fusion), channel_id=1, source_target_pairs={{0,1},{1,0},{2,3},{3,2},{4,5},{5,4},{6,7},{7,6},{8,9},{9,8},{10,11... | collective-permute-start | bytes 1179656 | tf_op jit(solution)/shard_map/ppermute | solution.py:129
  100.6 6.2 %collective-permute-start.16 = (f32[64,768]{1,0:T(8,128)S(1)}, f32[64,768]{1,0:T(8,128)S(1)}, u32[]{:S(2)}, u32[]{:S(2)}) collective-permute-start(f32[64,768]{1,0:T(8,128)S(1)} %slice_add_fusion.2), channel_id=1, source_target_pairs={{0,2},{1,3},{2,0},{3,1},{4,6},{5,7},{6,4},{7,5},{8,10},{9,11},{10,... | collective-permute-start | bytes 589832 | tf_op jit(solution)/shard_map/ppermute | solution.py:130

commit v3 on v2

v3 whole, which is shorter than its diff:
```python
import functools

import jax
import jax.numpy as jnp
from jax import lax
from jax.experimental import pallas as pl
from jax.experimental.pallas import tpu as pltpu
from jax.sharding import PartitionSpec as P

P_SIZE = 256
CAP = 16
NY, NZ, NH = 4, 8, 2
CORE = [(0, 1), (1, 0), (2, 3), (3, 2)]
CHIP = [(0, 2), (1, 3), (2, 0), (3, 1)]
HIGH = lax.Precision.HIGH


def couple(block, diag, off, pairs):
    joined = off * pairs.astype(jnp.float32)
    zero_row = jnp.zeros_like(block[:1])
    after = jnp.concatenate([block[1:], zero_row], 0)
    before = jnp.concatenate([zero_row, block[:-1]], 0)
    lower = jnp.concatenate([jnp.zeros_like(joined[:1]), joined[:-1]], 0)
    return diag[:, None] * block + joined[:, None] * after + lower[:, None] * before


def couple_lanes(block, diag, off, pairs):
    joined = off * pairs.astype(jnp.float32)
    zero = jnp.zeros_like(block[:, :1])
    after = jnp.concatenate([block[:, 1:], zero], 1)
    before = jnp.concatenate([zero, block[:, :-1]], 1)
    lower = jnp.concatenate([jnp.zeros_like(joined[:1]), joined[:-1]], 0)
    return diag[None, :] * block + joined[None, :] * after + lower[None, :] * before


def shift(dy, dz, dh):
    pairs = []
    for y in range(NY):
        for z in range(NZ):
            for h in range(NH):
                to = ((y + dy) % NY * NZ + (z + dz) % NZ) * NH + (h + dh) % NH
                pairs.append(((y * NZ + z) * NH + h, to))
    return pairs


def moved(block, offsets, step):
    got = lax.ppermute(block, "wide", shift(*step))
    return got, [
        ((y - step[0]) % NY, (z - step[1]) % NZ, (h - step[2]) % NH) for y, z, h in offsets
    ]


def gather_tiles(block):
    rows = block.shape[0]
    held, at = block, [(0, 0, 0)]
    for step in ((0, 4, 0), (0, 2, 0), (2, 1, 0)):
        got, its = moved(held, at, step)
        held, at = jnp.concatenate([held, got], 0), at + its
    half = len(at) // 2
    cut = half * rows
    ahead = moved(held, at, (1, 0, 0))
    behind = moved(held, at, (-1, 0, 0))
    over = moved(held, at, (0, 0, 1))
    up = moved(held[:cut], at[:half], (0, 1, 0))
    down = moved(held[cut:], at[half:], (0, -1, 0))
    early = [(held, at), ahead, behind, over, up, down]
    mixed = jnp.concatenate([ahead[0][cut:], behind[0][:cut]], 0)
    late = [
        moved(mixed, ahead[1][half:] + behind[1][:half], (0, 0, 1)),
        moved(over[0][:cut], over[1][:half], (1, 0, 0)),
        moved(over[0][cut:], over[1][half:], (-1, 0, 0)),
        moved(over[0][:cut], over[1][:half], (0, 1, 0)),
        moved(over[0][cut:], over[1][half:], (0, -1, 0)),
    ]
    return early, late


def split(value):
    big = value.astype(jnp.bfloat16)
    return big, (value - big.astype(jnp.float32)).astype(jnp.bfloat16)


def dot3(left, right, dims):
    def dot(x, y):
        return lax.dot_general(x, y, (dims, ((), ())), preferred_element_type=jnp.float32)

    return dot(left[0], right[0]) + (dot(left[0], right[1]) + dot(left[1], right[0]))


def slots_kernel(low_ref, row_ref, column_ref, lt_ref, a_ref, out_ref, pick_ref):
    step = pl.program_id(0)
    width = lt_ref.shape[1]
    depth = lt_ref.shape[0]
    count = row_ref.shape[1]

    def rows_of(value):
        total = None
        for _ in range(3):
            part = value.astype(jnp.bfloat16)
            value = value - part.astype(jnp.float32)
            got = lax.dot_general(
                part, pick_ref[...], (((1,), (1,)), ((), ())), preferred_element_type=jnp.float32
            )
            total = got if total is None else total + got
        return total

    @pl.when(step == 0)
    def _():
        low = low_ref[0]
        row = row_ref[...] - low
        mine = (row >= 0) & (row < width)
        before = lax.broadcasted_iota(jnp.int32, (count, count), 0) < lax.broadcasted_iota(
            jnp.int32, (count, count), 1
        )
        ones = jnp.broadcast_to(jnp.where(mine, 1.0, 0.0), (16, count)).astype(jnp.bfloat16)
        rank = jnp.dot(ones, before.astype(jnp.float32).astype(jnp.bfloat16), preferred_element_type=jnp.float32)
        slot = lax.broadcasted_iota(jnp.int32, (128, count), 0).astype(jnp.float32)
        hit = jnp.where((slot == rank[:1]) & mine, 1.0, 0.0).astype(jnp.bfloat16)
        column = column_ref[...] - low
        there = jnp.where(
            column == lax.broadcasted_iota(jnp.int32, (count, width), 1), 1.0, 0.0
        ).astype(jnp.bfloat16)
        pick_ref[...] = jnp.dot(hit, there, preferred_element_type=jnp.float32).astype(jnp.bfloat16)
        extra = rows_of(a_ref[...]).T
        total = pl.num_programs(0) * depth
        out_ref[:, total:] = jnp.concatenate([extra[:CAP], jnp.zeros_like(extra[:CAP])], 1)

    out_ref[:, pl.ds(pl.multiple_of(step * depth, 128), depth)] = rows_of(lt_ref[...]).T[:CAP]


def tile_slots(flat, low, prior_lt, a_first):
    k_local, width = prior_lt.shape
    blocks = a_first.shape[0]
    count = flat.shape[0]
    depth = k_local // 4
    return pl.pallas_call(
        slots_kernel,
        grid=(4,),
        in_specs=[
            pl.BlockSpec(memory_space=pltpu.SMEM),
            pl.BlockSpec((1, count), lambda i: (0, 0)),
            pl.BlockSpec((count, 1), lambda i: (0, 0)),
            pl.BlockSpec((depth, width), lambda i: (i, 0)),
            pl.BlockSpec((blocks, width), lambda i: (0, 0)),
        ],
        out_specs=pl.BlockSpec((CAP, k_local + 2 * blocks), lambda i: (0, 0)),
        out_shape=jax.ShapeDtypeStruct((CAP, k_local + 2 * blocks), jnp.float32),
        scratch_shapes=[pltpu.VMEM((128, width), jnp.bfloat16)],
        compiler_params=pltpu.CompilerParams(vmem_limit_bytes=32 * 2**20),
    )(low.reshape(1), flat.reshape(1, count), flat.reshape(count, 1), prior_lt, a_first)


def fill_parts(parts_ref, pieces):
    total = parts_ref.shape[0] // 2
    start = 0
    for ref in pieces:
        size = ref.shape[0]
        big, small = split(ref[...])
        parts_ref[start : start + size, :] = big
        parts_ref[total + start : total + start + size, :] = small
        start += size


def hits(index, base, total):
    slot = base + lax.broadcasted_iota(jnp.int32, (index.shape[0], total), 1)
    hit = jnp.where(index == slot, 1.0, 0.0).astype(jnp.bfloat16)
    return jnp.concatenate([hit, hit], 1)


def early_kernel(index_ref, *refs):
    *pieces, out_ref, parts_ref = refs
    fill_parts(parts_ref, pieces)
    total = parts_ref.shape[0] // 2
    hit = hits(index_ref[...], 0, total)
    for low in range(0, out_ref.shape[1], 384):
        out_ref[:, low : low + 384] = jnp.dot(
            hit, parts_ref[:, low : low + 384], preferred_element_type=jnp.float32
        )


def send_kernel(index_ref, weight_ref, carry_ref, lt_big_ref, lt_small_ref, *refs, base):
    *pieces, out_ref, second_ref, big_ref, small_ref, parts_ref = refs
    fill_parts(parts_ref, pieces)
    total = parts_ref.shape[0] // 2
    rows, k_local = out_ref.shape[0], lt_big_ref.shape[0]
    tile_rows = lt_big_ref.shape[1]
    hit = hits(index_ref[: rows + P_SIZE], base, total)
    taken = carry_ref[: rows + P_SIZE, :] + jnp.dot(
        hit, parts_ref[...], preferred_element_type=jnp.float32
    )
    second = taken[rows:]
    second_ref[...] = second
    second = second[:, :k_local]
    after = pltpu.roll(second, k_local - 1, 1)
    before = pltpu.roll(second, 1, 1)
    coupled = split(
        weight_ref[0:1, :] * second + weight_ref[1:2, :] * after + weight_ref[2:3, :] * before
    )
    big_ref[...] = coupled[0]
    small_ref[...] = coupled[1]
    first = split(taken[:rows, :k_local])
    out_ref[:, :tile_rows] = dot3(first, (lt_big_ref[...], lt_small_ref[...]), ((1,), (0,)))
    out_ref[:, tile_rows:] = dot3(first, coupled, ((1,), (1,)))


def keep_kernel(index_ref, carry_ref, lt_big_ref, lt_small_ref, parts_ref, big_ref, small_ref, out_ref, *, base):
    total = parts_ref.shape[0] // 2
    rows, k_local = out_ref.shape[0], lt_big_ref.shape[0]
    tile_rows = lt_big_ref.shape[1]
    hit = hits(index_ref[rows + P_SIZE :], base, total)
    taken = carry_ref[rows + P_SIZE :, :k_local] + jnp.dot(
        hit, parts_ref[:, :k_local], preferred_element_type=jnp.float32
    )
    first = split(taken)
    out_ref[:, :tile_rows] = dot3(first, (lt_big_ref[...], lt_small_ref[...]), ((1,), (0,)))
    out_ref[:, tile_rows:] = dot3(first, (big_ref[...], small_ref[...]), ((1,), (1,)))


def second_kernel(quarter_ref, second_ref, lt_big_ref, lt_small_ref, out_ref):
    k_local = lt_big_ref.shape[0]
    blocks = out_ref.shape[0] // 4
    for i in range(4):
        start = pl.multiple_of(quarter_ref[i] * blocks, blocks)
        rows = split(second_ref[pl.ds(start, blocks), :k_local])
        out_ref[i * blocks : (i + 1) * blocks, :] = dot3(
            rows, (lt_big_ref[...], lt_small_ref[...]), ((1,), (0,))
        )


def local_call(kernel, out_shape, flops, *args, scratch=(), smem=0):
    specs = [pl.BlockSpec(memory_space=pltpu.SMEM)] * smem
    specs += [pl.BlockSpec(memory_space=pltpu.VMEM)] * (len(args) - smem)
    return pl.pallas_call(
        kernel,
        in_specs=specs,
        out_shape=out_shape,
        scratch_shapes=list(scratch),
        compiler_params=pltpu.CompilerParams(vmem_limit_bytes=48 * 2**20),
        cost_estimate=pl.CostEstimate(
            flops=flops, bytes_accessed=4 * sum(x.size for x in args), transcendentals=0
        ),
    )(*args)


def quarter_order(me):
    core, chip = me % 2, me // 2
    return [(1 - chip) * 2 + 1 - core, chip * 2 + 1 - core, (1 - chip) * 2 + core, me]


def in_quarters(rows, quarters, blocks):
    return jnp.concatenate([lax.dynamic_slice_in_dim(rows, q * blocks, blocks) for q in quarters], 0)


def finish_sum(send, keep):
    half = keep.shape[0] // 2
    got = lax.ppermute(send, "narrow", CORE)
    away = lax.ppermute(keep[:half] + got[:half], "narrow", CHIP)
    return keep[half:] + got[half:] + away


def shards(
    prior_lt, prior_d, prior_e, prior_pairs, pivots, a_first, a_second, inv_d, inv_e, panel_pairs
):
    k_local, tile_rows = prior_lt.shape
    blocks = a_first.shape[0]
    here = lax.axis_index("wide")
    flat = pivots.reshape(-1)
    tile = flat // tile_rows
    count = flat.shape[0]
    order = jnp.arange(count)
    rank = jnp.sum((tile[:, None] == tile[None, :]) & (order[None, :] < order[:, None]), 1)
    block = tile_slots(flat, here * tile_rows, prior_lt, a_first)
    early, late = gather_tiles(block)
    offsets = [o for piece in early + late for o in piece[1]]
    ty, tz, th = tile // (NZ * NH), tile // NH % NZ, tile % NH
    hy, hz, hh = here // (NZ * NH), here // NH % NZ, here % NH
    rel = ((ty - hy) % NY * NZ + (tz - hz) % NZ) * NH + (th - hh) % NH
    place_of = [0] * (NY * NZ * NH)
    for i, (y, z, h) in enumerate(offsets):
        place_of[(y * NZ + z) * NH + h] = i
    place = jnp.sum(
        jnp.where(rel[:, None] == jnp.arange(NY * NZ * NH)[None, :], jnp.array(place_of)[None, :], 0), 1
    )
    where = place * CAP + rank
    quarters = quarter_order(lax.axis_index("narrow"))
    ordered = in_quarters(where[:P_SIZE], quarters, blocks)
    half = P_SIZE // 2
    where = jnp.concatenate([ordered[:half], where[P_SIZE:], ordered[half:]]).reshape(-1, 1)
    early_rows = CAP * sum(len(piece[1]) for piece in early)
    late_rows = CAP * sum(len(piece[1]) for piece in late)
    width = block.shape[1]
    wide = tile_rows + P_SIZE
    f32, b16 = jnp.float32, jnp.bfloat16
    shape = jax.ShapeDtypeStruct
    coupled_lt = couple(prior_lt, prior_d, prior_e, prior_pairs)
    rounded = lax.reduce_precision(coupled_lt, exponent_bits=8, mantissa_bits=7)
    lt_big, lt_small = rounded.astype(b16), (coupled_lt - rounded).astype(b16)
    joined = prior_e * prior_pairs.astype(f32)
    weights = jnp.stack([prior_d, joined, jnp.concatenate([jnp.zeros_like(joined[:1]), joined[:-1]])])
    carry = local_call(
        early_kernel,
        shape((2 * P_SIZE, width), f32),
        4 * 2 * P_SIZE * early_rows * width,
        where,
        *[piece[0] for piece in early],
        scratch=[pltpu.VMEM((2 * early_rows, width), b16)],
    )
    send, second, second_big, second_small, parts = local_call(
        functools.partial(send_kernel, base=early_rows),
        (
            shape((half, wide), f32),
            shape((P_SIZE, width), f32),
            shape((P_SIZE, k_local), b16),
            shape((P_SIZE, k_local), b16),
            shape((2 * late_rows, width), b16),
        ),
        4 * (half + P_SIZE) * late_rows * width + 6 * half * k_local * wide,
        where,
        weights,
        carry,
        lt_big,
        lt_small,
        *[piece[0] for piece in late],
    )
    keep = local_call(
        functools.partial(keep_kernel, base=early_rows),
        shape((half, wide), f32),
        4 * half * late_rows * width + 6 * half * k_local * wide,
        where,
        carry,
        lt_big,
        lt_small,
        parts,
        second_big,
        second_small,
    )
    summed = finish_sum(send, keep)
    update_second = local_call(
        second_kernel,
        shape((P_SIZE, tile_rows), f32),
        6 * P_SIZE * k_local * tile_rows,
        jnp.stack(quarters),
        second,
        lt_big,
        lt_small,
        smem=1,
    )
    w_first = a_first - summed[:, :tile_rows]
    l_first = couple(w_first, inv_d[0], inv_e[0], panel_pairs[0])
    w_crossed = second[:, k_local : k_local + blocks] - summed[:, tile_rows:].T
    crossed = couple_lanes(w_crossed, inv_d[0], inv_e[0], panel_pairs[0])
    plain = (((1,), (0,)), ((), ()))
    halves = []
    for low in (0, 2):
        rows = in_quarters(crossed, quarters[low : low + 2], blocks)
        part = update_second[low * blocks : (low + 2) * blocks]
        halves.append(part + lax.dot_general(rows, w_first, plain, precision=HIGH))
    w_second = a_second - finish_sum(*halves)
    l_second = couple(w_second, inv_d[1], inv_e[1], panel_pairs[1])
    return (l_first, l_second)


def solution(mesh):
    in_specs = (
        P("narrow", "wide"),
        P("narrow"),
        P("narrow"),
        P("narrow"),
        P(),
        P("narrow", "wide"),
        P("narrow", "wide"),
        P(None, "narrow"),
        P(None, "narrow"),
        P(None, "narrow"),
    )
    out_specs = (P("narrow", "wide"), P("narrow", "wide"))
    return jax.shard_map(shards, mesh=mesh, in_specs=in_specs, out_specs=out_specs, check_vma=False)
```

time: 108 us -> 123 us (1.14)
  local copies, waits for them, and re-layouts: 8.44 us -> 30 us
  matrix products: 14.3 us -> 0.88 us
  waiting for transfers between devices: 36.6 us -> 26.5 us
  Pallas kernels: 9.6 us -> 18.1 us
  other arithmetic: 6.71 us -> 13.7 us
    unnamed x37 -> x83, local copies, waits for them, and re-layouts: 6.09 us -> 22.6 us
    dot_general x10 -> x2, matrix products: 14.3 us -> 0.88 us  [shards(): halves.append(part + lax.dot_general(rows, w_first, plain, precision=HIGH))]
    ppermute x2, waiting for transfers between devices: 16.8 us -> 4.71 us  [finish_sum(): away = lax.ppermute(keep[:half] + got[:half], 'narrow', CHIP)]
    pallas_call x2 -> x5, Pallas kernels: 9.6 us -> 18.1 us  [the longest x4 15.2 us: local_call(): pl.pallas_call(kernel, in_specs=specs, out_shape=out_shape, scratch_shape...]
    convert_element_type x0 -> x2, other arithmetic: none -> 8.26 us  [shards(): lt_big, lt_small = (rounded.astype(b16), (coupled_lt - rounded).astype(b16))]
    pallas_call x0 -> x1, local copies, waits for them, and re-layouts: none -> 2.71 us  [local_call(): pl.pallas_call(kernel, in_specs=specs, out_shape=out_shape, scratch_shape...]
    slice x3, local copies, waits for them, and re-layouts: 0.67 us -> 3.27 us  [couple(): after = jnp.concatenate([block[1:], zero_row], 0)]
    add x3 -> x2, other arithmetic: 3.4 us -> 1.57 us  [couple(): diag[:, None] * block + joined[:, None] * after + lower[:, None] * before]
  transfers between devices with their start and end apart: 17 -> 17, of which waited for: 7 -> 5; matrix products, arithmetic and copies ran while one was open for 12% -> 15% of each run, Pallas kernels for 5% -> 8%
where the time goes in v3:
time: 123 us; the launch traced here: 122 us
  starting transfers between devices  31.5 us (26%)
  local copies, waits for them, and re-layouts  30 us (24%)
  waiting for transfers between devices  26.5 us (22%)
  Pallas kernels  18.1 us (15%)
  other arithmetic  13.7 us (11%)
    ppermute x13, starting transfers between devices, moved(): got = lax.ppermute(block, 'wide', shift(*step))  25.5 us
    unnamed x83, local copies, waits for them, and re-layouts  22.6 us
    ppermute x13, waiting for transfers between devices, moved(): got = lax.ppermute(block, 'wide', shift(*step))  20.7 us
    pallas_call x4, Pallas kernels, local_call(): pl.pallas_call(kernel, in_specs=specs, out_shape=out_shape, scratch_shape...  15.2 us
    convert_element_type x2, other arithmetic, shards(): lt_big, lt_small = (rounded.astype(b16), (coupled_lt - rounded).astype(b16))  8.26 us
    ppermute x2, waiting for transfers between devices, finish_sum(): away = lax.ppermute(keep[:half] + got[:half], 'narrow', CHIP)  4.71 us
    ppermute x2, starting transfers between devices, finish_sum(): got = lax.ppermute(send, 'narrow', CORE)  4.63 us
    slice x3, local copies, waits for them, and re-layouts, couple(): after = jnp.concatenate([block[1:], zero_row], 0)  3.27 us
  transfers between devices with their start and end apart: 17, of which 5 were waited for; matrix products, arithmetic and copies ran while one was open for 15% of the time, Pallas kernels for 8%

profile of v3, /device:TPU:1, one launch (start us, length us, event | category | flops | bytes accessed | tf_op | source)
XLA Modules:
  0.0 121.9 jit_solution(11876446481474896768)
XLA Ops:
  1.6 1.9 %copy-done = f32[1024,768]{1,0:T(8,128)S(1)} copy-done((f32[1024,768]{1,0:T(8,128)S(1)}, f32[1024,768]{1,0:T(8,128)}, u32[]{:S(2)}) %copy-start) | copy-done | bytes 3145752
  3.4 0.9 copy-done.9
  4.4 3.0 %shard_map.122 = f32[16,1152]{1,0:T(8,128)S(1)} custom-call(s32[1]{0:T(128)} %bitcast.2.low_ref, s32[1,512]{1,0:T(1,128)S(1)} %bitcast.38, s32[512,1]{1,0:T(8,128)S(1)} %bitcast.36, f32[1024,768]{1,0:T(8,128)S(1)} %copy-done, f32[64,768]{1,0:T(8,128)S(1)} %copy-done.9), custom_call_target="tpu_custom_call" | custom-call | tf_op jit(solution)/shard_map/pallas_call | solution.py:136
  7.3 7.8 %collective-permute-start = (f32[16,1152]{1,0:T(8,128)S(1)}, f32[16,1152]{1,0:T(8,128)S(1)}, u32[]{:S(2)}, u32[]{:S(2)}) collective-permute-start(f32[16,1152]{1,0:T(8,128)S(1)} %shard_map.122), channel_id=1, source_target_pairs={{0,32},{4,36},{8,40},{12,44},{16,48},{20,52},{24,56},{28,60},{32,0... | collective-permute-start | bytes 221192 | tf_op jit(solution)/shard_map/ppermute | solution.py:47
  15.2 3.2 %fusion.32 = (f32[1023,768]{1,0:T(8,128)}, f32[1023,768]{1,0:T(8,128)}) fusion(f32[1024,768]{1,0:T(8,128)S(1)} %copy-done.1), kind=kLoop, calls=%fused_computation.91 | loop fusion | bytes 12570624 | tf_op jit(solution)/shard_map/slice | solution.py:21
  18.9 5.0 %fusion = (bf16[1024,768]{1,0:T(8,128)(2,1)}, f32[1024,768]{1,0:T(8,128)}) fusion(f32[1023,768]{1,0:T(8,128)} %get-tuple-element.17, f32[1024]{0:T(1024)S(1)} %pad_maximum_fusion.5, f32[1023,768]{1,0:T(8,128)} %get-tuple-element.16, f32[1024]{0:T(1024)S(1)} %convert_multiply_fusion, f32[1024,768]{1,0:T(8,128)S(1)} %copy-done.1, f32[1024]{0:T(1024)S(1)} %copy-done.33), kind=kLoop, calls=%fused_computation.2 | loop fusion | flops 6291456 | bytes 14161920 | tf_op jit(solution)/shard_map/convert_element_type | solution.py:297
  24.0 1.3 %collective-permute-start.1 = (f32[32,1152]{1,0:T(8,128)S(1)}, f32[32,1152]{1,0:T(8,128)S(1)}, u32[]{:S(2)}, u32[]{:S(2)}) collective-permute-start(f32[32,1152]{1,0:T(8,128)S(1)} %pad_maximum_fusion.3), channel_id=1, source_target_pairs={{0,16},{4,20},{8,24},{12,28},{16,32},{20,36},{24,40},{28,44},{32,4... | collective-permute-start | bytes 442376 | tf_op jit(solution)/shard_map/ppermute | solution.py:47
  25.3 9.0 %collective-permute-done.1 = f32[32,1152]{1,0:T(8,128)S(1)} collective-permute-done((f32[32,1152]{1,0:T(8,128)S(1)}, f32[32,1152]{1,0:T(8,128)S(1)}, u32[]{:S(2)}, u32[]{:S(2)}) %collective-permute-start.1) | collective-permute-done | bytes 147488 | tf_op jit(solution)/shard_map/ppermute | solution.py:47
  34.3 1.5 %collective-permute-start.2 = (f32[64,1152]{1,0:T(8,128)S(1)}, f32[64,1152]{1,0:T(8,128)S(1)}, u32[]{:S(2)}, u32[]{:S(2)}) collective-permute-start(f32[64,1152]{1,0:T(8,128)S(1)} %pad_maximum_fusion.2), channel_id=1, source_target_pairs={{0,136},{4,140},{8,144},{12,148},{16,152},{20,156},{24,160},{28,16... | collective-permute-start | bytes 884744 | tf_op jit(solution)/shard_map/ppermute | solution.py:47
  35.8 9.4 %collective-permute-done.2 = f32[64,1152]{1,0:T(8,128)S(1)} collective-permute-done((f32[64,1152]{1,0:T(8,128)S(1)}, f32[64,1152]{1,0:T(8,128)S(1)}, u32[]{:S(2)}, u32[]{:S(2)}) %collective-permute-start.2) | collective-permute-done | bytes 294944 | tf_op jit(solution)/shard_map/ppermute | solution.py:47
  45.2 1.4 %collective-permute-start.3 = (f32[128,1152]{1,0:T(8,128)S(1)}, f32[128,1152]{1,0:T(8,128)S(1)}, u32[]{:S(2)}, u32[]{:S(2)}) collective-permute-start(f32[128,1152]{1,0:T(8,128)S(1)} %pad_maximum_fusion.refs_0_), channel_id=1, source_target_pairs={{0,64},{4,68},{8,72},{12,76},{16,80},{20,84},{24,88},{28,92},{32,9... | collective-permute-start | bytes 1769480 | tf_op jit(solution)/shard_map/ppermute | solution.py:47
  46.6 1.6 %collective-permute-start.4 = (f32[128,1152]{1,0:T(8,128)S(1)}, f32[128,1152]{1,0:T(8,128)S(1)}, u32[]{:S(2)}, u32[]{:S(2)}) collective-permute-start(f32[128,1152]{1,0:T(8,128)S(1)} %pad_maximum_fusion.refs_0_), channel_id=1, source_target_pairs={{0,192},{4,196},{8,200},{12,204},{16,208},{20,212},{24,216},{28,22... | collective-permute-start | bytes 1769480 | tf_op jit(solution)/shard_map/ppermute | solution.py:47
  48.3 2.8 %collective-permute-start.5 = (f32[128,1152]{1,0:T(8,128)S(1)}, f32[128,1152]{1,0:T(8,128)S(1)}, u32[]{:S(2)}, u32[]{:S(2)}) collective-permute-start(f32[128,1152]{1,0:T(8,128)S(1)} %pad_maximum_fusion.refs_0_), channel_id=1, source_target_pairs={{0,4},{4,0},{8,12},{12,8},{16,20},{20,16},{24,28},{28,24},{32,36},... | collective-permute-start | bytes 1769480 | tf_op jit(solution)/shard_map/ppermute | solution.py:47
  51.0 3.2 %reduce-precision_convert_fusion.lt_big_ref = bf16[1024,768]{1,0:T(8,128)(2,1)} fusion(f32[1024,768]{1,0:T(8,128)} %get-tuple-element.13), kind=kLoop, calls=%fused_computation.1 | loop fusion | flops 1572864 | bytes 4718592 | tf_op jit(solution)/shard_map/convert_element_type | solution.py:297
  54.3 2.7 %collective-permute-start.7 = (f32[64,1152]{1,0:T(8,128)S(1)}, f32[64,1152]{1,0:T(8,128)S(1)}, u32[]{:S(2)}, u32[]{:S(2)}) collective-permute-start(f32[64,1152]{1,0:T(8,128)S(1)} %collective-permute-done.2), channel_id=1, source_target_pairs={{0,56},{4,60},{8,0},{12,4},{16,8},{20,12},{24,16},{28,20},{32,24},... | collective-permute-start | bytes 884744 | tf_op jit(solution)/shard_map/ppermute | solution.py:47
  56.9 2.4 %collective-permute-done.3.refs_1_ = f32[128,1152]{1,0:T(8,128)S(1)} collective-permute-done((f32[128,1152]{1,0:T(8,128)S(1)}, f32[128,1152]{1,0:T(8,128)S(1)}, u32[]{:S(2)}, u32[]{:S(2)}) %collective-permute-start.3) | collective-permute-done | bytes 589856 | tf_op jit(solution)/shard_map/ppermute | solution.py:47
  59.4 1.0 pad_maximum_fusion.1
  60.4 2.7 %collective-permute-start.8 = (f32[128,1152]{1,0:T(8,128)}, f32[128,1152]{1,0:T(8,128)S(1)}, u32[]{:S(2)}, u32[]{:S(2)}) collective-permute-start(f32[128,1152]{1,0:T(8,128)} %pad_maximum_fusion.1), channel_id=1, source_target_pairs={{0,4},{4,0},{8,12},{12,8},{16,20},{20,16},{24,28},{28,24},{32,36},... | collective-permute-start | bytes 1769480 | tf_op jit(solution)/shard_map/ppermute | solution.py:47
  63.1 0.9 fusion.33
  64.0 2.5 %collective-permute-start.10 = (f32[64,1152]{1,0:T(8,128)}, f32[64,1152]{1,0:T(8,128)S(1)}, u32[]{:S(2)}, u32[]{:S(2)}) collective-permute-start(f32[64,1152]{1,0:T(8,128)} %get-tuple-element.18), channel_id=1, source_target_pairs={{0,192},{4,196},{8,200},{12,204},{16,208},{20,212},{24,216},{28,22... | collective-permute-start | bytes 884744 | tf_op jit(solution)/shard_map/ppermute | solution.py:47
  67.2 1.5 %collective-permute-start.11 = (f32[64,1152]{1,0:T(8,128)}, f32[64,1152]{1,0:T(8,128)S(1)}, u32[]{:S(2)}, u32[]{:S(2)}) collective-permute-start(f32[64,1152]{1,0:T(8,128)} %get-tuple-element.19), channel_id=1, source_target_pairs={{0,8},{4,12},{8,16},{12,20},{16,24},{20,28},{24,32},{28,36},{32,40... | collective-permute-start | bytes 884744 | tf_op jit(solution)/shard_map/ppermute | solution.py:47
  69.7 1.1 copy-done.22
  70.8 1.1 copy-done.24
  71.8 1.0 copy-done.26
  72.8 1.0 copy-done.28
  73.8 2.4 %shard_map.123.carry_ref = f32[512,1152]{1,0:T(8,128)S(1)} custom-call(s32[512,1]{1,0:T(8,128)S(1)} %copy.22.index_ref, f32[128,1152]{1,0:T(8,128)S(1)} %pad_maximum_fusion.refs_0_, f32[128,1152]{1,0:T(8,128)S(1)} %copy-done.22, f32[128,1152]{1,0:T(8,128)S(1)} %copy-done.24, f32[128,1152]{1,0:T(8,128)S(1)} %collective-permute-done.5.refs_3_, ...), custom_call_target="tpu_custom_call" | custom-call | flops 1509949440 | bytes 2951168 | tf_op jit(solution)/shard_map/pallas_call | solution.py:233
  76.2 1.4 %copy-done.4 = f32[512,1152]{1,0:T(8,128)} copy-done((f32[512,1152]{1,0:T(8,128)}, f32[512,1152]{1,0:T(8,128)S(1)}, u32[]{:S(2)}) %copy-start.4) | copy-done | bytes 2359320
  80.5 0.8 copy-done.11
  81.3 1.1 copy-done.12
  82.4 1.0 copy-done.14
  83.4 1.0 copy-done.16
  84.3 1.0 copy-done.18
  85.3 1.0 copy-done.20
  86.3 5.1 %shard_map.124 = (f32[128,1024]{1,0:T(8,128)S(1)}, f32[256,1152]{1,0:T(8,128)S(1)}, bf16[256,1024]{1,0:T(8,128)(2,1)S(1)}, bf16[256,1024]{1,0:T(8,128)(2,1)S(1)}, bf16[768,1152]{1,0:T(8,128)(2,1)}) custom-call(s32[512,1]{1,0:T(8,128)S(1)} %copy.22.index_ref, f32[3,1024]{1,0:T(4,128)S(1)} %pad_maximum_fusion.4.weight_ref, f32[512,1152]{1,0:T(8,128)} %copy-done.4, ...), custom_call_target="tpu_custom_call" | custom-call | flops 1484783616 | bytes 10434560 | tf_op jit(solution)/shard_map/pallas_call | solution.py:233
  91.4 1.0 copy-done.5
  92.4 4.4 %collective-permute-start.13 = (f32[128,1024]{1,0:T(8,128)S(1)}, f32[128,1024]{1,0:T(8,128)S(1)}, u32[]{:S(2)}, u32[]{:S(2)}) collective-permute-start(f32[128,1024]{1,0:T(8,128)S(1)} %get-tuple-element.10), channel_id=1, source_target_pairs={{0,1},{1,0},{2,3},{3,2},{4,5},{5,4},{6,7},{7,6},{8,9},{9,8},{10,11... | collective-permute-start | bytes 1572872 | tf_op jit(solution)/shard_map/ppermute | solution.py:256
  96.8 3.7 %shard_map.125 = f32[128,1024]{1,0:T(8,128)S(1)} custom-call(s32[512,1]{1,0:T(8,128)S(1)} %copy.22.index_ref, f32[512,1152]{1,0:T(8,128)} %copy-done.4, bf16[1024,768]{1,0:T(8,128)(2,1)S(1)} %copy-done.3, bf16[1024,768]{1,0:T(8,128)(2,1)S(1)} %copy-done.2, bf16[768,1152]{1,0:T(8,128)(2,1)} %get-tuple-element.7.parts_ref, ...), custom_call_target="tpu_custom_call" | custom-call | flops 1031798784 | bytes 14288896 | tf_op jit(solution)/shard_map/pallas_call | solution.py:233
  100.6 0.8 copy-done.7
  102.2 2.7 %copy.23 = f32[256,1152]{0,1:T(8,128)} copy(f32[256,1152]{1,0:T(8,128)} %copy-done.5) | data formatting | bytes 2359296 | tf_op jit(solution)/shard_map/pallas_call | solution.py:233
  104.9 1.3 %copy-done.6 = f32[256,1152]{1,0:T(8,128)S(1)} copy-done((f32[256,1152]{1,0:T(8,128)S(1)}, f32[256,1152]{1,0:T(8,128)}, u32[]{:S(2)}) %copy-start.6) | copy-done | bytes 1179672
  106.2 3.9 %shard_map.126 = f32[256,768]{1,0:T(8,128)S(1)} custom-call(s32[4]{0:T(128)S(1)} %pad_add_fusion.quarter_ref, f32[256,1152]{1,0:T(8,128)S(1)} %copy-done.6, bf16[1024,768]{1,0:T(8,128)(2,1)S(1)} %copy-done.3, bf16[1024,768]{1,0:T(8,128)(2,1)S(1)} %copy-done.2), custom_call_target="tpu_custom_call" | custom-call | flops 1207959552 | bytes 7471120 | tf_op jit(solution)/shard_map/pallas_call | solution.py:233
  110.1 1.0 fusion.2
  111.2 0.9 fusion.5
  113.5 1.1 collective-permute-done.15
  114.6 0.9 collective-permute-start.16
  115.5 0.8 multiply_add_fusion.2
  116.3 4.7 %collective-permute-done.16 = f32[64,768]{1,0:T(8,128)S(1)} collective-permute-done((f32[64,768]{1,0:T(8,128)S(1)}, f32[64,768]{1,0:T(8,128)S(1)}, u32[]{:S(2)}, u32[]{:S(2)}) %collective-permute-start.16) | collective-permute-done | bytes 196640 | tf_op jit(solution)/shard_map/ppermute | solution.py:257
  121.1 0.8 multiply_add_fusion.1
  (121 shorter events, 8.8 us)
Async XLA Ops:
  0.6 14.5 %copy-start.32 = (s32[2,256]{1,0:T(2,128)S(1)}, s32[2,256]{1,0:T(2,128)}, u32[]{:S(2)}) copy-start(s32[2,256]{1,0:T(2,128)} %param.15) | copy-start | bytes 6148
  1.5 1.9 %copy-start = (f32[1024,768]{1,0:T(8,128)S(1)}, f32[1024,768]{1,0:T(8,128)}, u32[]{:S(2)}) copy-start(f32[1024,768]{1,0:T(8,128)} %lt_ref.1) | copy-start | bytes 9437188
  3.4 0.9 copy-start.9
  4.4 10.8 %copy-start.1 = (f32[1024,768]{1,0:T(8,128)S(1)}, f32[1024,768]{1,0:T(8,128)}, u32[]{:S(2)}) copy-start(f32[1024,768]{1,0:T(8,128)} %lt_ref.1) | copy-start | bytes 9437188
  7.3 16.7 %collective-permute-start = (f32[16,1152]{1,0:T(8,128)S(1)}, f32[16,1152]{1,0:T(8,128)S(1)}, u32[]{:S(2)}, u32[]{:S(2)}) collective-permute-start(f32[16,1152]{1,0:T(8,128)S(1)} %shard_map.122), channel_id=1, source_target_pairs={{0,32},{4,36},{8,40},{12,44},{16,48},{20,52},{24,56},{28,60},{32,0... | collective-permute-start | bytes 221192 | tf_op jit(solution)/shard_map/ppermute | solution.py:47
  15.2 3.6 %copy-start.34 = (f32[1024]{0:T(1024)S(1)}, f32[1024]{0:T(1024)}, u32[]{:S(2)}) copy-start(f32[1024]{0:T(1024)} %param.13) | copy-start | bytes 12292
  15.2 3.6 %copy-start.35 = (s32[1024]{0:T(1024)S(1)}, s32[1024]{0:T(1024)}, u32[]{:S(2)}) copy-start(s32[1024]{0:T(1024)} %param.14) | copy-start | bytes 12292
  15.2 3.7 %copy-start.33 = (f32[1024]{0:T(1024)S(1)}, f32[1024]{0:T(1024)}, u32[]{:S(2)}) copy-start(f32[1024]{0:T(1024)} %param.12) | copy-start | bytes 12292
  18.9 5.0 %copy-start.39 = (s32[64]{0:T(128)S(1)}, s32[64]{0:T(128)}, u32[]{:S(2)}) copy-start(s32[64]{0:T(128)} %constant.137.clone) | copy-start | bytes 772
  18.9 16.9 %copy-start.36 = (s32[2,64]{1,0:T(2,128)S(1)}, s32[2,64]{1,0:T(2,128)}, u32[]{:S(2)}) copy-start(s32[2,64]{1,0:T(2,128)} %param.20) | copy-start | bytes 1540
  18.9 16.9 %copy-start.37 = (f32[2,64]{1,0:T(2,128)S(1)}, f32[2,64]{1,0:T(2,128)}, u32[]{:S(2)}) copy-start(f32[2,64]{1,0:T(2,128)} %param.19) | copy-start | bytes 1540
  24.0 10.2 %collective-permute-start.1 = (f32[32,1152]{1,0:T(8,128)S(1)}, f32[32,1152]{1,0:T(8,128)S(1)}, u32[]{:S(2)}, u32[]{:S(2)}) collective-permute-start(f32[32,1152]{1,0:T(8,128)S(1)} %pad_maximum_fusion.3), channel_id=1, source_target_pairs={{0,16},{4,20},{8,24},{12,28},{16,32},{20,36},{24,40},{28,44},{32,4... | collective-permute-start | bytes 442376 | tf_op jit(solution)/shard_map/ppermute | solution.py:47
  34.3 10.9 %collective-permute-start.2 = (f32[64,1152]{1,0:T(8,128)S(1)}, f32[64,1152]{1,0:T(8,128)S(1)}, u32[]{:S(2)}, u32[]{:S(2)}) collective-permute-start(f32[64,1152]{1,0:T(8,128)S(1)} %pad_maximum_fusion.2), channel_id=1, source_target_pairs={{0,136},{4,140},{8,144},{12,148},{16,152},{20,156},{24,160},{28,16... | collective-permute-start | bytes 884744 | tf_op jit(solution)/shard_map/ppermute | solution.py:47
  45.2 14.1 %collective-permute-start.3 = (f32[128,1152]{1,0:T(8,128)S(1)}, f32[128,1152]{1,0:T(8,128)S(1)}, u32[]{:S(2)}, u32[]{:S(2)}) collective-permute-start(f32[128,1152]{1,0:T(8,128)S(1)} %pad_maximum_fusion.refs_0_), channel_id=1, source_target_pairs={{0,64},{4,68},{8,72},{12,76},{16,80},{20,84},{24,88},{28,92},{32,9... | collective-permute-start | bytes 1769480 | tf_op jit(solution)/shard_map/ppermute | solution.py:47
  46.6 12.7 %collective-permute-start.4 = (f32[128,1152]{1,0:T(8,128)S(1)}, f32[128,1152]{1,0:T(8,128)S(1)}, u32[]{:S(2)}, u32[]{:S(2)}) collective-permute-start(f32[128,1152]{1,0:T(8,128)S(1)} %pad_maximum_fusion.refs_0_), channel_id=1, source_target_pairs={{0,192},{4,196},{8,200},{12,204},{16,208},{20,212},{24,216},{28,22... | collective-permute-start | bytes 1769480 | tf_op jit(solution)/shard_map/ppermute | solution.py:47
  48.3 14.8 %collective-permute-start.5 = (f32[128,1152]{1,0:T(8,128)S(1)}, f32[128,1152]{1,0:T(8,128)S(1)}, u32[]{:S(2)}, u32[]{:S(2)}) collective-permute-start(f32[128,1152]{1,0:T(8,128)S(1)} %pad_maximum_fusion.refs_0_), channel_id=1, source_target_pairs={{0,4},{4,0},{8,12},{12,8},{16,20},{20,16},{24,28},{28,24},{32,36},... | collective-permute-start | bytes 1769480 | tf_op jit(solution)/shard_map/ppermute | solution.py:47
  54.3 12.2 %collective-permute-start.6 = (f32[64,1152]{1,0:T(8,128)S(1)}, f32[64,1152]{1,0:T(8,128)S(1)}, u32[]{:S(2)}, u32[]{:S(2)}) collective-permute-start(f32[64,1152]{1,0:T(8,128)S(1)} %pad_maximum_fusion.2), channel_id=1, source_target_pairs={{0,8},{4,12},{8,16},{12,20},{16,24},{20,28},{24,32},{28,36},{32,40... | collective-permute-start | bytes 884744 | tf_op jit(solution)/shard_map/ppermute | solution.py:47
  54.3 14.4 %collective-permute-start.7 = (f32[64,1152]{1,0:T(8,128)S(1)}, f32[64,1152]{1,0:T(8,128)S(1)}, u32[]{:S(2)}, u32[]{:S(2)}) collective-permute-start(f32[64,1152]{1,0:T(8,128)S(1)} %collective-permute-done.2), channel_id=1, source_target_pairs={{0,56},{4,60},{8,0},{12,4},{16,8},{20,12},{24,16},{28,20},{32,24},... | collective-permute-start | bytes 884744 | tf_op jit(solution)/shard_map/ppermute | solution.py:47
  59.3 9.3 %copy-start.21 = (f32[128,1152]{1,0:T(8,128)}, f32[128,1152]{1,0:T(8,128)S(1)}, u32[]{:S(2)}) copy-start(f32[128,1152]{1,0:T(8,128)S(1)} %collective-permute-done.3.refs_1_) | copy-start | bytes 1769476
  59.4 9.3 %copy-start.23 = (f32[128,1152]{1,0:T(8,128)}, f32[128,1152]{1,0:T(8,128)S(1)}, u32[]{:S(2)}) copy-start(f32[128,1152]{1,0:T(8,128)S(1)} %collective-permute-done.4.refs_2_) | copy-start | bytes 1769476
  60.4 20.1 %collective-permute-start.8 = (f32[128,1152]{1,0:T(8,128)}, f32[128,1152]{1,0:T(8,128)S(1)}, u32[]{:S(2)}, u32[]{:S(2)}) collective-permute-start(f32[128,1152]{1,0:T(8,128)} %pad_maximum_fusion.1), channel_id=1, source_target_pairs={{0,4},{4,0},{8,12},{12,8},{16,20},{20,16},{24,28},{28,24},{32,36},... | collective-permute-start | bytes 1769480 | tf_op jit(solution)/shard_map/ppermute | solution.py:47
  64.0 13.7 %collective-permute-start.10 = (f32[64,1152]{1,0:T(8,128)}, f32[64,1152]{1,0:T(8,128)S(1)}, u32[]{:S(2)}, u32[]{:S(2)}) collective-permute-start(f32[64,1152]{1,0:T(8,128)} %get-tuple-element.18), channel_id=1, source_target_pairs={{0,192},{4,196},{8,200},{12,204},{16,208},{20,212},{24,216},{28,22... | collective-permute-start | bytes 884744 | tf_op jit(solution)/shard_map/ppermute | solution.py:47
  66.4 12.6 %collective-permute-start.12 = (f32[64,1152]{1,0:T(8,128)}, f32[64,1152]{1,0:T(8,128)S(1)}, u32[]{:S(2)}, u32[]{:S(2)}) collective-permute-start(f32[64,1152]{1,0:T(8,128)} %get-tuple-element.18), channel_id=1, source_target_pairs={{0,56},{4,60},{8,0},{12,4},{16,8},{20,12},{24,16},{28,20},{32,24},... | collective-permute-start | bytes 884744 | tf_op jit(solution)/shard_map/ppermute | solution.py:47
  67.2 11.2 %collective-permute-start.11 = (f32[64,1152]{1,0:T(8,128)}, f32[64,1152]{1,0:T(8,128)S(1)}, u32[]{:S(2)}, u32[]{:S(2)}) collective-permute-start(f32[64,1152]{1,0:T(8,128)} %get-tuple-element.19), channel_id=1, source_target_pairs={{0,8},{4,12},{8,16},{12,20},{16,24},{20,28},{24,32},{28,36},{32,40... | collective-permute-start | bytes 884744 | tf_op jit(solution)/shard_map/ppermute | solution.py:47
  69.4 10.4 %collective-permute-start.9 = (f32[64,1152]{1,0:T(8,128)}, f32[64,1152]{1,0:T(8,128)S(1)}, u32[]{:S(2)}, u32[]{:S(2)}) collective-permute-start(f32[64,1152]{1,0:T(8,128)} %get-tuple-element.19), channel_id=1, source_target_pairs={{0,64},{4,68},{8,72},{12,76},{16,80},{20,84},{24,88},{28,92},{32,9... | collective-permute-start | bytes 884744 | tf_op jit(solution)/shard_map/ppermute | solution.py:47
  69.7 1.1 copy-start.22
  70.8 1.1 copy-start.24
  71.8 1.0 copy-start.26
  72.8 1.0 copy-start.28
  76.2 1.4 %copy-start.4 = (f32[512,1152]{1,0:T(8,128)}, f32[512,1152]{1,0:T(8,128)S(1)}, u32[]{:S(2)}) copy-start(f32[512,1152]{1,0:T(8,128)S(1)} %shard_map.123.carry_ref) | copy-start | bytes 7077892
  81.3 1.1 copy-start.12
  82.4 1.0 copy-start.14
  83.4 1.0 copy-start.16
  84.3 1.0 copy-start.18
  85.3 1.0 copy-start.20
  86.3 10.5 %copy-start.38 = (f32[2,64]{1,0:T(2,128)S(1)}, f32[2,64]{1,0:T(2,128)}, u32[]{:S(2)}) copy-start(f32[2,64]{1,0:T(2,128)} %param.18) | copy-start | bytes 1540
  86.3 10.5 %copy-start.2 = (bf16[1024,768]{1,0:T(8,128)(2,1)S(1)}, bf16[1024,768]{1,0:T(8,128)(2,1)}, u32[]{:S(2)}) copy-start(bf16[1024,768]{1,0:T(8,128)(2,1)} %get-tuple-element.12.lt_small_ref) | copy-start | bytes 4718596
  86.3 10.5 %copy-start.3 = (bf16[1024,768]{1,0:T(8,128)(2,1)S(1)}, bf16[1024,768]{1,0:T(8,128)(2,1)}, u32[]{:S(2)}) copy-start(bf16[1024,768]{1,0:T(8,128)(2,1)} %reduce-precision_convert_fusion.lt_big_ref) | copy-start | bytes 4718596
  91.4 1.0 copy-start.5
  92.4 8.2 %collective-permute-start.13 = (f32[128,1024]{1,0:T(8,128)S(1)}, f32[128,1024]{1,0:T(8,128)S(1)}, u32[]{:S(2)}, u32[]{:S(2)}) collective-permute-start(f32[128,1024]{1,0:T(8,128)S(1)} %get-tuple-element.10), channel_id=1, source_target_pairs={{0,1},{1,0},{2,3},{3,2},{4,5},{5,4},{6,7},{7,6},{8,9},{9,8},{10,11... | collective-permute-start | bytes 1572872 | tf_op jit(solution)/shard_map/ppermute | solution.py:256
  101.4 8.7 %collective-permute-start.14 = (f32[64,1024]{1,0:T(8,128)S(1)}, f32[64,1024]{1,0:T(8,128)}, u32[]{:S(2)}, u32[]{:S(2)}) collective-permute-start(f32[64,1024]{1,0:T(8,128)S(1)} %slice_add_fusion.2), channel_id=1, source_target_pairs={{0,2},{1,3},{2,0},{3,1},{4,6},{5,7},{6,4},{7,5},{8,10},{9,11},{10,... | collective-permute-start | bytes 786440 | tf_op jit(solution)/shard_map/ppermute | solution.py:257
  104.9 1.3 %copy-start.6 = (f32[256,1152]{1,0:T(8,128)S(1)}, f32[256,1152]{1,0:T(8,128)}, u32[]{:S(2)}) copy-start(f32[256,1152]{1,0:T(8,128)} %copy-done.5) | copy-start | bytes 3538948
  106.2 3.9 %copy-start.8 = (f32[128,1024]{1,0:T(8,128)S(1)}, f32[128,1024]{1,0:T(8,128)}, u32[]{:S(2)}) copy-start(f32[128,1024]{1,0:T(8,128)} %copy-done.7) | copy-start | bytes 1572868
  106.2 3.9 %copy-start.30 = (f32[128,1024]{1,0:T(8,128)S(1)}, f32[128,1024]{1,0:T(8,128)}, u32[]{:S(2)}) copy-start(f32[128,1024]{1,0:T(8,128)} %copy-done.29) | copy-start | bytes 1572868
  106.2 4.9 %copy-start.10 = (f32[64,768]{1,0:T(8,128)S(1)}, f32[64,768]{1,0:T(8,128)}, u32[]{:S(2)}) copy-start(f32[64,768]{1,0:T(8,128)} %a_ref.1) | copy-start | bytes 589828
  111.1 9.9 %copy-start.31 = (f32[64,768]{1,0:T(8,128)S(1)}, f32[64,768]{1,0:T(8,128)}, u32[]{:S(2)}) copy-start(f32[64,768]{1,0:T(8,128)} %param.17) | copy-start | bytes 589828
  112.8 1.8 %collective-permute-start.15 = (f32[128,768]{1,0:T(8,128)S(1)}, f32[128,768]{1,0:T(8,128)S(1)}, u32[]{:S(2)}, u32[]{:S(2)}) collective-permute-start(f32[128,768]{1,0:T(8,128)S(1)} %slice_add_fusion), channel_id=1, source_target_pairs={{0,1},{1,0},{2,3},{3,2},{4,5},{5,4},{6,7},{7,6},{8,9},{9,8},{10,11... | collective-permute-start | bytes 1179656 | tf_op jit(solution)/shard_map/ppermute | solution.py:256
  114.6 6.4 %collective-permute-start.16 = (f32[64,768]{1,0:T(8,128)S(1)}, f32[64,768]{1,0:T(8,128)S(1)}, u32[]{:S(2)}, u32[]{:S(2)}) collective-permute-start(f32[64,768]{1,0:T(8,128)S(1)} %slice_add_fusion.4), channel_id=1, source_target_pairs={{0,2},{1,3},{2,0},{3,1},{4,6},{5,7},{6,4},{7,5},{8,10},{9,11},{10,... | collective-permute-start | bytes 589832 | tf_op jit(solution)/shard_map/ppermute | solution.py:257
  (9 other events, 6.8 us)

commit v4 on v3

--- a/solution.py
+++ b/solution.py
@@ -53,16 +53,18 @@
 def gather_tiles(block):
     rows = block.shape[0]
     held, at = block, [(0, 0, 0)]
-    for step in ((0, 4, 0), (0, 2, 0), (2, 1, 0)):
-        got, its = moved(held, at, step)
-        held, at = jnp.concatenate([held, got], 0), at + its
+    got, its = moved(held, at, (0, 4, 0))
+    held, at = jnp.concatenate([held, got], 0), at + its
+    parts = [moved(held, at, step) for step in ((2, 1, 0), (2, -1, 0), (0, 2, 0))]
+    held = jnp.concatenate([held] + [p[0] for p in parts], 0)
+    at = at + parts[0][1] + parts[1][1] + parts[2][1]
     half = len(at) // 2
     cut = half * rows
     ahead = moved(held, at, (1, 0, 0))
     behind = moved(held, at, (-1, 0, 0))
     over = moved(held, at, (0, 0, 1))
     up = moved(held[:cut], at[:half], (0, 1, 0))
-    down = moved(held[cut:], at[half:], (0, -1, 0))
+    down = moved(held[:cut], at[:half], (0, -1, 0))
     early = [(held, at), ahead, behind, over, up, down]
     mixed = jnp.concatenate([ahead[0][cut:], behind[0][:cut]], 0)
     late = [
@@ -70,7 +72,7 @@
         moved(over[0][:cut], over[1][:half], (1, 0, 0)),
         moved(over[0][cut:], over[1][half:], (-1, 0, 0)),
         moved(over[0][:cut], over[1][:half], (0, 1, 0)),
-        moved(over[0][cut:], over[1][half:], (0, -1, 0)),
+        moved(over[0][:cut], over[1][:half], (0, -1, 0)),
     ]
     return early, late
 
@@ -87,67 +89,97 @@
     return dot(left[0], right[0]) + (dot(left[0], right[1]) + dot(left[1], right[0]))
 
 
-def slots_kernel(low_ref, row_ref, column_ref, lt_ref, a_ref, out_ref, pick_ref):
-    step = pl.program_id(0)
-    width = lt_ref.shape[1]
-    depth = lt_ref.shape[0]
-    count = row_ref.shape[1]
+def slots_kernel(low_ref, pivots_ref, a_ref, lt_ref, out_ref, lt_buf, sems):
+    k_local, width = lt_ref.shape
+    depth = k_local // sems.shape[0]
+    copies = []
+    for i in range(sems.shape[0]):
+        rows = slice(i * depth, (i + 1) * depth)
+        copies.append(pltpu.make_async_copy(lt_ref.at[rows], lt_buf.at[rows], sems.at[i]))
+        copies[-1].start()
+    row = jnp.concatenate([pivots_ref[0:1, :], pivots_ref[1:2, :]], 1) - low_ref[0]
+    count = row.shape[1]
+    mine = (row >= 0) & (row < width)
+    before = lax.broadcasted_iota(jnp.int32, (count, count), 0) < lax.broadcasted_iota(
+        jnp.int32, (count, count), 1
+    )
+    ones = jnp.broadcast_to(jnp.where(mine, 1.0, 0.0), (16, count)).astype(jnp.bfloat16)
+    rank = jnp.dot(
+        ones, jnp.where(before, 1.0, 0.0).astype(jnp.bfloat16), preferred_element_type=jnp.float32
+    )
+    slot = lax.broadcasted_iota(jnp.int32, (128, count), 0).astype(jnp.float32)
+    hit = jnp.where((slot == rank[:1]) & mine, 1.0, 0.0).astype(jnp.bfloat16)
+    there = jnp.where(row == lax.broadcasted_iota(jnp.int32, (width, count), 0), 1.0, 0.0)
+    across = (((1,), (1,)), ((), ()))
+    pick = lax.dot_general(
+        hit, there.astype(jnp.bfloat16), across, preferred_element_type=jnp.float32
+    ).astype(jnp.bfloat16)
 
     def rows_of(value):
         total = None
         for _ in range(3):
             part = value.astype(jnp.bfloat16)
             value = value - part.astype(jnp.float32)
-            got = lax.dot_general(
-                part, pick_ref[...], (((1,), (1,)), ((), ())), preferred_element_type=jnp.float32
-            )
+            got = lax.dot_general(part, pick, across, preferred_element_type=jnp.float32)
             total = got if total is None else total + got
-        return total
-
-    @pl.when(step == 0)
-    def _():
-        low = low_ref[0]
-        row = row_ref[...] - low
-        mine = (row >= 0) & (row < width)
-        before = lax.broadcasted_iota(jnp.int32, (count, count), 0) < lax.broadcasted_iota(
-            jnp.int32, (count, count), 1
-        )
-        ones = jnp.broadcast_to(jnp.where(mine, 1.0, 0.0), (16, count)).astype(jnp.bfloat16)
-        rank = jnp.dot(ones, before.astype(jnp.float32).astype(jnp.bfloat16), preferred_element_type=jnp.float32)
-        slot = lax.broadcasted_iota(jnp.int32, (128, count), 0).astype(jnp.float32)
-        hit = jnp.where((slot == rank[:1]) & mine, 1.0, 0.0).astype(jnp.bfloat16)
-        column = column_ref[...] - low
-        there = jnp.where(
-            column == lax.broadcasted_iota(jnp.int32, (count, width), 1), 1.0, 0.0
-        ).astype(jnp.bfloat16)
-        pick_ref[...] = jnp.dot(hit, there, preferred_element_type=jnp.float32).astype(jnp.bfloat16)
-        extra = rows_of(a_ref[...]).T
-        total = pl.num_programs(0) * depth
-        out_ref[:, total:] = jnp.concatenate([extra[:CAP], jnp.zeros_like(extra[:CAP])], 1)
-
-    out_ref[:, pl.ds(pl.multiple_of(step * depth, 128), depth)] = rows_of(lt_ref[...]).T[:CAP]
-
-
-def tile_slots(flat, low, prior_lt, a_first):
+        return total.T[:CAP]
+
+    extra = rows_of(a_ref[...])
+    out_ref[:, k_local:] = jnp.concatenate([extra, jnp.zeros_like(extra)], 1)
+    for i, copy in enumerate(copies):
+        copy.wait()
+        rows = slice(i * depth, (i + 1) * depth)
+        out_ref[:, rows] = rows_of(lt_buf[rows, :])
+
+
+def tile_slots(pivots, low, prior_lt, a_first):
     k_local, width = prior_lt.shape
     blocks = a_first.shape[0]
-    count = flat.shape[0]
-    depth = k_local // 4
+    vmem = pl.BlockSpec(memory_space=pltpu.VMEM)
     return pl.pallas_call(
         slots_kernel,
+        in_specs=[
+            pl.BlockSpec(memory_space=pltpu.SMEM),
+            vmem,
+            vmem,
+            pl.BlockSpec(memory_space=pltpu.HBM),
+        ],
+        out_specs=vmem,
+        out_shape=jax.ShapeDtypeStruct((CAP, k_local + 2 * blocks), jnp.float32),
+        scratch_shapes=[pltpu.VMEM((k_local, width), jnp.float32), pltpu.SemaphoreType.DMA((4,))],
+        compiler_params=pltpu.CompilerParams(vmem_limit_bytes=20 * 2**20),
+    )(low.reshape(1), pivots, a_first, prior_lt)
+
+
+def couple_kernel(weight_ref, lt_ref, after_ref, big_ref, small_ref):
+    value = lt_ref[...]
+    rows = value.shape[0]
+    after = pltpu.roll(value, rows - 1, 0)
+    before = pltpu.roll(value, 1, 0)
+    mixed = weight_ref[:, 0:1] * value + weight_ref[:, 1:2] * after + weight_ref[:, 2:3] * before
+    big_ref[...], small_ref[...] = split(mixed)
+
+
+def coupled_parts(weights, prior_lt, following):
+    k_local, width = prior_lt.shape
+    depth = k_local // 4
+    block = pl.BlockSpec((depth, width), lambda i: (i, 0))
+    shape = jax.ShapeDtypeStruct((k_local, width), jnp.bfloat16)
+    return pl.pallas_call(
+        couple_kernel,
         grid=(4,),
         in_specs=[
-            pl.BlockSpec(memory_space=pltpu.SMEM),
-            pl.BlockSpec((1, count), lambda i: (0, 0)),
-            pl.BlockSpec((count, 1), lambda i: (0, 0)),
-            pl.BlockSpec((depth, width), lambda i: (i, 0)),
-            pl.BlockSpec((blocks, width), lambda i: (0, 0)),
+            pl.BlockSpec((depth, 3), lambda i: (i, 0)),
+            block,
+            pl.BlockSpec(memory_space=pl.ANY),
         ],
-        out_specs=pl.BlockSpec((CAP, k_local + 2 * blocks), lambda i: (0, 0)),
-        out_shape=jax.ShapeDtypeStruct((CAP, k_local + 2 * blocks), jnp.float32),
-        scratch_shapes=[pltpu.VMEM((128, width), jnp.bfloat16)],
-        compiler_params=pltpu.CompilerParams(vmem_limit_bytes=32 * 2**20),
-    )(low.reshape(1), flat.reshape(1, count), flat.reshape(count, 1), prior_lt, a_first)
+        out_specs=(block, block),
+        out_shape=(shape, shape),
+        compiler_params=pltpu.CompilerParams(vmem_limit_bytes=20 * 2**20),
+        cost_estimate=pl.CostEstimate(
+            flops=8 * k_local * width, bytes_accessed=8 * k_local * width, transcendentals=0
+        ),
+    )(weights, prior_lt, following)
 
 
 def fill_parts(parts_ref, pieces):
@@ -179,18 +211,18 @@
 
 
 def send_kernel(index_ref, weight_ref, carry_ref, lt_big_ref, lt_small_ref, *refs, base):
-    *pieces, out_ref, second_ref, big_ref, small_ref, parts_ref = refs
+    *pieces, out_ref, second_ref, entries_ref, big_ref, small_ref, keep_ref, parts_ref = refs
     fill_parts(parts_ref, pieces)
     total = parts_ref.shape[0] // 2
     rows, k_local = out_ref.shape[0], lt_big_ref.shape[0]
     tile_rows = lt_big_ref.shape[1]
-    hit = hits(index_ref[: rows + P_SIZE], base, total)
-    taken = carry_ref[: rows + P_SIZE, :] + jnp.dot(
-        hit, parts_ref[...], preferred_element_type=jnp.float32
-    )
-    second = taken[rows:]
+    hit = hits(index_ref[...], base, total)
+    taken = carry_ref[...] + jnp.dot(hit, parts_ref[...], preferred_element_type=jnp.float32)
+    keep_ref[...] = taken[rows + P_SIZE :, :k_local]
+    second = taken[rows : rows + P_SIZE]
+    entries_ref[...] = second[:, k_local:]
+    second = second[:, :k_local]
     second_ref[...] = second
-    second = second[:, :k_local]
     after = pltpu.roll(second, k_local - 1, 1)
     before = pltpu.roll(second, 1, 1)
     coupled = split(
@@ -203,39 +235,32 @@
     out_ref[:, tile_rows:] = dot3(first, coupled, ((1,), (1,)))
 
 
-def keep_kernel(index_ref, carry_ref, lt_big_ref, lt_small_ref, parts_ref, big_ref, small_ref, out_ref, *, base):
-    total = parts_ref.shape[0] // 2
-    rows, k_local = out_ref.shape[0], lt_big_ref.shape[0]
+def keep_kernel(taken_ref, lt_big_ref, lt_small_ref, big_ref, small_ref, out_ref):
     tile_rows = lt_big_ref.shape[1]
-    hit = hits(index_ref[rows + P_SIZE :], base, total)
-    taken = carry_ref[rows + P_SIZE :, :k_local] + jnp.dot(
-        hit, parts_ref[:, :k_local], preferred_element_type=jnp.float32
-    )
-    first = split(taken)
+    first = split(taken_ref[...])
     out_ref[:, :tile_rows] = dot3(first, (lt_big_ref[...], lt_small_ref[...]), ((1,), (0,)))
     out_ref[:, tile_rows:] = dot3(first, (big_ref[...], small_ref[...]), ((1,), (1,)))
 
 
-def second_kernel(quarter_ref, second_ref, lt_big_ref, lt_small_ref, out_ref):
-    k_local = lt_big_ref.shape[0]
+def second_kernel(quarter_ref, second_ref, lt_big_ref, lt_small_ref, out_ref, whole_ref):
     blocks = out_ref.shape[0] // 4
+    rows = split(second_ref[...])
+    whole_ref[...] = dot3(rows, (lt_big_ref[...], lt_small_ref[...]), ((1,), (0,)))
     for i in range(4):
         start = pl.multiple_of(quarter_ref[i] * blocks, blocks)
-        rows = split(second_ref[pl.ds(start, blocks), :k_local])
-        out_ref[i * blocks : (i + 1) * blocks, :] = dot3(
-            rows, (lt_big_ref[...], lt_small_ref[...]), ((1,), (0,))
-        )
+        out_ref[i * blocks : (i + 1) * blocks, :] = whole_ref[pl.ds(start, blocks), :]
 
 
 def local_call(kernel, out_shape, flops, *args, scratch=(), smem=0):
-    specs = [pl.BlockSpec(memory_space=pltpu.SMEM)] * smem
-    specs += [pl.BlockSpec(memory_space=pltpu.VMEM)] * (len(args) - smem)
+    vmem = pl.BlockSpec(memory_space=pltpu.VMEM)
+    specs = [pl.BlockSpec(memory_space=pltpu.SMEM)] * smem + [vmem] * (len(args) - smem)
     return pl.pallas_call(
         kernel,
         in_specs=specs,
+        out_specs=jax.tree.map(lambda _: vmem, out_shape),
         out_shape=out_shape,
         scratch_shapes=list(scratch),
-        compiler_params=pltpu.CompilerParams(vmem_limit_bytes=48 * 2**20),
+        compiler_params=pltpu.CompilerParams(vmem_limit_bytes=20 * 2**20),
         cost_estimate=pl.CostEstimate(
             flops=flops, bytes_accessed=4 * sum(x.size for x in args), transcendentals=0
         ),
@@ -269,7 +294,7 @@
     count = flat.shape[0]
     order = jnp.arange(count)
     rank = jnp.sum((tile[:, None] == tile[None, :]) & (order[None, :] < order[:, None]), 1)
-    block = tile_slots(flat, here * tile_rows, prior_lt, a_first)
+    block = tile_slots(pivots, here * tile_rows, prior_lt, a_first)
     early, late = gather_tiles(block)
     offsets = [o for piece in early + late for o in piece[1]]
     ty, tz, th = tile // (NZ * NH), tile // NH % NZ, tile % NH
@@ -292,11 +317,9 @@
     wide = tile_rows + P_SIZE
     f32, b16 = jnp.float32, jnp.bfloat16
     shape = jax.ShapeDtypeStruct
-    coupled_lt = couple(prior_lt, prior_d, prior_e, prior_pairs)
-    rounded = lax.reduce_precision(coupled_lt, exponent_bits=8, mantissa_bits=7)
-    lt_big, lt_small = rounded.astype(b16), (coupled_lt - rounded).astype(b16)
     joined = prior_e * prior_pairs.astype(f32)
     weights = jnp.stack([prior_d, joined, jnp.concatenate([jnp.zeros_like(joined[:1]), joined[:-1]])])
+    lt_big, lt_small = coupled_parts(weights.T, prior_lt, early[0][0])
     carry = local_call(
         early_kernel,
         shape((2 * P_SIZE, width), f32),
@@ -305,32 +328,32 @@
         *[piece[0] for piece in early],
         scratch=[pltpu.VMEM((2 * early_rows, width), b16)],
     )
-    send, second, second_big, second_small, parts = local_call(
+    send, second, entries, second_big, second_small, taken = local_call(
         functools.partial(send_kernel, base=early_rows),
         (
             shape((half, wide), f32),
-            shape((P_SIZE, width), f32),
+            shape((P_SIZE, k_local), f32),
+            shape((P_SIZE, width - k_local), f32),
             shape((P_SIZE, k_local), b16),
             shape((P_SIZE, k_local), b16),
-            shape((2 * late_rows, width), b16),
+            shape((half, k_local), f32),
         ),
-        4 * (half + P_SIZE) * late_rows * width + 6 * half * k_local * wide,
+        8 * P_SIZE * late_rows * width + 6 * half * k_local * wide,
         where,
         weights,
         carry,
         lt_big,
         lt_small,
         *[piece[0] for piece in late],
+        scratch=[pltpu.VMEM((2 * late_rows, width), b16)],
     )
     keep = local_call(
-        functools.partial(keep_kernel, base=early_rows),
+        keep_kernel,
         shape((half, wide), f32),
-        4 * half * late_rows * width + 6 * half * k_local * wide,
-        where,
-        carry,
+        6 * half * k_local * wide,
+        taken,
         lt_big,
         lt_small,
-        parts,
         second_big,
         second_small,
     )
@@ -343,11 +366,12 @@
         second,
         lt_big,
         lt_small,
+        scratch=[pltpu.VMEM((P_SIZE, tile_rows), f32)],
         smem=1,
     )
     w_first = a_first - summed[:, :tile_rows]
     l_first = couple(w_first, inv_d[0], inv_e[0], panel_pairs[0])
-    w_crossed = second[:, k_local : k_local + blocks] - summed[:, tile_rows:].T
+    w_crossed = entries[:, :blocks] - summed[:, tile_rows:].T
     crossed = couple_lanes(w_crossed, inv_d[0], inv_e[0], panel_pairs[0])
     plain = (((1,), (0,)), ((), ()))
     halves = []

time: 123 us -> 97 us (0.79)
  local copies, waits for them, and re-layouts: 30 us -> 10.2 us
  starting transfers between devices: 31.5 us -> 43 us
  other arithmetic: 13.7 us -> 4.89 us
  waiting for transfers between devices: 26.5 us -> 21.8 us
  Pallas kernels: 18.1 us -> 14.6 us
    unnamed x83 -> x73, local copies, waits for them, and re-layouts: 22.6 us -> 8.44 us
    ppermute x13 -> x14, starting transfers between devices: 25.5 us -> 34.9 us  [moved(): got = lax.ppermute(block, 'wide', shift(*step))]
    convert_element_type x2 -> x0, other arithmetic: 8.26 us -> none  [shards(): lt_big, lt_small = (rounded.astype(b16), (coupled_lt - rounded).astype(b16))]
    ppermute x13 -> x14, waiting for transfers between devices: 20.7 us -> 13.6 us  [moved(): got = lax.ppermute(block, 'wide', shift(*step))]
    pallas_call x5 -> x6, Pallas kernels: 18.1 us -> 14.6 us  [the longest x4 8.26 us: local_call(): pl.pallas_call(kernel, in_specs=specs, out_specs=jax.tree.map(lambda _: v...]
    slice x3 -> x2, local copies, waits for them, and re-layouts: 3.27 us -> 0.05 us  [couple(): after = jnp.concatenate([block[1:], zero_row], 0)]
    pallas_call x1, local copies, waits for them, and re-layouts: 2.71 us -> 0.1 us  [local_call(): pl.pallas_call(kernel, in_specs=specs, out_specs=jax.tree.map(lambda _: v...]
    ppermute x2, waiting for transfers between devices: 4.71 us -> 7.16 us  [finish_sum(): away = lax.ppermute(keep[:half] + got[:half], 'narrow', CHIP)]
  transfers between devices with their start and end apart: 17 -> 18, of which waited for: 5 -> 9; matrix products, arithmetic and copies ran while one was open for 15% -> 4% of each run, Pallas kernels for 8% -> 8%
where the time goes in v4:
time: 97 us; the launch traced here: 96.7 us
  starting transfers between devices  43 us (44%)
  waiting for transfers between devices  21.8 us (22%)
  Pallas kernels  14.6 us (15%)
  local copies, waits for them, and re-layouts  10.2 us (11%)
  other arithmetic  4.89 us (5%)
  between operations  1.27 us (1%)
    ppermute x14, starting transfers between devices, moved(): got = lax.ppermute(block, 'wide', shift(*step))  34.9 us
    ppermute x14, waiting for transfers between devices, moved(): got = lax.ppermute(block, 'wide', shift(*step))  13.6 us
    unnamed x73, local copies, waits for them, and re-layouts  8.44 us
    pallas_call x4, Pallas kernels, local_call(): pl.pallas_call(kernel, in_specs=specs, out_specs=jax.tree.map(lambda _: v...  8.26 us
    ppermute x2, waiting for transfers between devices, finish_sum(): away = lax.ppermute(keep[:half] + got[:half], 'narrow', CHIP)  7.16 us
    ppermute x2, starting transfers between devices, finish_sum(): got = lax.ppermute(send, 'narrow', CORE)  5.11 us
    pallas_call x1, Pallas kernels, tile_slots(): pl.pallas_call(slots_kernel, in_specs=[pl.BlockSpec(memory_space=pltpu.SM...  4.4 us
    ppermute x2, starting transfers between devices, finish_sum(): away = lax.ppermute(keep[:half] + got[:half], 'narrow', CHIP)  3.02 us
  transfers between devices with their start and end apart: 18, of which 9 were waited for; matrix products, arithmetic and copies ran while one was open for 4% of the time, Pallas kernels for 8%

profile of v4, /device:TPU:1, one launch (start us, length us, event | category | flops | bytes accessed | tf_op | source)
XLA Modules:
  0.0 96.7 jit_solution(6112844476019662640)
XLA Ops:
  0.7 1.9 %copy-done = f32[1024,768]{1,0:T(8,128)S(1)} copy-done((f32[1024,768]{1,0:T(8,128)S(1)}, f32[1024,768]{1,0:T(8,128)}, u32[]{:S(2)}) %copy-start) | copy-done | bytes 3145752
  2.6 0.9 copy-done.7
  3.5 0.7 copy-done.18
  4.2 4.4 %shard_map.122 = f32[16,1152]{1,0:T(8,128)S(1)} custom-call(s32[1]{0:T(128)} %bitcast.5.low_ref, s32[2,256]{1,0:T(2,128)S(1)} %copy-done.18, f32[64,768]{1,0:T(8,128)S(1)} %copy-done.7, f32[1024,768]{1,0:T(8,128)S(1)} %copy-done), custom_call_target="tpu_custom_call" | custom-call | tf_op jit(solution)/shard_map/pallas_call | solution.py:139
  8.6 7.8 %collective-permute-start = (f32[16,1152]{1,0:T(8,128)S(1)}, f32[16,1152]{1,0:T(8,128)S(1)}, u32[]{:S(2)}, u32[]{:S(2)}) collective-permute-start(f32[16,1152]{1,0:T(8,128)S(1)} %shard_map.122), channel_id=1, source_target_pairs={{0,32},{4,36},{8,40},{12,44},{16,48},{20,52},{24,56},{28,60},{32,0... | collective-permute-start | bytes 221192 | tf_op jit(solution)/shard_map/ppermute | solution.py:47
  16.6 0.2 convert_reduce_fusion
  16.8 0.1 select_reduce_fusion
  17.1 1.2 %collective-permute-done = f32[16,1152]{1,0:T(8,128)S(1)} collective-permute-done((f32[16,1152]{1,0:T(8,128)S(1)}, f32[16,1152]{1,0:T(8,128)S(1)}, u32[]{:S(2)}, u32[]{:S(2)}) %collective-permute-start) | collective-permute-done | bytes 73760 | tf_op jit(solution)/shard_map/ppermute | solution.py:47
  18.3 3.3 %collective-permute-start.1 = (f32[32,1152]{1,0:T(8,128)S(1)}, f32[32,1152]{1,0:T(8,128)S(1)}, u32[]{:S(2)}, u32[]{:S(2)}) collective-permute-start(f32[32,1152]{1,0:T(8,128)S(1)} %pad_maximum_fusion.2), channel_id=1, source_target_pairs={{0,136},{4,140},{8,144},{12,148},{16,152},{20,156},{24,160},{28,16... | collective-permute-start | bytes 442376 | tf_op jit(solution)/shard_map/ppermute | solution.py:47
  21.6 4.2 %collective-permute-start.2 = (f32[32,1152]{1,0:T(8,128)S(1)}, f32[32,1152]{1,0:T(8,128)S(1)}, u32[]{:S(2)}, u32[]{:S(2)}) collective-permute-start(f32[32,1152]{1,0:T(8,128)S(1)} %pad_maximum_fusion.2), channel_id=1, source_target_pairs={{0,184},{4,188},{8,128},{12,132},{16,136},{20,140},{24,144},{28,14... | collective-permute-start | bytes 442376 | tf_op jit(solution)/shard_map/ppermute | solution.py:47
  25.9 3.9 %collective-permute-done.1 = f32[32,1152]{1,0:T(8,128)S(1)} collective-permute-done((f32[32,1152]{1,0:T(8,128)S(1)}, f32[32,1152]{1,0:T(8,128)S(1)}, u32[]{:S(2)}, u32[]{:S(2)}) %collective-permute-start.1) | collective-permute-done | bytes 147488 | tf_op jit(solution)/shard_map/ppermute | solution.py:47
  29.8 5.3 %collective-permute-done.3 = f32[32,1152]{1,0:T(8,128)S(1)} collective-permute-done((f32[32,1152]{1,0:T(8,128)S(1)}, f32[32,1152]{1,0:T(8,128)S(1)}, u32[]{:S(2)}, u32[]{:S(2)}) %collective-permute-start.3) | collective-permute-done | bytes 147488 | tf_op jit(solution)/shard_map/ppermute | solution.py:47
  35.3 2.7 %collective-permute-start.5 = (f32[128,1152]{1,0:T(8,128)S(1)}, f32[128,1152]{1,0:T(8,128)S(1)}, u32[]{:S(2)}, u32[]{:S(2)}) collective-permute-start(f32[128,1152]{1,0:T(8,128)S(1)} %constant_dynamic-update-slice_fusion.refs_0_.after_ref), channel_id=1, source_target_pairs={{0,192},{4,196},{8,200},{12,204},{16,208},{20,212},{24,216},{28,22... | collective-permute-start | bytes 1769480 | tf_op jit(solution)/shard_map/ppermute | solution.py:47
  38.1 0.1 copy.21.index_ref
  38.3 0.5 convert_multiply_fusion.1
  38.8 3.4 %collective-permute-start.6 = (f32[128,1152]{1,0:T(8,128)S(1)}, f32[128,1152]{1,0:T(8,128)S(1)}, u32[]{:S(2)}, u32[]{:S(2)}) collective-permute-start(f32[128,1152]{1,0:T(8,128)S(1)} %constant_dynamic-update-slice_fusion.refs_0_.after_ref), channel_id=1, source_target_pairs={{0,4},{4,0},{8,12},{12,8},{16,20},{20,16},{24,28},{28,24},{32,36},... | collective-permute-start | bytes 1769480 | tf_op jit(solution)/shard_map/ppermute | solution.py:47
  42.2 1.1 %copy.20.weight_ref = f32[1024,3]{1,0:T(8,128)} copy(f32[1024,3]{0,1:T(4,128)S(1)} %get-tuple-element.32) | data formatting | bytes 24576 | tf_op jit(solution)/shard_map/transpose | solution.py:322
  43.4 2.7 %collective-permute-start.8 = (f32[64,1152]{1,0:T(8,128)S(1)}, f32[64,1152]{1,0:T(8,128)S(1)}, u32[]{:S(2)}, u32[]{:S(2)}) collective-permute-start(f32[64,1152]{1,0:T(8,128)S(1)} %pad_maximum_fusion.1), channel_id=1, source_target_pairs={{0,56},{4,60},{8,0},{12,4},{16,8},{20,12},{24,16},{28,20},{32,24},... | collective-permute-start | bytes 884744 | tf_op jit(solution)/shard_map/ppermute | solution.py:47
  46.0 2.3 %collective-permute-done.4.refs_1_ = f32[128,1152]{1,0:T(8,128)S(1)} collective-permute-done((f32[128,1152]{1,0:T(8,128)S(1)}, f32[128,1152]{1,0:T(8,128)S(1)}, u32[]{:S(2)}, u32[]{:S(2)}) %collective-permute-start.4) | collective-permute-done | bytes 589856 | tf_op jit(solution)/shard_map/ppermute | solution.py:47
  48.4 5.2 %collective-permute-start.9 = (f32[128,1152]{1,0:T(8,128)S(1)}, f32[128,1152]{1,0:T(8,128)S(1)}, u32[]{:S(2)}, u32[]{:S(2)}) collective-permute-start(f32[128,1152]{1,0:T(8,128)S(1)} %pad_maximum_fusion), channel_id=1, source_target_pairs={{0,4},{4,0},{8,12},{12,8},{16,20},{20,16},{24,28},{28,24},{32,36},... | collective-permute-start | bytes 1769480 | tf_op jit(solution)/shard_map/ppermute | solution.py:47
  53.8 0.3 collective-permute-start.12
  54.1 2.7 %collective-permute-start.13 = (f32[64,1152]{1,0:T(8,128)S(1)}, f32[64,1152]{1,0:T(8,128)S(1)}, u32[]{:S(2)}, u32[]{:S(2)}) collective-permute-start(f32[64,1152]{1,0:T(8,128)S(1)} %get-tuple-element.21), channel_id=1, source_target_pairs={{0,56},{4,60},{8,0},{12,4},{16,8},{20,12},{24,16},{28,20},{32,24},... | collective-permute-start | bytes 884744 | tf_op jit(solution)/shard_map/ppermute | solution.py:47
  56.8 2.4 %collective-permute-start.11 = (f32[64,1152]{1,0:T(8,128)S(1)}, f32[64,1152]{1,0:T(8,128)S(1)}, u32[]{:S(2)}, u32[]{:S(2)}) collective-permute-start(f32[64,1152]{1,0:T(8,128)S(1)} %get-tuple-element.20), channel_id=1, source_target_pairs={{0,192},{4,196},{8,200},{12,204},{16,208},{20,212},{24,216},{28,22... | collective-permute-start | bytes 884744 | tf_op jit(solution)/shard_map/ppermute | solution.py:47
  59.2 1.9 %copy-done.1 = f32[1024,768]{1,0:T(8,128)S(1)} copy-done((f32[1024,768]{1,0:T(8,128)S(1)}, f32[1024,768]{1,0:T(8,128)}, u32[]{:S(2)}) %copy-start.1) | copy-done | bytes 3145752
  61.1 1.1 %copy-done.10 = f32[128,1152]{1,0:T(8,128)S(1)} copy-done((f32[128,1152]{1,0:T(8,128)S(1)}, f32[128,1152]{1,0:T(8,128)}, u32[]{:S(2)}) %copy-start.10) | copy-done | bytes 589848
  62.2 1.9 %shard_map.124 = (bf16[1024,768]{1,0:T(8,128)(2,1)S(1)}, bf16[1024,768]{1,0:T(8,128)(2,1)S(1)}) custom-call(f32[1024,3]{1,0:T(8,128)S(1)} %copy-done.4, f32[1024,768]{1,0:T(8,128)S(1)} %copy-done.1, f32[128,1152]{1,0:T(8,128)S(1)} %copy-done.10), custom_call_target="tpu_custom_call" | custom-call | flops 6291456 | bytes 6291456 | tf_op jit(solution)/shard_map/pallas_call | solution.py:168
  64.1 2.4 %shard_map.123.carry_ref = f32[512,1152]{1,0:T(8,128)S(1)} custom-call(s32[512,1]{1,0:T(8,128)S(1)} %copy.21.index_ref, f32[128,1152]{1,0:T(8,128)S(1)} %copy-done.11, f32[128,1152]{1,0:T(8,128)S(1)} %copy-done.15, f32[128,1152]{1,0:T(8,128)S(1)} %copy-done.17, f32[128,1152]{1,0:T(8,128)S(1)} %copy-done.13, f32[64,1152]{1,0:T(8,128)S(1)} %collective-permute-done.7.refs_4_, ...), custom_call_target="tpu_custom_call" | custom-call | flops 1509949440 | bytes 2951168 | tf_op jit(solution)/shard_map/pallas_call | solution.py:257
  66.6 0.9 collective-permute-done.9.refs_0_
  67.5 2.6 %shard_map.125 = (f32[128,1024]{1,0:T(8,128)S(1)}, f32[256,1024]{1,0:T(8,128)S(1)}, f32[256,128]{1,0:T(8,128)S(1)}, bf16[256,1024]{1,0:T(8,128)(2,1)S(1)}, bf16[...) custom-call(s32[512,1]{1,0:T(8,128)S(1)} %copy.21.index_ref, f32[3,1024]{1,0:T(4,128)S(1)} %get-tuple-element.33.weight_ref, ...), custom_call_target="tpu_custom_call" | custom-call | flops 1711276032 | bytes 10434560 | tf_op jit(solution)/shard_map/pallas_call | solution.py:257
  70.1 4.2 %collective-permute-start.14 = (f32[128,1024]{1,0:T(8,128)S(1)}, f32[128,1024]{1,0:T(8,128)S(1)}, u32[]{:S(2)}, u32[]{:S(2)}) collective-permute-start(f32[128,1024]{1,0:T(8,128)S(1)} %get-tuple-element.15), channel_id=1, source_target_pairs={{0,1},{1,0},{2,3},{3,2},{4,5},{5,4},{6,7},{7,6},{8,9},{9,8},{10,11... | collective-permute-start | bytes 1572872 | tf_op jit(solution)/shard_map/ppermute | solution.py:281
  74.4 1.2 %shard_map.126 = f32[128,1024]{1,0:T(8,128)S(1)} custom-call(f32[128,1024]{1,0:T(8,128)S(1)} %get-tuple-element.12.taken_ref, bf16[1024,768]{1,0:T(8,128)(2,1)S(1)} %get-tuple-element.10.lt_big_ref, bf16[1024,768]{1,0:T(8,128)(2,1)S(1)} %get-tuple-element.11.lt_small_ref, bf16[256,1024]{1,0:T(8,128)(2,1)S(1)} %get-tuple-element.13.big_ref, ...), custom_call_target="tpu_custom_call" | custom-call | flops 805306368 | bytes 8912896 | tf_op jit(solution)/shard_map/pallas_call | solution.py:257
  75.7 0.2 collective-permute-done.14
  75.9 0.6 copy-done.2
  76.5 0.8 slice_add_fusion.2
  77.3 1.5 %collective-permute-start.15 = (f32[64,1024]{1,0:T(8,128)}, f32[64,1024]{1,0:T(8,128)}, u32[]{:S(2)}, u32[]{:S(2)}) collective-permute-start(f32[64,1024]{1,0:T(8,128)} %slice_add_fusion.2), channel_id=1, source_target_pairs={{0,2},{1,3},{2,0},{3,1},{4,6},{5,7},{6,4},{7,5},{8,10},{9,11},{10,... | collective-permute-start | bytes 786440 | tf_op jit(solution)/shard_map/ppermute | solution.py:282
  79.0 1.2 %copy-done.6 = f32[256,1024]{1,0:T(8,128)S(1)} copy-done((f32[256,1024]{1,0:T(8,128)S(1)}, f32[256,1024]{1,0:T(8,128)}, u32[]{:S(2)}) %copy-start.6) | copy-done | bytes 1048600
  80.2 2.0 %shard_map.127 = f32[256,768]{1,0:T(8,128)S(1)} custom-call(s32[4]{0:T(128)S(1)} %pad_add_fusion.quarter_ref, f32[256,1024]{1,0:T(8,128)S(1)} %copy-done.6, bf16[1024,768]{1,0:T(8,128)(2,1)S(1)} %get-tuple-element.10.lt_big_ref, bf16[1024,768]{1,0:T(8,128)(2,1)S(1)} %get-tuple-element.11.lt_small_ref), custom_call_target="tpu_custom_call" | custom-call | flops 1207959552 | bytes 7340048 | tf_op jit(solution)/shard_map/pallas_call | solution.py:257
  82.2 3.3 %collective-permute-done.15 = f32[64,1024]{1,0:T(8,128)} collective-permute-done((f32[64,1024]{1,0:T(8,128)}, f32[64,1024]{1,0:T(8,128)}, u32[]{:S(2)}, u32[]{:S(2)}) %collective-permute-start.15) | collective-permute-done | bytes 262176 | tf_op jit(solution)/shard_map/ppermute | solution.py:282
  85.5 1.0 %fusion.1 = f32[64,1024]{1,0:T(8,128)S(1)} fusion(f32[64,1024]{1,0:T(8,128)} %collective-permute-done.15, f32[128,1024]{1,0:T(8,128)S(1)} %copy-done.21, f32[128,1024]{1,0:T(8,128)S(1)} %copy-done.3), kind=kLoop, calls=%fused_computation.9 | loop fusion | flops 131072 | bytes 1048576 | tf_op jit(solution)/shard_map/add | solution.py:283
  86.7 0.1 constant_dynamic-slice_fusion.3
  86.9 0.4 slice_add_fusion
  87.3 0.9 collective-permute-start.16
  88.2 0.4 slice_add_fusion.1
  88.7 0.9 collective-permute-done.16
  89.6 1.5 %collective-permute-start.17 = (f32[64,768]{1,0:T(8,128)S(1)}, f32[64,768]{1,0:T(8,128)S(1)}, u32[]{:S(2)}, u32[]{:S(2)}) collective-permute-start(f32[64,768]{1,0:T(8,128)S(1)} %slice_add_fusion.4), channel_id=1, source_target_pairs={{0,2},{1,3},{2,0},{3,1},{4,6},{5,7},{6,4},{7,5},{8,10},{9,11},{10,... | collective-permute-start | bytes 589832 | tf_op jit(solution)/shard_map/ppermute | solution.py:282
  91.1 0.8 multiply_add_fusion.1
  91.9 3.9 %collective-permute-done.17 = f32[64,768]{1,0:T(8,128)S(1)} collective-permute-done((f32[64,768]{1,0:T(8,128)S(1)}, f32[64,768]{1,0:T(8,128)S(1)}, u32[]{:S(2)}, u32[]{:S(2)}) %collective-permute-start.17) | collective-permute-done | bytes 196640 | tf_op jit(solution)/shard_map/ppermute | solution.py:282
  95.9 0.8 multiply_add_fusion
  (112 shorter events, 1.5 us)
Async XLA Ops:
  0.6 16.2 %copy-start.33 = (s32[64]{0:T(128)S(1)}, s32[64]{0:T(128)}, u32[]{:S(2)}) copy-start(s32[64]{0:T(128)} %constant.137.clone) | copy-start | bytes 772
  0.6 15.8 %copy-start.19 = (s32[2,256]{1,0:T(2,128)S(1)}, s32[2,256]{1,0:T(2,128)}, u32[]{:S(2)}) copy-start(s32[2,256]{1,0:T(2,128)} %pivots_ref.1) | copy-start | bytes 6148
  0.7 16.3 %copy-start.25 = (f32[1024]{0:T(1024)S(1)}, f32[1024]{0:T(1024)}, u32[]{:S(2)}) copy-start(f32[1024]{0:T(1024)} %param.13) | copy-start | bytes 12292
  0.7 16.3 %copy-start.26 = (s32[1024]{0:T(1024)S(1)}, s32[1024]{0:T(1024)}, u32[]{:S(2)}) copy-start(s32[1024]{0:T(1024)} %param.14) | copy-start | bytes 12292
  0.7 1.9 %copy-start = (f32[1024,768]{1,0:T(8,128)S(1)}, f32[1024,768]{1,0:T(8,128)}, u32[]{:S(2)}) copy-start(f32[1024,768]{1,0:T(8,128)} %lt_ref.3) | copy-start | bytes 9437188
  4.2 34.1 %copy-start.30 = (s32[2,64]{1,0:T(2,128)S(1)}, s32[2,64]{1,0:T(2,128)}, u32[]{:S(2)}) copy-start(s32[2,64]{1,0:T(2,128)} %param.20) | copy-start | bytes 1540
  4.2 34.1 %copy-start.31 = (f32[2,64]{1,0:T(2,128)S(1)}, f32[2,64]{1,0:T(2,128)}, u32[]{:S(2)}) copy-start(f32[2,64]{1,0:T(2,128)} %param.19) | copy-start | bytes 1540
  4.2 38.0 %copy-start.27 = (f32[1024]{0:T(1024)S(1)}, f32[1024]{0:T(1024)}, u32[]{:S(2)}) copy-start(f32[1024]{0:T(1024)} %param.12) | copy-start | bytes 12292
  8.6 9.7 %collective-permute-start = (f32[16,1152]{1,0:T(8,128)S(1)}, f32[16,1152]{1,0:T(8,128)S(1)}, u32[]{:S(2)}, u32[]{:S(2)}) collective-permute-start(f32[16,1152]{1,0:T(8,128)S(1)} %shard_map.122), channel_id=1, source_target_pairs={{0,32},{4,36},{8,40},{12,44},{16,48},{20,52},{24,56},{28,60},{32,0... | collective-permute-start | bytes 221192 | tf_op jit(solution)/shard_map/ppermute | solution.py:47
  18.3 11.5 %collective-permute-start.1 = (f32[32,1152]{1,0:T(8,128)S(1)}, f32[32,1152]{1,0:T(8,128)S(1)}, u32[]{:S(2)}, u32[]{:S(2)}) collective-permute-start(f32[32,1152]{1,0:T(8,128)S(1)} %pad_maximum_fusion.2), channel_id=1, source_target_pairs={{0,136},{4,140},{8,144},{12,148},{16,152},{20,156},{24,160},{28,16... | collective-permute-start | bytes 442376 | tf_op jit(solution)/shard_map/ppermute | solution.py:47
  21.6 8.2 %collective-permute-start.2 = (f32[32,1152]{1,0:T(8,128)S(1)}, f32[32,1152]{1,0:T(8,128)S(1)}, u32[]{:S(2)}, u32[]{:S(2)}) collective-permute-start(f32[32,1152]{1,0:T(8,128)S(1)} %pad_maximum_fusion.2), channel_id=1, source_target_pairs={{0,184},{4,188},{8,128},{12,132},{16,136},{20,140},{24,144},{28,14... | collective-permute-start | bytes 442376 | tf_op jit(solution)/shard_map/ppermute | solution.py:47
  25.9 9.3 %collective-permute-start.3 = (f32[32,1152]{1,0:T(8,128)S(1)}, f32[32,1152]{1,0:T(8,128)S(1)}, u32[]{:S(2)}, u32[]{:S(2)}) collective-permute-start(f32[32,1152]{1,0:T(8,128)S(1)} %pad_maximum_fusion.2), channel_id=1, source_target_pairs={{0,16},{4,20},{8,24},{12,28},{16,32},{20,36},{24,40},{28,44},{32,4... | collective-permute-start | bytes 442376 | tf_op jit(solution)/shard_map/ppermute | solution.py:47
  35.2 18.5 %copy-start.9 = (f32[128,1152]{1,0:T(8,128)}, f32[128,1152]{1,0:T(8,128)S(1)}, u32[]{:S(2)}) copy-start(f32[128,1152]{1,0:T(8,128)S(1)} %constant_dynamic-update-slice_fusion.refs_0_.after_ref) | copy-start | bytes 1769476
  35.2 13.1 %collective-permute-start.4 = (f32[128,1152]{1,0:T(8,128)S(1)}, f32[128,1152]{1,0:T(8,128)S(1)}, u32[]{:S(2)}, u32[]{:S(2)}) collective-permute-start(f32[128,1152]{1,0:T(8,128)S(1)} %constant_dynamic-update-slice_fusion.refs_0_.after_ref), channel_id=1, source_target_pairs={{0,64},{4,68},{8,72},{12,76},{16,80},{20,84},{24,88},{28,92},{32,9... | collective-permute-start | bytes 1769480 | tf_op jit(solution)/shard_map/ppermute | solution.py:47
  35.3 13.1 %collective-permute-start.5 = (f32[128,1152]{1,0:T(8,128)S(1)}, f32[128,1152]{1,0:T(8,128)S(1)}, u32[]{:S(2)}, u32[]{:S(2)}) collective-permute-start(f32[128,1152]{1,0:T(8,128)S(1)} %constant_dynamic-update-slice_fusion.refs_0_.after_ref), channel_id=1, source_target_pairs={{0,192},{4,196},{8,200},{12,204},{16,208},{20,212},{24,216},{28,22... | collective-permute-start | bytes 1769480 | tf_op jit(solution)/shard_map/ppermute | solution.py:47
  38.8 20.4 %copy-start.23 = (f32[1,64]{1,0:T(1,128)}, f32[1,64]{1,0:T(1,128)S(1)}, u32[]{:S(2)}) copy-start(f32[1,64]{1,0:T(1,128)S(1)} %get-tuple-element.35) | copy-start | bytes 772
  38.8 14.9 %collective-permute-start.6 = (f32[128,1152]{1,0:T(8,128)S(1)}, f32[128,1152]{1,0:T(8,128)S(1)}, u32[]{:S(2)}, u32[]{:S(2)}) collective-permute-start(f32[128,1152]{1,0:T(8,128)S(1)} %constant_dynamic-update-slice_fusion.refs_0_.after_ref), channel_id=1, source_target_pairs={{0,4},{4,0},{8,12},{12,8},{16,20},{20,16},{24,28},{28,24},{32,36},... | collective-permute-start | bytes 1769480 | tf_op jit(solution)/shard_map/ppermute | solution.py:47
  43.3 15.9 %copy-start.4 = (f32[1024,3]{1,0:T(8,128)S(1)}, f32[1024,3]{1,0:T(8,128)}, u32[]{:S(2)}) copy-start(f32[1024,3]{1,0:T(8,128)} %copy.20.weight_ref) | copy-start | bytes 36868
  43.3 10.8 %collective-permute-start.7 = (f32[64,1152]{1,0:T(8,128)S(1)}, f32[64,1152]{1,0:T(8,128)S(1)}, u32[]{:S(2)}, u32[]{:S(2)}) collective-permute-start(f32[64,1152]{1,0:T(8,128)S(1)} %pad_maximum_fusion.1), channel_id=1, source_target_pairs={{0,8},{4,12},{8,16},{12,20},{16,24},{20,28},{24,32},{28,36},{32,40... | collective-permute-start | bytes 884744 | tf_op jit(solution)/shard_map/ppermute | solution.py:47
  43.4 13.4 %collective-permute-start.8 = (f32[64,1152]{1,0:T(8,128)S(1)}, f32[64,1152]{1,0:T(8,128)S(1)}, u32[]{:S(2)}, u32[]{:S(2)}) collective-permute-start(f32[64,1152]{1,0:T(8,128)S(1)} %pad_maximum_fusion.1), channel_id=1, source_target_pairs={{0,56},{4,60},{8,0},{12,4},{16,8},{20,12},{24,16},{28,20},{32,24},... | collective-permute-start | bytes 884744 | tf_op jit(solution)/shard_map/ppermute | solution.py:47
  48.3 10.9 %copy-start.14 = (f32[128,1152]{1,0:T(8,128)}, f32[128,1152]{1,0:T(8,128)S(1)}, u32[]{:S(2)}) copy-start(f32[128,1152]{1,0:T(8,128)S(1)} %collective-permute-done.4.refs_1_) | copy-start | bytes 1769476
  48.3 10.8 %copy-start.16 = (f32[128,1152]{1,0:T(8,128)}, f32[128,1152]{1,0:T(8,128)S(1)}, u32[]{:S(2)}) copy-start(f32[128,1152]{1,0:T(8,128)S(1)} %collective-permute-done.5.refs_2_) | copy-start | bytes 1769476
  48.4 19.1 %collective-permute-start.9 = (f32[128,1152]{1,0:T(8,128)S(1)}, f32[128,1152]{1,0:T(8,128)S(1)}, u32[]{:S(2)}, u32[]{:S(2)}) collective-permute-start(f32[128,1152]{1,0:T(8,128)S(1)} %pad_maximum_fusion), channel_id=1, source_target_pairs={{0,4},{4,0},{8,12},{12,8},{16,20},{20,16},{24,28},{28,24},{32,36},... | collective-permute-start | bytes 1769480 | tf_op jit(solution)/shard_map/ppermute | solution.py:47
  53.7 5.5 %copy-start.12 = (f32[128,1152]{1,0:T(8,128)}, f32[128,1152]{1,0:T(8,128)S(1)}, u32[]{:S(2)}) copy-start(f32[128,1152]{1,0:T(8,128)S(1)} %collective-permute-done.6.refs_3_) | copy-start | bytes 1769476
  53.7 12.8 %collective-permute-start.10 = (f32[64,1152]{1,0:T(8,128)S(1)}, f32[64,1152]{1,0:T(8,128)S(1)}, u32[]{:S(2)}, u32[]{:S(2)}) collective-permute-start(f32[64,1152]{1,0:T(8,128)S(1)} %get-tuple-element.21), channel_id=1, source_target_pairs={{0,64},{4,68},{8,72},{12,76},{16,80},{20,84},{24,88},{28,92},{32,9... | collective-permute-start | bytes 884744 | tf_op jit(solution)/shard_map/ppermute | solution.py:47
  53.8 12.8 %collective-permute-start.12 = (f32[64,1152]{1,0:T(8,128)S(1)}, f32[64,1152]{1,0:T(8,128)S(1)}, u32[]{:S(2)}, u32[]{:S(2)}) collective-permute-start(f32[64,1152]{1,0:T(8,128)S(1)} %get-tuple-element.21), channel_id=1, source_target_pairs={{0,8},{4,12},{8,16},{12,20},{16,24},{20,28},{24,32},{28,36},{32,40... | collective-permute-start | bytes 884744 | tf_op jit(solution)/shard_map/ppermute | solution.py:47
  54.1 12.5 %collective-permute-start.13 = (f32[64,1152]{1,0:T(8,128)S(1)}, f32[64,1152]{1,0:T(8,128)S(1)}, u32[]{:S(2)}, u32[]{:S(2)}) collective-permute-start(f32[64,1152]{1,0:T(8,128)S(1)} %get-tuple-element.21), channel_id=1, source_target_pairs={{0,56},{4,60},{8,0},{12,4},{16,8},{20,12},{24,16},{28,20},{32,24},... | collective-permute-start | bytes 884744 | tf_op jit(solution)/shard_map/ppermute | solution.py:47
  56.8 9.8 %collective-permute-start.11 = (f32[64,1152]{1,0:T(8,128)S(1)}, f32[64,1152]{1,0:T(8,128)S(1)}, u32[]{:S(2)}, u32[]{:S(2)}) collective-permute-start(f32[64,1152]{1,0:T(8,128)S(1)} %get-tuple-element.20), channel_id=1, source_target_pairs={{0,192},{4,196},{8,200},{12,204},{16,208},{20,212},{24,216},{28,22... | collective-permute-start | bytes 884744 | tf_op jit(solution)/shard_map/ppermute | solution.py:47
  59.2 1.9 %copy-start.1 = (f32[1024,768]{1,0:T(8,128)S(1)}, f32[1024,768]{1,0:T(8,128)}, u32[]{:S(2)}) copy-start(f32[1024,768]{1,0:T(8,128)} %lt_ref.3) | copy-start | bytes 9437188
  62.2 1.9 %copy-start.11 = (f32[128,1152]{1,0:T(8,128)S(1)}, f32[128,1152]{1,0:T(8,128)}, u32[]{:S(2)}) copy-start(f32[128,1152]{1,0:T(8,128)} %copy-done.9) | copy-start | bytes 1769476
  62.2 2.0 %copy-start.13 = (f32[128,1152]{1,0:T(8,128)S(1)}, f32[128,1152]{1,0:T(8,128)}, u32[]{:S(2)}) copy-start(f32[128,1152]{1,0:T(8,128)} %copy-done.12) | copy-start | bytes 1769476
  62.2 2.0 %copy-start.15 = (f32[128,1152]{1,0:T(8,128)S(1)}, f32[128,1152]{1,0:T(8,128)}, u32[]{:S(2)}) copy-start(f32[128,1152]{1,0:T(8,128)} %copy-done.14) | copy-start | bytes 1769476
  62.2 2.0 %copy-start.17 = (f32[128,1152]{1,0:T(8,128)S(1)}, f32[128,1152]{1,0:T(8,128)}, u32[]{:S(2)}) copy-start(f32[128,1152]{1,0:T(8,128)} %copy-done.16) | copy-start | bytes 1769476
  67.5 6.9 %copy-start.28 = (f32[1,64]{1,0:T(1,128)S(1)}, f32[1,64]{1,0:T(1,128)}, u32[]{:S(2)}) copy-start(f32[1,64]{1,0:T(1,128)} %get-tuple-element.34) | copy-start | bytes 772
  67.5 6.9 %copy-start.32 = (f32[2,64]{1,0:T(2,128)S(1)}, f32[2,64]{1,0:T(2,128)}, u32[]{:S(2)}) copy-start(f32[2,64]{1,0:T(2,128)} %param.18) | copy-start | bytes 1540
  70.1 5.6 %copy-start.5 = (f32[256,1024]{1,0:T(8,128)}, f32[256,1024]{1,0:T(8,128)S(1)}, u32[]{:S(2)}) copy-start(f32[256,1024]{1,0:T(8,128)S(1)} %get-tuple-element.16.second_ref) | copy-start | bytes 3145732
  70.1 5.8 %collective-permute-start.14 = (f32[128,1024]{1,0:T(8,128)S(1)}, f32[128,1024]{1,0:T(8,128)S(1)}, u32[]{:S(2)}, u32[]{:S(2)}) collective-permute-start(f32[128,1024]{1,0:T(8,128)S(1)} %get-tuple-element.15), channel_id=1, source_target_pairs={{0,1},{1,0},{2,3},{3,2},{4,5},{5,4},{6,7},{7,6},{8,9},{9,8},{10,11... | collective-permute-start | bytes 1572872 | tf_op jit(solution)/shard_map/ppermute | solution.py:281
  76.5 2.3 %copy-start.20 = (f32[128,1024]{1,0:T(8,128)}, f32[128,1024]{1,0:T(8,128)S(1)}, u32[]{:S(2)}) copy-start(f32[128,1024]{1,0:T(8,128)S(1)} %collective-permute-done.14) | copy-start | bytes 1572868
  77.3 8.3 %collective-permute-start.15 = (f32[64,1024]{1,0:T(8,128)}, f32[64,1024]{1,0:T(8,128)}, u32[]{:S(2)}, u32[]{:S(2)}) collective-permute-start(f32[64,1024]{1,0:T(8,128)} %slice_add_fusion.2), channel_id=1, source_target_pairs={{0,2},{1,3},{2,0},{3,1},{4,6},{5,7},{6,4},{7,5},{8,10},{9,11},{10,... | collective-permute-start | bytes 786440 | tf_op jit(solution)/shard_map/ppermute | solution.py:282
  79.0 1.2 %copy-start.6 = (f32[256,1024]{1,0:T(8,128)S(1)}, f32[256,1024]{1,0:T(8,128)}, u32[]{:S(2)}) copy-start(f32[256,1024]{1,0:T(8,128)} %copy-done.5) | copy-start | bytes 3145732
  80.2 5.3 %copy-start.3 = (f32[128,1024]{1,0:T(8,128)S(1)}, f32[128,1024]{1,0:T(8,128)}, u32[]{:S(2)}) copy-start(f32[128,1024]{1,0:T(8,128)} %copy-done.2) | copy-start | bytes 1572868
  80.2 5.3 %copy-start.21 = (f32[128,1024]{1,0:T(8,128)S(1)}, f32[128,1024]{1,0:T(8,128)}, u32[]{:S(2)}) copy-start(f32[128,1024]{1,0:T(8,128)} %copy-done.20) | copy-start | bytes 1572868
  80.2 6.3 %copy-start.8 = (f32[64,768]{1,0:T(8,128)S(1)}, f32[64,768]{1,0:T(8,128)}, u32[]{:S(2)}) copy-start(f32[64,768]{1,0:T(8,128)} %a_ref.1) | copy-start | bytes 589828
  80.2 6.4 %copy-start.24 = (f32[1,64]{1,0:T(1,128)S(1)}, f32[1,64]{1,0:T(1,128)}, u32[]{:S(2)}) copy-start(f32[1,64]{1,0:T(1,128)} %copy-done.23) | copy-start | bytes 772
  86.6 9.1 %copy-start.22 = (f32[64,768]{1,0:T(8,128)S(1)}, f32[64,768]{1,0:T(8,128)}, u32[]{:S(2)}) copy-start(f32[64,768]{1,0:T(8,128)} %param.17) | copy-start | bytes 589828
  87.3 8.6 %copy-start.29 = (f32[1,64]{1,0:T(1,128)S(1)}, f32[1,64]{1,0:T(1,128)}, u32[]{:S(2)}) copy-start(f32[1,64]{1,0:T(1,128)} %get-tuple-element.34) | copy-start | bytes 772
  87.3 2.2 %collective-permute-start.16 = (f32[128,768]{1,0:T(8,128)S(1)}, f32[128,768]{1,0:T(8,128)S(1)}, u32[]{:S(2)}, u32[]{:S(2)}) collective-permute-start(f32[128,768]{1,0:T(8,128)S(1)} %slice_add_fusion), channel_id=1, source_target_pairs={{0,1},{1,0},{2,3},{3,2},{4,5},{5,4},{6,7},{7,6},{8,9},{9,8},{10,11... | collective-permute-start | bytes 1179656 | tf_op jit(solution)/shard_map/ppermute | solution.py:281
  89.6 6.2 %collective-permute-start.17 = (f32[64,768]{1,0:T(8,128)S(1)}, f32[64,768]{1,0:T(8,128)S(1)}, u32[]{:S(2)}, u32[]{:S(2)}) collective-permute-start(f32[64,768]{1,0:T(8,128)S(1)} %slice_add_fusion.4), channel_id=1, source_target_pairs={{0,2},{1,3},{2,0},{3,1},{4,6},{5,7},{6,4},{7,5},{8,10},{9,11},{10,... | collective-permute-start | bytes 589832 | tf_op jit(solution)/shard_map/ppermute | solution.py:282
  (4 other events, 3.5 us)

commit v5 on v4

--- a/solution.py
+++ b/solution.py
@@ -50,7 +50,7 @@
     ]
 
 
-def gather_tiles(block):
+def gather_tiles(block, made):
     rows = block.shape[0]
     held, at = block, [(0, 0, 0)]
     got, its = moved(held, at, (0, 4, 0))
@@ -60,21 +60,61 @@
     at = at + parts[0][1] + parts[1][1] + parts[2][1]
     half = len(at) // 2
     cut = half * rows
+    over = moved(held, at, (0, 0, 1))
     ahead = moved(held, at, (1, 0, 0))
     behind = moved(held, at, (-1, 0, 0))
-    over = moved(held, at, (0, 0, 1))
     up = moved(held[:cut], at[:half], (0, 1, 0))
     down = moved(held[:cut], at[:half], (0, -1, 0))
     early = [(held, at), ahead, behind, over, up, down]
-    mixed = jnp.concatenate([ahead[0][cut:], behind[0][:cut]], 0)
+    few = half // 2
+    edge = few * rows
+    ready = made(held)
+    mixed = cuts([(ahead[0], held.shape[0] - edge, edge, 0, 0), (behind[0], 0, edge, 0, edge)], [2 * edge])
+    low, high, middle = cuts(
+        [(over[0], 0, 3 * edge, 0, 0), (over[0], edge, 3 * edge, 1, 0), (over[0], 0, cut, 2, 0)],
+        [3 * edge, 3 * edge, cut],
+        ready[0],
+    )
     late = [
-        moved(mixed, ahead[1][half:] + behind[1][:half], (0, 0, 1)),
-        moved(over[0][:cut], over[1][:half], (1, 0, 0)),
-        moved(over[0][cut:], over[1][half:], (-1, 0, 0)),
-        moved(over[0][:cut], over[1][:half], (0, 1, 0)),
-        moved(over[0][:cut], over[1][:half], (0, -1, 0)),
+        moved(mixed[0], ahead[1][-few:] + behind[1][:few], (0, 0, 1)),
+        moved(low, over[1][:-few], (1, 0, 0)),
+        moved(high, over[1][few:], (-1, 0, 0)),
+        moved(middle, over[1][:half], (0, 1, 0)),
+        moved(middle, over[1][:half], (0, -1, 0)),
     ]
-    return early, late
+    return early, late, ready
+
+
+def in_hbm(value):
+    return pltpu.with_memory_space_constraint(value, pltpu.HBM)
+
+
+def cuts_kernel(*refs, parts, inputs):
+    sems = refs[-1]
+    outs = refs[inputs:-1]
+    copies = []
+    for i, (start, size, out, to) in enumerate(parts):
+        copies.append(
+            pltpu.make_async_copy(
+                refs[i].at[pl.ds(start, size)], outs[out].at[pl.ds(to, size)], sems.at[i]
+            )
+        )
+        copies[-1].start()
+    for copy in copies:
+        copy.wait()
+
+
+def cuts(parts, sizes, following=None):
+    args = [in_hbm(part[0]) for part in parts] + ([] if following is None else [following])
+    width = parts[0][0].shape[1]
+    return pl.pallas_call(
+        functools.partial(cuts_kernel, parts=[part[1:] for part in parts], inputs=len(args)),
+        in_specs=[pl.BlockSpec(memory_space=pl.ANY)] * len(args),
+        out_specs=[pl.BlockSpec(memory_space=pltpu.VMEM)] * len(sizes),
+        out_shape=[jax.ShapeDtypeStruct((size, width), jnp.float32) for size in sizes],
+        scratch_shapes=[pltpu.SemaphoreType.DMA((len(parts),))],
+        compiler_params=pltpu.CompilerParams(vmem_limit_bytes=20 * 2**20),
+    )(*args)
 
 
 def split(value):
@@ -89,14 +129,21 @@
     return dot(left[0], right[0]) + (dot(left[0], right[1]) + dot(left[1], right[0]))
 
 
-def slots_kernel(low_ref, pivots_ref, a_ref, lt_ref, out_ref, lt_buf, sems):
+def slots_kernel(low_ref, pivots_hbm, a_hbm, lt_ref, out_ref, lt_buf, pivots_ref, a_ref, sems, more):
     k_local, width = lt_ref.shape
     depth = k_local // sems.shape[0]
     copies = []
+    small = [
+        pltpu.make_async_copy(pivots_hbm, pivots_ref, more.at[0]),
+        pltpu.make_async_copy(a_hbm, a_ref, more.at[1]),
+    ]
+    for copy in small:
+        copy.start()
     for i in range(sems.shape[0]):
         rows = slice(i * depth, (i + 1) * depth)
         copies.append(pltpu.make_async_copy(lt_ref.at[rows], lt_buf.at[rows], sems.at[i]))
         copies[-1].start()
+    small[0].wait()
     row = jnp.concatenate([pivots_ref[0:1, :], pivots_ref[1:2, :]], 1) - low_ref[0]
     count = row.shape[1]
     mine = (row >= 0) & (row < width)
@@ -108,12 +155,11 @@
         ones, jnp.where(before, 1.0, 0.0).astype(jnp.bfloat16), preferred_element_type=jnp.float32
     )
     slot = lax.broadcasted_iota(jnp.int32, (128, count), 0).astype(jnp.float32)
-    hit = jnp.where((slot == rank[:1]) & mine, 1.0, 0.0).astype(jnp.bfloat16)
-    there = jnp.where(row == lax.broadcasted_iota(jnp.int32, (width, count), 0), 1.0, 0.0)
+    hit = (slot == rank[:1]) & mine
+    offset = jnp.sum(jnp.where(hit, row + 1, 0).astype(jnp.float32), 1, keepdims=True) - 1.0
+    column = lax.broadcasted_iota(jnp.int32, (128, width), 1).astype(jnp.float32)
+    pick = jnp.where(column == offset, 1.0, 0.0).astype(jnp.bfloat16)
     across = (((1,), (1,)), ((), ()))
-    pick = lax.dot_general(
-        hit, there.astype(jnp.bfloat16), across, preferred_element_type=jnp.float32
-    ).astype(jnp.bfloat16)
 
     def rows_of(value):
         total = None
@@ -124,6 +170,7 @@
             total = got if total is None else total + got
         return total.T[:CAP]
 
+    small[1].wait()
     extra = rows_of(a_ref[...])
     out_ref[:, k_local:] = jnp.concatenate([extra, jnp.zeros_like(extra)], 1)
     for i, copy in enumerate(copies):
@@ -140,15 +187,21 @@
         slots_kernel,
         in_specs=[
             pl.BlockSpec(memory_space=pltpu.SMEM),
-            vmem,
-            vmem,
-            pl.BlockSpec(memory_space=pltpu.HBM),
+            pl.BlockSpec(memory_space=pl.ANY),
+            pl.BlockSpec(memory_space=pl.ANY),
+            pl.BlockSpec(memory_space=pl.ANY),
         ],
         out_specs=vmem,
         out_shape=jax.ShapeDtypeStruct((CAP, k_local + 2 * blocks), jnp.float32),
-        scratch_shapes=[pltpu.VMEM((k_local, width), jnp.float32), pltpu.SemaphoreType.DMA((4,))],
+        scratch_shapes=[
+            pltpu.VMEM((k_local, width), jnp.float32),
+            pltpu.VMEM(pivots.shape, jnp.int32),
+            pltpu.VMEM((blocks, width), jnp.float32),
+            pltpu.SemaphoreType.DMA((4,)),
+            pltpu.SemaphoreType.DMA((2,)),
+        ],
         compiler_params=pltpu.CompilerParams(vmem_limit_bytes=20 * 2**20),
-    )(low.reshape(1), pivots, a_first, prior_lt)
+    )(low.reshape(1), in_hbm(pivots), in_hbm(a_first), in_hbm(prior_lt))
 
 
 def couple_kernel(weight_ref, lt_ref, after_ref, big_ref, small_ref):
@@ -156,7 +209,8 @@
     rows = value.shape[0]
     after = pltpu.roll(value, rows - 1, 0)
     before = pltpu.roll(value, 1, 0)
-    mixed = weight_ref[:, 0:1] * value + weight_ref[:, 1:2] * after + weight_ref[:, 2:3] * before
+    weight = weight_ref[...].T
+    mixed = weight[:, 0:1] * value + weight[:, 1:2] * after + weight[:, 2:3] * before
     big_ref[...], small_ref[...] = split(mixed)
 
 
@@ -169,7 +223,7 @@
         couple_kernel,
         grid=(4,),
         in_specs=[
-            pl.BlockSpec((depth, 3), lambda i: (i, 0)),
+            pl.BlockSpec((8, depth), lambda i: (0, i)),
             block,
             pl.BlockSpec(memory_space=pl.ANY),
         ],
@@ -179,7 +233,7 @@
         cost_estimate=pl.CostEstimate(
             flops=8 * k_local * width, bytes_accessed=8 * k_local * width, transcendentals=0
         ),
-    )(weights, prior_lt, following)
+    )(weights, in_hbm(prior_lt), following)
 
 
 def fill_parts(parts_ref, pieces):
@@ -200,10 +254,21 @@
 
 
 def early_kernel(index_ref, *refs):
-    *pieces, out_ref, parts_ref = refs
-    fill_parts(parts_ref, pieces)
-    total = parts_ref.shape[0] // 2
+    *pieces, out_ref, rows_ref, parts_ref, sems = refs
+    total = rows_ref.shape[0]
+    start, copies = 0, []
+    for i, ref in enumerate(pieces):
+        size = ref.shape[0]
+        rows = slice(start, start + size)
+        copies.append((rows, pltpu.make_async_copy(ref, rows_ref.at[rows], sems.at[i])))
+        copies[-1][1].start()
+        start += size
     hit = hits(index_ref[...], 0, total)
+    for rows, copy in copies:
+        copy.wait()
+        big, small = split(rows_ref[rows, :])
+        parts_ref[rows, :] = big
+        parts_ref[total + rows.start : total + rows.stop, :] = small
     for low in range(0, out_ref.shape[1], 384):
         out_ref[:, low : low + 384] = jnp.dot(
             hit, parts_ref[:, low : low + 384], preferred_element_type=jnp.float32
@@ -251,9 +316,10 @@
         out_ref[i * blocks : (i + 1) * blocks, :] = whole_ref[pl.ds(start, blocks), :]
 
 
-def local_call(kernel, out_shape, flops, *args, scratch=(), smem=0):
+def local_call(kernel, out_shape, flops, *args, scratch=(), smem=0, hbm=0):
     vmem = pl.BlockSpec(memory_space=pltpu.VMEM)
-    specs = [pl.BlockSpec(memory_space=pltpu.SMEM)] * smem + [vmem] * (len(args) - smem)
+    specs = [pl.BlockSpec(memory_space=pltpu.SMEM)] * smem + [vmem] * (len(args) - smem - hbm)
+    specs += [pl.BlockSpec(memory_space=pl.ANY)] * hbm
     return pl.pallas_call(
         kernel,
         in_specs=specs,
@@ -295,7 +361,12 @@
     order = jnp.arange(count)
     rank = jnp.sum((tile[:, None] == tile[None, :]) & (order[None, :] < order[:, None]), 1)
     block = tile_slots(pivots, here * tile_rows, prior_lt, a_first)
-    early, late = gather_tiles(block)
+    joined = prior_e * prior_pairs.astype(jnp.float32)
+    lower = jnp.concatenate([jnp.zeros_like(joined[:1]), joined[:-1]])
+    weights = jnp.pad(jnp.stack([prior_d, joined, lower]), ((0, 5), (0, 0)))
+    early, late, (lt_big, lt_small) = gather_tiles(
+        block, lambda held: coupled_parts(weights, prior_lt, held)
+    )
     offsets = [o for piece in early + late for o in piece[1]]
     ty, tz, th = tile // (NZ * NH), tile // NH % NZ, tile % NH
     hy, hz, hh = here // (NZ * NH), here // NH % NZ, here % NH
@@ -317,16 +388,18 @@
     wide = tile_rows + P_SIZE
     f32, b16 = jnp.float32, jnp.bfloat16
     shape = jax.ShapeDtypeStruct
-    joined = prior_e * prior_pairs.astype(f32)
-    weights = jnp.stack([prior_d, joined, jnp.concatenate([jnp.zeros_like(joined[:1]), joined[:-1]])])
-    lt_big, lt_small = coupled_parts(weights.T, prior_lt, early[0][0])
     carry = local_call(
         early_kernel,
         shape((2 * P_SIZE, width), f32),
         4 * 2 * P_SIZE * early_rows * width,
         where,
-        *[piece[0] for piece in early],
-        scratch=[pltpu.VMEM((2 * early_rows, width), b16)],
+        *[in_hbm(piece[0]) for piece in early],
+        scratch=[
+            pltpu.VMEM((early_rows, width), f32),
+            pltpu.VMEM((2 * early_rows, width), b16),
+            pltpu.SemaphoreType.DMA((len(early),)),
+        ],
+        hbm=len(early),
     )
     send, second, entries, second_big, second_small, taken = local_call(
         functools.partial(send_kernel, base=early_rows),

time: 97 us -> 97.6 us (level)
  Pallas kernels: 14.6 us -> 24.2 us
  waiting for transfers between devices: 21.8 us -> 16.3 us
  local copies, waits for them, and re-layouts: 10.2 us -> 7.47 us
    pallas_call x1 -> x3, Pallas kernels: 1.92 us -> 7.26 us  [the longest x1 4.09 us: coupled_parts(): pl.pallas_call(couple_kernel, grid=(4,), in_specs=[pl.BlockSpec((8, depth...]
    ppermute x14, waiting for transfers between devices: 13.6 us -> 9.05 us  [moved(): got = lax.ppermute(block, 'wide', shift(*step))]
    unnamed x73 -> x41, local copies, waits for them, and re-layouts: 8.44 us -> 5.29 us
    pallas_call x4, Pallas kernels: 8.26 us -> 11.4 us  [local_call(): pl.pallas_call(kernel, in_specs=specs, out_specs=jax.tree.map(lambda _: v...]
    ppermute x14, starting transfers between devices: 34.9 us -> 33.7 us  [moved(): got = lax.ppermute(block, 'wide', shift(*step))]
    pallas_call x1, Pallas kernels: 4.4 us -> 5.5 us  [tile_slots(): pl.pallas_call(slots_kernel, in_specs=[pl.BlockSpec(memory_space=pltpu.SM...]
    transpose x1 -> x0, local copies, waits for them, and re-layouts: 1.05 us -> none  [shards(): lt_big, lt_small = coupled_parts(weights.T, prior_lt, early[0][0])]
  transfers between devices with their start and end apart: 18 -> 18, of which waited for: 9 -> 8; matrix products, arithmetic and copies ran while one was open for 4% -> 7% of each run, Pallas kernels for 8% -> 15%
where the time goes in v5:
time: 97.6 us; the launch traced here: 97.2 us
  starting transfers between devices  42.2 us (43%)
  Pallas kernels  24.2 us (25%)
  waiting for transfers between devices  16.3 us (17%)
  local copies, waits for them, and re-layouts  7.47 us (8%)
  other arithmetic  5.07 us (5%)
  between operations  1.1 us (1%)
    ppermute x14, starting transfers between devices, moved(): got = lax.ppermute(block, 'wide', shift(*step))  33.7 us
    pallas_call x4, Pallas kernels, local_call(): pl.pallas_call(kernel, in_specs=specs, out_specs=jax.tree.map(lambda _: v...  11.4 us
    ppermute x14, waiting for transfers between devices, moved(): got = lax.ppermute(block, 'wide', shift(*step))  9.05 us
    ppermute x2, waiting for transfers between devices, finish_sum(): away = lax.ppermute(keep[:half] + got[:half], 'narrow', CHIP)  6.29 us
    ppermute x2, starting transfers between devices, finish_sum(): got = lax.ppermute(send, 'narrow', CORE)  5.67 us
    pallas_call x1, Pallas kernels, tile_slots(): pl.pallas_call(slots_kernel, in_specs=[pl.BlockSpec(memory_space=pltpu.SM...  5.5 us
    unnamed x41, local copies, waits for them, and re-layouts  5.29 us
    pallas_call x1, Pallas kernels, coupled_parts(): pl.pallas_call(couple_kernel, grid=(4,), in_specs=[pl.BlockSpec((8, depth...  4.09 us
  transfers between devices with their start and end apart: 18, of which 8 were waited for; matrix products, arithmetic and copies ran while one was open for 7% of the time, Pallas kernels for 15%

profile of v5, /device:TPU:1, one launch (start us, length us, event | category | flops | bytes accessed | tf_op | source)
XLA Modules:
  0.0 97.2 jit_solution(10202681212113096580)
XLA Ops:
  0.7 5.5 %shard_map.122 = f32[16,1152]{1,0:T(8,128)S(1)} custom-call(s32[1]{0:T(128)} %bitcast.5.low_ref, s32[2,256]{1,0:T(2,128)} %pivots_hbm.1, f32[64,768]{1,0:T(8,128)} %a_hbm.1, f32[1024,768]{1,0:T(8,128)} %lt_ref.3), custom_call_target="tpu_custom_call" | custom-call | tf_op jit(solution)/shard_map/pallas_call | solution.py:186
  6.2 7.8 %collective-permute-start = (f32[16,1152]{1,0:T(8,128)S(1)}, f32[16,1152]{1,0:T(8,128)S(1)}, u32[]{:S(2)}, u32[]{:S(2)}) collective-permute-start(f32[16,1152]{1,0:T(8,128)S(1)} %shard_map.122), channel_id=1, source_target_pairs={{0,32},{4,36},{8,40},{12,44},{16,48},{20,52},{24,56},{28,60},{32,0... | collective-permute-start | bytes 221192 | tf_op jit(solution)/shard_map/ppermute | solution.py:47
  14.1 0.6 constant_dynamic-update-slice_fusion.4
  14.8 0.2 convert_reduce_fusion
  15.2 0.7 collective-permute-done
  15.9 3.3 %collective-permute-start.1 = (f32[32,1152]{1,0:T(8,128)S(1)}, f32[32,1152]{1,0:T(8,128)S(1)}, u32[]{:S(2)}, u32[]{:S(2)}) collective-permute-start(f32[32,1152]{1,0:T(8,128)S(1)} %pad_maximum_fusion.1), channel_id=1, source_target_pairs={{0,136},{4,140},{8,144},{12,148},{16,152},{20,156},{24,160},{28,16... | collective-permute-start | bytes 442376 | tf_op jit(solution)/shard_map/ppermute | solution.py:47
  19.2 4.2 %collective-permute-start.2 = (f32[32,1152]{1,0:T(8,128)S(1)}, f32[32,1152]{1,0:T(8,128)S(1)}, u32[]{:S(2)}, u32[]{:S(2)}) collective-permute-start(f32[32,1152]{1,0:T(8,128)S(1)} %pad_maximum_fusion.1), channel_id=1, source_target_pairs={{0,184},{4,188},{8,128},{12,132},{16,136},{20,140},{24,144},{28,14... | collective-permute-start | bytes 442376 | tf_op jit(solution)/shard_map/ppermute | solution.py:47
  23.5 0.6 constant_dynamic-update-slice_fusion.3
  24.1 3.3 %collective-permute-done.1 = f32[32,1152]{1,0:T(8,128)S(1)} collective-permute-done((f32[32,1152]{1,0:T(8,128)S(1)}, f32[32,1152]{1,0:T(8,128)S(1)}, u32[]{:S(2)}, u32[]{:S(2)}) %collective-permute-start.1) | collective-permute-done | bytes 147488 | tf_op jit(solution)/shard_map/ppermute | solution.py:47
  27.4 0.7 constant_dynamic-update-slice_fusion.2
  28.1 0.7 constant_dynamic-update-slice_fusion.1
  28.7 4.0 %collective-permute-done.3 = f32[32,1152]{1,0:T(8,128)S(1)} collective-permute-done((f32[32,1152]{1,0:T(8,128)S(1)}, f32[32,1152]{1,0:T(8,128)S(1)}, u32[]{:S(2)}, u32[]{:S(2)}) %collective-permute-start.3) | collective-permute-done | bytes 147488 | tf_op jit(solution)/shard_map/ppermute | solution.py:47
  32.8 0.7 constant_dynamic-update-slice_fusion.refs_0_.after_ref
  33.4 3.4 %collective-permute-start.6 = (f32[128,1152]{1,0:T(8,128)}, f32[128,1152]{1,0:T(8,128)}, u32[]{:S(2)}, u32[]{:S(2)}) collective-permute-start(f32[128,1152]{1,0:T(8,128)} %constant_dynamic-update-slice_fusion.refs_0_.after_ref), channel_id=1, source_target_pairs={{0,4},{4,0},{8,12},{12,8},{16,20},{20,16},{24,28},{28,24},{32,36},... | collective-permute-start | bytes 1769480 | tf_op jit(solution)/shard_map/ppermute | solution.py:47
  36.9 2.7 %collective-permute-start.5 = (f32[128,1152]{1,0:T(8,128)}, f32[128,1152]{1,0:T(8,128)}, u32[]{:S(2)}, u32[]{:S(2)}) collective-permute-start(f32[128,1152]{1,0:T(8,128)} %constant_dynamic-update-slice_fusion.refs_0_.after_ref), channel_id=1, source_target_pairs={{0,192},{4,196},{8,200},{12,204},{16,208},{20,212},{24,216},{28,22... | collective-permute-start | bytes 1769480 | tf_op jit(solution)/shard_map/ppermute | solution.py:47
  39.6 0.7 pad_maximum_fusion
  40.4 2.7 %collective-permute-start.8 = (f32[64,1152]{1,0:T(8,128)}, f32[64,1152]{1,0:T(8,128)}, u32[]{:S(2)}, u32[]{:S(2)}) collective-permute-start(f32[64,1152]{1,0:T(8,128)} %pad_maximum_fusion), channel_id=1, source_target_pairs={{0,56},{4,60},{8,0},{12,4},{16,8},{20,12},{24,16},{28,20},{32,24},... | collective-permute-start | bytes 884744 | tf_op jit(solution)/shard_map/ppermute | solution.py:47
  43.1 4.1 %shard_map.124 = (bf16[1024,768]{1,0:T(8,128)(2,1)S(1)}, bf16[1024,768]{1,0:T(8,128)(2,1)S(1)}) custom-call(f32[8,1024]{1,0:T(8,128)S(1)} %select_maximum_fusion.weight_ref, f32[1024,768]{1,0:T(8,128)} %lt_ref.3, f32[128,1152]{1,0:T(8,128)} %constant_dynamic-update-slice_fusion.refs_0_.after_ref), custom_call_target="tpu_custom_call" | custom-call | flops 6291456 | bytes 6291456 | tf_op jit(solution)/shard_map/pallas_call | solution.py:222
  47.2 1.0 collective-permute-done.6.refs_3_.refs_0_.refs_1_.refs_2_
  48.1 2.2 %shard_map.126 = (f32[96,1152]{1,0:T(8,128)}, f32[96,1152]{1,0:T(8,128)}, f32[64,1152]{1,0:T(8,128)S(1)}) custom-call(f32[128,1152]{1,0:T(8,128)} %collective-permute-done.6.refs_3_.refs_0_.refs_1_.refs_2_, f32[128,1152]{1,0:T(8,128)} %collective-permute-done.6.refs_3_.refs_0_.refs_1_.refs_2_, ...), custom_call_target="tpu_custom_call" | custom-call | tf_op jit(solution)/shard_map/pallas_call | solution.py:110
  50.3 0.7 copy-done.5
  51.0 2.8 %collective-permute-start.11 = (f32[96,1152]{1,0:T(8,128)}, f32[96,1152]{1,0:T(8,128)}, u32[]{:S(2)}, u32[]{:S(2)}) collective-permute-start(f32[96,1152]{1,0:T(8,128)} %get-tuple-element.16), channel_id=1, source_target_pairs={{0,192},{4,196},{8,200},{12,204},{16,208},{20,212},{24,216},{28,22... | collective-permute-start | bytes 1327112 | tf_op jit(solution)/shard_map/ppermute | solution.py:47
  54.0 0.1 copy.18.index_ref
  54.2 0.3 collective-permute-start.12
  54.5 1.0 %shard_map.125 = f32[64,1152]{1,0:T(8,128)S(1)} custom-call(f32[128,1152]{1,0:T(8,128)} %collective-permute-done.4.refs_1_.refs_0_, f32[128,1152]{1,0:T(8,128)} %collective-permute-done.5.refs_2_.refs_1_), custom_call_target="tpu_custom_call" | custom-call | tf_op jit(solution)/shard_map/pallas_call | solution.py:110
  55.5 2.7 %collective-permute-start.13 = (f32[64,1152]{1,0:T(8,128)}, f32[64,1152]{1,0:T(8,128)S(1)}, u32[]{:S(2)}, u32[]{:S(2)}) collective-permute-start(f32[64,1152]{1,0:T(8,128)} %copy-done.5), channel_id=1, source_target_pairs={{0,56},{4,60},{8,0},{12,4},{16,8},{20,12},{24,16},{28,20},{32,24},... | collective-permute-start | bytes 884744 | tf_op jit(solution)/shard_map/ppermute | solution.py:47
  58.2 3.7 %collective-permute-start.9 = (f32[64,1152]{1,0:T(8,128)S(1)}, f32[64,1152]{1,0:T(8,128)S(1)}, u32[]{:S(2)}, u32[]{:S(2)}) collective-permute-start(f32[64,1152]{1,0:T(8,128)S(1)} %shard_map.125), channel_id=1, source_target_pairs={{0,4},{4,0},{8,12},{12,8},{16,20},{20,16},{24,28},{28,24},{32,36},... | collective-permute-start | bytes 884744 | tf_op jit(solution)/shard_map/ppermute | solution.py:47
  61.9 4.0 %shard_map.123.carry_ref = f32[512,1152]{1,0:T(8,128)S(1)} custom-call(s32[512,1]{1,0:T(8,128)S(1)} %copy.18.index_ref, f32[128,1152]{1,0:T(8,128)} %constant_dynamic-update-slice_fusion.refs_0_.after_ref, f32[128,1152]{1,0:T(8,128)} %collective-permute-done.4.refs_1_.refs_0_, f32[128,1152]{1,0:T(8,128)} %collective-permute-done.5.refs_2_.refs_1_, ...), custom_call_target="tpu_custom_call" | custom-call | flops 1509949440 | bytes 2951168 | tf_op jit(solution)/shard_map/pallas_call | solution.py:323
  66.0 4.0 %shard_map.127 = (f32[128,1024]{1,0:T(8,128)S(1)}, f32[256,1024]{1,0:T(8,128)S(1)}, f32[256,128]{1,0:T(8,128)S(1)}, bf16[256,1024]{1,0:T(8,128)(2,1)S(1)}, bf16[...) custom-call(s32[512,1]{1,0:T(8,128)S(1)} %copy.18.index_ref, f32[8,1024]{1,0:T(8,128)S(1)} %select_maximum_fusion.weight_ref, ...), custom_call_target="tpu_custom_call" | custom-call | flops 1711276032 | bytes 10455040 | tf_op jit(solution)/shard_map/pallas_call | solution.py:323
  70.1 4.8 %collective-permute-start.14 = (f32[128,1024]{1,0:T(8,128)S(1)}, f32[128,1024]{1,0:T(8,128)S(1)}, u32[]{:S(2)}, u32[]{:S(2)}) collective-permute-start(f32[128,1024]{1,0:T(8,128)S(1)} %get-tuple-element.21), channel_id=1, source_target_pairs={{0,1},{1,0},{2,3},{3,2},{4,5},{5,4},{6,7},{7,6},{8,9},{9,8},{10,11... | collective-permute-start | bytes 1572872 | tf_op jit(solution)/shard_map/ppermute | solution.py:347
  75.0 1.3 %shard_map.128 = f32[128,1024]{1,0:T(8,128)S(1)} custom-call(f32[128,1024]{1,0:T(8,128)S(1)} %get-tuple-element.18.taken_ref, bf16[1024,768]{1,0:T(8,128)(2,1)S(1)} %get-tuple-element.13.refs_3_.lt_big_ref, bf16[1024,768]{1,0:T(8,128)(2,1)S(1)} %get-tuple-element.14.lt_small_ref, bf16[256,1024]{1,0:T(8,128)(2,1)S(1)} %get-tuple-element.19.big_ref, ...), custom_call_target="tpu_custom_call" | custom-call | flops 805306368 | bytes 8912896 | tf_op jit(solution)/shard_map/pallas_call | solution.py:323
  76.4 0.7 copy-done
  77.1 0.8 slice_add_fusion.2
  77.9 1.4 %collective-permute-start.15 = (f32[64,1024]{1,0:T(8,128)}, f32[64,1024]{1,0:T(8,128)}, u32[]{:S(2)}, u32[]{:S(2)}) collective-permute-start(f32[64,1024]{1,0:T(8,128)} %slice_add_fusion.2), channel_id=1, source_target_pairs={{0,2},{1,3},{2,0},{3,1},{4,6},{5,7},{6,4},{7,5},{8,10},{9,11},{10,... | collective-permute-start | bytes 786440 | tf_op jit(solution)/shard_map/ppermute | solution.py:348
  79.5 1.0 %copy.19 = f32[256,128]{0,1:T(8,128)S(1)} copy(f32[256,128]{1,0:T(8,128)} %copy-done.4) | data formatting | bytes 262144 | tf_op jit(solution)/shard_map/pallas_call | solution.py:323
  80.5 1.2 %copy-done.3 = f32[256,1024]{1,0:T(8,128)S(1)} copy-done((f32[256,1024]{1,0:T(8,128)S(1)}, f32[256,1024]{1,0:T(8,128)}, u32[]{:S(2)}) %copy-start.3) | copy-done | bytes 1048600
  81.7 2.1 %shard_map.129 = f32[256,768]{1,0:T(8,128)S(1)} custom-call(s32[4]{0:T(128)S(1)} %pad_add_fusion.quarter_ref, f32[256,1024]{1,0:T(8,128)S(1)} %copy-done.3, bf16[1024,768]{1,0:T(8,128)(2,1)S(1)} %get-tuple-element.13.refs_3_.lt_big_ref, bf16[1024,768]{1,0:T(8,128)(2,1)S(1)} %get-tuple-element.14.lt_small_ref), custom_call_target="tpu_custom_call" | custom-call | flops 1207959552 | bytes 7340048 | tf_op jit(solution)/shard_map/pallas_call | solution.py:323
  83.8 2.4 %collective-permute-done.15 = f32[64,1024]{1,0:T(8,128)} collective-permute-done((f32[64,1024]{1,0:T(8,128)}, f32[64,1024]{1,0:T(8,128)}, u32[]{:S(2)}, u32[]{:S(2)}) %collective-permute-start.15) | collective-permute-done | bytes 262176 | tf_op jit(solution)/shard_map/ppermute | solution.py:348
  86.2 1.0 %fusion.1 = f32[64,1024]{1,0:T(8,128)S(1)} fusion(f32[64,1024]{1,0:T(8,128)} %collective-permute-done.15, f32[128,1024]{1,0:T(8,128)S(1)} %copy-done.8, f32[128,1024]{1,0:T(8,128)S(1)} %copy-done.1), kind=kLoop, calls=%fused_computation.8 | loop fusion | flops 131072 | bytes 1048576 | tf_op jit(solution)/shard_map/add | solution.py:349
  87.4 0.1 constant_dynamic-slice_fusion.3
  87.5 0.4 slice_add_fusion
  87.9 0.9 collective-permute-start.16
  88.8 0.4 slice_add_fusion.1
  89.3 0.9 collective-permute-done.16
  90.2 1.5 %collective-permute-start.17 = (f32[64,768]{1,0:T(8,128)S(1)}, f32[64,768]{1,0:T(8,128)S(1)}, u32[]{:S(2)}, u32[]{:S(2)}) collective-permute-start(f32[64,768]{1,0:T(8,128)S(1)} %slice_add_fusion.4), channel_id=1, source_target_pairs={{0,2},{1,3},{2,0},{3,1},{4,6},{5,7},{6,4},{7,5},{8,10},{9,11},{10,... | collective-permute-start | bytes 589832 | tf_op jit(solution)/shard_map/ppermute | solution.py:348
  91.7 0.8 multiply_add_fusion.1
  92.5 3.9 %collective-permute-done.17 = f32[64,768]{1,0:T(8,128)S(1)} collective-permute-done((f32[64,768]{1,0:T(8,128)S(1)}, f32[64,768]{1,0:T(8,128)S(1)}, u32[]{:S(2)}, u32[]{:S(2)}) %collective-permute-start.17) | collective-permute-done | bytes 196640 | tf_op jit(solution)/shard_map/ppermute | solution.py:348
  96.5 0.8 multiply_add_fusion
  (77 shorter events, 1.2 us)
Async XLA Ops:
  0.6 14.4 %copy-start.17 = (s32[64]{0:T(128)S(1)}, s32[64]{0:T(128)}, u32[]{:S(2)}) copy-start(s32[64]{0:T(128)} %constant.138.clone) | copy-start | bytes 772
  0.6 13.4 %copy-start.10 = (s32[2,256]{1,0:T(2,128)S(1)}, s32[2,256]{1,0:T(2,128)}, u32[]{:S(2)}) copy-start(s32[2,256]{1,0:T(2,128)} %pivots_hbm.1) | copy-start | bytes 6148
  0.7 14.5 %copy-start.11 = (f32[1024]{0:T(1024)S(1)}, f32[1024]{0:T(1024)}, u32[]{:S(2)}) copy-start(f32[1024]{0:T(1024)} %param.13) | copy-start | bytes 12292
  0.7 14.5 %copy-start.12 = (s32[1024]{0:T(1024)S(1)}, s32[1024]{0:T(1024)}, u32[]{:S(2)}) copy-start(s32[1024]{0:T(1024)} %param.14) | copy-start | bytes 12292
  0.7 38.9 %copy-start.13 = (f32[1024]{0:T(1024)S(1)}, f32[1024]{0:T(1024)}, u32[]{:S(2)}) copy-start(f32[1024]{0:T(1024)} %param.12) | copy-start | bytes 12292
  0.7 42.4 %copy-start.14 = (s32[2,64]{1,0:T(2,128)S(1)}, s32[2,64]{1,0:T(2,128)}, u32[]{:S(2)}) copy-start(s32[2,64]{1,0:T(2,128)} %param.20) | copy-start | bytes 1540
  0.7 42.4 %copy-start.15 = (f32[2,64]{1,0:T(2,128)S(1)}, f32[2,64]{1,0:T(2,128)}, u32[]{:S(2)}) copy-start(f32[2,64]{1,0:T(2,128)} %param.19) | copy-start | bytes 1540
  6.2 9.7 %collective-permute-start = (f32[16,1152]{1,0:T(8,128)S(1)}, f32[16,1152]{1,0:T(8,128)S(1)}, u32[]{:S(2)}, u32[]{:S(2)}) collective-permute-start(f32[16,1152]{1,0:T(8,128)S(1)} %shard_map.122), channel_id=1, source_target_pairs={{0,32},{4,36},{8,40},{12,44},{16,48},{20,52},{24,56},{28,60},{32,0... | collective-permute-start | bytes 221192 | tf_op jit(solution)/shard_map/ppermute | solution.py:47
  15.9 11.5 %collective-permute-start.1 = (f32[32,1152]{1,0:T(8,128)S(1)}, f32[32,1152]{1,0:T(8,128)S(1)}, u32[]{:S(2)}, u32[]{:S(2)}) collective-permute-start(f32[32,1152]{1,0:T(8,128)S(1)} %pad_maximum_fusion.1), channel_id=1, source_target_pairs={{0,136},{4,140},{8,144},{12,148},{16,152},{20,156},{24,160},{28,16... | collective-permute-start | bytes 442376 | tf_op jit(solution)/shard_map/ppermute | solution.py:47
  19.2 8.8 %collective-permute-start.2 = (f32[32,1152]{1,0:T(8,128)S(1)}, f32[32,1152]{1,0:T(8,128)S(1)}, u32[]{:S(2)}, u32[]{:S(2)}) collective-permute-start(f32[32,1152]{1,0:T(8,128)S(1)} %pad_maximum_fusion.1), channel_id=1, source_target_pairs={{0,184},{4,188},{8,128},{12,132},{16,136},{20,140},{24,144},{28,14... | collective-permute-start | bytes 442376 | tf_op jit(solution)/shard_map/ppermute | solution.py:47
  23.5 9.3 %collective-permute-start.3 = (f32[32,1152]{1,0:T(8,128)S(1)}, f32[32,1152]{1,0:T(8,128)S(1)}, u32[]{:S(2)}, u32[]{:S(2)}) collective-permute-start(f32[32,1152]{1,0:T(8,128)S(1)} %pad_maximum_fusion.1), channel_id=1, source_target_pairs={{0,16},{4,20},{8,24},{12,28},{16,32},{20,36},{24,40},{28,44},{32,4... | collective-permute-start | bytes 442376 | tf_op jit(solution)/shard_map/ppermute | solution.py:47
  33.4 17.6 %collective-permute-start.4 = (f32[128,1152]{1,0:T(8,128)}, f32[128,1152]{1,0:T(8,128)}, u32[]{:S(2)}, u32[]{:S(2)}) collective-permute-start(f32[128,1152]{1,0:T(8,128)} %constant_dynamic-update-slice_fusion.refs_0_.after_ref), channel_id=1, source_target_pairs={{0,64},{4,68},{8,72},{12,76},{16,80},{20,84},{24,88},{28,92},{32,9... | collective-permute-start | bytes 1769480 | tf_op jit(solution)/shard_map/ppermute | solution.py:47
  33.4 14.7 %collective-permute-start.6 = (f32[128,1152]{1,0:T(8,128)}, f32[128,1152]{1,0:T(8,128)}, u32[]{:S(2)}, u32[]{:S(2)}) collective-permute-start(f32[128,1152]{1,0:T(8,128)} %constant_dynamic-update-slice_fusion.refs_0_.after_ref), channel_id=1, source_target_pairs={{0,4},{4,0},{8,12},{12,8},{16,20},{20,16},{24,28},{28,24},{32,36},... | collective-permute-start | bytes 1769480 | tf_op jit(solution)/shard_map/ppermute | solution.py:47
  36.9 17.3 %collective-permute-start.5 = (f32[128,1152]{1,0:T(8,128)}, f32[128,1152]{1,0:T(8,128)}, u32[]{:S(2)}, u32[]{:S(2)}) collective-permute-start(f32[128,1152]{1,0:T(8,128)} %constant_dynamic-update-slice_fusion.refs_0_.after_ref), channel_id=1, source_target_pairs={{0,192},{4,196},{8,200},{12,204},{16,208},{20,212},{24,216},{28,22... | collective-permute-start | bytes 1769480 | tf_op jit(solution)/shard_map/ppermute | solution.py:47
  40.4 15.1 %collective-permute-start.7 = (f32[64,1152]{1,0:T(8,128)}, f32[64,1152]{1,0:T(8,128)}, u32[]{:S(2)}, u32[]{:S(2)}) collective-permute-start(f32[64,1152]{1,0:T(8,128)} %pad_maximum_fusion), channel_id=1, source_target_pairs={{0,8},{4,12},{8,16},{12,20},{16,24},{20,28},{24,32},{28,36},{32,40... | collective-permute-start | bytes 884744 | tf_op jit(solution)/shard_map/ppermute | solution.py:47
  40.4 17.8 %collective-permute-start.8 = (f32[64,1152]{1,0:T(8,128)}, f32[64,1152]{1,0:T(8,128)}, u32[]{:S(2)}, u32[]{:S(2)}) collective-permute-start(f32[64,1152]{1,0:T(8,128)} %pad_maximum_fusion), channel_id=1, source_target_pairs={{0,56},{4,60},{8,0},{12,4},{16,8},{20,12},{24,16},{28,20},{32,24},... | collective-permute-start | bytes 884744 | tf_op jit(solution)/shard_map/ppermute | solution.py:47
  50.3 0.7 copy-start.5
  51.0 15.0 %collective-permute-start.10 = (f32[96,1152]{1,0:T(8,128)}, f32[96,1152]{1,0:T(8,128)}, u32[]{:S(2)}, u32[]{:S(2)}) collective-permute-start(f32[96,1152]{1,0:T(8,128)} %get-tuple-element.15), channel_id=1, source_target_pairs={{0,64},{4,68},{8,72},{12,76},{16,80},{20,84},{24,88},{28,92},{32,9... | collective-permute-start | bytes 1327112 | tf_op jit(solution)/shard_map/ppermute | solution.py:47
  51.0 15.0 %collective-permute-start.11 = (f32[96,1152]{1,0:T(8,128)}, f32[96,1152]{1,0:T(8,128)}, u32[]{:S(2)}, u32[]{:S(2)}) collective-permute-start(f32[96,1152]{1,0:T(8,128)} %get-tuple-element.16), channel_id=1, source_target_pairs={{0,192},{4,196},{8,200},{12,204},{16,208},{20,212},{24,216},{28,22... | collective-permute-start | bytes 1327112 | tf_op jit(solution)/shard_map/ppermute | solution.py:47
  54.2 11.8 %collective-permute-start.12 = (f32[64,1152]{1,0:T(8,128)}, f32[64,1152]{1,0:T(8,128)S(1)}, u32[]{:S(2)}, u32[]{:S(2)}) collective-permute-start(f32[64,1152]{1,0:T(8,128)} %copy-done.5), channel_id=1, source_target_pairs={{0,8},{4,12},{8,16},{12,20},{16,24},{20,28},{24,32},{28,36},{32,40... | collective-permute-start | bytes 884744 | tf_op jit(solution)/shard_map/ppermute | solution.py:47
  55.5 10.5 %collective-permute-start.13 = (f32[64,1152]{1,0:T(8,128)}, f32[64,1152]{1,0:T(8,128)S(1)}, u32[]{:S(2)}, u32[]{:S(2)}) collective-permute-start(f32[64,1152]{1,0:T(8,128)} %copy-done.5), channel_id=1, source_target_pairs={{0,56},{4,60},{8,0},{12,4},{16,8},{20,12},{24,16},{28,20},{32,24},... | collective-permute-start | bytes 884744 | tf_op jit(solution)/shard_map/ppermute | solution.py:47
  58.2 7.8 %collective-permute-start.9 = (f32[64,1152]{1,0:T(8,128)S(1)}, f32[64,1152]{1,0:T(8,128)S(1)}, u32[]{:S(2)}, u32[]{:S(2)}) collective-permute-start(f32[64,1152]{1,0:T(8,128)S(1)} %shard_map.125), channel_id=1, source_target_pairs={{0,4},{4,0},{8,12},{12,8},{16,20},{20,16},{24,28},{28,24},{32,36},... | collective-permute-start | bytes 884744 | tf_op jit(solution)/shard_map/ppermute | solution.py:47
  66.0 8.9 %copy-start.16 = (f32[2,64]{1,0:T(2,128)S(1)}, f32[2,64]{1,0:T(2,128)}, u32[]{:S(2)}) copy-start(f32[2,64]{1,0:T(2,128)} %param.18) | copy-start | bytes 1540
  70.1 6.2 %copy-start.2 = (f32[256,1024]{1,0:T(8,128)}, f32[256,1024]{1,0:T(8,128)S(1)}, u32[]{:S(2)}) copy-start(f32[256,1024]{1,0:T(8,128)S(1)} %get-tuple-element.22.second_ref) | copy-start | bytes 3145732
  70.1 6.2 %copy-start.4 = (f32[256,128]{1,0:T(8,128)}, f32[256,128]{1,0:T(8,128)S(1)}, u32[]{:S(2)}) copy-start(f32[256,128]{1,0:T(8,128)S(1)} %get-tuple-element.23) | copy-start | bytes 393220
  70.1 6.3 %collective-permute-start.14 = (f32[128,1024]{1,0:T(8,128)S(1)}, f32[128,1024]{1,0:T(8,128)S(1)}, u32[]{:S(2)}, u32[]{:S(2)}) collective-permute-start(f32[128,1024]{1,0:T(8,128)S(1)} %get-tuple-element.21), channel_id=1, source_target_pairs={{0,1},{1,0},{2,3},{3,2},{4,5},{5,4},{6,7},{7,6},{8,9},{9,8},{10,11... | collective-permute-start | bytes 1572872 | tf_op jit(solution)/shard_map/ppermute | solution.py:347
  76.3 0.8 copy-start
  77.1 2.3 %copy-start.7 = (f32[128,1024]{1,0:T(8,128)}, f32[128,1024]{1,0:T(8,128)S(1)}, u32[]{:S(2)}) copy-start(f32[128,1024]{1,0:T(8,128)S(1)} %collective-permute-done.14) | copy-start | bytes 1572868
  77.9 8.2 %collective-permute-start.15 = (f32[64,1024]{1,0:T(8,128)}, f32[64,1024]{1,0:T(8,128)}, u32[]{:S(2)}, u32[]{:S(2)}) collective-permute-start(f32[64,1024]{1,0:T(8,128)} %slice_add_fusion.2), channel_id=1, source_target_pairs={{0,2},{1,3},{2,0},{3,1},{4,6},{5,7},{6,4},{7,5},{8,10},{9,11},{10,... | collective-permute-start | bytes 786440 | tf_op jit(solution)/shard_map/ppermute | solution.py:348
  80.5 1.2 %copy-start.3 = (f32[256,1024]{1,0:T(8,128)S(1)}, f32[256,1024]{1,0:T(8,128)}, u32[]{:S(2)}) copy-start(f32[256,1024]{1,0:T(8,128)} %copy-done.2) | copy-start | bytes 3145732
  81.7 4.5 %copy-start.1 = (f32[128,1024]{1,0:T(8,128)S(1)}, f32[128,1024]{1,0:T(8,128)}, u32[]{:S(2)}) copy-start(f32[128,1024]{1,0:T(8,128)} %copy-done) | copy-start | bytes 1572868
  81.7 4.5 %copy-start.8 = (f32[128,1024]{1,0:T(8,128)S(1)}, f32[128,1024]{1,0:T(8,128)}, u32[]{:S(2)}) copy-start(f32[128,1024]{1,0:T(8,128)} %copy-done.7) | copy-start | bytes 1572868
  81.7 5.4 %copy-start.6 = (f32[64,768]{1,0:T(8,128)S(1)}, f32[64,768]{1,0:T(8,128)}, u32[]{:S(2)}) copy-start(f32[64,768]{1,0:T(8,128)} %a_hbm.1) | copy-start | bytes 589828
  87.2 9.1 %copy-start.9 = (f32[64,768]{1,0:T(8,128)S(1)}, f32[64,768]{1,0:T(8,128)}, u32[]{:S(2)}) copy-start(f32[64,768]{1,0:T(8,128)} %param.17) | copy-start | bytes 589828
  87.9 2.2 %collective-permute-start.16 = (f32[128,768]{1,0:T(8,128)S(1)}, f32[128,768]{1,0:T(8,128)S(1)}, u32[]{:S(2)}, u32[]{:S(2)}) collective-permute-start(f32[128,768]{1,0:T(8,128)S(1)} %slice_add_fusion), channel_id=1, source_target_pairs={{0,1},{1,0},{2,3},{3,2},{4,5},{5,4},{6,7},{7,6},{8,9},{9,8},{10,11... | collective-permute-start | bytes 1179656 | tf_op jit(solution)/shard_map/ppermute | solution.py:347
  90.2 6.2 %collective-permute-start.17 = (f32[64,768]{1,0:T(8,128)S(1)}, f32[64,768]{1,0:T(8,128)S(1)}, u32[]{:S(2)}, u32[]{:S(2)}) collective-permute-start(f32[64,768]{1,0:T(8,128)S(1)} %slice_add_fusion.4), channel_id=1, source_target_pairs={{0,2},{1,3},{2,0},{3,1},{4,6},{5,7},{6,4},{7,5},{8,10},{9,11},{10,... | collective-permute-start | bytes 589832 | tf_op jit(solution)/shard_map/ppermute | solution.py:348

commit v6 on v5

--- a/solution.py
+++ b/solution.py
@@ -66,19 +66,11 @@
     up = moved(held[:cut], at[:half], (0, 1, 0))
     down = moved(held[:cut], at[:half], (0, -1, 0))
     early = [(held, at), ahead, behind, over, up, down]
-    few = half // 2
-    edge = few * rows
     ready = made(held)
-    mixed = cuts([(ahead[0], held.shape[0] - edge, edge, 0, 0), (behind[0], 0, edge, 0, edge)], [2 * edge])
-    low, high, middle = cuts(
-        [(over[0], 0, 3 * edge, 0, 0), (over[0], edge, 3 * edge, 1, 0), (over[0], 0, cut, 2, 0)],
-        [3 * edge, 3 * edge, cut],
-        ready[0],
-    )
+    middle, *_ = cuts([(over[0], 0, cut, 0, 0)], [cut], ready[0])
     late = [
-        moved(mixed[0], ahead[1][-few:] + behind[1][:few], (0, 0, 1)),
-        moved(low, over[1][:-few], (1, 0, 0)),
-        moved(high, over[1][few:], (-1, 0, 0)),
+        moved(over[0], over[1], (1, 0, 0)),
+        moved(over[0], over[1], (-1, 0, 0)),
         moved(middle, over[1][:half], (0, 1, 0)),
         moved(middle, over[1][:half], (0, -1, 0)),
     ]
@@ -163,7 +155,7 @@
 
     def rows_of(value):
         total = None
-        for _ in range(3):
+        for _ in range(2):
             part = value.astype(jnp.bfloat16)
             value = value - part.astype(jnp.float32)
             got = lax.dot_general(part, pick, across, preferred_element_type=jnp.float32)
@@ -417,7 +409,7 @@
         carry,
         lt_big,
         lt_small,
-        *[piece[0] for piece in late],
+        *[pltpu.with_memory_space_constraint(piece[0], pltpu.VMEM) for piece in late],
         scratch=[pltpu.VMEM((2 * late_rows, width), b16)],
     )
     keep = local_call(

time: 97.6 us -> 91.5 us (0.938)
  waiting for transfers between devices: 16.3 us -> 24.1 us
  starting transfers between devices: 42.2 us -> 34.6 us
  Pallas kernels: 24.2 us -> 19.6 us
  local copies, waits for them, and re-layouts: 7.47 us -> 5.78 us
    ppermute x14 -> x13, waiting for transfers between devices: 9.05 us -> 15.4 us  [moved(): got = lax.ppermute(block, 'wide', shift(*step))]
    ppermute x14 -> x13, starting transfers between devices: 33.7 us -> 28.4 us  [moved(): got = lax.ppermute(block, 'wide', shift(*step))]
    pallas_call x2 -> x1, Pallas kernels: 3.18 us -> 0.97 us  [cuts(): pl.pallas_call(functools.partial(cuts_kernel, parts=[part[1:] for part in...]
    ppermute x2, starting transfers between devices: 5.67 us -> 3.61 us  [finish_sum(): got = lax.ppermute(send, 'narrow', CORE)]
    pallas_call x4, Pallas kernels: 11.4 us -> 9.89 us  [local_call(): pl.pallas_call(kernel, in_specs=specs, out_specs=jax.tree.map(lambda _: v...]
    ppermute x2, waiting for transfers between devices: 6.29 us -> 7.63 us  [finish_sum(): away = lax.ppermute(keep[:half] + got[:half], 'narrow', CHIP)]
  transfers between devices with their start and end apart: 18 -> 17, of which waited for: 8 -> 10; matrix products, arithmetic and copies ran while one was open for 7% -> 6% of each run, Pallas kernels for 15% -> 14%
where the time goes in v6:
time: 91.5 us; the launch traced here: 90.9 us
  starting transfers between devices  34.6 us (38%)
  waiting for transfers between devices  24.1 us (26%)
  Pallas kernels  19.6 us (21%)
  local copies, waits for them, and re-layouts  5.78 us (6%)
  other arithmetic  5.03 us (5%)
  between operations  1 us (1%)
    ppermute x13, starting transfers between devices, moved(): got = lax.ppermute(block, 'wide', shift(*step))  28.4 us
    ppermute x13, waiting for transfers between devices, moved(): got = lax.ppermute(block, 'wide', shift(*step))  15.4 us
    pallas_call x4, Pallas kernels, local_call(): pl.pallas_call(kernel, in_specs=specs, out_specs=jax.tree.map(lambda _: v...  9.89 us
    ppermute x2, waiting for transfers between devices, finish_sum(): away = lax.ppermute(keep[:half] + got[:half], 'narrow', CHIP)  7.63 us
    pallas_call x1, Pallas kernels, tile_slots(): pl.pallas_call(slots_kernel, in_specs=[pl.BlockSpec(memory_space=pltpu.SM...  4.63 us
    unnamed x41, local copies, waits for them, and re-layouts  4.51 us
    pallas_call x1, Pallas kernels, coupled_parts(): pl.pallas_call(couple_kernel, grid=(4,), in_specs=[pl.BlockSpec((8, depth...  4.09 us
    ppermute x2, starting transfers between devices, finish_sum(): got = lax.ppermute(send, 'narrow', CORE)  3.61 us
  transfers between devices with their start and end apart: 17, of which 10 were waited for; matrix products, arithmetic and copies ran while one was open for 6% of the time, Pallas kernels for 14%

profile of v6, /device:TPU:1, one launch (start us, length us, event | category | flops | bytes accessed | tf_op | source)
XLA Modules:
  0.0 90.9 jit_solution(6773970859820901000)
XLA Ops:
  0.7 4.6 %shard_map.122 = f32[16,1152]{1,0:T(8,128)S(1)} custom-call(s32[1]{0:T(128)} %bitcast.5.low_ref, s32[2,256]{1,0:T(2,128)} %pivots_hbm.1, f32[64,768]{1,0:T(8,128)} %a_hbm.1, f32[1024,768]{1,0:T(8,128)} %lt_ref.3), custom_call_target="tpu_custom_call" | custom-call | tf_op jit(solution)/shard_map/pallas_call | solution.py:178
  5.3 7.8 %collective-permute-start = (f32[16,1152]{1,0:T(8,128)S(1)}, f32[16,1152]{1,0:T(8,128)S(1)}, u32[]{:S(2)}, u32[]{:S(2)}) collective-permute-start(f32[16,1152]{1,0:T(8,128)S(1)} %shard_map.122), channel_id=1, source_target_pairs={{0,32},{4,36},{8,40},{12,44},{16,48},{20,52},{24,56},{28,60},{32,0... | collective-permute-start | bytes 221192 | tf_op jit(solution)/shard_map/ppermute | solution.py:47
  13.2 0.6 constant_dynamic-update-slice_fusion.4
  13.9 0.2 convert_reduce_fusion
  14.2 0.1 select_reduce_fusion
  14.3 0.7 collective-permute-done
  15.0 3.3 %collective-permute-start.1 = (f32[32,1152]{1,0:T(8,128)S(1)}, f32[32,1152]{1,0:T(8,128)S(1)}, u32[]{:S(2)}, u32[]{:S(2)}) collective-permute-start(f32[32,1152]{1,0:T(8,128)S(1)} %pad_maximum_fusion.1), channel_id=1, source_target_pairs={{0,136},{4,140},{8,144},{12,148},{16,152},{20,156},{24,160},{28,16... | collective-permute-start | bytes 442376 | tf_op jit(solution)/shard_map/ppermute | solution.py:47
  18.4 4.2 %collective-permute-start.2 = (f32[32,1152]{1,0:T(8,128)S(1)}, f32[32,1152]{1,0:T(8,128)S(1)}, u32[]{:S(2)}, u32[]{:S(2)}) collective-permute-start(f32[32,1152]{1,0:T(8,128)S(1)} %pad_maximum_fusion.1), channel_id=1, source_target_pairs={{0,184},{4,188},{8,128},{12,132},{16,136},{20,140},{24,144},{28,14... | collective-permute-start | bytes 442376 | tf_op jit(solution)/shard_map/ppermute | solution.py:47
  22.6 0.6 constant_dynamic-update-slice_fusion.3
  23.2 3.3 %collective-permute-done.1 = f32[32,1152]{1,0:T(8,128)S(1)} collective-permute-done((f32[32,1152]{1,0:T(8,128)S(1)}, f32[32,1152]{1,0:T(8,128)S(1)}, u32[]{:S(2)}, u32[]{:S(2)}) %collective-permute-start.1) | collective-permute-done | bytes 147488 | tf_op jit(solution)/shard_map/ppermute | solution.py:47
  26.5 0.7 constant_dynamic-update-slice_fusion.2
  27.2 0.7 constant_dynamic-update-slice_fusion.1
  27.9 4.0 %collective-permute-done.3 = f32[32,1152]{1,0:T(8,128)S(1)} collective-permute-done((f32[32,1152]{1,0:T(8,128)S(1)}, f32[32,1152]{1,0:T(8,128)S(1)}, u32[]{:S(2)}, u32[]{:S(2)}) %collective-permute-start.3) | collective-permute-done | bytes 147488 | tf_op jit(solution)/shard_map/ppermute | solution.py:47
  31.9 0.7 constant_dynamic-update-slice_fusion.refs_0_.after_ref
  32.6 3.4 %collective-permute-start.6 = (f32[128,1152]{1,0:T(8,128)}, f32[128,1152]{1,0:T(8,128)}, u32[]{:S(2)}, u32[]{:S(2)}) collective-permute-start(f32[128,1152]{1,0:T(8,128)} %constant_dynamic-update-slice_fusion.refs_0_.after_ref), channel_id=1, source_target_pairs={{0,4},{4,0},{8,12},{12,8},{16,20},{20,16},{24,28},{28,24},{32,36},... | collective-permute-start | bytes 1769480 | tf_op jit(solution)/shard_map/ppermute | solution.py:47
  35.9 0.7 pad_maximum_fusion
  36.8 2.7 %collective-permute-start.5 = (f32[128,1152]{1,0:T(8,128)}, f32[128,1152]{1,0:T(8,128)}, u32[]{:S(2)}, u32[]{:S(2)}) collective-permute-start(f32[128,1152]{1,0:T(8,128)} %constant_dynamic-update-slice_fusion.refs_0_.after_ref), channel_id=1, source_target_pairs={{0,192},{4,196},{8,200},{12,204},{16,208},{20,212},{24,216},{28,22... | collective-permute-start | bytes 1769480 | tf_op jit(solution)/shard_map/ppermute | solution.py:47
  39.6 0.1 copy.18.index_ref
  39.8 2.7 %collective-permute-start.8 = (f32[64,1152]{1,0:T(8,128)}, f32[64,1152]{1,0:T(8,128)S(1)}, u32[]{:S(2)}, u32[]{:S(2)}) collective-permute-start(f32[64,1152]{1,0:T(8,128)} %pad_maximum_fusion), channel_id=1, source_target_pairs={{0,56},{4,60},{8,0},{12,4},{16,8},{20,12},{24,16},{28,20},{32,24},... | collective-permute-start | bytes 884744 | tf_op jit(solution)/shard_map/ppermute | solution.py:47
  42.5 5.1 %collective-permute-done.6.refs_3_.refs_0_ = f32[128,1152]{1,0:T(8,128)} collective-permute-done((f32[128,1152]{1,0:T(8,128)}, f32[128,1152]{1,0:T(8,128)}, u32[]{:S(2)}, u32[]{:S(2)}) %collective-permute-start.6) | collective-permute-done | bytes 589856 | tf_op jit(solution)/shard_map/ppermute | solution.py:47
  47.7 1.5 %collective-permute-start.9 = (f32[128,1152]{1,0:T(8,128)}, f32[128,1152]{1,0:T(8,128)S(1)}, u32[]{:S(2)}, u32[]{:S(2)}) collective-permute-start(f32[128,1152]{1,0:T(8,128)} %collective-permute-done.6.refs_3_.refs_0_), channel_id=1, source_target_pairs={{0,64},{4,68},{8,72},{12,76},{16,80},{20,84},{24,88},{28,92},{32,9... | collective-permute-start | bytes 1769480 | tf_op jit(solution)/shard_map/ppermute | solution.py:47
  49.2 4.1 %shard_map.124 = (bf16[1024,768]{1,0:T(8,128)(2,1)S(1)}, bf16[1024,768]{1,0:T(8,128)(2,1)S(1)}) custom-call(f32[8,1024]{1,0:T(8,128)S(1)} %select_maximum_fusion.weight_ref, f32[1024,768]{1,0:T(8,128)} %lt_ref.3, f32[128,1152]{1,0:T(8,128)} %constant_dynamic-update-slice_fusion.refs_0_.after_ref), custom_call_target="tpu_custom_call" | custom-call | flops 6291456 | bytes 6291456 | tf_op jit(solution)/shard_map/pallas_call | solution.py:214
  53.3 1.0 %shard_map.125 = f32[64,1152]{1,0:T(8,128)S(1)} custom-call(f32[128,1152]{1,0:T(8,128)} %collective-permute-done.6.refs_3_.refs_0_, bf16[1024,768]{1,0:T(8,128)(2,1)S(1)} %get-tuple-element.10.refs_1_.lt_big_ref), custom_call_target="tpu_custom_call" | custom-call | tf_op jit(solution)/shard_map/pallas_call | solution.py:102
  54.3 0.4 collective-permute-start.11
  54.7 2.3 %collective-permute-start.12 = (f32[64,1152]{1,0:T(8,128)S(1)}, f32[64,1152]{1,0:T(8,128)S(1)}, u32[]{:S(2)}, u32[]{:S(2)}) collective-permute-start(f32[64,1152]{1,0:T(8,128)S(1)} %shard_map.125), channel_id=1, source_target_pairs={{0,56},{4,60},{8,0},{12,4},{16,8},{20,12},{24,16},{28,20},{32,24},... | collective-permute-start | bytes 884744 | tf_op jit(solution)/shard_map/ppermute | solution.py:47
  57.0 4.0 %shard_map.123.carry_ref = f32[512,1152]{1,0:T(8,128)S(1)} custom-call(s32[512,1]{1,0:T(8,128)S(1)} %copy.18.index_ref, f32[128,1152]{1,0:T(8,128)} %constant_dynamic-update-slice_fusion.refs_0_.after_ref, f32[128,1152]{1,0:T(8,128)} %collective-permute-done.4.refs_1_, f32[128,1152]{1,0:T(8,128)} %collective-permute-done.5.refs_2_, ...), custom_call_target="tpu_custom_call" | custom-call | flops 1509949440 | bytes 2951168 | tf_op jit(solution)/shard_map/pallas_call | solution.py:315
  61.1 0.3 collective-permute-done.11.refs_2_
  61.4 1.9 %collective-permute-done.10.refs_1_ = f32[128,1152]{1,0:T(8,128)S(1)} collective-permute-done((f32[128,1152]{1,0:T(8,128)}, f32[128,1152]{1,0:T(8,128)S(1)}, u32[]{:S(2)}, u32[]{:S(2)}) %collective-permute-start.10) | collective-permute-done | bytes 589856 | tf_op jit(solution)/shard_map/ppermute | solution.py:47
  63.3 2.6 %shard_map.126 = (f32[128,1024]{1,0:T(8,128)S(1)}, f32[256,1024]{1,0:T(8,128)S(1)}, f32[256,128]{1,0:T(8,128)S(1)}, bf16[256,1024]{1,0:T(8,128)(2,1)S(1)}, bf16[...) custom-call(s32[512,1]{1,0:T(8,128)S(1)} %copy.18.index_ref, f32[8,1024]{1,0:T(8,128)S(1)} %select_maximum_fusion.weight_ref, ...), custom_call_target="tpu_custom_call" | custom-call | flops 1711276032 | bytes 10455040 | tf_op jit(solution)/shard_map/pallas_call | solution.py:315
  65.9 2.7 %collective-permute-start.13 = (f32[128,1024]{1,0:T(8,128)S(1)}, f32[128,1024]{1,0:T(8,128)S(1)}, u32[]{:S(2)}, u32[]{:S(2)}) collective-permute-start(f32[128,1024]{1,0:T(8,128)S(1)} %get-tuple-element.15), channel_id=1, source_target_pairs={{0,1},{1,0},{2,3},{3,2},{4,5},{5,4},{6,7},{7,6},{8,9},{9,8},{10,11... | collective-permute-start | bytes 1572872 | tf_op jit(solution)/shard_map/ppermute | solution.py:339
  68.7 1.2 %shard_map.127 = f32[128,1024]{1,0:T(8,128)S(1)} custom-call(f32[128,1024]{1,0:T(8,128)S(1)} %get-tuple-element.12.taken_ref, bf16[1024,768]{1,0:T(8,128)(2,1)S(1)} %get-tuple-element.10.refs_1_.lt_big_ref, bf16[1024,768]{1,0:T(8,128)(2,1)S(1)} %get-tuple-element.11.lt_small_ref, bf16[256,1024]{1,0:T(8,128)(2,1)S(1)} %get-tuple-element.13.big_ref, ...), custom_call_target="tpu_custom_call" | custom-call | flops 805306368 | bytes 8912896 | tf_op jit(solution)/shard_map/pallas_call | solution.py:315
  70.0 0.2 collective-permute-done.13
  70.2 0.6 copy-done
  70.8 0.8 slice_add_fusion.2
  71.6 1.2 %collective-permute-start.14 = (f32[64,1024]{1,0:T(8,128)}, f32[64,1024]{1,0:T(8,128)}, u32[]{:S(2)}, u32[]{:S(2)}) collective-permute-start(f32[64,1024]{1,0:T(8,128)} %slice_add_fusion.2), channel_id=1, source_target_pairs={{0,2},{1,3},{2,0},{3,1},{4,6},{5,7},{6,4},{7,5},{8,10},{9,11},{10,... | collective-permute-start | bytes 786440 | tf_op jit(solution)/shard_map/ppermute | solution.py:340
  73.1 1.2 %copy-done.3 = f32[256,1024]{1,0:T(8,128)S(1)} copy-done((f32[256,1024]{1,0:T(8,128)S(1)}, f32[256,1024]{1,0:T(8,128)}, u32[]{:S(2)}) %copy-start.3) | copy-done | bytes 1048600
  74.3 2.0 %shard_map.128 = f32[256,768]{1,0:T(8,128)S(1)} custom-call(s32[4]{0:T(128)S(1)} %pad_add_fusion.quarter_ref, f32[256,1024]{1,0:T(8,128)S(1)} %copy-done.3, bf16[1024,768]{1,0:T(8,128)(2,1)S(1)} %get-tuple-element.10.refs_1_.lt_big_ref, bf16[1024,768]{1,0:T(8,128)(2,1)S(1)} %get-tuple-element.11.lt_small_ref), custom_call_target="tpu_custom_call" | custom-call | flops 1207959552 | bytes 7340048 | tf_op jit(solution)/shard_map/pallas_call | solution.py:315
  76.3 3.5 %collective-permute-done.14 = f32[64,1024]{1,0:T(8,128)} collective-permute-done((f32[64,1024]{1,0:T(8,128)}, f32[64,1024]{1,0:T(8,128)}, u32[]{:S(2)}, u32[]{:S(2)}) %collective-permute-start.14) | collective-permute-done | bytes 262176 | tf_op jit(solution)/shard_map/ppermute | solution.py:340
  79.9 1.0 %fusion.1 = f32[64,1024]{1,0:T(8,128)S(1)} fusion(f32[64,1024]{1,0:T(8,128)} %collective-permute-done.14, f32[128,1024]{1,0:T(8,128)S(1)} %copy-done.6, f32[128,1024]{1,0:T(8,128)S(1)} %copy-done.1), kind=kLoop, calls=%fused_computation.8 | loop fusion | flops 131072 | bytes 1048576 | tf_op jit(solution)/shard_map/add | solution.py:341
  81.0 0.1 constant_dynamic-slice_fusion.3
  81.2 0.4 slice_add_fusion
  81.6 0.9 collective-permute-start.15
  82.5 0.4 slice_add_fusion.1
  83.0 0.9 collective-permute-done.15
  83.9 1.3 %collective-permute-start.16 = (f32[64,768]{1,0:T(8,128)S(1)}, f32[64,768]{1,0:T(8,128)S(1)}, u32[]{:S(2)}, u32[]{:S(2)}) collective-permute-start(f32[64,768]{1,0:T(8,128)S(1)} %slice_add_fusion.4), channel_id=1, source_target_pairs={{0,2},{1,3},{2,0},{3,1},{4,6},{5,7},{6,4},{7,5},{8,10},{9,11},{10,... | collective-permute-start | bytes 589832 | tf_op jit(solution)/shard_map/ppermute | solution.py:340
  85.2 0.8 multiply_add_fusion.1
  86.0 4.1 %collective-permute-done.16 = f32[64,768]{1,0:T(8,128)S(1)} collective-permute-done((f32[64,768]{1,0:T(8,128)S(1)}, f32[64,768]{1,0:T(8,128)S(1)}, u32[]{:S(2)}, u32[]{:S(2)}) %collective-permute-start.16) | collective-permute-done | bytes 196640 | tf_op jit(solution)/shard_map/ppermute | solution.py:340
  90.2 0.8 multiply_add_fusion
  (74 shorter events, 1.0 us)
Async XLA Ops:
  0.6 13.5 %copy-start.15 = (s32[64]{0:T(128)S(1)}, s32[64]{0:T(128)}, u32[]{:S(2)}) copy-start(s32[64]{0:T(128)} %constant.138.clone) | copy-start | bytes 772
  0.6 12.5 %copy-start.8 = (s32[2,256]{1,0:T(2,128)S(1)}, s32[2,256]{1,0:T(2,128)}, u32[]{:S(2)}) copy-start(s32[2,256]{1,0:T(2,128)} %pivots_hbm.1) | copy-start | bytes 6148
  0.7 13.6 %copy-start.9 = (f32[1024]{0:T(1024)S(1)}, f32[1024]{0:T(1024)}, u32[]{:S(2)}) copy-start(f32[1024]{0:T(1024)} %param.13) | copy-start | bytes 12292
  0.7 13.6 %copy-start.10 = (s32[1024]{0:T(1024)S(1)}, s32[1024]{0:T(1024)}, u32[]{:S(2)}) copy-start(s32[1024]{0:T(1024)} %param.14) | copy-start | bytes 12292
  0.7 41.8 %copy-start.11 = (f32[1024]{0:T(1024)S(1)}, f32[1024]{0:T(1024)}, u32[]{:S(2)}) copy-start(f32[1024]{0:T(1024)} %param.12) | copy-start | bytes 12292
  0.7 48.5 %copy-start.12 = (s32[2,64]{1,0:T(2,128)S(1)}, s32[2,64]{1,0:T(2,128)}, u32[]{:S(2)}) copy-start(s32[2,64]{1,0:T(2,128)} %param.20) | copy-start | bytes 1540
  0.7 48.4 %copy-start.13 = (f32[2,64]{1,0:T(2,128)S(1)}, f32[2,64]{1,0:T(2,128)}, u32[]{:S(2)}) copy-start(f32[2,64]{1,0:T(2,128)} %param.19) | copy-start | bytes 1540
  5.3 9.7 %collective-permute-start = (f32[16,1152]{1,0:T(8,128)S(1)}, f32[16,1152]{1,0:T(8,128)S(1)}, u32[]{:S(2)}, u32[]{:S(2)}) collective-permute-start(f32[16,1152]{1,0:T(8,128)S(1)} %shard_map.122), channel_id=1, source_target_pairs={{0,32},{4,36},{8,40},{12,44},{16,48},{20,52},{24,56},{28,60},{32,0... | collective-permute-start | bytes 221192 | tf_op jit(solution)/shard_map/ppermute | solution.py:47
  15.0 11.5 %collective-permute-start.1 = (f32[32,1152]{1,0:T(8,128)S(1)}, f32[32,1152]{1,0:T(8,128)S(1)}, u32[]{:S(2)}, u32[]{:S(2)}) collective-permute-start(f32[32,1152]{1,0:T(8,128)S(1)} %pad_maximum_fusion.1), channel_id=1, source_target_pairs={{0,136},{4,140},{8,144},{12,148},{16,152},{20,156},{24,160},{28,16... | collective-permute-start | bytes 442376 | tf_op jit(solution)/shard_map/ppermute | solution.py:47
  18.4 8.8 %collective-permute-start.2 = (f32[32,1152]{1,0:T(8,128)S(1)}, f32[32,1152]{1,0:T(8,128)S(1)}, u32[]{:S(2)}, u32[]{:S(2)}) collective-permute-start(f32[32,1152]{1,0:T(8,128)S(1)} %pad_maximum_fusion.1), channel_id=1, source_target_pairs={{0,184},{4,188},{8,128},{12,132},{16,136},{20,140},{24,144},{28,14... | collective-permute-start | bytes 442376 | tf_op jit(solution)/shard_map/ppermute | solution.py:47
  22.6 9.3 %collective-permute-start.3 = (f32[32,1152]{1,0:T(8,128)S(1)}, f32[32,1152]{1,0:T(8,128)S(1)}, u32[]{:S(2)}, u32[]{:S(2)}) collective-permute-start(f32[32,1152]{1,0:T(8,128)S(1)} %pad_maximum_fusion.1), channel_id=1, source_target_pairs={{0,16},{4,20},{8,24},{12,28},{16,32},{20,36},{24,40},{28,44},{32,4... | collective-permute-start | bytes 442376 | tf_op jit(solution)/shard_map/ppermute | solution.py:47
  32.6 15.1 %collective-permute-start.6 = (f32[128,1152]{1,0:T(8,128)}, f32[128,1152]{1,0:T(8,128)}, u32[]{:S(2)}, u32[]{:S(2)}) collective-permute-start(f32[128,1152]{1,0:T(8,128)} %constant_dynamic-update-slice_fusion.refs_0_.after_ref), channel_id=1, source_target_pairs={{0,4},{4,0},{8,12},{12,8},{16,20},{20,16},{24,28},{28,24},{32,36},... | collective-permute-start | bytes 1769480 | tf_op jit(solution)/shard_map/ppermute | solution.py:47
  35.9 18.8 %collective-permute-start.4 = (f32[128,1152]{1,0:T(8,128)}, f32[128,1152]{1,0:T(8,128)}, u32[]{:S(2)}, u32[]{:S(2)}) collective-permute-start(f32[128,1152]{1,0:T(8,128)} %constant_dynamic-update-slice_fusion.refs_0_.after_ref), channel_id=1, source_target_pairs={{0,64},{4,68},{8,72},{12,76},{16,80},{20,84},{24,88},{28,92},{32,9... | collective-permute-start | bytes 1769480 | tf_op jit(solution)/shard_map/ppermute | solution.py:47
  36.7 11.0 %collective-permute-start.7 = (f32[64,1152]{1,0:T(8,128)}, f32[64,1152]{1,0:T(8,128)S(1)}, u32[]{:S(2)}, u32[]{:S(2)}) collective-permute-start(f32[64,1152]{1,0:T(8,128)} %pad_maximum_fusion), channel_id=1, source_target_pairs={{0,8},{4,12},{8,16},{12,20},{16,24},{20,28},{24,32},{28,36},{32,40... | collective-permute-start | bytes 884744 | tf_op jit(solution)/shard_map/ppermute | solution.py:47
  36.8 20.3 %collective-permute-start.5 = (f32[128,1152]{1,0:T(8,128)}, f32[128,1152]{1,0:T(8,128)}, u32[]{:S(2)}, u32[]{:S(2)}) collective-permute-start(f32[128,1152]{1,0:T(8,128)} %constant_dynamic-update-slice_fusion.refs_0_.after_ref), channel_id=1, source_target_pairs={{0,192},{4,196},{8,200},{12,204},{16,208},{20,212},{24,216},{28,22... | collective-permute-start | bytes 1769480 | tf_op jit(solution)/shard_map/ppermute | solution.py:47
  39.8 14.5 %collective-permute-start.8 = (f32[64,1152]{1,0:T(8,128)}, f32[64,1152]{1,0:T(8,128)S(1)}, u32[]{:S(2)}, u32[]{:S(2)}) collective-permute-start(f32[64,1152]{1,0:T(8,128)} %pad_maximum_fusion), channel_id=1, source_target_pairs={{0,56},{4,60},{8,0},{12,4},{16,8},{20,12},{24,16},{28,20},{32,24},... | collective-permute-start | bytes 884744 | tf_op jit(solution)/shard_map/ppermute | solution.py:47
  47.7 15.6 %collective-permute-start.10 = (f32[128,1152]{1,0:T(8,128)}, f32[128,1152]{1,0:T(8,128)S(1)}, u32[]{:S(2)}, u32[]{:S(2)}) collective-permute-start(f32[128,1152]{1,0:T(8,128)} %collective-permute-done.6.refs_3_.refs_0_), channel_id=1, source_target_pairs={{0,192},{4,196},{8,200},{12,204},{16,208},{20,212},{24,216},{28,22... | collective-permute-start | bytes 1769480 | tf_op jit(solution)/shard_map/ppermute | solution.py:47
  47.7 1.5 %copy-start.16 = (f32[64,1152]{1,0:T(8,128)}, f32[64,1152]{1,0:T(8,128)S(1)}, u32[]{:S(2)}) copy-start(f32[64,1152]{1,0:T(8,128)S(1)} %collective-permute-done.7.refs_4_) | copy-start | bytes 884740
  47.7 15.6 %collective-permute-start.9 = (f32[128,1152]{1,0:T(8,128)}, f32[128,1152]{1,0:T(8,128)S(1)}, u32[]{:S(2)}, u32[]{:S(2)}) collective-permute-start(f32[128,1152]{1,0:T(8,128)} %collective-permute-done.6.refs_3_.refs_0_), channel_id=1, source_target_pairs={{0,64},{4,68},{8,72},{12,76},{16,80},{20,84},{24,88},{28,92},{32,9... | collective-permute-start | bytes 1769480 | tf_op jit(solution)/shard_map/ppermute | solution.py:47
  54.2 2.8 %copy-start.17 = (f32[64,1152]{1,0:T(8,128)}, f32[64,1152]{1,0:T(8,128)S(1)}, u32[]{:S(2)}) copy-start(f32[64,1152]{1,0:T(8,128)S(1)} %collective-permute-done.8.refs_5_) | copy-start | bytes 884740
  54.3 7.2 %collective-permute-start.11 = (f32[64,1152]{1,0:T(8,128)S(1)}, f32[64,1152]{1,0:T(8,128)S(1)}, u32[]{:S(2)}, u32[]{:S(2)}) collective-permute-start(f32[64,1152]{1,0:T(8,128)S(1)} %shard_map.125), channel_id=1, source_target_pairs={{0,8},{4,12},{8,16},{12,20},{16,24},{20,28},{24,32},{28,36},{32,40... | collective-permute-start | bytes 884744 | tf_op jit(solution)/shard_map/ppermute | solution.py:47
  54.7 6.7 %collective-permute-start.12 = (f32[64,1152]{1,0:T(8,128)S(1)}, f32[64,1152]{1,0:T(8,128)S(1)}, u32[]{:S(2)}, u32[]{:S(2)}) collective-permute-start(f32[64,1152]{1,0:T(8,128)S(1)} %shard_map.125), channel_id=1, source_target_pairs={{0,56},{4,60},{8,0},{12,4},{16,8},{20,12},{24,16},{28,20},{32,24},... | collective-permute-start | bytes 884744 | tf_op jit(solution)/shard_map/ppermute | solution.py:47
  63.3 5.4 %copy-start.14 = (f32[2,64]{1,0:T(2,128)S(1)}, f32[2,64]{1,0:T(2,128)}, u32[]{:S(2)}) copy-start(f32[2,64]{1,0:T(2,128)} %param.18) | copy-start | bytes 1540
  65.9 4.1 %copy-start.2 = (f32[256,1024]{1,0:T(8,128)}, f32[256,1024]{1,0:T(8,128)S(1)}, u32[]{:S(2)}) copy-start(f32[256,1024]{1,0:T(8,128)S(1)} %get-tuple-element.16.second_ref) | copy-start | bytes 3145732
  65.9 4.3 %collective-permute-start.13 = (f32[128,1024]{1,0:T(8,128)S(1)}, f32[128,1024]{1,0:T(8,128)S(1)}, u32[]{:S(2)}, u32[]{:S(2)}) collective-permute-start(f32[128,1024]{1,0:T(8,128)S(1)} %get-tuple-element.15), channel_id=1, source_target_pairs={{0,1},{1,0},{2,3},{3,2},{4,5},{5,4},{6,7},{7,6},{8,9},{9,8},{10,11... | collective-permute-start | bytes 1572872 | tf_op jit(solution)/shard_map/ppermute | solution.py:339
  70.0 0.8 copy-start
  70.8 2.1 %copy-start.5 = (f32[128,1024]{1,0:T(8,128)}, f32[128,1024]{1,0:T(8,128)S(1)}, u32[]{:S(2)}) copy-start(f32[128,1024]{1,0:T(8,128)S(1)} %collective-permute-done.13) | copy-start | bytes 1572868
  71.6 8.2 %collective-permute-start.14 = (f32[64,1024]{1,0:T(8,128)}, f32[64,1024]{1,0:T(8,128)}, u32[]{:S(2)}, u32[]{:S(2)}) collective-permute-start(f32[64,1024]{1,0:T(8,128)} %slice_add_fusion.2), channel_id=1, source_target_pairs={{0,2},{1,3},{2,0},{3,1},{4,6},{5,7},{6,4},{7,5},{8,10},{9,11},{10,... | collective-permute-start | bytes 786440 | tf_op jit(solution)/shard_map/ppermute | solution.py:340
  73.1 1.2 %copy-start.3 = (f32[256,1024]{1,0:T(8,128)S(1)}, f32[256,1024]{1,0:T(8,128)}, u32[]{:S(2)}) copy-start(f32[256,1024]{1,0:T(8,128)} %copy-done.2) | copy-start | bytes 3145732
  74.3 5.5 %copy-start.1 = (f32[128,1024]{1,0:T(8,128)S(1)}, f32[128,1024]{1,0:T(8,128)}, u32[]{:S(2)}) copy-start(f32[128,1024]{1,0:T(8,128)} %copy-done) | copy-start | bytes 1572868
  74.3 5.5 %copy-start.6 = (f32[128,1024]{1,0:T(8,128)S(1)}, f32[128,1024]{1,0:T(8,128)}, u32[]{:S(2)}) copy-start(f32[128,1024]{1,0:T(8,128)} %copy-done.5) | copy-start | bytes 1572868
  74.3 6.5 %copy-start.4 = (f32[64,768]{1,0:T(8,128)S(1)}, f32[64,768]{1,0:T(8,128)}, u32[]{:S(2)}) copy-start(f32[64,768]{1,0:T(8,128)} %a_hbm.1) | copy-start | bytes 589828
  80.9 9.1 %copy-start.7 = (f32[64,768]{1,0:T(8,128)S(1)}, f32[64,768]{1,0:T(8,128)}, u32[]{:S(2)}) copy-start(f32[64,768]{1,0:T(8,128)} %param.17) | copy-start | bytes 589828
  81.6 2.2 %collective-permute-start.15 = (f32[128,768]{1,0:T(8,128)S(1)}, f32[128,768]{1,0:T(8,128)S(1)}, u32[]{:S(2)}, u32[]{:S(2)}) collective-permute-start(f32[128,768]{1,0:T(8,128)S(1)} %slice_add_fusion), channel_id=1, source_target_pairs={{0,1},{1,0},{2,3},{3,2},{4,5},{5,4},{6,7},{7,6},{8,9},{9,8},{10,11... | collective-permute-start | bytes 1179656 | tf_op jit(solution)/shard_map/ppermute | solution.py:339
  83.9 6.2 %collective-permute-start.16 = (f32[64,768]{1,0:T(8,128)S(1)}, f32[64,768]{1,0:T(8,128)S(1)}, u32[]{:S(2)}, u32[]{:S(2)}) collective-permute-start(f32[64,768]{1,0:T(8,128)S(1)} %slice_add_fusion.4), channel_id=1, source_target_pairs={{0,2},{1,3},{2,0},{3,1},{4,6},{5,7},{6,4},{7,5},{8,10},{9,11},{10,... | collective-permute-start | bytes 589832 | tf_op jit(solution)/shard_map/ppermute | solution.py:340

commit v7 on v6

--- a/solution.py
+++ b/solution.py
@@ -12,25 +12,6 @@
 NY, NZ, NH = 4, 8, 2
 CORE = [(0, 1), (1, 0), (2, 3), (3, 2)]
 CHIP = [(0, 2), (1, 3), (2, 0), (3, 1)]
-HIGH = lax.Precision.HIGH
-
-
-def couple(block, diag, off, pairs):
-    joined = off * pairs.astype(jnp.float32)
-    zero_row = jnp.zeros_like(block[:1])
-    after = jnp.concatenate([block[1:], zero_row], 0)
-    before = jnp.concatenate([zero_row, block[:-1]], 0)
-    lower = jnp.concatenate([jnp.zeros_like(joined[:1]), joined[:-1]], 0)
-    return diag[:, None] * block + joined[:, None] * after + lower[:, None] * before
-
-
-def couple_lanes(block, diag, off, pairs):
-    joined = off * pairs.astype(jnp.float32)
-    zero = jnp.zeros_like(block[:, :1])
-    after = jnp.concatenate([block[:, 1:], zero], 1)
-    before = jnp.concatenate([zero, block[:, :-1]], 1)
-    lower = jnp.concatenate([jnp.zeros_like(joined[:1]), joined[:-1]], 0)
-    return diag[None, :] * block + joined[None, :] * after + lower[None, :] * before
 
 
 def shift(dy, dz, dh):
@@ -55,19 +36,23 @@
     held, at = block, [(0, 0, 0)]
     got, its = moved(held, at, (0, 4, 0))
     held, at = jnp.concatenate([held, got], 0), at + its
+    ready = made(got)
     parts = [moved(held, at, step) for step in ((2, 1, 0), (2, -1, 0), (0, 2, 0))]
-    held = jnp.concatenate([held] + [p[0] for p in parts], 0)
+    pair = 2 * rows
+    blocks = [held] + [p[0] for p in parts]
+    places = [(piece, 0, pair, 0, pair * i) for i, piece in enumerate(blocks)]
+    places += [(blocks[i], 0, pair, 1, pair * i) for i in range(2)]
+    held, low = cuts(places, [4 * pair, 2 * pair], ready[0])
     at = at + parts[0][1] + parts[1][1] + parts[2][1]
     half = len(at) // 2
     cut = half * rows
     over = moved(held, at, (0, 0, 1))
     ahead = moved(held, at, (1, 0, 0))
     behind = moved(held, at, (-1, 0, 0))
-    up = moved(held[:cut], at[:half], (0, 1, 0))
-    down = moved(held[:cut], at[:half], (0, -1, 0))
+    up = moved(low, at[:half], (0, 1, 0))
+    down = moved(low, at[:half], (0, -1, 0))
     early = [(held, at), ahead, behind, over, up, down]
-    ready = made(held)
-    middle, *_ = cuts([(over[0], 0, cut, 0, 0)], [cut], ready[0])
+    (middle,) = cuts([(over[0], 0, cut, 0, 0)], [cut])
     late = [
         moved(over[0], over[1], (1, 0, 0)),
         moved(over[0], over[1], (-1, 0, 0)),
@@ -197,13 +182,7 @@
 
 
 def couple_kernel(weight_ref, lt_ref, after_ref, big_ref, small_ref):
-    value = lt_ref[...]
-    rows = value.shape[0]
-    after = pltpu.roll(value, rows - 1, 0)
-    before = pltpu.roll(value, 1, 0)
-    weight = weight_ref[...].T
-    mixed = weight[:, 0:1] * value + weight[:, 1:2] * after + weight[:, 2:3] * before
-    big_ref[...], small_ref[...] = split(mixed)
+    big_ref[...], small_ref[...] = split(couple_rows(lt_ref[...], weight_ref[...].T))
 
 
 def coupled_parts(weights, prior_lt, following):
@@ -228,39 +207,39 @@
     )(weights, in_hbm(prior_lt), following)
 
 
-def fill_parts(parts_ref, pieces):
-    total = parts_ref.shape[0] // 2
-    start = 0
-    for ref in pieces:
-        size = ref.shape[0]
-        big, small = split(ref[...])
-        parts_ref[start : start + size, :] = big
-        parts_ref[total + start : total + start + size, :] = small
-        start += size
-
-
-def hits(index, base, total):
-    slot = base + lax.broadcasted_iota(jnp.int32, (index.shape[0], total), 1)
-    hit = jnp.where(index == slot, 1.0, 0.0).astype(jnp.bfloat16)
-    return jnp.concatenate([hit, hit], 1)
-
-
-def early_kernel(index_ref, *refs):
-    *pieces, out_ref, rows_ref, parts_ref, sems = refs
+def fill_parts(parts_ref, pieces, rows_ref, sems):
     total = rows_ref.shape[0]
     start, copies = 0, []
     for i, ref in enumerate(pieces):
-        size = ref.shape[0]
-        rows = slice(start, start + size)
+        rows = slice(start, start + ref.shape[0])
         copies.append((rows, pltpu.make_async_copy(ref, rows_ref.at[rows], sems.at[i])))
         copies[-1][1].start()
-        start += size
-    hit = hits(index_ref[...], 0, total)
+        start += ref.shape[0]
     for rows, copy in copies:
         copy.wait()
         big, small = split(rows_ref[rows, :])
         parts_ref[rows, :] = big
         parts_ref[total + rows.start : total + rows.stop, :] = small
+
+
+def piece_scratch(rows, width, pieces):
+    return [
+        pltpu.VMEM((2 * rows, width), jnp.bfloat16),
+        pltpu.VMEM((rows, width), jnp.float32),
+        pltpu.SemaphoreType.DMA((len(pieces),)),
+    ]
+
+
+def hits(index, base, total):
+    slot = base + lax.broadcasted_iota(jnp.int32, (index.shape[0], total), 1)
+    hit = jnp.where(index == slot, 1.0, 0.0).astype(jnp.bfloat16)
+    return jnp.concatenate([hit, hit], 1)
+
+
+def early_kernel(index_ref, *refs):
+    *pieces, out_ref, parts_ref, rows_ref, sems = refs
+    hit = hits(index_ref[...], 0, rows_ref.shape[0])
+    fill_parts(parts_ref, pieces, rows_ref, sems)
     for low in range(0, out_ref.shape[1], 384):
         out_ref[:, low : low + 384] = jnp.dot(
             hit, parts_ref[:, low : low + 384], preferred_element_type=jnp.float32
@@ -268,9 +247,9 @@
 
 
 def send_kernel(index_ref, weight_ref, carry_ref, lt_big_ref, lt_small_ref, *refs, base):
-    *pieces, out_ref, second_ref, entries_ref, big_ref, small_ref, keep_ref, parts_ref = refs
-    fill_parts(parts_ref, pieces)
-    total = parts_ref.shape[0] // 2
+    *pieces, out_ref, second_ref, entries_ref, big_ref, small_ref, keep_ref, parts_ref, rows_ref, sems = refs
+    fill_parts(parts_ref, pieces, rows_ref, sems)
+    total = rows_ref.shape[0]
     rows, k_local = out_ref.shape[0], lt_big_ref.shape[0]
     tile_rows = lt_big_ref.shape[1]
     hit = hits(index_ref[...], base, total)
@@ -334,11 +313,62 @@
     return jnp.concatenate([lax.dynamic_slice_in_dim(rows, q * blocks, blocks) for q in quarters], 0)
 
 
-def finish_sum(send, keep):
-    half = keep.shape[0] // 2
+def in_vmem(value):
+    return pltpu.with_memory_space_constraint(value, pltpu.VMEM)
+
+
+def add_kernel(keep_ref, got_ref, away_ref, rest_ref):
+    half = away_ref.shape[0]
+    away_ref[...] = keep_ref[:half, :] + got_ref[:half, :]
+    rest_ref[...] = keep_ref[half:, :] + got_ref[half:, :]
+
+
+def hop_sum(send, keep):
     got = lax.ppermute(send, "narrow", CORE)
-    away = lax.ppermute(keep[:half] + got[:half], "narrow", CHIP)
-    return keep[half:] + got[half:] + away
+    part = jax.ShapeDtypeStruct((keep.shape[0] // 2, keep.shape[1]), keep.dtype)
+    away, rest = local_call(add_kernel, (part, part), keep.size, in_vmem(keep), in_vmem(got))
+    return rest, lax.ppermute(away, "narrow", CHIP)
+
+
+def couple_rows(value, weight):
+    rows = value.shape[0]
+    after = pltpu.roll(value, rows - 1, 0)
+    before = pltpu.roll(value, 1, 0)
+    return weight[:, 0:1] * value + weight[:, 1:2] * after + weight[:, 2:3] * before
+
+
+def middle_kernel(
+    quarter_ref, weight_ref, a_ref, entries_ref, update_ref, rest_ref, away_ref,
+    out_ref, send_ref, keep_ref, turned_ref,
+):
+    blocks, tile_rows = a_ref.shape
+    half = send_ref.shape[0]
+    summed = rest_ref[...] + away_ref[...]
+    weight = weight_ref[...].T[:blocks]
+    w_first = a_ref[...] - summed[:, :tile_rows]
+    out_ref[...] = couple_rows(w_first, weight)
+    crossed = couple_rows(entries_ref[...].T[:blocks] - summed[:, tile_rows:], weight)
+    turned_ref[:, :blocks] = crossed.T
+    right = split(w_first)
+    for i, ref in enumerate((send_ref, keep_ref)):
+        left = [
+            turned_ref[pl.ds(pl.multiple_of(quarter_ref[2 * i + j] * blocks, blocks), blocks), :blocks]
+            for j in range(2)
+        ]
+        left = split(jnp.concatenate(left, 0))
+        ref[...] = update_ref[i * half : (i + 1) * half, :] + dot3(left, right, ((1,), (0,)))
+
+
+def last_kernel(weight_ref, a_ref, rest_ref, away_ref, out_ref):
+    weight = weight_ref[...].T[: a_ref.shape[0]]
+    out_ref[...] = couple_rows(a_ref[...] - (rest_ref[...] + away_ref[...]), weight)
+
+
+def operator_rows(diag, off, pairs):
+    joined = off * pairs.astype(jnp.float32)
+    lower = jnp.concatenate([jnp.zeros_like(joined[:1]), joined[:-1]])
+    rows = jnp.stack([diag, joined, lower])
+    return jnp.pad(rows, ((0, 5), (0, -diag.shape[0] % 128)))
 
 
 def shards(
@@ -353,9 +383,7 @@
     order = jnp.arange(count)
     rank = jnp.sum((tile[:, None] == tile[None, :]) & (order[None, :] < order[:, None]), 1)
     block = tile_slots(pivots, here * tile_rows, prior_lt, a_first)
-    joined = prior_e * prior_pairs.astype(jnp.float32)
-    lower = jnp.concatenate([jnp.zeros_like(joined[:1]), joined[:-1]])
-    weights = jnp.pad(jnp.stack([prior_d, joined, lower]), ((0, 5), (0, 0)))
+    weights = operator_rows(prior_d, prior_e, prior_pairs)
     early, late, (lt_big, lt_small) = gather_tiles(
         block, lambda held: coupled_parts(weights, prior_lt, held)
     )
@@ -386,11 +414,7 @@
         4 * 2 * P_SIZE * early_rows * width,
         where,
         *[in_hbm(piece[0]) for piece in early],
-        scratch=[
-            pltpu.VMEM((early_rows, width), f32),
-            pltpu.VMEM((2 * early_rows, width), b16),
-            pltpu.SemaphoreType.DMA((len(early),)),
-        ],
+        scratch=piece_scratch(early_rows, width, early),
         hbm=len(early),
     )
     send, second, entries, second_big, second_small, taken = local_call(
@@ -409,8 +433,9 @@
         carry,
         lt_big,
         lt_small,
-        *[pltpu.with_memory_space_constraint(piece[0], pltpu.VMEM) for piece in late],
-        scratch=[pltpu.VMEM((2 * late_rows, width), b16)],
+        *[in_hbm(piece[0]) for piece in late],
+        scratch=piece_scratch(late_rows, width, late),
+        hbm=len(late),
     )
     keep = local_call(
         keep_kernel,
@@ -422,7 +447,7 @@
         second_big,
         second_small,
     )
-    summed = finish_sum(send, keep)
+    rest, away = hop_sum(send, keep)
     update_second = local_call(
         second_kernel,
         shape((P_SIZE, tile_rows), f32),
@@ -434,18 +459,30 @@
         scratch=[pltpu.VMEM((P_SIZE, tile_rows), f32)],
         smem=1,
     )
-    w_first = a_first - summed[:, :tile_rows]
-    l_first = couple(w_first, inv_d[0], inv_e[0], panel_pairs[0])
-    w_crossed = entries[:, :blocks] - summed[:, tile_rows:].T
-    crossed = couple_lanes(w_crossed, inv_d[0], inv_e[0], panel_pairs[0])
-    plain = (((1,), (0,)), ((), ()))
-    halves = []
-    for low in (0, 2):
-        rows = in_quarters(crossed, quarters[low : low + 2], blocks)
-        part = update_second[low * blocks : (low + 2) * blocks]
-        halves.append(part + lax.dot_general(rows, w_first, plain, precision=HIGH))
-    w_second = a_second - finish_sum(*halves)
-    l_second = couple(w_second, inv_d[1], inv_e[1], panel_pairs[1])
+    l_first, send, keep = local_call(
+        middle_kernel,
+        (shape((blocks, tile_rows), f32), shape((half, tile_rows), f32), shape((half, tile_rows), f32)),
+        6 * P_SIZE * blocks * tile_rows,
+        jnp.stack(quarters),
+        operator_rows(inv_d[0], inv_e[0], panel_pairs[0]),
+        a_first,
+        entries,
+        update_second,
+        in_vmem(rest),
+        in_vmem(away),
+        scratch=[pltpu.VMEM((P_SIZE, 128), f32)],
+        smem=1,
+    )
+    rest, away = hop_sum(send, keep)
+    l_second = local_call(
+        last_kernel,
+        shape((blocks, tile_rows), f32),
+        8 * blocks * tile_rows,
+        operator_rows(inv_d[1], inv_e[1], panel_pairs[1]),
+        a_second,
+        in_vmem(rest),
+        in_vmem(away),
+    )
     return (l_first, l_second)
 
 

time: 91.5 us -> 92.9 us (1.015)
  Pallas kernels: 19.6 us -> 25.7 us
  local copies, waits for them, and re-layouts: 5.78 us -> 1.12 us
  other arithmetic: 5.03 us -> 0.77 us
  waiting for transfers between devices: 24.1 us -> 28 us
  starting transfers between devices: 34.6 us -> 36.1 us
    pallas_call x4 -> x8, Pallas kernels: 9.89 us -> 13.7 us  [local_call(): pl.pallas_call(kernel, in_specs=specs, out_specs=jax.tree.map(lambda _: v...]
    unnamed x41 -> x29, local copies, waits for them, and re-layouts: 4.51 us -> 0.79 us
    add x6 -> x0, other arithmetic: 3.46 us -> none  [the longest x2 1.57 us: couple(): diag[:, None] * block + joined[:, None] * after + lower[:, None] * before]
    ppermute x13, waiting for transfers between devices: 15.4 us -> 17.8 us  [moved(): got = lax.ppermute(block, 'wide', shift(*step))]
    pallas_call x1 -> x2, Pallas kernels: 0.97 us -> 3.22 us  [cuts(): pl.pallas_call(functools.partial(cuts_kernel, parts=[part[1:] for part in...]
    ppermute x4, waiting for transfers between devices: 8.68 us -> 10.3 us  [the longest x2 8.71 us: hop_sum(): return (rest, lax.ppermute(away, 'narrow', CHIP))]
    ppermute x4, starting transfers between devices: 6.15 us -> 7.52 us  [the longest x2 4.24 us: hop_sum(): got = lax.ppermute(send, 'narrow', CORE)]
  transfers between devices with their start and end apart: 17 -> 17, of which waited for: 10 -> 9; matrix products, arithmetic and copies ran while one was open for 6% -> 1% of each run, Pallas kernels for 14% -> 13%
where the time goes in v7:
time: 92.9 us; the launch traced here: 92.6 us
  starting transfers between devices  36.1 us (39%)
  waiting for transfers between devices  28 us (30%)
  Pallas kernels  25.7 us (28%)
  local copies, waits for them, and re-layouts  1.12 us (1%)
  between operations  0.96 us (1%)
    ppermute x13, starting transfers between devices, moved(): got = lax.ppermute(block, 'wide', shift(*step))  28.5 us
    ppermute x13, waiting for transfers between devices, moved(): got = lax.ppermute(block, 'wide', shift(*step))  17.8 us
    pallas_call x8, Pallas kernels, local_call(): pl.pallas_call(kernel, in_specs=specs, out_specs=jax.tree.map(lambda _: v...  13.7 us
    ppermute x2, waiting for transfers between devices, hop_sum(): return (rest, lax.ppermute(away, 'narrow', CHIP))  8.71 us
    pallas_call x1, Pallas kernels, tile_slots(): pl.pallas_call(slots_kernel, in_specs=[pl.BlockSpec(memory_space=pltpu.SM...  4.63 us
    ppermute x2, starting transfers between devices, hop_sum(): got = lax.ppermute(send, 'narrow', CORE)  4.24 us
    pallas_call x1, Pallas kernels, coupled_parts(): pl.pallas_call(couple_kernel, grid=(4,), in_specs=[pl.BlockSpec((8, depth...  4.09 us
    ppermute x2, starting transfers between devices, hop_sum(): return (rest, lax.ppermute(away, 'narrow', CHIP))  3.27 us
  transfers between devices with their start and end apart: 17, of which 9 were waited for; matrix products, arithmetic and copies ran while one was open for 1% of the time, Pallas kernels for 13%

profile of v7, /device:TPU:1, one launch (start us, length us, event | category | flops | bytes accessed | tf_op | source)
XLA Modules:
  0.0 92.6 jit_solution(13478882542080744071)
XLA Ops:
  0.7 4.6 %shard_map.122 = f32[16,1152]{1,0:T(8,128)S(1)} custom-call(s32[1]{0:T(128)} %bitcast.10.low_ref, s32[2,256]{1,0:T(2,128)} %pivots_hbm.1, f32[64,768]{1,0:T(8,128)} %a_ref.2, f32[1024,768]{1,0:T(8,128)} %lt_ref.3), custom_call_target="tpu_custom_call" | custom-call | tf_op jit(solution)/shard_map/pallas_call | solution.py:163
  5.3 7.8 %collective-permute-start = (f32[16,1152]{1,0:T(8,128)S(1)}, f32[16,1152]{1,0:T(8,128)S(1)}, u32[]{:S(2)}, u32[]{:S(2)}) collective-permute-start(f32[16,1152]{1,0:T(8,128)S(1)} %shard_map.122), channel_id=1, source_target_pairs={{0,32},{4,36},{8,40},{12,44},{16,48},{20,52},{24,56},{28,60},{32,0... | collective-permute-start | bytes 221192 | tf_op jit(solution)/shard_map/ppermute | solution.py:28
  13.2 1.8 %collective-permute-done.after_ref = f32[16,1152]{1,0:T(8,128)S(1)} collective-permute-done((f32[16,1152]{1,0:T(8,128)S(1)}, f32[16,1152]{1,0:T(8,128)S(1)}, u32[]{:S(2)}, u32[]{:S(2)}) %collective-permute-start) | collective-permute-done | bytes 73760 | tf_op jit(solution)/shard_map/ppermute | solution.py:28
  15.0 0.0 copy-start.2
  15.0 3.3 %collective-permute-start.1 = (f32[32,1152]{1,0:T(8,128)S(1)}, f32[32,1152]{1,0:T(8,128)}, u32[]{:S(2)}, u32[]{:S(2)}) collective-permute-start(f32[32,1152]{1,0:T(8,128)S(1)} %pad_maximum_fusion.refs_0_.refs_4_), channel_id=1, source_target_pairs={{0,136},{4,140},{8,144},{12,148},{16,152},{20,156},{24,160},{28,16... | collective-permute-start | bytes 442376 | tf_op jit(solution)/shard_map/ppermute | solution.py:28
  18.4 4.2 %collective-permute-start.2 = (f32[32,1152]{1,0:T(8,128)S(1)}, f32[32,1152]{1,0:T(8,128)}, u32[]{:S(2)}, u32[]{:S(2)}) collective-permute-start(f32[32,1152]{1,0:T(8,128)S(1)} %pad_maximum_fusion.refs_0_.refs_4_), channel_id=1, source_target_pairs={{0,184},{4,188},{8,128},{12,132},{16,136},{20,140},{24,144},{28,14... | collective-permute-start | bytes 442376 | tf_op jit(solution)/shard_map/ppermute | solution.py:28
  22.6 0.1 pad_maximum_fusion.1
  22.7 0.0 copy-start.12
  22.8 4.1 %shard_map.123 = (bf16[1024,768]{1,0:T(8,128)(2,1)S(1)}, bf16[1024,768]{1,0:T(8,128)(2,1)S(1)}) custom-call(f32[8,1024]{1,0:T(8,128)S(1)} %select_maximum_fusion.weight_ref, f32[1024,768]{1,0:T(8,128)} %lt_ref.3, f32[16,1152]{1,0:T(8,128)S(1)} %collective-permute-done.after_ref), custom_call_target="tpu_custom_call" | custom-call | flops 6291456 | bytes 6291456 | tf_op jit(solution)/shard_map/pallas_call | solution.py:193
  26.9 5.1 %collective-permute-done.3.refs_3_ = f32[32,1152]{1,0:T(8,128)} collective-permute-done((f32[32,1152]{1,0:T(8,128)S(1)}, f32[32,1152]{1,0:T(8,128)}, u32[]{:S(2)}, u32[]{:S(2)}) %collective-permute-start.3) | collective-permute-done | bytes 147488 | tf_op jit(solution)/shard_map/ppermute | solution.py:28
  32.0 2.2 %shard_map.124 = (f32[128,1152]{1,0:T(8,128)}, f32[64,1152]{1,0:T(8,128)}) custom-call(f32[32,1152]{1,0:T(8,128)} %copy-done.2, f32[32,1152]{1,0:T(8,128)} %collective-permute-done.1.refs_1_.refs_5_, f32[32,1152]{1,0:T(8,128)} %collective-permute-done.2.refs_2_, f32[32,1152]{1,0:T(8,128)} %collective-permute-done.3.refs_3_, f32[32,1152]{1,0:T(8,128)} %copy-done.2, ...), custom_call_target="tpu_custom_call" | custom-call | tf_op jit(solution)/shard_map/pallas_call | solution.py:87
  34.2 3.5 %collective-permute-start.6 = (f32[128,1152]{1,0:T(8,128)}, f32[128,1152]{1,0:T(8,128)}, u32[]{:S(2)}, u32[]{:S(2)}) collective-permute-start(f32[128,1152]{1,0:T(8,128)} %get-tuple-element.20.refs_0_), channel_id=1, source_target_pairs={{0,4},{4,0},{8,12},{12,8},{16,20},{20,16},{24,28},{28,24},{32,36},... | collective-permute-start | bytes 1769480 | tf_op jit(solution)/shard_map/ppermute | solution.py:28
  37.7 0.2 convert_reduce_fusion
  38.0 0.1 collective-permute-start.4
  38.1 0.1 collective-permute-start.7
  38.2 0.1 select_reduce_fusion
  38.3 2.6 %collective-permute-start.5 = (f32[128,1152]{1,0:T(8,128)}, f32[128,1152]{1,0:T(8,128)}, u32[]{:S(2)}, u32[]{:S(2)}) collective-permute-start(f32[128,1152]{1,0:T(8,128)} %get-tuple-element.20.refs_0_), channel_id=1, source_target_pairs={{0,192},{4,196},{8,200},{12,204},{16,208},{20,212},{24,216},{28,22... | collective-permute-start | bytes 1769480 | tf_op jit(solution)/shard_map/ppermute | solution.py:28
  40.9 2.7 %collective-permute-start.8 = (f32[64,1152]{1,0:T(8,128)}, f32[64,1152]{1,0:T(8,128)}, u32[]{:S(2)}, u32[]{:S(2)}) collective-permute-start(f32[64,1152]{1,0:T(8,128)} %get-tuple-element.21), channel_id=1, source_target_pairs={{0,56},{4,60},{8,0},{12,4},{16,8},{20,12},{24,16},{28,20},{32,24},... | collective-permute-start | bytes 884744 | tf_op jit(solution)/shard_map/ppermute | solution.py:28
  43.6 5.8 %collective-permute-done.6.refs_3_.refs_0_ = f32[128,1152]{1,0:T(8,128)} collective-permute-done((f32[128,1152]{1,0:T(8,128)}, f32[128,1152]{1,0:T(8,128)}, u32[]{:S(2)}, u32[]{:S(2)}) %collective-permute-start.6) | collective-permute-done | bytes 589856 | tf_op jit(solution)/shard_map/ppermute | solution.py:28
  49.4 0.7 copy-done.13
  50.1 1.5 %collective-permute-start.9 = (f32[128,1152]{1,0:T(8,128)}, f32[128,1152]{1,0:T(8,128)}, u32[]{:S(2)}, u32[]{:S(2)}) collective-permute-start(f32[128,1152]{1,0:T(8,128)} %collective-permute-done.6.refs_3_.refs_0_), channel_id=1, source_target_pairs={{0,64},{4,68},{8,72},{12,76},{16,80},{20,84},{24,88},{28,92},{32,9... | collective-permute-start | bytes 1769480 | tf_op jit(solution)/shard_map/ppermute | solution.py:28
  51.6 0.1 fusion.17
  51.7 0.1 concatenate.20
  51.8 0.1 copy.16.index_ref
  51.9 1.0 %shard_map.126 = f32[64,1152]{1,0:T(8,128)S(1)} custom-call(f32[128,1152]{1,0:T(8,128)} %collective-permute-done.6.refs_3_.refs_0_), custom_call_target="tpu_custom_call" | custom-call | tf_op jit(solution)/shard_map/pallas_call | solution.py:87
  52.9 0.1 collective-permute-start.11
  53.0 2.7 %collective-permute-start.12 = (f32[64,1152]{1,0:T(8,128)S(1)}, f32[64,1152]{1,0:T(8,128)S(1)}, u32[]{:S(2)}, u32[]{:S(2)}) collective-permute-start(f32[64,1152]{1,0:T(8,128)S(1)} %shard_map.126), channel_id=1, source_target_pairs={{0,56},{4,60},{8,0},{12,4},{16,8},{20,12},{24,16},{28,20},{32,24},... | collective-permute-start | bytes 884744 | tf_op jit(solution)/shard_map/ppermute | solution.py:28
  55.7 4.0 %shard_map.125.carry_ref = f32[512,1152]{1,0:T(8,128)S(1)} custom-call(s32[512,1]{1,0:T(8,128)S(1)} %copy.16.index_ref, f32[128,1152]{1,0:T(8,128)} %get-tuple-element.20.refs_0_, f32[128,1152]{1,0:T(8,128)} %collective-permute-done.4.refs_1_, f32[128,1152]{1,0:T(8,128)} %collective-permute-done.5.refs_2_, ...), custom_call_target="tpu_custom_call" | custom-call | flops 1509949440 | bytes 2951168 | tf_op jit(solution)/shard_map/pallas_call | solution.py:294
  59.8 0.4 collective-permute-done.11.refs_2_
  60.2 4.6 %collective-permute-done.10.refs_1_ = f32[128,1152]{1,0:T(8,128)} collective-permute-done((f32[128,1152]{1,0:T(8,128)}, f32[128,1152]{1,0:T(8,128)}, u32[]{:S(2)}, u32[]{:S(2)}) %collective-permute-start.10) | collective-permute-done | bytes 589856 | tf_op jit(solution)/shard_map/ppermute | solution.py:28
  64.8 4.0 %shard_map.127 = (f32[128,1024]{1,0:T(8,128)S(1)}, f32[256,1024]{1,0:T(8,128)S(1)}, f32[256,128]{1,0:T(8,128)S(1)}, bf16[256,1024]{1,0:T(8,128)(2,1)S(1)}, bf16[...) custom-call(s32[512,1]{1,0:T(8,128)S(1)} %copy.16.index_ref, f32[8,1024]{1,0:T(8,128)S(1)} %select_maximum_fusion.weight_ref, ...), custom_call_target="tpu_custom_call" | custom-call | flops 1711276032 | bytes 10455040 | tf_op jit(solution)/shard_map/pallas_call | solution.py:294
  68.8 3.2 %collective-permute-start.13 = (f32[128,1024]{1,0:T(8,128)S(1)}, f32[128,1024]{1,0:T(8,128)S(1)}, u32[]{:S(2)}, u32[]{:S(2)}) collective-permute-start(f32[128,1024]{1,0:T(8,128)S(1)} %get-tuple-element.28), channel_id=1, source_target_pairs={{0,1},{1,0},{2,3},{3,2},{4,5},{5,4},{6,7},{7,6},{8,9},{9,8},{10,11... | collective-permute-start | bytes 1572872 | tf_op jit(solution)/shard_map/ppermute | solution.py:327
  72.1 0.1 fusion.13
  72.2 1.2 %shard_map.129.keep_ref = f32[128,1024]{1,0:T(8,128)S(1)} custom-call(f32[128,1024]{1,0:T(8,128)S(1)} %get-tuple-element.25.taken_ref, bf16[1024,768]{1,0:T(8,128)(2,1)S(1)} %get-tuple-element.19.refs_6_.lt_big_ref, bf16[1024,768]{1,0:T(8,128)(2,1)S(1)} %get-tuple-element.22.lt_small_ref, bf16[256,1024]{1,0:T(8,128)(2,1)S(1)} %get-tuple-element.26.big_ref, ...), custom_call_target="tpu_custom_call" | custom-call | flops 805306368 | bytes 8912896 | tf_op jit(solution)/shard_map/pallas_call | solution.py:294
  73.4 0.2 collective-permute-done.13.got_ref
  73.6 0.1 shard_map.130
  73.7 1.7 %collective-permute-start.14 = (f32[64,1024]{1,0:T(8,128)S(1)}, f32[64,1024]{1,0:T(8,128)S(1)}, u32[]{:S(2)}, u32[]{:S(2)}) collective-permute-start(f32[64,1024]{1,0:T(8,128)S(1)} %get-tuple-element.30), channel_id=1, source_target_pairs={{0,2},{1,3},{2,0},{3,1},{4,6},{5,7},{6,4},{7,5},{8,10},{9,11},{10,... | collective-permute-start | bytes 786440 | tf_op jit(solution)/shard_map/ppermute | solution.py:330
  75.4 0.1 pad_add_fusion.quarter_ref
  75.5 2.0 %shard_map.128.update_ref = f32[256,768]{1,0:T(8,128)S(1)} custom-call(s32[4]{0:T(128)S(1)} %pad_add_fusion.quarter_ref, f32[256,1024]{1,0:T(8,128)S(1)} %get-tuple-element.24.second_ref, bf16[1024,768]{1,0:T(8,128)(2,1)S(1)} %get-tuple-element.19.refs_6_.lt_big_ref, bf16[1024,768]{1,0:T(8,128)(2,1)S(1)} %get-tuple-element.22.lt_small_ref), custom_call_target="tpu_custom_call" | custom-call | flops 1207959552 | bytes 7340048 | tf_op jit(solution)/shard_map/pallas_call | solution.py:294
  77.5 4.1 %collective-permute-done.14.away_ref = f32[64,1024]{1,0:T(8,128)S(1)} collective-permute-done((f32[64,1024]{1,0:T(8,128)S(1)}, f32[64,1024]{1,0:T(8,128)S(1)}, u32[]{:S(2)}, u32[]{:S(2)}) %collective-permute-start.14) | collective-permute-done | bytes 262176 | tf_op jit(solution)/shard_map/ppermute | solution.py:330
  81.7 1.5 %shard_map.131 = (f32[64,768]{1,0:T(8,128)}, f32[128,768]{1,0:T(8,128)S(1)}, f32[128,768]{1,0:T(8,128)S(1)}) custom-call(s32[4]{0:T(128)S(1)} %pad_add_fusion.quarter_ref, f32[8,128]{1,0:T(8,128)S(1)} %select_maximum_fusion.4.weight_ref, f32[64,768]{1,0:T(8,128)S(1)} %copy-done, f32[256,128]{1,0:T(8,128)S(1)} %get-tuple-element.23.entries_ref, ...), custom_call_target="tpu_custom_call" | custom-call | flops 75497472 | bytes 1642512 | tf_op jit(solution)/shard_map/pallas_call | solution.py:294
  83.1 1.0 %collective-permute-start.15 = (f32[128,768]{1,0:T(8,128)S(1)}, f32[128,768]{1,0:T(8,128)S(1)}, u32[]{:S(2)}, u32[]{:S(2)}) collective-permute-start(f32[128,768]{1,0:T(8,128)S(1)} %get-tuple-element.33), channel_id=1, source_target_pairs={{0,1},{1,0},{2,3},{3,2},{4,5},{5,4},{6,7},{7,6},{8,9},{9,8},{10,11... | collective-permute-start | bytes 1179656 | tf_op jit(solution)/shard_map/ppermute | solution.py:327
  84.1 1.3 %collective-permute-done.15.got_ref = f32[128,768]{1,0:T(8,128)S(1)} collective-permute-done((f32[128,768]{1,0:T(8,128)S(1)}, f32[128,768]{1,0:T(8,128)S(1)}, u32[]{:S(2)}, u32[]{:S(2)}) %collective-permute-start.15) | collective-permute-done | bytes 393248 | tf_op jit(solution)/shard_map/ppermute | solution.py:327
  85.5 0.1 shard_map.132
  85.5 1.5 %collective-permute-start.16 = (f32[64,768]{1,0:T(8,128)S(1)}, f32[64,768]{1,0:T(8,128)S(1)}, u32[]{:S(2)}, u32[]{:S(2)}) collective-permute-start(f32[64,768]{1,0:T(8,128)S(1)} %get-tuple-element.35), channel_id=1, source_target_pairs={{0,2},{1,3},{2,0},{3,1},{4,6},{5,7},{6,4},{7,5},{8,10},{9,11},{10,... | collective-permute-start | bytes 589832 | tf_op jit(solution)/shard_map/ppermute | solution.py:330
  87.1 0.1 fusion.14
  87.2 4.6 %collective-permute-done.16.away_ref = f32[64,768]{1,0:T(8,128)S(1)} collective-permute-done((f32[64,768]{1,0:T(8,128)S(1)}, f32[64,768]{1,0:T(8,128)S(1)}, u32[]{:S(2)}, u32[]{:S(2)}) %collective-permute-start.16) | collective-permute-done | bytes 196640 | tf_op jit(solution)/shard_map/ppermute | solution.py:330
  91.7 0.9 shard_map.133
  (50 shorter events, 0.2 us)
Async XLA Ops:
  0.6 12.5 %copy-start.5 = (s32[2,256]{1,0:T(2,128)S(1)}, s32[2,256]{1,0:T(2,128)}, u32[]{:S(2)}) copy-start(s32[2,256]{1,0:T(2,128)} %pivots_hbm.1) | copy-start | bytes 6148
  0.6 12.5 %copy-start.6 = (f32[1024]{0:T(1024)S(1)}, f32[1024]{0:T(1024)}, u32[]{:S(2)}) copy-start(f32[1024]{0:T(1024)} %param.13) | copy-start | bytes 12292
  0.7 12.5 %copy-start.7 = (s32[1024]{0:T(1024)S(1)}, s32[1024]{0:T(1024)}, u32[]{:S(2)}) copy-start(s32[1024]{0:T(1024)} %param.14) | copy-start | bytes 12292
  0.7 22.0 %copy-start.8 = (f32[1024]{0:T(1024)S(1)}, f32[1024]{0:T(1024)}, u32[]{:S(2)}) copy-start(f32[1024]{0:T(1024)} %param.12) | copy-start | bytes 12292
  5.3 9.7 %collective-permute-start = (f32[16,1152]{1,0:T(8,128)S(1)}, f32[16,1152]{1,0:T(8,128)S(1)}, u32[]{:S(2)}, u32[]{:S(2)}) collective-permute-start(f32[16,1152]{1,0:T(8,128)S(1)} %shard_map.122), channel_id=1, source_target_pairs={{0,32},{4,36},{8,40},{12,44},{16,48},{20,52},{24,56},{28,60},{32,0... | collective-permute-start | bytes 221192 | tf_op jit(solution)/shard_map/ppermute | solution.py:28
  15.0 17.0 %copy-start.2 = (f32[32,1152]{1,0:T(8,128)}, f32[32,1152]{1,0:T(8,128)S(1)}, u32[]{:S(2)}) copy-start(f32[32,1152]{1,0:T(8,128)S(1)} %pad_maximum_fusion.refs_0_.refs_4_) | copy-start | bytes 442372
  15.0 11.9 %collective-permute-start.1 = (f32[32,1152]{1,0:T(8,128)S(1)}, f32[32,1152]{1,0:T(8,128)}, u32[]{:S(2)}, u32[]{:S(2)}) collective-permute-start(f32[32,1152]{1,0:T(8,128)S(1)} %pad_maximum_fusion.refs_0_.refs_4_), channel_id=1, source_target_pairs={{0,136},{4,140},{8,144},{12,148},{16,152},{20,156},{24,160},{28,16... | collective-permute-start | bytes 442376 | tf_op jit(solution)/shard_map/ppermute | solution.py:28
  18.4 8.5 %collective-permute-start.2 = (f32[32,1152]{1,0:T(8,128)S(1)}, f32[32,1152]{1,0:T(8,128)}, u32[]{:S(2)}, u32[]{:S(2)}) collective-permute-start(f32[32,1152]{1,0:T(8,128)S(1)} %pad_maximum_fusion.refs_0_.refs_4_), channel_id=1, source_target_pairs={{0,184},{4,188},{8,128},{12,132},{16,136},{20,140},{24,144},{28,14... | collective-permute-start | bytes 442376 | tf_op jit(solution)/shard_map/ppermute | solution.py:28
  22.6 9.4 %collective-permute-start.3 = (f32[32,1152]{1,0:T(8,128)S(1)}, f32[32,1152]{1,0:T(8,128)}, u32[]{:S(2)}, u32[]{:S(2)}) collective-permute-start(f32[32,1152]{1,0:T(8,128)S(1)} %pad_maximum_fusion.refs_0_.refs_4_), channel_id=1, source_target_pairs={{0,16},{4,20},{8,24},{12,28},{16,32},{20,36},{24,40},{28,44},{32,4... | collective-permute-start | bytes 442376 | tf_op jit(solution)/shard_map/ppermute | solution.py:28
  22.7 15.4 %copy-start.12 = (s32[64]{0:T(128)S(1)}, s32[64]{0:T(128)}, u32[]{:S(2)}) copy-start(s32[64]{0:T(128)} %constant.136.clone) | copy-start | bytes 772
  26.8 28.8 %copy-start.9 = (s32[2,64]{1,0:T(2,128)S(1)}, s32[2,64]{1,0:T(2,128)}, u32[]{:S(2)}) copy-start(s32[2,64]{1,0:T(2,128)} %param.20) | copy-start | bytes 1540
  26.9 28.8 %copy-start.10 = (f32[2,64]{1,0:T(2,128)S(1)}, f32[2,64]{1,0:T(2,128)}, u32[]{:S(2)}) copy-start(f32[2,64]{1,0:T(2,128)} %param.19) | copy-start | bytes 1540
  34.2 15.2 %collective-permute-start.6 = (f32[128,1152]{1,0:T(8,128)}, f32[128,1152]{1,0:T(8,128)}, u32[]{:S(2)}, u32[]{:S(2)}) collective-permute-start(f32[128,1152]{1,0:T(8,128)} %get-tuple-element.20.refs_0_), channel_id=1, source_target_pairs={{0,4},{4,0},{8,12},{12,8},{16,20},{20,16},{24,28},{28,24},{32,36},... | collective-permute-start | bytes 1769480 | tf_op jit(solution)/shard_map/ppermute | solution.py:28
  38.0 15.0 %collective-permute-start.4 = (f32[128,1152]{1,0:T(8,128)}, f32[128,1152]{1,0:T(8,128)}, u32[]{:S(2)}, u32[]{:S(2)}) collective-permute-start(f32[128,1152]{1,0:T(8,128)} %get-tuple-element.20.refs_0_), channel_id=1, source_target_pairs={{0,64},{4,68},{8,72},{12,76},{16,80},{20,84},{24,88},{28,92},{32,9... | collective-permute-start | bytes 1769480 | tf_op jit(solution)/shard_map/ppermute | solution.py:28
  38.1 11.4 %collective-permute-start.7 = (f32[64,1152]{1,0:T(8,128)}, f32[64,1152]{1,0:T(8,128)S(1)}, u32[]{:S(2)}, u32[]{:S(2)}) collective-permute-start(f32[64,1152]{1,0:T(8,128)} %get-tuple-element.21), channel_id=1, source_target_pairs={{0,8},{4,12},{8,16},{12,20},{16,24},{20,28},{24,32},{28,36},{32,40... | collective-permute-start | bytes 884744 | tf_op jit(solution)/shard_map/ppermute | solution.py:28
  38.3 17.4 %collective-permute-start.5 = (f32[128,1152]{1,0:T(8,128)}, f32[128,1152]{1,0:T(8,128)}, u32[]{:S(2)}, u32[]{:S(2)}) collective-permute-start(f32[128,1152]{1,0:T(8,128)} %get-tuple-element.20.refs_0_), channel_id=1, source_target_pairs={{0,192},{4,196},{8,200},{12,204},{16,208},{20,212},{24,216},{28,22... | collective-permute-start | bytes 1769480 | tf_op jit(solution)/shard_map/ppermute | solution.py:28
  40.9 12.0 %collective-permute-start.8 = (f32[64,1152]{1,0:T(8,128)}, f32[64,1152]{1,0:T(8,128)}, u32[]{:S(2)}, u32[]{:S(2)}) collective-permute-start(f32[64,1152]{1,0:T(8,128)} %get-tuple-element.21), channel_id=1, source_target_pairs={{0,56},{4,60},{8,0},{12,4},{16,8},{20,12},{24,16},{28,20},{32,24},... | collective-permute-start | bytes 884744 | tf_op jit(solution)/shard_map/ppermute | solution.py:28
  49.4 15.4 %collective-permute-start.10 = (f32[128,1152]{1,0:T(8,128)}, f32[128,1152]{1,0:T(8,128)}, u32[]{:S(2)}, u32[]{:S(2)}) collective-permute-start(f32[128,1152]{1,0:T(8,128)} %collective-permute-done.6.refs_3_.refs_0_), channel_id=1, source_target_pairs={{0,192},{4,196},{8,200},{12,204},{16,208},{20,212},{24,216},{28,22... | collective-permute-start | bytes 1769480 | tf_op jit(solution)/shard_map/ppermute | solution.py:28
  49.4 0.7 copy-start.13
  50.1 14.7 %collective-permute-start.9 = (f32[128,1152]{1,0:T(8,128)}, f32[128,1152]{1,0:T(8,128)}, u32[]{:S(2)}, u32[]{:S(2)}) collective-permute-start(f32[128,1152]{1,0:T(8,128)} %collective-permute-done.6.refs_3_.refs_0_), channel_id=1, source_target_pairs={{0,64},{4,68},{8,72},{12,76},{16,80},{20,84},{24,88},{28,92},{32,9... | collective-permute-start | bytes 1769480 | tf_op jit(solution)/shard_map/ppermute | solution.py:28
  52.9 7.3 %collective-permute-start.11 = (f32[64,1152]{1,0:T(8,128)S(1)}, f32[64,1152]{1,0:T(8,128)S(1)}, u32[]{:S(2)}, u32[]{:S(2)}) collective-permute-start(f32[64,1152]{1,0:T(8,128)S(1)} %shard_map.126), channel_id=1, source_target_pairs={{0,8},{4,12},{8,16},{12,20},{16,24},{20,28},{24,32},{28,36},{32,40... | collective-permute-start | bytes 884744 | tf_op jit(solution)/shard_map/ppermute | solution.py:28
  53.0 7.2 %collective-permute-start.12 = (f32[64,1152]{1,0:T(8,128)S(1)}, f32[64,1152]{1,0:T(8,128)S(1)}, u32[]{:S(2)}, u32[]{:S(2)}) collective-permute-start(f32[64,1152]{1,0:T(8,128)S(1)} %shard_map.126), channel_id=1, source_target_pairs={{0,56},{4,60},{8,0},{12,4},{16,8},{20,12},{24,16},{28,20},{32,24},... | collective-permute-start | bytes 884744 | tf_op jit(solution)/shard_map/ppermute | solution.py:28
  60.2 4.6 %copy-start.3 = (f32[64,1152]{1,0:T(8,128)}, f32[64,1152]{1,0:T(8,128)S(1)}, u32[]{:S(2)}) copy-start(f32[64,1152]{1,0:T(8,128)S(1)} %collective-permute-done.11.refs_2_) | copy-start | bytes 884740
  60.2 4.6 %copy-start.4 = (f32[64,1152]{1,0:T(8,128)}, f32[64,1152]{1,0:T(8,128)S(1)}, u32[]{:S(2)}) copy-start(f32[64,1152]{1,0:T(8,128)S(1)} %collective-permute-done.12.refs_3_) | copy-start | bytes 884740
  64.8 7.4 %copy-start.11 = (f32[2,64]{1,0:T(2,128)S(1)}, f32[2,64]{1,0:T(2,128)}, u32[]{:S(2)}) copy-start(f32[2,64]{1,0:T(2,128)} %param.18) | copy-start | bytes 1540
  68.8 4.8 %collective-permute-start.13 = (f32[128,1024]{1,0:T(8,128)S(1)}, f32[128,1024]{1,0:T(8,128)S(1)}, u32[]{:S(2)}, u32[]{:S(2)}) collective-permute-start(f32[128,1024]{1,0:T(8,128)S(1)} %get-tuple-element.28), channel_id=1, source_target_pairs={{0,1},{1,0},{2,3},{3,2},{4,5},{5,4},{6,7},{7,6},{8,9},{9,8},{10,11... | collective-permute-start | bytes 1572872 | tf_op jit(solution)/shard_map/ppermute | solution.py:327
  73.7 8.0 %collective-permute-start.14 = (f32[64,1024]{1,0:T(8,128)S(1)}, f32[64,1024]{1,0:T(8,128)S(1)}, u32[]{:S(2)}, u32[]{:S(2)}) collective-permute-start(f32[64,1024]{1,0:T(8,128)S(1)} %get-tuple-element.30), channel_id=1, source_target_pairs={{0,2},{1,3},{2,0},{3,1},{4,6},{5,7},{6,4},{7,5},{8,10},{9,11},{10,... | collective-permute-start | bytes 786440 | tf_op jit(solution)/shard_map/ppermute | solution.py:330
  75.5 6.2 %copy-start = (f32[64,768]{1,0:T(8,128)S(1)}, f32[64,768]{1,0:T(8,128)}, u32[]{:S(2)}) copy-start(f32[64,768]{1,0:T(8,128)} %a_ref.2) | copy-start | bytes 589828
  77.5 14.2 %copy-start.1 = (f32[64,768]{1,0:T(8,128)S(1)}, f32[64,768]{1,0:T(8,128)}, u32[]{:S(2)}) copy-start(f32[64,768]{1,0:T(8,128)} %a_ref.3) | copy-start | bytes 589828
  83.1 2.4 %collective-permute-start.15 = (f32[128,768]{1,0:T(8,128)S(1)}, f32[128,768]{1,0:T(8,128)S(1)}, u32[]{:S(2)}, u32[]{:S(2)}) collective-permute-start(f32[128,768]{1,0:T(8,128)S(1)} %get-tuple-element.33), channel_id=1, source_target_pairs={{0,1},{1,0},{2,3},{3,2},{4,5},{5,4},{6,7},{7,6},{8,9},{9,8},{10,11... | collective-permute-start | bytes 1179656 | tf_op jit(solution)/shard_map/ppermute | solution.py:327
  85.5 6.2 %collective-permute-start.16 = (f32[64,768]{1,0:T(8,128)S(1)}, f32[64,768]{1,0:T(8,128)S(1)}, u32[]{:S(2)}, u32[]{:S(2)}) collective-permute-start(f32[64,768]{1,0:T(8,128)S(1)} %get-tuple-element.35), channel_id=1, source_target_pairs={{0,2},{1,3},{2,0},{3,1},{4,6},{5,7},{6,4},{7,5},{8,10},{9,11},{10,... | collective-permute-start | bytes 589832 | tf_op jit(solution)/shard_map/ppermute | solution.py:330

commit v8 on v7

--- a/solution.py
+++ b/solution.py
@@ -36,23 +36,19 @@
     held, at = block, [(0, 0, 0)]
     got, its = moved(held, at, (0, 4, 0))
     held, at = jnp.concatenate([held, got], 0), at + its
-    ready = made(got)
     parts = [moved(held, at, step) for step in ((2, 1, 0), (2, -1, 0), (0, 2, 0))]
-    pair = 2 * rows
-    blocks = [held] + [p[0] for p in parts]
-    places = [(piece, 0, pair, 0, pair * i) for i, piece in enumerate(blocks)]
-    places += [(blocks[i], 0, pair, 1, pair * i) for i in range(2)]
-    held, low = cuts(places, [4 * pair, 2 * pair], ready[0])
+    held = jnp.concatenate([held] + [p[0] for p in parts], 0)
     at = at + parts[0][1] + parts[1][1] + parts[2][1]
     half = len(at) // 2
     cut = half * rows
     over = moved(held, at, (0, 0, 1))
     ahead = moved(held, at, (1, 0, 0))
     behind = moved(held, at, (-1, 0, 0))
-    up = moved(low, at[:half], (0, 1, 0))
-    down = moved(low, at[:half], (0, -1, 0))
+    up = moved(held[:cut], at[:half], (0, 1, 0))
+    down = moved(held[:cut], at[:half], (0, -1, 0))
     early = [(held, at), ahead, behind, over, up, down]
-    (middle,) = cuts([(over[0], 0, cut, 0, 0)], [cut])
+    ready = made(held)
+    (middle,) = cuts([(over[0], 0, cut, 0, 0)], [cut], ready[0])
     late = [
         moved(over[0], over[1], (1, 0, 0)),
         moved(over[0], over[1], (-1, 0, 0)),
@@ -82,7 +78,7 @@
 
 
 def cuts(parts, sizes, following=None):
-    args = [in_hbm(part[0]) for part in parts] + ([] if following is None else [following])
+    args = [in_vmem(part[0]) for part in parts] + ([] if following is None else [following])
     width = parts[0][0].shape[1]
     return pl.pallas_call(
         functools.partial(cuts_kernel, parts=[part[1:] for part in parts], inputs=len(args)),
@@ -207,27 +203,14 @@
     )(weights, in_hbm(prior_lt), following)
 
 
-def fill_parts(parts_ref, pieces, rows_ref, sems):
-    total = rows_ref.shape[0]
-    start, copies = 0, []
-    for i, ref in enumerate(pieces):
-        rows = slice(start, start + ref.shape[0])
-        copies.append((rows, pltpu.make_async_copy(ref, rows_ref.at[rows], sems.at[i])))
-        copies[-1][1].start()
-        start += ref.shape[0]
-    for rows, copy in copies:
-        copy.wait()
-        big, small = split(rows_ref[rows, :])
-        parts_ref[rows, :] = big
-        parts_ref[total + rows.start : total + rows.stop, :] = small
-
-
-def piece_scratch(rows, width, pieces):
-    return [
-        pltpu.VMEM((2 * rows, width), jnp.bfloat16),
-        pltpu.VMEM((rows, width), jnp.float32),
-        pltpu.SemaphoreType.DMA((len(pieces),)),
-    ]
+def fill_parts(parts_ref, pieces):
+    start, total = 0, parts_ref.shape[0] // 2
+    for ref in pieces:
+        size = ref.shape[0]
+        big, small = split(ref[...])
+        parts_ref[start : start + size, :] = big
+        parts_ref[total + start : total + start + size, :] = small
+        start += size
 
 
 def hits(index, base, total):
@@ -237,9 +220,9 @@
 
 
 def early_kernel(index_ref, *refs):
-    *pieces, out_ref, parts_ref, rows_ref, sems = refs
-    hit = hits(index_ref[...], 0, rows_ref.shape[0])
-    fill_parts(parts_ref, pieces, rows_ref, sems)
+    *pieces, out_ref, parts_ref = refs
+    fill_parts(parts_ref, pieces)
+    hit = hits(index_ref[...], 0, parts_ref.shape[0] // 2)
     for low in range(0, out_ref.shape[1], 384):
         out_ref[:, low : low + 384] = jnp.dot(
             hit, parts_ref[:, low : low + 384], preferred_element_type=jnp.float32
@@ -247,9 +230,9 @@
 
 
 def send_kernel(index_ref, weight_ref, carry_ref, lt_big_ref, lt_small_ref, *refs, base):
-    *pieces, out_ref, second_ref, entries_ref, big_ref, small_ref, keep_ref, parts_ref, rows_ref, sems = refs
-    fill_parts(parts_ref, pieces, rows_ref, sems)
-    total = rows_ref.shape[0]
+    *pieces, out_ref, second_ref, entries_ref, big_ref, small_ref, keep_ref, parts_ref = refs
+    fill_parts(parts_ref, pieces)
+    total = parts_ref.shape[0] // 2
     rows, k_local = out_ref.shape[0], lt_big_ref.shape[0]
     tile_rows = lt_big_ref.shape[1]
     hit = hits(index_ref[...], base, total)
@@ -287,10 +270,9 @@
         out_ref[i * blocks : (i + 1) * blocks, :] = whole_ref[pl.ds(start, blocks), :]
 
 
-def local_call(kernel, out_shape, flops, *args, scratch=(), smem=0, hbm=0):
+def local_call(kernel, out_shape, flops, *args, scratch=(), smem=0):
     vmem = pl.BlockSpec(memory_space=pltpu.VMEM)
-    specs = [pl.BlockSpec(memory_space=pltpu.SMEM)] * smem + [vmem] * (len(args) - smem - hbm)
-    specs += [pl.BlockSpec(memory_space=pl.ANY)] * hbm
+    specs = [pl.BlockSpec(memory_space=pltpu.SMEM)] * smem + [vmem] * (len(args) - smem)
     return pl.pallas_call(
         kernel,
         in_specs=specs,
@@ -413,9 +395,8 @@
         shape((2 * P_SIZE, width), f32),
         4 * 2 * P_SIZE * early_rows * width,
         where,
-        *[in_hbm(piece[0]) for piece in early],
-        scratch=piece_scratch(early_rows, width, early),
-        hbm=len(early),
+        *[in_vmem(piece[0]) for piece in early],
+        scratch=[pltpu.VMEM((2 * early_rows, width), b16)],
     )
     send, second, entries, second_big, second_small, taken = local_call(
         functools.partial(send_kernel, base=early_rows),
@@ -433,9 +414,8 @@
         carry,
         lt_big,
         lt_small,
-        *[in_hbm(piece[0]) for piece in late],
-        scratch=piece_scratch(late_rows, width, late),
-        hbm=len(late),
+        *[in_vmem(piece[0]) for piece in late],
+        scratch=[pltpu.VMEM((2 * late_rows, width), b16)],
     )
     keep = local_call(
         keep_kernel,

time: 92.9 us -> 88.2 us (0.949)
  Pallas kernels: 25.7 us -> 19.6 us
  waiting for transfers between devices: 28 us -> 31.9 us
  starting transfers between devices: 36.1 us -> 34.4 us
    pallas_call x2 -> x1, Pallas kernels: 3.22 us -> 0.07 us  [cuts(): pl.pallas_call(functools.partial(cuts_kernel, parts=[part[1:] for part in...]
    ppermute x13, waiting for transfers between devices: 17.8 us -> 20.8 us  [moved(): got = lax.ppermute(block, 'wide', shift(*step))]
    pallas_call x8, Pallas kernels: 13.7 us -> 10.7 us  [local_call(): pl.pallas_call(kernel, in_specs=specs, out_specs=jax.tree.map(lambda _: v...]
    ppermute x2, starting transfers between devices: 3.27 us -> 2.12 us  [hop_sum(): return (rest, lax.ppermute(away, 'narrow', CHIP))]
  transfers between devices with their start and end apart: 17 -> 17, of which waited for: 9 -> 11; matrix products, arithmetic and copies ran while one was open for 1% -> 1% of each run, Pallas kernels for 13% -> 11%
where the time goes in v8:
time: 88.2 us; the launch traced here: 88.1 us
  starting transfers between devices  34.4 us (39%)
  waiting for transfers between devices  31.9 us (36%)
  Pallas kernels  19.6 us (22%)
  between operations  1.01 us (1%)
    ppermute x13, starting transfers between devices, moved(): got = lax.ppermute(block, 'wide', shift(*step))  28.4 us
    ppermute x13, waiting for transfers between devices, moved(): got = lax.ppermute(block, 'wide', shift(*step))  20.8 us
    pallas_call x8, Pallas kernels, local_call(): pl.pallas_call(kernel, in_specs=specs, out_specs=jax.tree.map(lambda _: v...  10.7 us
    ppermute x2, waiting for transfers between devices, hop_sum(): return (rest, lax.ppermute(away, 'narrow', CHIP))  9.49 us
    pallas_call x1, Pallas kernels, tile_slots(): pl.pallas_call(slots_kernel, in_specs=[pl.BlockSpec(memory_space=pltpu.SM...  4.73 us
    pallas_call x1, Pallas kernels, coupled_parts(): pl.pallas_call(couple_kernel, grid=(4,), in_specs=[pl.BlockSpec((8, depth...  4.09 us
    ppermute x2, starting transfers between devices, hop_sum(): got = lax.ppermute(send, 'narrow', CORE)  3.85 us
    ppermute x2, starting transfers between devices, hop_sum(): return (rest, lax.ppermute(away, 'narrow', CHIP))  2.12 us
  transfers between devices with their start and end apart: 17, of which 11 were waited for; matrix products, arithmetic and copies ran while one was open for 1% of the time, Pallas kernels for 11%

profile of v8, /device:TPU:1, one launch (start us, length us, event | category | flops | bytes accessed | tf_op | source)
XLA Modules:
  0.0 88.1 jit_solution(3824747019051785955)
XLA Ops:
  0.6 0.0 copy-start.9
  0.7 4.7 %shard_map.122 = f32[16,1152]{1,0:T(8,128)S(1)} custom-call(s32[1]{0:T(128)} %bitcast.10.low_ref, s32[2,256]{1,0:T(2,128)} %pivots_hbm.1, f32[64,768]{1,0:T(8,128)} %a_ref.2, f32[1024,768]{1,0:T(8,128)} %lt_ref.3), custom_call_target="tpu_custom_call" | custom-call | tf_op jit(solution)/shard_map/pallas_call | solution.py:159
  5.4 7.8 %collective-permute-start = (f32[16,1152]{1,0:T(8,128)S(1)}, f32[16,1152]{1,0:T(8,128)S(1)}, u32[]{:S(2)}, u32[]{:S(2)}) collective-permute-start(f32[16,1152]{1,0:T(8,128)S(1)} %shard_map.122), channel_id=1, source_target_pairs={{0,32},{4,36},{8,40},{12,44},{16,48},{20,52},{24,56},{28,60},{32,0... | collective-permute-start | bytes 221192 | tf_op jit(solution)/shard_map/ppermute | solution.py:28
  13.4 0.2 convert_reduce_fusion
  13.7 0.1 select_reduce_fusion
  13.8 1.3 %collective-permute-done = f32[16,1152]{1,0:T(8,128)S(1)} collective-permute-done((f32[16,1152]{1,0:T(8,128)S(1)}, f32[16,1152]{1,0:T(8,128)S(1)}, u32[]{:S(2)}, u32[]{:S(2)}) %collective-permute-start) | collective-permute-done | bytes 73760 | tf_op jit(solution)/shard_map/ppermute | solution.py:28
  15.1 3.3 %collective-permute-start.1 = (f32[32,1152]{1,0:T(8,128)S(1)}, f32[32,1152]{1,0:T(8,128)S(1)}, u32[]{:S(2)}, u32[]{:S(2)}) collective-permute-start(f32[32,1152]{1,0:T(8,128)S(1)} %pad_maximum_fusion.1), channel_id=1, source_target_pairs={{0,136},{4,140},{8,144},{12,148},{16,152},{20,156},{24,160},{28,16... | collective-permute-start | bytes 442376 | tf_op jit(solution)/shard_map/ppermute | solution.py:28
  18.5 4.2 %collective-permute-start.2 = (f32[32,1152]{1,0:T(8,128)S(1)}, f32[32,1152]{1,0:T(8,128)S(1)}, u32[]{:S(2)}, u32[]{:S(2)}) collective-permute-start(f32[32,1152]{1,0:T(8,128)S(1)} %pad_maximum_fusion.1), channel_id=1, source_target_pairs={{0,184},{4,188},{8,128},{12,132},{16,136},{20,140},{24,144},{28,14... | collective-permute-start | bytes 442376 | tf_op jit(solution)/shard_map/ppermute | solution.py:28
  22.7 3.9 %collective-permute-done.1 = f32[32,1152]{1,0:T(8,128)S(1)} collective-permute-done((f32[32,1152]{1,0:T(8,128)S(1)}, f32[32,1152]{1,0:T(8,128)S(1)}, u32[]{:S(2)}, u32[]{:S(2)}) %collective-permute-start.1) | collective-permute-done | bytes 147488 | tf_op jit(solution)/shard_map/ppermute | solution.py:28
  26.6 5.3 %collective-permute-done.3 = f32[32,1152]{1,0:T(8,128)S(1)} collective-permute-done((f32[32,1152]{1,0:T(8,128)S(1)}, f32[32,1152]{1,0:T(8,128)S(1)}, u32[]{:S(2)}, u32[]{:S(2)}) %collective-permute-start.3) | collective-permute-done | bytes 147488 | tf_op jit(solution)/shard_map/ppermute | solution.py:28
  32.0 3.4 %collective-permute-start.6 = (f32[128,1152]{1,0:T(8,128)S(1)}, f32[128,1152]{1,0:T(8,128)S(1)}, u32[]{:S(2)}, u32[]{:S(2)}) collective-permute-start(f32[128,1152]{1,0:T(8,128)S(1)} %constant_dynamic-update-slice_fusion.refs_0_.after_ref), channel_id=1, source_target_pairs={{0,4},{4,0},{8,12},{12,8},{16,20},{20,16},{24,28},{28,24},{32,36},... | collective-permute-start | bytes 1769480 | tf_op jit(solution)/shard_map/ppermute | solution.py:28
  35.4 2.7 %collective-permute-start.5 = (f32[128,1152]{1,0:T(8,128)S(1)}, f32[128,1152]{1,0:T(8,128)S(1)}, u32[]{:S(2)}, u32[]{:S(2)}) collective-permute-start(f32[128,1152]{1,0:T(8,128)S(1)} %constant_dynamic-update-slice_fusion.refs_0_.after_ref), channel_id=1, source_target_pairs={{0,192},{4,196},{8,200},{12,204},{16,208},{20,212},{24,216},{28,22... | collective-permute-start | bytes 1769480 | tf_op jit(solution)/shard_map/ppermute | solution.py:28
  38.1 0.1 collective-permute-start.7
  38.3 2.6 %collective-permute-start.8 = (f32[64,1152]{1,0:T(8,128)S(1)}, f32[64,1152]{1,0:T(8,128)S(1)}, u32[]{:S(2)}, u32[]{:S(2)}) collective-permute-start(f32[64,1152]{1,0:T(8,128)S(1)} %pad_maximum_fusion), channel_id=1, source_target_pairs={{0,56},{4,60},{8,0},{12,4},{16,8},{20,12},{24,16},{28,20},{32,24},... | collective-permute-start | bytes 884744 | tf_op jit(solution)/shard_map/ppermute | solution.py:28
  40.9 0.1 fusion.17
  41.0 0.1 concatenate.27
  41.1 0.1 copy.16.index_ref
  41.2 5.6 %collective-permute-done.6.refs_3_.refs_0_ = f32[128,1152]{1,0:T(8,128)S(1)} collective-permute-done((f32[128,1152]{1,0:T(8,128)S(1)}, f32[128,1152]{1,0:T(8,128)S(1)}, u32[]{:S(2)}, u32[]{:S(2)}) %collective-permute-start.6) | collective-permute-done | bytes 589856 | tf_op jit(solution)/shard_map/ppermute | solution.py:28
  46.9 1.5 %collective-permute-start.9 = (f32[128,1152]{1,0:T(8,128)S(1)}, f32[128,1152]{1,0:T(8,128)S(1)}, u32[]{:S(2)}, u32[]{:S(2)}) collective-permute-start(f32[128,1152]{1,0:T(8,128)S(1)} %collective-permute-done.6.refs_3_.refs_0_), channel_id=1, source_target_pairs={{0,64},{4,68},{8,72},{12,76},{16,80},{20,84},{24,88},{28,92},{32,9... | collective-permute-start | bytes 1769480 | tf_op jit(solution)/shard_map/ppermute | solution.py:28
  48.3 0.1 pad_maximum_fusion.2
  48.4 0.0 copy-start.6
  48.4 4.1 %shard_map.124 = (bf16[1024,768]{1,0:T(8,128)(2,1)S(1)}, bf16[1024,768]{1,0:T(8,128)(2,1)S(1)}) custom-call(f32[8,1024]{1,0:T(8,128)S(1)} %select_maximum_fusion.weight_ref, f32[1024,768]{1,0:T(8,128)} %lt_ref.3, f32[128,1152]{1,0:T(8,128)S(1)} %constant_dynamic-update-slice_fusion.refs_0_.after_ref), custom_call_target="tpu_custom_call" | custom-call | flops 6291456 | bytes 6291456 | tf_op jit(solution)/shard_map/pallas_call | solution.py:189
  52.5 0.1 shard_map.125
  52.6 0.1 collective-permute-start.11
  52.7 2.7 %collective-permute-start.12 = (f32[64,1152]{1,0:T(8,128)S(1)}, f32[64,1152]{1,0:T(8,128)S(1)}, u32[]{:S(2)}, u32[]{:S(2)}) collective-permute-start(f32[64,1152]{1,0:T(8,128)S(1)} %shard_map.125), channel_id=1, source_target_pairs={{0,56},{4,60},{8,0},{12,4},{16,8},{20,12},{24,16},{28,20},{32,24},... | collective-permute-start | bytes 884744 | tf_op jit(solution)/shard_map/ppermute | solution.py:28
  55.4 2.4 %shard_map.123.carry_ref = f32[512,1152]{1,0:T(8,128)S(1)} custom-call(s32[512,1]{1,0:T(8,128)S(1)} %copy.16.index_ref, f32[128,1152]{1,0:T(8,128)S(1)} %constant_dynamic-update-slice_fusion.refs_0_.after_ref, f32[128,1152]{1,0:T(8,128)S(1)} %collective-permute-done.4.refs_1_, f32[128,1152]{1,0:T(8,128)S(1)} %collective-permute-done.5.refs_2_, ...), custom_call_target="tpu_custom_call" | custom-call | flops 1509949440 | bytes 2951168 | tf_op jit(solution)/shard_map/pallas_call | solution.py:276
  57.8 1.9 %collective-permute-done.11.refs_2_ = f32[64,1152]{1,0:T(8,128)S(1)} collective-permute-done((f32[64,1152]{1,0:T(8,128)S(1)}, f32[64,1152]{1,0:T(8,128)S(1)}, u32[]{:S(2)}, u32[]{:S(2)}) %collective-permute-start.11) | collective-permute-done | bytes 294944 | tf_op jit(solution)/shard_map/ppermute | solution.py:28
  59.8 1.8 %collective-permute-done.10.refs_1_ = f32[128,1152]{1,0:T(8,128)S(1)} collective-permute-done((f32[128,1152]{1,0:T(8,128)S(1)}, f32[128,1152]{1,0:T(8,128)S(1)}, u32[]{:S(2)}, u32[]{:S(2)}) %collective-permute-start.10) | collective-permute-done | bytes 589856 | tf_op jit(solution)/shard_map/ppermute | solution.py:28
  61.6 0.8 collective-permute-done.9.refs_0_
  62.5 2.6 %shard_map.126 = (f32[128,1024]{1,0:T(8,128)S(1)}, f32[256,1024]{1,0:T(8,128)S(1)}, f32[256,128]{1,0:T(8,128)S(1)}, bf16[256,1024]{1,0:T(8,128)(2,1)S(1)}, bf16[...) custom-call(s32[512,1]{1,0:T(8,128)S(1)} %copy.16.index_ref, f32[8,1024]{1,0:T(8,128)S(1)} %select_maximum_fusion.weight_ref, ...), custom_call_target="tpu_custom_call" | custom-call | flops 1711276032 | bytes 10455040 | tf_op jit(solution)/shard_map/pallas_call | solution.py:276
  65.1 2.7 %collective-permute-start.13 = (f32[128,1024]{1,0:T(8,128)S(1)}, f32[128,1024]{1,0:T(8,128)S(1)}, u32[]{:S(2)}, u32[]{:S(2)}) collective-permute-start(f32[128,1024]{1,0:T(8,128)S(1)} %get-tuple-element.24), channel_id=1, source_target_pairs={{0,1},{1,0},{2,3},{3,2},{4,5},{5,4},{6,7},{7,6},{8,9},{9,8},{10,11... | collective-permute-start | bytes 1572872 | tf_op jit(solution)/shard_map/ppermute | solution.py:309
  67.7 0.1 fusion.13
  67.8 1.2 %shard_map.128.keep_ref = f32[128,1024]{1,0:T(8,128)S(1)} custom-call(f32[128,1024]{1,0:T(8,128)S(1)} %get-tuple-element.21.taken_ref, bf16[1024,768]{1,0:T(8,128)(2,1)S(1)} %get-tuple-element.17.refs_1_.lt_big_ref, bf16[1024,768]{1,0:T(8,128)(2,1)S(1)} %get-tuple-element.18.lt_small_ref, bf16[256,1024]{1,0:T(8,128)(2,1)S(1)} %get-tuple-element.22.big_ref, ...), custom_call_target="tpu_custom_call" | custom-call | flops 805306368 | bytes 8912896 | tf_op jit(solution)/shard_map/pallas_call | solution.py:276
  69.1 0.2 collective-permute-done.13.got_ref
  69.3 0.1 shard_map.129
  69.3 1.1 %collective-permute-start.14 = (f32[64,1024]{1,0:T(8,128)S(1)}, f32[64,1024]{1,0:T(8,128)S(1)}, u32[]{:S(2)}, u32[]{:S(2)}) collective-permute-start(f32[64,1024]{1,0:T(8,128)S(1)} %get-tuple-element.26), channel_id=1, source_target_pairs={{0,2},{1,3},{2,0},{3,1},{4,6},{5,7},{6,4},{7,5},{8,10},{9,11},{10,... | collective-permute-start | bytes 786440 | tf_op jit(solution)/shard_map/ppermute | solution.py:312
  70.4 0.1 pad_add_fusion.quarter_ref
  70.5 2.0 %shard_map.127.update_ref = f32[256,768]{1,0:T(8,128)S(1)} custom-call(s32[4]{0:T(128)S(1)} %pad_add_fusion.quarter_ref, f32[256,1024]{1,0:T(8,128)S(1)} %get-tuple-element.20.second_ref, bf16[1024,768]{1,0:T(8,128)(2,1)S(1)} %get-tuple-element.17.refs_1_.lt_big_ref, bf16[1024,768]{1,0:T(8,128)(2,1)S(1)} %get-tuple-element.18.lt_small_ref), custom_call_target="tpu_custom_call" | custom-call | flops 1207959552 | bytes 7340048 | tf_op jit(solution)/shard_map/pallas_call | solution.py:276
  72.5 0.0 copy-start.1
  72.5 4.4 %collective-permute-done.14.away_ref = f32[64,1024]{1,0:T(8,128)S(1)} collective-permute-done((f32[64,1024]{1,0:T(8,128)S(1)}, f32[64,1024]{1,0:T(8,128)S(1)}, u32[]{:S(2)}, u32[]{:S(2)}) %collective-permute-start.14) | collective-permute-done | bytes 262176 | tf_op jit(solution)/shard_map/ppermute | solution.py:312
  76.9 1.5 %shard_map.130 = (f32[64,768]{1,0:T(8,128)}, f32[128,768]{1,0:T(8,128)S(1)}, f32[128,768]{1,0:T(8,128)S(1)}) custom-call(s32[4]{0:T(128)S(1)} %pad_add_fusion.quarter_ref, f32[8,128]{1,0:T(8,128)S(1)} %select_maximum_fusion.4.weight_ref, f32[64,768]{1,0:T(8,128)S(1)} %copy-done, f32[256,128]{1,0:T(8,128)S(1)} %get-tuple-element.19.entries_ref, ...), custom_call_target="tpu_custom_call" | custom-call | flops 75497472 | bytes 1642512 | tf_op jit(solution)/shard_map/pallas_call | solution.py:276
  78.4 1.2 %collective-permute-start.15 = (f32[128,768]{1,0:T(8,128)S(1)}, f32[128,768]{1,0:T(8,128)S(1)}, u32[]{:S(2)}, u32[]{:S(2)}) collective-permute-start(f32[128,768]{1,0:T(8,128)S(1)} %get-tuple-element.29), channel_id=1, source_target_pairs={{0,1},{1,0},{2,3},{3,2},{4,5},{5,4},{6,7},{7,6},{8,9},{9,8},{10,11... | collective-permute-start | bytes 1179656 | tf_op jit(solution)/shard_map/ppermute | solution.py:309
  79.6 1.3 %collective-permute-done.15.got_ref = f32[128,768]{1,0:T(8,128)S(1)} collective-permute-done((f32[128,768]{1,0:T(8,128)S(1)}, f32[128,768]{1,0:T(8,128)S(1)}, u32[]{:S(2)}, u32[]{:S(2)}) %collective-permute-start.15) | collective-permute-done | bytes 393248 | tf_op jit(solution)/shard_map/ppermute | solution.py:309
  80.9 0.1 shard_map.131
  81.0 1.1 %collective-permute-start.16 = (f32[64,768]{1,0:T(8,128)S(1)}, f32[64,768]{1,0:T(8,128)S(1)}, u32[]{:S(2)}, u32[]{:S(2)}) collective-permute-start(f32[64,768]{1,0:T(8,128)S(1)} %get-tuple-element.31), channel_id=1, source_target_pairs={{0,2},{1,3},{2,0},{3,1},{4,6},{5,7},{6,4},{7,5},{8,10},{9,11},{10,... | collective-permute-start | bytes 589832 | tf_op jit(solution)/shard_map/ppermute | solution.py:312
  82.1 0.1 fusion.14
  82.1 5.1 %collective-permute-done.16.away_ref = f32[64,768]{1,0:T(8,128)S(1)} collective-permute-done((f32[64,768]{1,0:T(8,128)S(1)}, f32[64,768]{1,0:T(8,128)S(1)}, u32[]{:S(2)}, u32[]{:S(2)}) %collective-permute-start.16) | collective-permute-done | bytes 196640 | tf_op jit(solution)/shard_map/ppermute | solution.py:312
  87.2 0.9 shard_map.132
  (47 shorter events, 0.3 us)
Async XLA Ops:
  0.6 13.0 %copy-start.9 = (s32[64]{0:T(128)S(1)}, s32[64]{0:T(128)}, u32[]{:S(2)}) copy-start(s32[64]{0:T(128)} %constant.136.clone) | copy-start | bytes 772
  0.6 12.6 %copy-start.2 = (s32[2,256]{1,0:T(2,128)S(1)}, s32[2,256]{1,0:T(2,128)}, u32[]{:S(2)}) copy-start(s32[2,256]{1,0:T(2,128)} %pivots_hbm.1) | copy-start | bytes 6148
  0.7 13.0 %copy-start.3 = (f32[1024]{0:T(1024)S(1)}, f32[1024]{0:T(1024)}, u32[]{:S(2)}) copy-start(f32[1024]{0:T(1024)} %param.13) | copy-start | bytes 12292
  0.7 13.0 %copy-start.4 = (s32[1024]{0:T(1024)S(1)}, s32[1024]{0:T(1024)}, u32[]{:S(2)}) copy-start(s32[1024]{0:T(1024)} %param.14) | copy-start | bytes 12292
  0.7 47.7 %copy-start.5 = (f32[1024]{0:T(1024)S(1)}, f32[1024]{0:T(1024)}, u32[]{:S(2)}) copy-start(f32[1024]{0:T(1024)} %param.12) | copy-start | bytes 12292
  5.4 9.7 %collective-permute-start = (f32[16,1152]{1,0:T(8,128)S(1)}, f32[16,1152]{1,0:T(8,128)S(1)}, u32[]{:S(2)}, u32[]{:S(2)}) collective-permute-start(f32[16,1152]{1,0:T(8,128)S(1)} %shard_map.122), channel_id=1, source_target_pairs={{0,32},{4,36},{8,40},{12,44},{16,48},{20,52},{24,56},{28,60},{32,0... | collective-permute-start | bytes 221192 | tf_op jit(solution)/shard_map/ppermute | solution.py:28
  15.1 11.5 %collective-permute-start.1 = (f32[32,1152]{1,0:T(8,128)S(1)}, f32[32,1152]{1,0:T(8,128)S(1)}, u32[]{:S(2)}, u32[]{:S(2)}) collective-permute-start(f32[32,1152]{1,0:T(8,128)S(1)} %pad_maximum_fusion.1), channel_id=1, source_target_pairs={{0,136},{4,140},{8,144},{12,148},{16,152},{20,156},{24,160},{28,16... | collective-permute-start | bytes 442376 | tf_op jit(solution)/shard_map/ppermute | solution.py:28
  18.5 8.2 %collective-permute-start.2 = (f32[32,1152]{1,0:T(8,128)S(1)}, f32[32,1152]{1,0:T(8,128)S(1)}, u32[]{:S(2)}, u32[]{:S(2)}) collective-permute-start(f32[32,1152]{1,0:T(8,128)S(1)} %pad_maximum_fusion.1), channel_id=1, source_target_pairs={{0,184},{4,188},{8,128},{12,132},{16,136},{20,140},{24,144},{28,14... | collective-permute-start | bytes 442376 | tf_op jit(solution)/shard_map/ppermute | solution.py:28
  22.7 9.3 %collective-permute-start.3 = (f32[32,1152]{1,0:T(8,128)S(1)}, f32[32,1152]{1,0:T(8,128)S(1)}, u32[]{:S(2)}, u32[]{:S(2)}) collective-permute-start(f32[32,1152]{1,0:T(8,128)S(1)} %pad_maximum_fusion.1), channel_id=1, source_target_pairs={{0,16},{4,20},{8,24},{12,28},{16,32},{20,36},{24,40},{28,44},{32,4... | collective-permute-start | bytes 442376 | tf_op jit(solution)/shard_map/ppermute | solution.py:28
  32.0 14.8 %collective-permute-start.6 = (f32[128,1152]{1,0:T(8,128)S(1)}, f32[128,1152]{1,0:T(8,128)S(1)}, u32[]{:S(2)}, u32[]{:S(2)}) collective-permute-start(f32[128,1152]{1,0:T(8,128)S(1)} %constant_dynamic-update-slice_fusion.refs_0_.after_ref), channel_id=1, source_target_pairs={{0,4},{4,0},{8,12},{12,8},{16,20},{20,16},{24,28},{28,24},{32,36},... | collective-permute-start | bytes 1769480 | tf_op jit(solution)/shard_map/ppermute | solution.py:28
  35.4 17.3 %collective-permute-start.4 = (f32[128,1152]{1,0:T(8,128)S(1)}, f32[128,1152]{1,0:T(8,128)S(1)}, u32[]{:S(2)}, u32[]{:S(2)}) collective-permute-start(f32[128,1152]{1,0:T(8,128)S(1)} %constant_dynamic-update-slice_fusion.refs_0_.after_ref), channel_id=1, source_target_pairs={{0,64},{4,68},{8,72},{12,76},{16,80},{20,84},{24,88},{28,92},{32,9... | collective-permute-start | bytes 1769480 | tf_op jit(solution)/shard_map/ppermute | solution.py:28
  35.4 20.0 %collective-permute-start.5 = (f32[128,1152]{1,0:T(8,128)S(1)}, f32[128,1152]{1,0:T(8,128)S(1)}, u32[]{:S(2)}, u32[]{:S(2)}) collective-permute-start(f32[128,1152]{1,0:T(8,128)S(1)} %constant_dynamic-update-slice_fusion.refs_0_.after_ref), channel_id=1, source_target_pairs={{0,192},{4,196},{8,200},{12,204},{16,208},{20,212},{24,216},{28,22... | collective-permute-start | bytes 1769480 | tf_op jit(solution)/shard_map/ppermute | solution.py:28
  38.1 8.7 %collective-permute-start.7 = (f32[64,1152]{1,0:T(8,128)S(1)}, f32[64,1152]{1,0:T(8,128)S(1)}, u32[]{:S(2)}, u32[]{:S(2)}) collective-permute-start(f32[64,1152]{1,0:T(8,128)S(1)} %pad_maximum_fusion), channel_id=1, source_target_pairs={{0,8},{4,12},{8,16},{12,20},{16,24},{20,28},{24,32},{28,36},{32,40... | collective-permute-start | bytes 884744 | tf_op jit(solution)/shard_map/ppermute | solution.py:28
  38.3 14.3 %collective-permute-start.8 = (f32[64,1152]{1,0:T(8,128)S(1)}, f32[64,1152]{1,0:T(8,128)S(1)}, u32[]{:S(2)}, u32[]{:S(2)}) collective-permute-start(f32[64,1152]{1,0:T(8,128)S(1)} %pad_maximum_fusion), channel_id=1, source_target_pairs={{0,56},{4,60},{8,0},{12,4},{16,8},{20,12},{24,16},{28,20},{32,24},... | collective-permute-start | bytes 884744 | tf_op jit(solution)/shard_map/ppermute | solution.py:28
  46.8 14.8 %collective-permute-start.10 = (f32[128,1152]{1,0:T(8,128)S(1)}, f32[128,1152]{1,0:T(8,128)S(1)}, u32[]{:S(2)}, u32[]{:S(2)}) collective-permute-start(f32[128,1152]{1,0:T(8,128)S(1)} %collective-permute-done.6.refs_3_.refs_0_), channel_id=1, source_target_pairs={{0,192},{4,196},{8,200},{12,204},{16,208},{20,212},{24,216},{28,22... | collective-permute-start | bytes 1769480 | tf_op jit(solution)/shard_map/ppermute | solution.py:28
  46.9 15.6 %collective-permute-start.9 = (f32[128,1152]{1,0:T(8,128)S(1)}, f32[128,1152]{1,0:T(8,128)S(1)}, u32[]{:S(2)}, u32[]{:S(2)}) collective-permute-start(f32[128,1152]{1,0:T(8,128)S(1)} %collective-permute-done.6.refs_3_.refs_0_), channel_id=1, source_target_pairs={{0,64},{4,68},{8,72},{12,76},{16,80},{20,84},{24,88},{28,92},{32,9... | collective-permute-start | bytes 1769480 | tf_op jit(solution)/shard_map/ppermute | solution.py:28
  48.4 7.0 %copy-start.6 = (s32[2,64]{1,0:T(2,128)S(1)}, s32[2,64]{1,0:T(2,128)}, u32[]{:S(2)}) copy-start(s32[2,64]{1,0:T(2,128)} %param.20) | copy-start | bytes 1540
  48.4 7.0 %copy-start.7 = (f32[2,64]{1,0:T(2,128)S(1)}, f32[2,64]{1,0:T(2,128)}, u32[]{:S(2)}) copy-start(f32[2,64]{1,0:T(2,128)} %param.19) | copy-start | bytes 1540
  52.6 7.2 %collective-permute-start.11 = (f32[64,1152]{1,0:T(8,128)S(1)}, f32[64,1152]{1,0:T(8,128)S(1)}, u32[]{:S(2)}, u32[]{:S(2)}) collective-permute-start(f32[64,1152]{1,0:T(8,128)S(1)} %shard_map.125), channel_id=1, source_target_pairs={{0,8},{4,12},{8,16},{12,20},{16,24},{20,28},{24,32},{28,36},{32,40... | collective-permute-start | bytes 884744 | tf_op jit(solution)/shard_map/ppermute | solution.py:28
  52.7 7.1 %collective-permute-start.12 = (f32[64,1152]{1,0:T(8,128)S(1)}, f32[64,1152]{1,0:T(8,128)S(1)}, u32[]{:S(2)}, u32[]{:S(2)}) collective-permute-start(f32[64,1152]{1,0:T(8,128)S(1)} %shard_map.125), channel_id=1, source_target_pairs={{0,56},{4,60},{8,0},{12,4},{16,8},{20,12},{24,16},{28,20},{32,24},... | collective-permute-start | bytes 884744 | tf_op jit(solution)/shard_map/ppermute | solution.py:28
  62.5 5.4 %copy-start.8 = (f32[2,64]{1,0:T(2,128)S(1)}, f32[2,64]{1,0:T(2,128)}, u32[]{:S(2)}) copy-start(f32[2,64]{1,0:T(2,128)} %param.18) | copy-start | bytes 1540
  65.1 4.2 %collective-permute-start.13 = (f32[128,1024]{1,0:T(8,128)S(1)}, f32[128,1024]{1,0:T(8,128)S(1)}, u32[]{:S(2)}, u32[]{:S(2)}) collective-permute-start(f32[128,1024]{1,0:T(8,128)S(1)} %get-tuple-element.24), channel_id=1, source_target_pairs={{0,1},{1,0},{2,3},{3,2},{4,5},{5,4},{6,7},{7,6},{8,9},{9,8},{10,11... | collective-permute-start | bytes 1572872 | tf_op jit(solution)/shard_map/ppermute | solution.py:309
  69.3 7.6 %collective-permute-start.14 = (f32[64,1024]{1,0:T(8,128)S(1)}, f32[64,1024]{1,0:T(8,128)S(1)}, u32[]{:S(2)}, u32[]{:S(2)}) collective-permute-start(f32[64,1024]{1,0:T(8,128)S(1)} %get-tuple-element.26), channel_id=1, source_target_pairs={{0,2},{1,3},{2,0},{3,1},{4,6},{5,7},{6,4},{7,5},{8,10},{9,11},{10,... | collective-permute-start | bytes 786440 | tf_op jit(solution)/shard_map/ppermute | solution.py:312
  70.5 6.5 %copy-start = (f32[64,768]{1,0:T(8,128)S(1)}, f32[64,768]{1,0:T(8,128)}, u32[]{:S(2)}) copy-start(f32[64,768]{1,0:T(8,128)} %a_ref.2) | copy-start | bytes 589828
  72.5 14.7 %copy-start.1 = (f32[64,768]{1,0:T(8,128)S(1)}, f32[64,768]{1,0:T(8,128)}, u32[]{:S(2)}) copy-start(f32[64,768]{1,0:T(8,128)} %a_ref.3) | copy-start | bytes 589828
  78.4 2.6 %collective-permute-start.15 = (f32[128,768]{1,0:T(8,128)S(1)}, f32[128,768]{1,0:T(8,128)S(1)}, u32[]{:S(2)}, u32[]{:S(2)}) collective-permute-start(f32[128,768]{1,0:T(8,128)S(1)} %get-tuple-element.29), channel_id=1, source_target_pairs={{0,1},{1,0},{2,3},{3,2},{4,5},{5,4},{6,7},{7,6},{8,9},{9,8},{10,11... | collective-permute-start | bytes 1179656 | tf_op jit(solution)/shard_map/ppermute | solution.py:309
  81.0 6.2 %collective-permute-start.16 = (f32[64,768]{1,0:T(8,128)S(1)}, f32[64,768]{1,0:T(8,128)S(1)}, u32[]{:S(2)}, u32[]{:S(2)}) collective-permute-start(f32[64,768]{1,0:T(8,128)S(1)} %get-tuple-element.31), channel_id=1, source_target_pairs={{0,2},{1,3},{2,0},{3,1},{4,6},{5,7},{6,4},{7,5},{8,10},{9,11},{10,... | collective-permute-start | bytes 589832 | tf_op jit(solution)/shard_map/ppermute | solution.py:312

commit v9 on v8

--- a/solution.py
+++ b/solution.py
@@ -36,19 +36,23 @@
     held, at = block, [(0, 0, 0)]
     got, its = moved(held, at, (0, 4, 0))
     held, at = jnp.concatenate([held, got], 0), at + its
+    ready = [in_hbm(part) for part in made(got)]
     parts = [moved(held, at, step) for step in ((2, 1, 0), (2, -1, 0), (0, 2, 0))]
-    held = jnp.concatenate([held] + [p[0] for p in parts], 0)
+    pair = 2 * rows
+    pieces = [held] + [p[0] for p in parts]
+    places = [(piece, 0, pair, 0, pair * i) for i, piece in enumerate(pieces)]
+    places += [(pieces[i], 0, pair, 1, pair * i) for i in range(2)]
+    held, low = cuts(places, [4 * pair, 2 * pair], ready[0])
     at = at + parts[0][1] + parts[1][1] + parts[2][1]
     half = len(at) // 2
     cut = half * rows
     over = moved(held, at, (0, 0, 1))
     ahead = moved(held, at, (1, 0, 0))
     behind = moved(held, at, (-1, 0, 0))
-    up = moved(held[:cut], at[:half], (0, 1, 0))
-    down = moved(held[:cut], at[:half], (0, -1, 0))
+    up = moved(low, at[:half], (0, 1, 0))
+    down = moved(low, at[:half], (0, -1, 0))
     early = [(held, at), ahead, behind, over, up, down]
-    ready = made(held)
-    (middle,) = cuts([(over[0], 0, cut, 0, 0)], [cut], ready[0])
+    (middle,) = cuts([(over[0], 0, cut, 0, 0)], [cut])
     late = [
         moved(over[0], over[1], (1, 0, 0)),
         moved(over[0], over[1], (-1, 0, 0)),
@@ -220,13 +224,21 @@
 
 
 def early_kernel(index_ref, *refs):
-    *pieces, out_ref, parts_ref = refs
+    *pieces, big_in, small_in, out_ref, big_out, small_out, parts_ref, sems = refs
+    copies = [
+        pltpu.make_async_copy(big_in, big_out, sems.at[0]),
+        pltpu.make_async_copy(small_in, small_out, sems.at[1]),
+    ]
+    for copy in copies:
+        copy.start()
     fill_parts(parts_ref, pieces)
     hit = hits(index_ref[...], 0, parts_ref.shape[0] // 2)
     for low in range(0, out_ref.shape[1], 384):
         out_ref[:, low : low + 384] = jnp.dot(
             hit, parts_ref[:, low : low + 384], preferred_element_type=jnp.float32
         )
+    for copy in copies:
+        copy.wait()
 
 
 def send_kernel(index_ref, weight_ref, carry_ref, lt_big_ref, lt_small_ref, *refs, base):
@@ -270,9 +282,10 @@
         out_ref[i * blocks : (i + 1) * blocks, :] = whole_ref[pl.ds(start, blocks), :]
 
 
-def local_call(kernel, out_shape, flops, *args, scratch=(), smem=0):
+def local_call(kernel, out_shape, flops, *args, scratch=(), smem=0, hbm=0):
     vmem = pl.BlockSpec(memory_space=pltpu.VMEM)
-    specs = [pl.BlockSpec(memory_space=pltpu.SMEM)] * smem + [vmem] * (len(args) - smem)
+    specs = [pl.BlockSpec(memory_space=pltpu.SMEM)] * smem + [vmem] * (len(args) - smem - hbm)
+    specs += [pl.BlockSpec(memory_space=pl.ANY)] * hbm
     return pl.pallas_call(
         kernel,
         in_specs=specs,
@@ -366,7 +379,7 @@
     rank = jnp.sum((tile[:, None] == tile[None, :]) & (order[None, :] < order[:, None]), 1)
     block = tile_slots(pivots, here * tile_rows, prior_lt, a_first)
     weights = operator_rows(prior_d, prior_e, prior_pairs)
-    early, late, (lt_big, lt_small) = gather_tiles(
+    early, late, parts = gather_tiles(
         block, lambda held: coupled_parts(weights, prior_lt, held)
     )
     offsets = [o for piece in early + late for o in piece[1]]
@@ -390,13 +403,16 @@
     wide = tile_rows + P_SIZE
     f32, b16 = jnp.float32, jnp.bfloat16
     shape = jax.ShapeDtypeStruct
-    carry = local_call(
+    part = shape((k_local, tile_rows), b16)
+    carry, lt_big, lt_small = local_call(
         early_kernel,
-        shape((2 * P_SIZE, width), f32),
+        (shape((2 * P_SIZE, width), f32), part, part),
         4 * 2 * P_SIZE * early_rows * width,
         where,
         *[in_vmem(piece[0]) for piece in early],
-        scratch=[pltpu.VMEM((2 * early_rows, width), b16)],
+        *parts,
+        scratch=[pltpu.VMEM((2 * early_rows, width), b16), pltpu.SemaphoreType.DMA((2,))],
+        hbm=2,
     )
     send, second, entries, second_big, second_small, taken = local_call(
         functools.partial(send_kernel, base=early_rows),

time: 88.2 us -> 91.6 us (1.039)
  Pallas kernels: 19.6 us -> 23.5 us
  starting transfers between devices: 34.4 us -> 32.2 us
  local copies, waits for them, and re-layouts: 0.44 us -> 1.55 us
    pallas_call x8, Pallas kernels: 10.7 us -> 12.8 us  [local_call(): pl.pallas_call(kernel, in_specs=specs, out_specs=jax.tree.map(lambda _: v...]
    pallas_call x1 -> x2, Pallas kernels: 0.07 us -> 1.97 us  [cuts(): pl.pallas_call(functools.partial(cuts_kernel, parts=[part[1:] for part in...]
    ppermute x13, starting transfers between devices: 28.4 us -> 27 us  [moved(): got = lax.ppermute(block, 'wide', shift(*step))]
    unnamed x25, local copies, waits for them, and re-layouts: 0.09 us -> 1.21 us
  transfers between devices with their start and end apart: 17 -> 17, of which waited for: 11 -> 12; matrix products, arithmetic and copies ran while one was open for 1% -> 1% of each run, Pallas kernels for 11% -> 12%
where the time goes in v9:
time: 91.6 us; the launch traced here: 91.4 us
  waiting for transfers between devices  32.6 us (36%)
  starting transfers between devices  32.2 us (35%)
  Pallas kernels  23.5 us (26%)
  local copies, waits for them, and re-layouts  1.55 us (2%)
    ppermute x13, starting transfers between devices, moved(): got = lax.ppermute(block, 'wide', shift(*step))  27 us
    ppermute x13, waiting for transfers between devices, moved(): got = lax.ppermute(block, 'wide', shift(*step))  21 us
    pallas_call x8, Pallas kernels, local_call(): pl.pallas_call(kernel, in_specs=specs, out_specs=jax.tree.map(lambda _: v...  12.8 us
    ppermute x2, waiting for transfers between devices, hop_sum(): return (rest, lax.ppermute(away, 'narrow', CHIP))  10.1 us
    pallas_call x1, Pallas kernels, tile_slots(): pl.pallas_call(slots_kernel, in_specs=[pl.BlockSpec(memory_space=pltpu.SM...  4.63 us
    pallas_call x1, Pallas kernels, coupled_parts(): pl.pallas_call(couple_kernel, grid=(4,), in_specs=[pl.BlockSpec((8, depth...  4.09 us
    ppermute x2, starting transfers between devices, hop_sum(): got = lax.ppermute(send, 'narrow', CORE)  3.59 us
    pallas_call x2, Pallas kernels, cuts(): pl.pallas_call(functools.partial(cuts_kernel, parts=[part[1:] for part in...  1.97 us
  transfers between devices with their start and end apart: 17, of which 12 were waited for; matrix products, arithmetic and copies ran while one was open for 1% of the time, Pallas kernels for 12%

profile of v9, /device:TPU:1, one launch (start us, length us, event | category | flops | bytes accessed | tf_op | source)
XLA Modules:
  0.0 91.4 jit_solution(10284734777874591889)
XLA Ops:
  0.7 4.6 %shard_map.122 = f32[16,1152]{1,0:T(8,128)S(1)} custom-call(s32[1]{0:T(128)} %bitcast.10.low_ref, s32[2,256]{1,0:T(2,128)} %pivots_hbm.1, f32[64,768]{1,0:T(8,128)} %a_ref.2, f32[1024,768]{1,0:T(8,128)} %lt_ref.3), custom_call_target="tpu_custom_call" | custom-call | tf_op jit(solution)/shard_map/pallas_call | solution.py:163
  5.3 7.8 %collective-permute-start = (f32[16,1152]{1,0:T(8,128)S(1)}, f32[16,1152]{1,0:T(8,128)S(1)}, u32[]{:S(2)}, u32[]{:S(2)}) collective-permute-start(f32[16,1152]{1,0:T(8,128)S(1)} %shard_map.122), channel_id=1, source_target_pairs={{0,32},{4,36},{8,40},{12,44},{16,48},{20,52},{24,56},{28,60},{32,0... | collective-permute-start | bytes 221192 | tf_op jit(solution)/shard_map/ppermute | solution.py:28
  13.2 1.8 %collective-permute-done.after_ref = f32[16,1152]{1,0:T(8,128)S(1)} collective-permute-done((f32[16,1152]{1,0:T(8,128)S(1)}, f32[16,1152]{1,0:T(8,128)S(1)}, u32[]{:S(2)}, u32[]{:S(2)}) %collective-permute-start) | collective-permute-done | bytes 73760 | tf_op jit(solution)/shard_map/ppermute | solution.py:28
  15.0 3.3 %collective-permute-start.1 = (f32[32,1152]{1,0:T(8,128)S(1)}, f32[32,1152]{1,0:T(8,128)S(1)}, u32[]{:S(2)}, u32[]{:S(2)}) collective-permute-start(f32[32,1152]{1,0:T(8,128)S(1)} %pad_maximum_fusion.refs_0_.refs_4_), channel_id=1, source_target_pairs={{0,136},{4,140},{8,144},{12,148},{16,152},{20,156},{24,160},{28,16... | collective-permute-start | bytes 442376 | tf_op jit(solution)/shard_map/ppermute | solution.py:28
  18.3 4.2 %collective-permute-start.2 = (f32[32,1152]{1,0:T(8,128)S(1)}, f32[32,1152]{1,0:T(8,128)S(1)}, u32[]{:S(2)}, u32[]{:S(2)}) collective-permute-start(f32[32,1152]{1,0:T(8,128)S(1)} %pad_maximum_fusion.refs_0_.refs_4_), channel_id=1, source_target_pairs={{0,184},{4,188},{8,128},{12,132},{16,136},{20,140},{24,144},{28,14... | collective-permute-start | bytes 442376 | tf_op jit(solution)/shard_map/ppermute | solution.py:28
  22.6 0.1 pad_maximum_fusion.1
  22.7 4.1 %shard_map.123 = (bf16[1024,768]{1,0:T(8,128)(2,1)S(1)}, bf16[1024,768]{1,0:T(8,128)(2,1)S(1)}) custom-call(f32[8,1024]{1,0:T(8,128)S(1)} %select_maximum_fusion.weight_ref, f32[1024,768]{1,0:T(8,128)} %lt_ref.3, f32[16,1152]{1,0:T(8,128)S(1)} %collective-permute-done.after_ref), custom_call_target="tpu_custom_call" | custom-call | flops 6291456 | bytes 6291456 | tf_op jit(solution)/shard_map/pallas_call | solution.py:193
  26.8 1.2 %copy-done = bf16[1024,768]{1,0:T(8,128)(2,1)} copy-done((bf16[1024,768]{1,0:T(8,128)(2,1)}, bf16[1024,768]{1,0:T(8,128)(2,1)S(1)}, u32[]{:S(2)}) %copy-start) | copy-done | bytes 1572888
  28.0 3.9 %collective-permute-done.3.refs_3_ = f32[32,1152]{1,0:T(8,128)S(1)} collective-permute-done((f32[32,1152]{1,0:T(8,128)S(1)}, f32[32,1152]{1,0:T(8,128)S(1)}, u32[]{:S(2)}, u32[]{:S(2)}) %collective-permute-start.3) | collective-permute-done | bytes 147488 | tf_op jit(solution)/shard_map/ppermute | solution.py:28
  31.9 1.9 %shard_map.124 = (f32[128,1152]{1,0:T(8,128)S(1)}, f32[64,1152]{1,0:T(8,128)}) custom-call(f32[32,1152]{1,0:T(8,128)S(1)} %pad_maximum_fusion.refs_0_.refs_4_, f32[32,1152]{1,0:T(8,128)S(1)} %collective-permute-done.1.refs_1_.refs_5_, f32[32,1152]{1,0:T(8,128)S(1)} %collective-permute-done.2.refs_2_, f32[32,1152]{1,0:T(8,128)S(1)} %collective-permute-done.3.refs_3_, ...), custom_call_target="tpu_custom_call" | custom-call | tf_op jit(solution)/shard_map/pallas_call | solution.py:87
  33.8 3.5 %collective-permute-start.6 = (f32[128,1152]{1,0:T(8,128)S(1)}, f32[128,1152]{1,0:T(8,128)S(1)}, u32[]{:S(2)}, u32[]{:S(2)}) collective-permute-start(f32[128,1152]{1,0:T(8,128)S(1)} %get-tuple-element.23.refs_0_), channel_id=1, source_target_pairs={{0,4},{4,0},{8,12},{12,8},{16,20},{20,16},{24,28},{28,24},{32,36},... | collective-permute-start | bytes 1769480 | tf_op jit(solution)/shard_map/ppermute | solution.py:28
  37.3 0.2 convert_reduce_fusion
  37.5 0.1 collective-permute-start.4
  37.6 0.1 collective-permute-start.7
  37.7 0.1 select_reduce_fusion
  37.8 2.6 %collective-permute-start.5 = (f32[128,1152]{1,0:T(8,128)S(1)}, f32[128,1152]{1,0:T(8,128)S(1)}, u32[]{:S(2)}, u32[]{:S(2)}) collective-permute-start(f32[128,1152]{1,0:T(8,128)S(1)} %get-tuple-element.23.refs_0_), channel_id=1, source_target_pairs={{0,192},{4,196},{8,200},{12,204},{16,208},{20,212},{24,216},{28,22... | collective-permute-start | bytes 1769480 | tf_op jit(solution)/shard_map/ppermute | solution.py:28
  40.4 2.7 %collective-permute-start.8 = (f32[64,1152]{1,0:T(8,128)}, f32[64,1152]{1,0:T(8,128)}, u32[]{:S(2)}, u32[]{:S(2)}) collective-permute-start(f32[64,1152]{1,0:T(8,128)} %get-tuple-element.24), channel_id=1, source_target_pairs={{0,56},{4,60},{8,0},{12,4},{16,8},{20,12},{24,16},{28,20},{32,24},... | collective-permute-start | bytes 884744 | tf_op jit(solution)/shard_map/ppermute | solution.py:28
  43.1 5.5 %collective-permute-done.6.refs_3_.refs_0_ = f32[128,1152]{1,0:T(8,128)S(1)} collective-permute-done((f32[128,1152]{1,0:T(8,128)S(1)}, f32[128,1152]{1,0:T(8,128)S(1)}, u32[]{:S(2)}, u32[]{:S(2)}) %collective-permute-start.6) | collective-permute-done | bytes 589856 | tf_op jit(solution)/shard_map/ppermute | solution.py:28
  48.7 1.5 %collective-permute-start.9 = (f32[128,1152]{1,0:T(8,128)S(1)}, f32[128,1152]{1,0:T(8,128)}, u32[]{:S(2)}, u32[]{:S(2)}) collective-permute-start(f32[128,1152]{1,0:T(8,128)S(1)} %collective-permute-done.6.refs_3_.refs_0_), channel_id=1, source_target_pairs={{0,64},{4,68},{8,72},{12,76},{16,80},{20,84},{24,88},{28,92},{32,9... | collective-permute-start | bytes 1769480 | tf_op jit(solution)/shard_map/ppermute | solution.py:28
  50.1 0.1 fusion.17
  50.2 0.1 concatenate.20
  50.3 0.1 copy.16.index_ref
  50.4 0.1 shard_map.126
  50.5 0.1 collective-permute-start.11
  50.6 1.5 %collective-permute-done.4.refs_1_ = f32[128,1152]{1,0:T(8,128)S(1)} collective-permute-done((f32[128,1152]{1,0:T(8,128)S(1)}, f32[128,1152]{1,0:T(8,128)S(1)}, u32[]{:S(2)}, u32[]{:S(2)}) %collective-permute-start.4) | collective-permute-done | bytes 589856 | tf_op jit(solution)/shard_map/ppermute | solution.py:28
  52.1 1.2 %collective-permute-start.12 = (f32[64,1152]{1,0:T(8,128)S(1)}, f32[64,1152]{1,0:T(8,128)S(1)}, u32[]{:S(2)}, u32[]{:S(2)}) collective-permute-start(f32[64,1152]{1,0:T(8,128)S(1)} %shard_map.126), channel_id=1, source_target_pairs={{0,56},{4,60},{8,0},{12,4},{16,8},{20,12},{24,16},{28,20},{32,24},... | collective-permute-start | bytes 884744 | tf_op jit(solution)/shard_map/ppermute | solution.py:28
  53.3 3.4 %shard_map.125 = (f32[512,1152]{1,0:T(8,128)S(1)}, bf16[1024,768]{1,0:T(8,128)(2,1)S(1)}, bf16[1024,768]{1,0:T(8,128)(2,1)S(1)}) custom-call(s32[512,1]{1,0:T(8,128)S(1)} %copy.16.index_ref, f32[128,1152]{1,0:T(8,128)S(1)} %get-tuple-element.23.refs_0_, f32[128,1152]{1,0:T(8,128)S(1)} %collective-permute-done.4.refs_1_, ...), custom_call_target="tpu_custom_call" | custom-call | flops 1509949440 | bytes 9242624 | tf_op jit(solution)/shard_map/pallas_call | solution.py:289
  56.7 1.1 %collective-permute-done.11.refs_2_ = f32[64,1152]{1,0:T(8,128)S(1)} collective-permute-done((f32[64,1152]{1,0:T(8,128)S(1)}, f32[64,1152]{1,0:T(8,128)S(1)}, u32[]{:S(2)}, u32[]{:S(2)}) %collective-permute-start.11) | collective-permute-done | bytes 294944 | tf_op jit(solution)/shard_map/ppermute | solution.py:28
  57.8 0.3 collective-permute-done.12.refs_3_
  58.1 6.1 %collective-permute-done.10.refs_1_ = f32[128,1152]{1,0:T(8,128)S(1)} collective-permute-done((f32[128,1152]{1,0:T(8,128)S(1)}, f32[128,1152]{1,0:T(8,128)S(1)}, u32[]{:S(2)}, u32[]{:S(2)}) %collective-permute-start.10) | collective-permute-done | bytes 589856 | tf_op jit(solution)/shard_map/ppermute | solution.py:28
  64.2 0.8 collective-permute-done.9.refs_0_
  65.0 3.7 %shard_map.127 = (f32[128,1024]{1,0:T(8,128)S(1)}, f32[256,1024]{1,0:T(8,128)S(1)}, f32[256,128]{1,0:T(8,128)S(1)}, bf16[256,1024]{1,0:T(8,128)(2,1)S(1)}, bf16[...) custom-call(s32[512,1]{1,0:T(8,128)S(1)} %copy.16.index_ref, f32[8,1024]{1,0:T(8,128)S(1)} %select_maximum_fusion.weight_ref, ...), custom_call_target="tpu_custom_call" | custom-call | flops 1711276032 | bytes 10455040 | tf_op jit(solution)/shard_map/pallas_call | solution.py:289
  68.7 2.4 %collective-permute-start.13 = (f32[128,1024]{1,0:T(8,128)S(1)}, f32[128,1024]{1,0:T(8,128)S(1)}, u32[]{:S(2)}, u32[]{:S(2)}) collective-permute-start(f32[128,1024]{1,0:T(8,128)S(1)} %get-tuple-element.34), channel_id=1, source_target_pairs={{0,1},{1,0},{2,3},{3,2},{4,5},{5,4},{6,7},{7,6},{8,9},{9,8},{10,11... | collective-permute-start | bytes 1572872 | tf_op jit(solution)/shard_map/ppermute | solution.py:322
  71.1 0.1 fusion.13
  71.2 1.2 %shard_map.129.keep_ref = f32[128,1024]{1,0:T(8,128)S(1)} custom-call(f32[128,1024]{1,0:T(8,128)S(1)} %get-tuple-element.31.taken_ref, bf16[1024,768]{1,0:T(8,128)(2,1)S(1)} %get-tuple-element.27.lt_big_ref, bf16[1024,768]{1,0:T(8,128)(2,1)S(1)} %get-tuple-element.28.lt_small_ref, bf16[256,1024]{1,0:T(8,128)(2,1)S(1)} %get-tuple-element.32.big_ref, ...), custom_call_target="tpu_custom_call" | custom-call | flops 805306368 | bytes 8912896 | tf_op jit(solution)/shard_map/pallas_call | solution.py:289
  72.4 0.2 collective-permute-done.13.got_ref
  72.6 0.1 shard_map.130
  72.7 0.8 collective-permute-start.14
  73.4 0.1 pad_add_fusion.quarter_ref
  73.5 2.0 %shard_map.128.update_ref = f32[256,768]{1,0:T(8,128)S(1)} custom-call(s32[4]{0:T(128)S(1)} %pad_add_fusion.quarter_ref, f32[256,1024]{1,0:T(8,128)S(1)} %get-tuple-element.30.second_ref, bf16[1024,768]{1,0:T(8,128)(2,1)S(1)} %get-tuple-element.27.lt_big_ref, bf16[1024,768]{1,0:T(8,128)(2,1)S(1)} %get-tuple-element.28.lt_small_ref), custom_call_target="tpu_custom_call" | custom-call | flops 1207959552 | bytes 7340048 | tf_op jit(solution)/shard_map/pallas_call | solution.py:289
  75.5 4.7 %collective-permute-done.14.away_ref = f32[64,1024]{1,0:T(8,128)S(1)} collective-permute-done((f32[64,1024]{1,0:T(8,128)S(1)}, f32[64,1024]{1,0:T(8,128)S(1)}, u32[]{:S(2)}, u32[]{:S(2)}) %collective-permute-start.14) | collective-permute-done | bytes 262176 | tf_op jit(solution)/shard_map/ppermute | solution.py:325
  80.3 1.5 %shard_map.131 = (f32[64,768]{1,0:T(8,128)}, f32[128,768]{1,0:T(8,128)S(1)}, f32[128,768]{1,0:T(8,128)S(1)}) custom-call(s32[4]{0:T(128)S(1)} %pad_add_fusion.quarter_ref, f32[8,128]{1,0:T(8,128)S(1)} %select_maximum_fusion.4.weight_ref, f32[64,768]{1,0:T(8,128)S(1)} %copy-done.2, f32[256,128]{1,0:T(8,128)S(1)} %get-tuple-element.29.entries_ref, ...), custom_call_target="tpu_custom_call" | custom-call | flops 75497472 | bytes 1642512 | tf_op jit(solution)/shard_map/pallas_call | solution.py:289
  81.7 1.2 %collective-permute-start.15 = (f32[128,768]{1,0:T(8,128)S(1)}, f32[128,768]{1,0:T(8,128)S(1)}, u32[]{:S(2)}, u32[]{:S(2)}) collective-permute-start(f32[128,768]{1,0:T(8,128)S(1)} %get-tuple-element.39), channel_id=1, source_target_pairs={{0,1},{1,0},{2,3},{3,2},{4,5},{5,4},{6,7},{7,6},{8,9},{9,8},{10,11... | collective-permute-start | bytes 1179656 | tf_op jit(solution)/shard_map/ppermute | solution.py:322
  82.9 1.3 %collective-permute-done.15.got_ref = f32[128,768]{1,0:T(8,128)S(1)} collective-permute-done((f32[128,768]{1,0:T(8,128)S(1)}, f32[128,768]{1,0:T(8,128)S(1)}, u32[]{:S(2)}, u32[]{:S(2)}) %collective-permute-start.15) | collective-permute-done | bytes 393248 | tf_op jit(solution)/shard_map/ppermute | solution.py:322
  84.3 0.8 collective-permute-start.16
  85.1 0.1 fusion.14
  85.2 5.3 %collective-permute-done.16.away_ref = f32[64,768]{1,0:T(8,128)S(1)} collective-permute-done((f32[64,768]{1,0:T(8,128)S(1)}, f32[64,768]{1,0:T(8,128)S(1)}, u32[]{:S(2)}, u32[]{:S(2)}) %collective-permute-start.16) | collective-permute-done | bytes 196640 | tf_op jit(solution)/shard_map/ppermute | solution.py:325
  90.5 0.9 shard_map.133
  (46 shorter events, 0.3 us)
Async XLA Ops:
  0.6 12.5 %copy-start.4 = (s32[2,256]{1,0:T(2,128)S(1)}, s32[2,256]{1,0:T(2,128)}, u32[]{:S(2)}) copy-start(s32[2,256]{1,0:T(2,128)} %pivots_hbm.1) | copy-start | bytes 6148
  0.6 12.5 %copy-start.5 = (f32[1024]{0:T(1024)S(1)}, f32[1024]{0:T(1024)}, u32[]{:S(2)}) copy-start(f32[1024]{0:T(1024)} %param.13) | copy-start | bytes 12292
  0.7 12.5 %copy-start.6 = (s32[1024]{0:T(1024)S(1)}, s32[1024]{0:T(1024)}, u32[]{:S(2)}) copy-start(s32[1024]{0:T(1024)} %param.14) | copy-start | bytes 12292
  0.7 22.0 %copy-start.7 = (f32[1024]{0:T(1024)S(1)}, f32[1024]{0:T(1024)}, u32[]{:S(2)}) copy-start(f32[1024]{0:T(1024)} %param.12) | copy-start | bytes 12292
  5.3 9.7 %collective-permute-start = (f32[16,1152]{1,0:T(8,128)S(1)}, f32[16,1152]{1,0:T(8,128)S(1)}, u32[]{:S(2)}, u32[]{:S(2)}) collective-permute-start(f32[16,1152]{1,0:T(8,128)S(1)} %shard_map.122), channel_id=1, source_target_pairs={{0,32},{4,36},{8,40},{12,44},{16,48},{20,52},{24,56},{28,60},{32,0... | collective-permute-start | bytes 221192 | tf_op jit(solution)/shard_map/ppermute | solution.py:28
  15.0 13.0 %collective-permute-start.1 = (f32[32,1152]{1,0:T(8,128)S(1)}, f32[32,1152]{1,0:T(8,128)S(1)}, u32[]{:S(2)}, u32[]{:S(2)}) collective-permute-start(f32[32,1152]{1,0:T(8,128)S(1)} %pad_maximum_fusion.refs_0_.refs_4_), channel_id=1, source_target_pairs={{0,136},{4,140},{8,144},{12,148},{16,152},{20,156},{24,160},{28,16... | collective-permute-start | bytes 442376 | tf_op jit(solution)/shard_map/ppermute | solution.py:28
  18.3 9.7 %collective-permute-start.2 = (f32[32,1152]{1,0:T(8,128)S(1)}, f32[32,1152]{1,0:T(8,128)S(1)}, u32[]{:S(2)}, u32[]{:S(2)}) collective-permute-start(f32[32,1152]{1,0:T(8,128)S(1)} %pad_maximum_fusion.refs_0_.refs_4_), channel_id=1, source_target_pairs={{0,184},{4,188},{8,128},{12,132},{16,136},{20,140},{24,144},{28,14... | collective-permute-start | bytes 442376 | tf_op jit(solution)/shard_map/ppermute | solution.py:28
  22.6 9.3 %collective-permute-start.3 = (f32[32,1152]{1,0:T(8,128)S(1)}, f32[32,1152]{1,0:T(8,128)S(1)}, u32[]{:S(2)}, u32[]{:S(2)}) collective-permute-start(f32[32,1152]{1,0:T(8,128)S(1)} %pad_maximum_fusion.refs_0_.refs_4_), channel_id=1, source_target_pairs={{0,16},{4,20},{8,24},{12,28},{16,32},{20,36},{24,40},{28,44},{32,4... | collective-permute-start | bytes 442376 | tf_op jit(solution)/shard_map/ppermute | solution.py:28
  26.8 1.2 %copy-start = (bf16[1024,768]{1,0:T(8,128)(2,1)}, bf16[1024,768]{1,0:T(8,128)(2,1)S(1)}, u32[]{:S(2)}) copy-start(bf16[1024,768]{1,0:T(8,128)(2,1)S(1)} %get-tuple-element.22.refs_6_) | copy-start | bytes 4718596
  28.0 20.7 %copy-start.1 = (bf16[1024,768]{1,0:T(8,128)(2,1)}, bf16[1024,768]{1,0:T(8,128)(2,1)S(1)}, u32[]{:S(2)}) copy-start(bf16[1024,768]{1,0:T(8,128)(2,1)S(1)} %get-tuple-element.25.refs_7_) | copy-start | bytes 4718596
  28.0 9.7 %copy-start.11 = (s32[64]{0:T(128)S(1)}, s32[64]{0:T(128)}, u32[]{:S(2)}) copy-start(s32[64]{0:T(128)} %constant.136.clone) | copy-start | bytes 772
  31.9 21.4 %copy-start.8 = (s32[2,64]{1,0:T(2,128)S(1)}, s32[2,64]{1,0:T(2,128)}, u32[]{:S(2)}) copy-start(s32[2,64]{1,0:T(2,128)} %param.20) | copy-start | bytes 1540
  31.9 21.4 %copy-start.9 = (f32[2,64]{1,0:T(2,128)S(1)}, f32[2,64]{1,0:T(2,128)}, u32[]{:S(2)}) copy-start(f32[2,64]{1,0:T(2,128)} %param.19) | copy-start | bytes 1540
  33.8 14.9 %collective-permute-start.6 = (f32[128,1152]{1,0:T(8,128)S(1)}, f32[128,1152]{1,0:T(8,128)S(1)}, u32[]{:S(2)}, u32[]{:S(2)}) collective-permute-start(f32[128,1152]{1,0:T(8,128)S(1)} %get-tuple-element.23.refs_0_), channel_id=1, source_target_pairs={{0,4},{4,0},{8,12},{12,8},{16,20},{20,16},{24,28},{28,24},{32,36},... | collective-permute-start | bytes 1769480 | tf_op jit(solution)/shard_map/ppermute | solution.py:28
  37.5 14.6 %collective-permute-start.4 = (f32[128,1152]{1,0:T(8,128)S(1)}, f32[128,1152]{1,0:T(8,128)S(1)}, u32[]{:S(2)}, u32[]{:S(2)}) collective-permute-start(f32[128,1152]{1,0:T(8,128)S(1)} %get-tuple-element.23.refs_0_), channel_id=1, source_target_pairs={{0,64},{4,68},{8,72},{12,76},{16,80},{20,84},{24,88},{28,92},{32,9... | collective-permute-start | bytes 1769480 | tf_op jit(solution)/shard_map/ppermute | solution.py:28
  37.6 11.1 %collective-permute-start.7 = (f32[64,1152]{1,0:T(8,128)}, f32[64,1152]{1,0:T(8,128)S(1)}, u32[]{:S(2)}, u32[]{:S(2)}) collective-permute-start(f32[64,1152]{1,0:T(8,128)} %get-tuple-element.24), channel_id=1, source_target_pairs={{0,8},{4,12},{8,16},{12,20},{16,24},{20,28},{24,32},{28,36},{32,40... | collective-permute-start | bytes 884744 | tf_op jit(solution)/shard_map/ppermute | solution.py:28
  37.8 15.5 %collective-permute-start.5 = (f32[128,1152]{1,0:T(8,128)S(1)}, f32[128,1152]{1,0:T(8,128)S(1)}, u32[]{:S(2)}, u32[]{:S(2)}) collective-permute-start(f32[128,1152]{1,0:T(8,128)S(1)} %get-tuple-element.23.refs_0_), channel_id=1, source_target_pairs={{0,192},{4,196},{8,200},{12,204},{16,208},{20,212},{24,216},{28,22... | collective-permute-start | bytes 1769480 | tf_op jit(solution)/shard_map/ppermute | solution.py:28
  40.4 10.1 %collective-permute-start.8 = (f32[64,1152]{1,0:T(8,128)}, f32[64,1152]{1,0:T(8,128)}, u32[]{:S(2)}, u32[]{:S(2)}) collective-permute-start(f32[64,1152]{1,0:T(8,128)} %get-tuple-element.24), channel_id=1, source_target_pairs={{0,56},{4,60},{8,0},{12,4},{16,8},{20,12},{24,16},{28,20},{32,24},... | collective-permute-start | bytes 884744 | tf_op jit(solution)/shard_map/ppermute | solution.py:28
  48.6 15.5 %collective-permute-start.10 = (f32[128,1152]{1,0:T(8,128)S(1)}, f32[128,1152]{1,0:T(8,128)S(1)}, u32[]{:S(2)}, u32[]{:S(2)}) collective-permute-start(f32[128,1152]{1,0:T(8,128)S(1)} %collective-permute-done.6.refs_3_.refs_0_), channel_id=1, source_target_pairs={{0,192},{4,196},{8,200},{12,204},{16,208},{20,212},{24,216},{28,22... | collective-permute-start | bytes 1769480 | tf_op jit(solution)/shard_map/ppermute | solution.py:28
  48.7 16.3 %collective-permute-start.9 = (f32[128,1152]{1,0:T(8,128)S(1)}, f32[128,1152]{1,0:T(8,128)}, u32[]{:S(2)}, u32[]{:S(2)}) collective-permute-start(f32[128,1152]{1,0:T(8,128)S(1)} %collective-permute-done.6.refs_3_.refs_0_), channel_id=1, source_target_pairs={{0,64},{4,68},{8,72},{12,76},{16,80},{20,84},{24,88},{28,92},{32,9... | collective-permute-start | bytes 1769480 | tf_op jit(solution)/shard_map/ppermute | solution.py:28
  50.5 7.3 %collective-permute-start.11 = (f32[64,1152]{1,0:T(8,128)S(1)}, f32[64,1152]{1,0:T(8,128)S(1)}, u32[]{:S(2)}, u32[]{:S(2)}) collective-permute-start(f32[64,1152]{1,0:T(8,128)S(1)} %shard_map.126), channel_id=1, source_target_pairs={{0,8},{4,12},{8,16},{12,20},{16,24},{20,28},{24,32},{28,36},{32,40... | collective-permute-start | bytes 884744 | tf_op jit(solution)/shard_map/ppermute | solution.py:28
  52.1 6.0 %collective-permute-start.12 = (f32[64,1152]{1,0:T(8,128)S(1)}, f32[64,1152]{1,0:T(8,128)S(1)}, u32[]{:S(2)}, u32[]{:S(2)}) collective-permute-start(f32[64,1152]{1,0:T(8,128)S(1)} %shard_map.126), channel_id=1, source_target_pairs={{0,56},{4,60},{8,0},{12,4},{16,8},{20,12},{24,16},{28,20},{32,24},... | collective-permute-start | bytes 884744 | tf_op jit(solution)/shard_map/ppermute | solution.py:28
  65.0 6.2 %copy-start.10 = (f32[2,64]{1,0:T(2,128)S(1)}, f32[2,64]{1,0:T(2,128)}, u32[]{:S(2)}) copy-start(f32[2,64]{1,0:T(2,128)} %param.18) | copy-start | bytes 1540
  68.7 3.9 %collective-permute-start.13 = (f32[128,1024]{1,0:T(8,128)S(1)}, f32[128,1024]{1,0:T(8,128)S(1)}, u32[]{:S(2)}, u32[]{:S(2)}) collective-permute-start(f32[128,1024]{1,0:T(8,128)S(1)} %get-tuple-element.34), channel_id=1, source_target_pairs={{0,1},{1,0},{2,3},{3,2},{4,5},{5,4},{6,7},{7,6},{8,9},{9,8},{10,11... | collective-permute-start | bytes 1572872 | tf_op jit(solution)/shard_map/ppermute | solution.py:322
  72.7 7.6 %collective-permute-start.14 = (f32[64,1024]{1,0:T(8,128)S(1)}, f32[64,1024]{1,0:T(8,128)S(1)}, u32[]{:S(2)}, u32[]{:S(2)}) collective-permute-start(f32[64,1024]{1,0:T(8,128)S(1)} %get-tuple-element.36), channel_id=1, source_target_pairs={{0,2},{1,3},{2,0},{3,1},{4,6},{5,7},{6,4},{7,5},{8,10},{9,11},{10,... | collective-permute-start | bytes 786440 | tf_op jit(solution)/shard_map/ppermute | solution.py:325
  73.5 6.8 %copy-start.2 = (f32[64,768]{1,0:T(8,128)S(1)}, f32[64,768]{1,0:T(8,128)}, u32[]{:S(2)}) copy-start(f32[64,768]{1,0:T(8,128)} %a_ref.2) | copy-start | bytes 589828
  75.5 15.0 %copy-start.3 = (f32[64,768]{1,0:T(8,128)S(1)}, f32[64,768]{1,0:T(8,128)}, u32[]{:S(2)}) copy-start(f32[64,768]{1,0:T(8,128)} %a_ref.3) | copy-start | bytes 589828
  81.7 2.6 %collective-permute-start.15 = (f32[128,768]{1,0:T(8,128)S(1)}, f32[128,768]{1,0:T(8,128)S(1)}, u32[]{:S(2)}, u32[]{:S(2)}) collective-permute-start(f32[128,768]{1,0:T(8,128)S(1)} %get-tuple-element.39), channel_id=1, source_target_pairs={{0,1},{1,0},{2,3},{3,2},{4,5},{5,4},{6,7},{7,6},{8,9},{9,8},{10,11... | collective-permute-start | bytes 1179656 | tf_op jit(solution)/shard_map/ppermute | solution.py:322
  84.3 6.2 %collective-permute-start.16 = (f32[64,768]{1,0:T(8,128)S(1)}, f32[64,768]{1,0:T(8,128)S(1)}, u32[]{:S(2)}, u32[]{:S(2)}) collective-permute-start(f32[64,768]{1,0:T(8,128)S(1)} %get-tuple-element.41), channel_id=1, source_target_pairs={{0,2},{1,3},{2,0},{3,1},{4,6},{5,7},{6,4},{7,5},{8,10},{9,11},{10,... | collective-permute-start | bytes 589832 | tf_op jit(solution)/shard_map/ppermute | solution.py:325

commit v10 on v8

--- a/solution.py
+++ b/solution.py
@@ -48,7 +48,7 @@
     down = moved(held[:cut], at[:half], (0, -1, 0))
     early = [(held, at), ahead, behind, over, up, down]
     ready = made(held)
-    (middle,) = cuts([(over[0], 0, cut, 0, 0)], [cut], ready[0])
+    (middle,) = cuts([(over[0], 0, cut, 0, 0)], [cut])
     late = [
         moved(over[0], over[1], (1, 0, 0)),
         moved(over[0], over[1], (-1, 0, 0)),
@@ -395,7 +395,8 @@
         shape((2 * P_SIZE, width), f32),
         4 * 2 * P_SIZE * early_rows * width,
         where,
-        *[in_vmem(piece[0]) for piece in early],
+        *[in_vmem(piece[0]) for piece in early[:4]],
+        *[in_hbm(piece[0]) for piece in early[4:]],
         scratch=[pltpu.VMEM((2 * early_rows, width), b16)],
     )
     send, second, entries, second_big, second_small, taken = local_call(

time: 88.2 us -> 88.2 us (level)
  Pallas kernels: 19.6 us -> 21 us
  starting transfers between devices: 34.4 us -> 33.3 us
    ppermute x13, starting transfers between devices: 28.4 us -> 26.9 us  [moved(): got = lax.ppermute(block, 'wide', shift(*step))]
    pallas_call x8, Pallas kernels: 10.7 us -> 12.1 us  [local_call(): pl.pallas_call(kernel, in_specs=specs, out_specs=jax.tree.map(lambda _: v...]
  transfers between devices with their start and end apart: 17 -> 17, of which waited for: 11 -> 11; matrix products, arithmetic and copies ran while one was open for 1% -> 1% of each run, Pallas kernels for 11% -> 13%
where the time goes in v10:
time: 88.2 us; the launch traced here: 88.1 us
  starting transfers between devices  33.3 us (38%)
  waiting for transfers between devices  31.6 us (36%)
  Pallas kernels  21 us (24%)
  between operations  1.05 us (1%)
    ppermute x13, starting transfers between devices, moved(): got = lax.ppermute(block, 'wide', shift(*step))  26.9 us
    ppermute x13, waiting for transfers between devices, moved(): got = lax.ppermute(block, 'wide', shift(*step))  20.9 us
    pallas_call x8, Pallas kernels, local_call(): pl.pallas_call(kernel, in_specs=specs, out_specs=jax.tree.map(lambda _: v...  12.1 us
    ppermute x2, waiting for transfers between devices, hop_sum(): return (rest, lax.ppermute(away, 'narrow', CHIP))  9.14 us
    pallas_call x1, Pallas kernels, tile_slots(): pl.pallas_call(slots_kernel, in_specs=[pl.BlockSpec(memory_space=pltpu.SM...  4.68 us
    pallas_call x1, Pallas kernels, coupled_parts(): pl.pallas_call(couple_kernel, grid=(4,), in_specs=[pl.BlockSpec((8, depth...  4.09 us
    ppermute x2, starting transfers between devices, hop_sum(): got = lax.ppermute(send, 'narrow', CORE)  3.94 us
    ppermute x2, starting transfers between devices, hop_sum(): return (rest, lax.ppermute(away, 'narrow', CHIP))  2.46 us
  transfers between devices with their start and end apart: 17, of which 11 were waited for; matrix products, arithmetic and copies ran while one was open for 1% of the time, Pallas kernels for 13%

profile of v10, /device:TPU:1, one launch (start us, length us, event | category | flops | bytes accessed | tf_op | source)
XLA Modules:
  0.0 88.1 jit_solution(1334465072129744536)
XLA Ops:
  0.6 0.0 copy-start.9
  0.7 4.7 %shard_map.122 = f32[16,1152]{1,0:T(8,128)S(1)} custom-call(s32[1]{0:T(128)} %bitcast.10.low_ref, s32[2,256]{1,0:T(2,128)} %pivots_hbm.1, f32[64,768]{1,0:T(8,128)} %a_ref.2, f32[1024,768]{1,0:T(8,128)} %lt_ref.3), custom_call_target="tpu_custom_call" | custom-call | tf_op jit(solution)/shard_map/pallas_call | solution.py:159
  5.4 7.8 %collective-permute-start = (f32[16,1152]{1,0:T(8,128)S(1)}, f32[16,1152]{1,0:T(8,128)S(1)}, u32[]{:S(2)}, u32[]{:S(2)}) collective-permute-start(f32[16,1152]{1,0:T(8,128)S(1)} %shard_map.122), channel_id=1, source_target_pairs={{0,32},{4,36},{8,40},{12,44},{16,48},{20,52},{24,56},{28,60},{32,0... | collective-permute-start | bytes 221192 | tf_op jit(solution)/shard_map/ppermute | solution.py:28
  13.4 0.2 convert_reduce_fusion
  13.7 0.1 select_reduce_fusion
  13.7 1.3 %collective-permute-done = f32[16,1152]{1,0:T(8,128)S(1)} collective-permute-done((f32[16,1152]{1,0:T(8,128)S(1)}, f32[16,1152]{1,0:T(8,128)S(1)}, u32[]{:S(2)}, u32[]{:S(2)}) %collective-permute-start) | collective-permute-done | bytes 73760 | tf_op jit(solution)/shard_map/ppermute | solution.py:28
  15.1 3.3 %collective-permute-start.1 = (f32[32,1152]{1,0:T(8,128)S(1)}, f32[32,1152]{1,0:T(8,128)S(1)}, u32[]{:S(2)}, u32[]{:S(2)}) collective-permute-start(f32[32,1152]{1,0:T(8,128)S(1)} %pad_maximum_fusion.1), channel_id=1, source_target_pairs={{0,136},{4,140},{8,144},{12,148},{16,152},{20,156},{24,160},{28,16... | collective-permute-start | bytes 442376 | tf_op jit(solution)/shard_map/ppermute | solution.py:28
  18.4 4.2 %collective-permute-start.2 = (f32[32,1152]{1,0:T(8,128)S(1)}, f32[32,1152]{1,0:T(8,128)S(1)}, u32[]{:S(2)}, u32[]{:S(2)}) collective-permute-start(f32[32,1152]{1,0:T(8,128)S(1)} %pad_maximum_fusion.1), channel_id=1, source_target_pairs={{0,184},{4,188},{8,128},{12,132},{16,136},{20,140},{24,144},{28,14... | collective-permute-start | bytes 442376 | tf_op jit(solution)/shard_map/ppermute | solution.py:28
  22.7 3.9 %collective-permute-done.1 = f32[32,1152]{1,0:T(8,128)S(1)} collective-permute-done((f32[32,1152]{1,0:T(8,128)S(1)}, f32[32,1152]{1,0:T(8,128)S(1)}, u32[]{:S(2)}, u32[]{:S(2)}) %collective-permute-start.1) | collective-permute-done | bytes 147488 | tf_op jit(solution)/shard_map/ppermute | solution.py:28
  26.6 5.3 %collective-permute-done.3 = f32[32,1152]{1,0:T(8,128)S(1)} collective-permute-done((f32[32,1152]{1,0:T(8,128)S(1)}, f32[32,1152]{1,0:T(8,128)S(1)}, u32[]{:S(2)}, u32[]{:S(2)}) %collective-permute-start.3) | collective-permute-done | bytes 147488 | tf_op jit(solution)/shard_map/ppermute | solution.py:28
  32.0 3.4 %collective-permute-start.6 = (f32[128,1152]{1,0:T(8,128)S(1)}, f32[128,1152]{1,0:T(8,128)S(1)}, u32[]{:S(2)}, u32[]{:S(2)}) collective-permute-start(f32[128,1152]{1,0:T(8,128)S(1)} %constant_dynamic-update-slice_fusion.refs_0_.after_ref), channel_id=1, source_target_pairs={{0,4},{4,0},{8,12},{12,8},{16,20},{20,16},{24,28},{28,24},{32,36},... | collective-permute-start | bytes 1769480 | tf_op jit(solution)/shard_map/ppermute | solution.py:28
  35.4 2.7 %collective-permute-start.5 = (f32[128,1152]{1,0:T(8,128)S(1)}, f32[128,1152]{1,0:T(8,128)}, u32[]{:S(2)}, u32[]{:S(2)}) collective-permute-start(f32[128,1152]{1,0:T(8,128)S(1)} %constant_dynamic-update-slice_fusion.refs_0_.after_ref), channel_id=1, source_target_pairs={{0,192},{4,196},{8,200},{12,204},{16,208},{20,212},{24,216},{28,22... | collective-permute-start | bytes 1769480 | tf_op jit(solution)/shard_map/ppermute | solution.py:28
  38.1 0.1 collective-permute-start.7
  38.3 2.6 %collective-permute-start.8 = (f32[64,1152]{1,0:T(8,128)S(1)}, f32[64,1152]{1,0:T(8,128)S(1)}, u32[]{:S(2)}, u32[]{:S(2)}) collective-permute-start(f32[64,1152]{1,0:T(8,128)S(1)} %pad_maximum_fusion), channel_id=1, source_target_pairs={{0,56},{4,60},{8,0},{12,4},{16,8},{20,12},{24,16},{28,20},{32,24},... | collective-permute-start | bytes 884744 | tf_op jit(solution)/shard_map/ppermute | solution.py:28
  40.9 0.1 pad_maximum_fusion.2
  41.0 5.9 %collective-permute-done.6.refs_3_.refs_0_ = f32[128,1152]{1,0:T(8,128)S(1)} collective-permute-done((f32[128,1152]{1,0:T(8,128)S(1)}, f32[128,1152]{1,0:T(8,128)S(1)}, u32[]{:S(2)}, u32[]{:S(2)}) %collective-permute-start.6) | collective-permute-done | bytes 589856 | tf_op jit(solution)/shard_map/ppermute | solution.py:28
  46.8 1.5 %collective-permute-start.9 = (f32[128,1152]{1,0:T(8,128)S(1)}, f32[128,1152]{1,0:T(8,128)S(1)}, u32[]{:S(2)}, u32[]{:S(2)}) collective-permute-start(f32[128,1152]{1,0:T(8,128)S(1)} %collective-permute-done.6.refs_3_.refs_0_), channel_id=1, source_target_pairs={{0,64},{4,68},{8,72},{12,76},{16,80},{20,84},{24,88},{28,92},{32,9... | collective-permute-start | bytes 1769480 | tf_op jit(solution)/shard_map/ppermute | solution.py:28
  48.3 0.1 shard_map.125
  48.4 0.1 collective-permute-start.11
  48.5 1.6 %collective-permute-done.4.refs_1_ = f32[128,1152]{1,0:T(8,128)} collective-permute-done((f32[128,1152]{1,0:T(8,128)S(1)}, f32[128,1152]{1,0:T(8,128)}, u32[]{:S(2)}, u32[]{:S(2)}) %collective-permute-start.4) | collective-permute-done | bytes 589856 | tf_op jit(solution)/shard_map/ppermute | solution.py:28
  50.1 1.1 %collective-permute-start.12 = (f32[64,1152]{1,0:T(8,128)S(1)}, f32[64,1152]{1,0:T(8,128)S(1)}, u32[]{:S(2)}, u32[]{:S(2)}) collective-permute-start(f32[64,1152]{1,0:T(8,128)S(1)} %shard_map.125), channel_id=1, source_target_pairs={{0,56},{4,60},{8,0},{12,4},{16,8},{20,12},{24,16},{28,20},{32,24},... | collective-permute-start | bytes 884744 | tf_op jit(solution)/shard_map/ppermute | solution.py:28
  51.2 0.1 fusion.17
  51.3 0.1 concatenate.27
  51.3 0.1 copy.16.index_ref
  51.5 4.1 %shard_map.124 = (bf16[1024,768]{1,0:T(8,128)(2,1)S(1)}, bf16[1024,768]{1,0:T(8,128)(2,1)S(1)}) custom-call(f32[8,1024]{1,0:T(8,128)S(1)} %select_maximum_fusion.weight_ref, f32[1024,768]{1,0:T(8,128)} %lt_ref.3, f32[128,1152]{1,0:T(8,128)S(1)} %constant_dynamic-update-slice_fusion.refs_0_.after_ref), custom_call_target="tpu_custom_call" | custom-call | flops 6291456 | bytes 6291456 | tf_op jit(solution)/shard_map/pallas_call | solution.py:189
  55.6 3.8 %shard_map.123.carry_ref = f32[512,1152]{1,0:T(8,128)S(1)} custom-call(s32[512,1]{1,0:T(8,128)S(1)} %copy.16.index_ref, f32[128,1152]{1,0:T(8,128)S(1)} %constant_dynamic-update-slice_fusion.refs_0_.after_ref, f32[128,1152]{1,0:T(8,128)} %collective-permute-done.4.refs_1_, f32[128,1152]{1,0:T(8,128)} %collective-permute-done.5.refs_2_, ...), custom_call_target="tpu_custom_call" | custom-call | flops 1509949440 | bytes 2951168 | tf_op jit(solution)/shard_map/pallas_call | solution.py:276
  59.5 2.1 %collective-permute-done.10.refs_1_ = f32[128,1152]{1,0:T(8,128)S(1)} collective-permute-done((f32[128,1152]{1,0:T(8,128)S(1)}, f32[128,1152]{1,0:T(8,128)S(1)}, u32[]{:S(2)}, u32[]{:S(2)}) %collective-permute-start.10) | collective-permute-done | bytes 589856 | tf_op jit(solution)/shard_map/ppermute | solution.py:28
  61.6 0.8 collective-permute-done.9.refs_0_
  62.4 2.6 %shard_map.126 = (f32[128,1024]{1,0:T(8,128)S(1)}, f32[256,1024]{1,0:T(8,128)S(1)}, f32[256,128]{1,0:T(8,128)S(1)}, bf16[256,1024]{1,0:T(8,128)(2,1)S(1)}, bf16[...) custom-call(s32[512,1]{1,0:T(8,128)S(1)} %copy.16.index_ref, f32[8,1024]{1,0:T(8,128)S(1)} %select_maximum_fusion.weight_ref, ...), custom_call_target="tpu_custom_call" | custom-call | flops 1711276032 | bytes 10455040 | tf_op jit(solution)/shard_map/pallas_call | solution.py:276
  65.0 2.7 %collective-permute-start.13 = (f32[128,1024]{1,0:T(8,128)S(1)}, f32[128,1024]{1,0:T(8,128)S(1)}, u32[]{:S(2)}, u32[]{:S(2)}) collective-permute-start(f32[128,1024]{1,0:T(8,128)S(1)} %get-tuple-element.24), channel_id=1, source_target_pairs={{0,1},{1,0},{2,3},{3,2},{4,5},{5,4},{6,7},{7,6},{8,9},{9,8},{10,11... | collective-permute-start | bytes 1572872 | tf_op jit(solution)/shard_map/ppermute | solution.py:309
  67.7 0.1 fusion.13
  67.8 1.2 %shard_map.128.keep_ref = f32[128,1024]{1,0:T(8,128)S(1)} custom-call(f32[128,1024]{1,0:T(8,128)S(1)} %get-tuple-element.21.taken_ref, bf16[1024,768]{1,0:T(8,128)(2,1)S(1)} %get-tuple-element.17.lt_big_ref, bf16[1024,768]{1,0:T(8,128)(2,1)S(1)} %get-tuple-element.18.lt_small_ref, bf16[256,1024]{1,0:T(8,128)(2,1)S(1)} %get-tuple-element.22.big_ref, ...), custom_call_target="tpu_custom_call" | custom-call | flops 805306368 | bytes 8912896 | tf_op jit(solution)/shard_map/pallas_call | solution.py:276
  69.1 0.2 collective-permute-done.13.got_ref
  69.3 0.1 shard_map.129
  69.3 1.2 %collective-permute-start.14 = (f32[64,1024]{1,0:T(8,128)S(1)}, f32[64,1024]{1,0:T(8,128)S(1)}, u32[]{:S(2)}, u32[]{:S(2)}) collective-permute-start(f32[64,1024]{1,0:T(8,128)S(1)} %get-tuple-element.26), channel_id=1, source_target_pairs={{0,2},{1,3},{2,0},{3,1},{4,6},{5,7},{6,4},{7,5},{8,10},{9,11},{10,... | collective-permute-start | bytes 786440 | tf_op jit(solution)/shard_map/ppermute | solution.py:312
  70.6 0.1 pad_add_fusion.quarter_ref
  70.6 0.0 copy-start
  70.7 2.0 %shard_map.127.update_ref = f32[256,768]{1,0:T(8,128)S(1)} custom-call(s32[4]{0:T(128)S(1)} %pad_add_fusion.quarter_ref, f32[256,1024]{1,0:T(8,128)S(1)} %get-tuple-element.20.second_ref, bf16[1024,768]{1,0:T(8,128)(2,1)S(1)} %get-tuple-element.17.lt_big_ref, bf16[1024,768]{1,0:T(8,128)(2,1)S(1)} %get-tuple-element.18.lt_small_ref), custom_call_target="tpu_custom_call" | custom-call | flops 1207959552 | bytes 7340048 | tf_op jit(solution)/shard_map/pallas_call | solution.py:276
  72.7 0.0 copy-start.1
  72.7 4.3 %collective-permute-done.14.away_ref = f32[64,1024]{1,0:T(8,128)S(1)} collective-permute-done((f32[64,1024]{1,0:T(8,128)S(1)}, f32[64,1024]{1,0:T(8,128)S(1)}, u32[]{:S(2)}, u32[]{:S(2)}) %collective-permute-start.14) | collective-permute-done | bytes 262176 | tf_op jit(solution)/shard_map/ppermute | solution.py:312
  76.9 1.5 %shard_map.130 = (f32[64,768]{1,0:T(8,128)}, f32[128,768]{1,0:T(8,128)S(1)}, f32[128,768]{1,0:T(8,128)S(1)}) custom-call(s32[4]{0:T(128)S(1)} %pad_add_fusion.quarter_ref, f32[8,128]{1,0:T(8,128)S(1)} %select_maximum_fusion.4.weight_ref, f32[64,768]{1,0:T(8,128)S(1)} %copy-done, f32[256,128]{1,0:T(8,128)S(1)} %get-tuple-element.19.entries_ref, ...), custom_call_target="tpu_custom_call" | custom-call | flops 75497472 | bytes 1642512 | tf_op jit(solution)/shard_map/pallas_call | solution.py:276
  78.4 1.2 %collective-permute-start.15 = (f32[128,768]{1,0:T(8,128)S(1)}, f32[128,768]{1,0:T(8,128)S(1)}, u32[]{:S(2)}, u32[]{:S(2)}) collective-permute-start(f32[128,768]{1,0:T(8,128)S(1)} %get-tuple-element.29), channel_id=1, source_target_pairs={{0,1},{1,0},{2,3},{3,2},{4,5},{5,4},{6,7},{7,6},{8,9},{9,8},{10,11... | collective-permute-start | bytes 1179656 | tf_op jit(solution)/shard_map/ppermute | solution.py:309
  79.6 1.3 %collective-permute-done.15.got_ref = f32[128,768]{1,0:T(8,128)S(1)} collective-permute-done((f32[128,768]{1,0:T(8,128)S(1)}, f32[128,768]{1,0:T(8,128)S(1)}, u32[]{:S(2)}, u32[]{:S(2)}) %collective-permute-start.15) | collective-permute-done | bytes 393248 | tf_op jit(solution)/shard_map/ppermute | solution.py:309
  80.9 0.1 shard_map.131
  81.0 1.2 %collective-permute-start.16 = (f32[64,768]{1,0:T(8,128)S(1)}, f32[64,768]{1,0:T(8,128)S(1)}, u32[]{:S(2)}, u32[]{:S(2)}) collective-permute-start(f32[64,768]{1,0:T(8,128)S(1)} %get-tuple-element.31), channel_id=1, source_target_pairs={{0,2},{1,3},{2,0},{3,1},{4,6},{5,7},{6,4},{7,5},{8,10},{9,11},{10,... | collective-permute-start | bytes 589832 | tf_op jit(solution)/shard_map/ppermute | solution.py:312
  82.2 0.1 fusion.14
  82.3 4.9 %collective-permute-done.16.away_ref = f32[64,768]{1,0:T(8,128)S(1)} collective-permute-done((f32[64,768]{1,0:T(8,128)S(1)}, f32[64,768]{1,0:T(8,128)S(1)}, u32[]{:S(2)}, u32[]{:S(2)}) %collective-permute-start.16) | collective-permute-done | bytes 196640 | tf_op jit(solution)/shard_map/ppermute | solution.py:312
  87.2 0.9 shard_map.132
  (51 shorter events, 0.3 us)
Async XLA Ops:
  0.6 13.0 %copy-start.9 = (s32[64]{0:T(128)S(1)}, s32[64]{0:T(128)}, u32[]{:S(2)}) copy-start(s32[64]{0:T(128)} %constant.136.clone) | copy-start | bytes 772
  0.6 12.6 %copy-start.2 = (s32[2,256]{1,0:T(2,128)S(1)}, s32[2,256]{1,0:T(2,128)}, u32[]{:S(2)}) copy-start(s32[2,256]{1,0:T(2,128)} %pivots_hbm.1) | copy-start | bytes 6148
  0.7 13.0 %copy-start.3 = (f32[1024]{0:T(1024)S(1)}, f32[1024]{0:T(1024)}, u32[]{:S(2)}) copy-start(f32[1024]{0:T(1024)} %param.13) | copy-start | bytes 12292
  0.7 13.0 %copy-start.4 = (s32[1024]{0:T(1024)S(1)}, s32[1024]{0:T(1024)}, u32[]{:S(2)}) copy-start(s32[1024]{0:T(1024)} %param.14) | copy-start | bytes 12292
  0.7 47.6 %copy-start.6 = (s32[2,64]{1,0:T(2,128)S(1)}, s32[2,64]{1,0:T(2,128)}, u32[]{:S(2)}) copy-start(s32[2,64]{1,0:T(2,128)} %param.20) | copy-start | bytes 1540
  0.7 47.6 %copy-start.7 = (f32[2,64]{1,0:T(2,128)S(1)}, f32[2,64]{1,0:T(2,128)}, u32[]{:S(2)}) copy-start(f32[2,64]{1,0:T(2,128)} %param.19) | copy-start | bytes 1540
  5.4 46.1 %copy-start.5 = (f32[1024]{0:T(1024)S(1)}, f32[1024]{0:T(1024)}, u32[]{:S(2)}) copy-start(f32[1024]{0:T(1024)} %param.12) | copy-start | bytes 12292
  5.4 9.7 %collective-permute-start = (f32[16,1152]{1,0:T(8,128)S(1)}, f32[16,1152]{1,0:T(8,128)S(1)}, u32[]{:S(2)}, u32[]{:S(2)}) collective-permute-start(f32[16,1152]{1,0:T(8,128)S(1)} %shard_map.122), channel_id=1, source_target_pairs={{0,32},{4,36},{8,40},{12,44},{16,48},{20,52},{24,56},{28,60},{32,0... | collective-permute-start | bytes 221192 | tf_op jit(solution)/shard_map/ppermute | solution.py:28
  15.1 11.5 %collective-permute-start.1 = (f32[32,1152]{1,0:T(8,128)S(1)}, f32[32,1152]{1,0:T(8,128)S(1)}, u32[]{:S(2)}, u32[]{:S(2)}) collective-permute-start(f32[32,1152]{1,0:T(8,128)S(1)} %pad_maximum_fusion.1), channel_id=1, source_target_pairs={{0,136},{4,140},{8,144},{12,148},{16,152},{20,156},{24,160},{28,16... | collective-permute-start | bytes 442376 | tf_op jit(solution)/shard_map/ppermute | solution.py:28
  18.4 8.2 %collective-permute-start.2 = (f32[32,1152]{1,0:T(8,128)S(1)}, f32[32,1152]{1,0:T(8,128)S(1)}, u32[]{:S(2)}, u32[]{:S(2)}) collective-permute-start(f32[32,1152]{1,0:T(8,128)S(1)} %pad_maximum_fusion.1), channel_id=1, source_target_pairs={{0,184},{4,188},{8,128},{12,132},{16,136},{20,140},{24,144},{28,14... | collective-permute-start | bytes 442376 | tf_op jit(solution)/shard_map/ppermute | solution.py:28
  22.7 9.3 %collective-permute-start.3 = (f32[32,1152]{1,0:T(8,128)S(1)}, f32[32,1152]{1,0:T(8,128)S(1)}, u32[]{:S(2)}, u32[]{:S(2)}) collective-permute-start(f32[32,1152]{1,0:T(8,128)S(1)} %pad_maximum_fusion.1), channel_id=1, source_target_pairs={{0,16},{4,20},{8,24},{12,28},{16,32},{20,36},{24,40},{28,44},{32,4... | collective-permute-start | bytes 442376 | tf_op jit(solution)/shard_map/ppermute | solution.py:28
  32.0 14.9 %collective-permute-start.6 = (f32[128,1152]{1,0:T(8,128)S(1)}, f32[128,1152]{1,0:T(8,128)S(1)}, u32[]{:S(2)}, u32[]{:S(2)}) collective-permute-start(f32[128,1152]{1,0:T(8,128)S(1)} %constant_dynamic-update-slice_fusion.refs_0_.after_ref), channel_id=1, source_target_pairs={{0,4},{4,0},{8,12},{12,8},{16,20},{20,16},{24,28},{28,24},{32,36},... | collective-permute-start | bytes 1769480 | tf_op jit(solution)/shard_map/ppermute | solution.py:28
  35.4 14.7 %collective-permute-start.4 = (f32[128,1152]{1,0:T(8,128)S(1)}, f32[128,1152]{1,0:T(8,128)}, u32[]{:S(2)}, u32[]{:S(2)}) collective-permute-start(f32[128,1152]{1,0:T(8,128)S(1)} %constant_dynamic-update-slice_fusion.refs_0_.after_ref), channel_id=1, source_target_pairs={{0,64},{4,68},{8,72},{12,76},{16,80},{20,84},{24,88},{28,92},{32,9... | collective-permute-start | bytes 1769480 | tf_op jit(solution)/shard_map/ppermute | solution.py:28
  35.4 20.2 %collective-permute-start.5 = (f32[128,1152]{1,0:T(8,128)S(1)}, f32[128,1152]{1,0:T(8,128)}, u32[]{:S(2)}, u32[]{:S(2)}) collective-permute-start(f32[128,1152]{1,0:T(8,128)S(1)} %constant_dynamic-update-slice_fusion.refs_0_.after_ref), channel_id=1, source_target_pairs={{0,192},{4,196},{8,200},{12,204},{16,208},{20,212},{24,216},{28,22... | collective-permute-start | bytes 1769480 | tf_op jit(solution)/shard_map/ppermute | solution.py:28
  38.1 8.7 %collective-permute-start.7 = (f32[64,1152]{1,0:T(8,128)S(1)}, f32[64,1152]{1,0:T(8,128)S(1)}, u32[]{:S(2)}, u32[]{:S(2)}) collective-permute-start(f32[64,1152]{1,0:T(8,128)S(1)} %pad_maximum_fusion), channel_id=1, source_target_pairs={{0,8},{4,12},{8,16},{12,20},{16,24},{20,28},{24,32},{28,36},{32,40... | collective-permute-start | bytes 884744 | tf_op jit(solution)/shard_map/ppermute | solution.py:28
  38.3 10.1 %collective-permute-start.8 = (f32[64,1152]{1,0:T(8,128)S(1)}, f32[64,1152]{1,0:T(8,128)S(1)}, u32[]{:S(2)}, u32[]{:S(2)}) collective-permute-start(f32[64,1152]{1,0:T(8,128)S(1)} %pad_maximum_fusion), channel_id=1, source_target_pairs={{0,56},{4,60},{8,0},{12,4},{16,8},{20,12},{24,16},{28,20},{32,24},... | collective-permute-start | bytes 884744 | tf_op jit(solution)/shard_map/ppermute | solution.py:28
  46.8 14.8 %collective-permute-start.10 = (f32[128,1152]{1,0:T(8,128)S(1)}, f32[128,1152]{1,0:T(8,128)S(1)}, u32[]{:S(2)}, u32[]{:S(2)}) collective-permute-start(f32[128,1152]{1,0:T(8,128)S(1)} %collective-permute-done.6.refs_3_.refs_0_), channel_id=1, source_target_pairs={{0,192},{4,196},{8,200},{12,204},{16,208},{20,212},{24,216},{28,22... | collective-permute-start | bytes 1769480 | tf_op jit(solution)/shard_map/ppermute | solution.py:28
  46.8 1.7 %copy-start.10 = (f32[64,1152]{1,0:T(8,128)}, f32[64,1152]{1,0:T(8,128)S(1)}, u32[]{:S(2)}) copy-start(f32[64,1152]{1,0:T(8,128)S(1)} %collective-permute-done.7.refs_4_) | copy-start | bytes 884740
  46.8 15.5 %collective-permute-start.9 = (f32[128,1152]{1,0:T(8,128)S(1)}, f32[128,1152]{1,0:T(8,128)S(1)}, u32[]{:S(2)}, u32[]{:S(2)}) collective-permute-start(f32[128,1152]{1,0:T(8,128)S(1)} %collective-permute-done.6.refs_3_.refs_0_), channel_id=1, source_target_pairs={{0,64},{4,68},{8,72},{12,76},{16,80},{20,84},{24,88},{28,92},{32,9... | collective-permute-start | bytes 1769480 | tf_op jit(solution)/shard_map/ppermute | solution.py:28
  48.4 2.9 %copy-start.11 = (f32[64,1152]{1,0:T(8,128)}, f32[64,1152]{1,0:T(8,128)S(1)}, u32[]{:S(2)}) copy-start(f32[64,1152]{1,0:T(8,128)S(1)} %collective-permute-done.8.refs_5_) | copy-start | bytes 884740
  48.4 11.1 %collective-permute-start.11 = (f32[64,1152]{1,0:T(8,128)S(1)}, f32[64,1152]{1,0:T(8,128)S(1)}, u32[]{:S(2)}, u32[]{:S(2)}) collective-permute-start(f32[64,1152]{1,0:T(8,128)S(1)} %shard_map.125), channel_id=1, source_target_pairs={{0,8},{4,12},{8,16},{12,20},{16,24},{20,28},{24,32},{28,36},{32,40... | collective-permute-start | bytes 884744 | tf_op jit(solution)/shard_map/ppermute | solution.py:28
  50.1 9.4 %collective-permute-start.12 = (f32[64,1152]{1,0:T(8,128)S(1)}, f32[64,1152]{1,0:T(8,128)S(1)}, u32[]{:S(2)}, u32[]{:S(2)}) collective-permute-start(f32[64,1152]{1,0:T(8,128)S(1)} %shard_map.125), channel_id=1, source_target_pairs={{0,56},{4,60},{8,0},{12,4},{16,8},{20,12},{24,16},{28,20},{32,24},... | collective-permute-start | bytes 884744 | tf_op jit(solution)/shard_map/ppermute | solution.py:28
  62.4 5.4 %copy-start.8 = (f32[2,64]{1,0:T(2,128)S(1)}, f32[2,64]{1,0:T(2,128)}, u32[]{:S(2)}) copy-start(f32[2,64]{1,0:T(2,128)} %param.18) | copy-start | bytes 1540
  65.0 4.3 %collective-permute-start.13 = (f32[128,1024]{1,0:T(8,128)S(1)}, f32[128,1024]{1,0:T(8,128)S(1)}, u32[]{:S(2)}, u32[]{:S(2)}) collective-permute-start(f32[128,1024]{1,0:T(8,128)S(1)} %get-tuple-element.24), channel_id=1, source_target_pairs={{0,1},{1,0},{2,3},{3,2},{4,5},{5,4},{6,7},{7,6},{8,9},{9,8},{10,11... | collective-permute-start | bytes 1572872 | tf_op jit(solution)/shard_map/ppermute | solution.py:309
  69.3 7.6 %collective-permute-start.14 = (f32[64,1024]{1,0:T(8,128)S(1)}, f32[64,1024]{1,0:T(8,128)S(1)}, u32[]{:S(2)}, u32[]{:S(2)}) collective-permute-start(f32[64,1024]{1,0:T(8,128)S(1)} %get-tuple-element.26), channel_id=1, source_target_pairs={{0,2},{1,3},{2,0},{3,1},{4,6},{5,7},{6,4},{7,5},{8,10},{9,11},{10,... | collective-permute-start | bytes 786440 | tf_op jit(solution)/shard_map/ppermute | solution.py:312
  70.6 6.3 %copy-start = (f32[64,768]{1,0:T(8,128)S(1)}, f32[64,768]{1,0:T(8,128)}, u32[]{:S(2)}) copy-start(f32[64,768]{1,0:T(8,128)} %a_ref.2) | copy-start | bytes 589828
  72.7 14.5 %copy-start.1 = (f32[64,768]{1,0:T(8,128)S(1)}, f32[64,768]{1,0:T(8,128)}, u32[]{:S(2)}) copy-start(f32[64,768]{1,0:T(8,128)} %a_ref.3) | copy-start | bytes 589828
  78.4 2.6 %collective-permute-start.15 = (f32[128,768]{1,0:T(8,128)S(1)}, f32[128,768]{1,0:T(8,128)S(1)}, u32[]{:S(2)}, u32[]{:S(2)}) collective-permute-start(f32[128,768]{1,0:T(8,128)S(1)} %get-tuple-element.29), channel_id=1, source_target_pairs={{0,1},{1,0},{2,3},{3,2},{4,5},{5,4},{6,7},{7,6},{8,9},{9,8},{10,11... | collective-permute-start | bytes 1179656 | tf_op jit(solution)/shard_map/ppermute | solution.py:309
  81.0 6.2 %collective-permute-start.16 = (f32[64,768]{1,0:T(8,128)S(1)}, f32[64,768]{1,0:T(8,128)S(1)}, u32[]{:S(2)}, u32[]{:S(2)}) collective-permute-start(f32[64,768]{1,0:T(8,128)S(1)} %get-tuple-element.31), channel_id=1, source_target_pairs={{0,2},{1,3},{2,0},{3,1},{4,6},{5,7},{6,4},{7,5},{8,10},{9,11},{10,... | collective-permute-start | bytes 589832 | tf_op jit(solution)/shard_map/ppermute | solution.py:312

commit v11 on v10

--- a/solution.py
+++ b/solution.py
@@ -170,7 +170,7 @@
             pltpu.VMEM((k_local, width), jnp.float32),
             pltpu.VMEM(pivots.shape, jnp.int32),
             pltpu.VMEM((blocks, width), jnp.float32),
-            pltpu.SemaphoreType.DMA((4,)),
+            pltpu.SemaphoreType.DMA((8,)),
             pltpu.SemaphoreType.DMA((2,)),
         ],
         compiler_params=pltpu.CompilerParams(vmem_limit_bytes=20 * 2**20),
@@ -183,12 +183,12 @@
 
 def coupled_parts(weights, prior_lt, following):
     k_local, width = prior_lt.shape
-    depth = k_local // 4
+    depth = k_local // 8
     block = pl.BlockSpec((depth, width), lambda i: (i, 0))
     shape = jax.ShapeDtypeStruct((k_local, width), jnp.bfloat16)
     return pl.pallas_call(
         couple_kernel,
-        grid=(4,),
+        grid=(8,),
         in_specs=[
             pl.BlockSpec((8, depth), lambda i: (0, i)),
             block,

time: 88.2 us -> 89.2 us (1.011)
  Pallas kernels: 21 us -> 23.3 us
  waiting for transfers between devices: 31.6 us -> 29.6 us
    ppermute x13, waiting for transfers between devices: 20.9 us -> 19.4 us  [moved(): got = lax.ppermute(block, 'wide', shift(*step))]
    pallas_call x1, Pallas kernels: 4.09 us -> 5.54 us  [coupled_parts(): pl.pallas_call(couple_kernel, grid=(8,), in_specs=[pl.BlockSpec((8, depth...]
  transfers between devices with their start and end apart: 17 -> 17, of which waited for: 11 -> 11; matrix products, arithmetic and copies ran while one was open for 1% -> 1% of each run, Pallas kernels for 13% -> 14%
where the time goes in v11:
time: 89.2 us; the launch traced here: 89 us
  starting transfers between devices  33.8 us (38%)
  waiting for transfers between devices  29.6 us (33%)
  Pallas kernels  23.3 us (26%)
  between operations  1.05 us (1%)
    ppermute x13, starting transfers between devices, moved(): got = lax.ppermute(block, 'wide', shift(*step))  26.9 us
    ppermute x13, waiting for transfers between devices, moved(): got = lax.ppermute(block, 'wide', shift(*step))  19.4 us
    pallas_call x8, Pallas kernels, local_call(): pl.pallas_call(kernel, in_specs=specs, out_specs=jax.tree.map(lambda _: v...  12.1 us
    ppermute x2, waiting for transfers between devices, hop_sum(): return (rest, lax.ppermute(away, 'narrow', CHIP))  8.66 us
    pallas_call x1, Pallas kernels, tile_slots(): pl.pallas_call(slots_kernel, in_specs=[pl.BlockSpec(memory_space=pltpu.SM...  5.55 us
    pallas_call x1, Pallas kernels, coupled_parts(): pl.pallas_call(couple_kernel, grid=(8,), in_specs=[pl.BlockSpec((8, depth...  5.54 us
    ppermute x2, starting transfers between devices, hop_sum(): got = lax.ppermute(send, 'narrow', CORE)  3.94 us
    ppermute x2, starting transfers between devices, hop_sum(): return (rest, lax.ppermute(away, 'narrow', CHIP))  2.95 us
  transfers between devices with their start and end apart: 17, of which 11 were waited for; matrix products, arithmetic and copies ran while one was open for 1% of the time, Pallas kernels for 14%

profile of v11, /device:TPU:1, one launch (start us, length us, event | category | flops | bytes accessed | tf_op | source)
XLA Modules:
  0.0 89.0 jit_solution(13756945071519782444)
XLA Ops:
  0.6 0.0 copy-start.9
  0.7 5.6 %shard_map.122 = f32[16,1152]{1,0:T(8,128)S(1)} custom-call(s32[1]{0:T(128)} %bitcast.10.low_ref, s32[2,256]{1,0:T(2,128)} %pivots_hbm.1, f32[64,768]{1,0:T(8,128)} %a_ref.2, f32[1024,768]{1,0:T(8,128)} %lt_ref.3), custom_call_target="tpu_custom_call" | custom-call | tf_op jit(solution)/shard_map/pallas_call | solution.py:159
  6.3 0.0 copy-start.5
  6.3 7.8 %collective-permute-start = (f32[16,1152]{1,0:T(8,128)S(1)}, f32[16,1152]{1,0:T(8,128)S(1)}, u32[]{:S(2)}, u32[]{:S(2)}) collective-permute-start(f32[16,1152]{1,0:T(8,128)S(1)} %shard_map.122), channel_id=1, source_target_pairs={{0,32},{4,36},{8,40},{12,44},{16,48},{20,52},{24,56},{28,60},{32,0... | collective-permute-start | bytes 221192 | tf_op jit(solution)/shard_map/ppermute | solution.py:28
  14.2 0.2 convert_reduce_fusion
  14.5 0.1 select_reduce_fusion
  14.6 1.3 %collective-permute-done = f32[16,1152]{1,0:T(8,128)S(1)} collective-permute-done((f32[16,1152]{1,0:T(8,128)S(1)}, f32[16,1152]{1,0:T(8,128)S(1)}, u32[]{:S(2)}, u32[]{:S(2)}) %collective-permute-start) | collective-permute-done | bytes 73760 | tf_op jit(solution)/shard_map/ppermute | solution.py:28
  16.0 3.3 %collective-permute-start.1 = (f32[32,1152]{1,0:T(8,128)S(1)}, f32[32,1152]{1,0:T(8,128)S(1)}, u32[]{:S(2)}, u32[]{:S(2)}) collective-permute-start(f32[32,1152]{1,0:T(8,128)S(1)} %pad_maximum_fusion.1), channel_id=1, source_target_pairs={{0,136},{4,140},{8,144},{12,148},{16,152},{20,156},{24,160},{28,16... | collective-permute-start | bytes 442376 | tf_op jit(solution)/shard_map/ppermute | solution.py:28
  19.3 4.2 %collective-permute-start.2 = (f32[32,1152]{1,0:T(8,128)S(1)}, f32[32,1152]{1,0:T(8,128)S(1)}, u32[]{:S(2)}, u32[]{:S(2)}) collective-permute-start(f32[32,1152]{1,0:T(8,128)S(1)} %pad_maximum_fusion.1), channel_id=1, source_target_pairs={{0,184},{4,188},{8,128},{12,132},{16,136},{20,140},{24,144},{28,14... | collective-permute-start | bytes 442376 | tf_op jit(solution)/shard_map/ppermute | solution.py:28
  23.6 3.9 %collective-permute-done.1 = f32[32,1152]{1,0:T(8,128)S(1)} collective-permute-done((f32[32,1152]{1,0:T(8,128)S(1)}, f32[32,1152]{1,0:T(8,128)S(1)}, u32[]{:S(2)}, u32[]{:S(2)}) %collective-permute-start.1) | collective-permute-done | bytes 147488 | tf_op jit(solution)/shard_map/ppermute | solution.py:28
  27.5 5.3 %collective-permute-done.3 = f32[32,1152]{1,0:T(8,128)S(1)} collective-permute-done((f32[32,1152]{1,0:T(8,128)S(1)}, f32[32,1152]{1,0:T(8,128)S(1)}, u32[]{:S(2)}, u32[]{:S(2)}) %collective-permute-start.3) | collective-permute-done | bytes 147488 | tf_op jit(solution)/shard_map/ppermute | solution.py:28
  32.8 3.4 %collective-permute-start.6 = (f32[128,1152]{1,0:T(8,128)S(1)}, f32[128,1152]{1,0:T(8,128)S(1)}, u32[]{:S(2)}, u32[]{:S(2)}) collective-permute-start(f32[128,1152]{1,0:T(8,128)S(1)} %constant_dynamic-update-slice_fusion.refs_0_.after_ref), channel_id=1, source_target_pairs={{0,4},{4,0},{8,12},{12,8},{16,20},{20,16},{24,28},{28,24},{32,36},... | collective-permute-start | bytes 1769480 | tf_op jit(solution)/shard_map/ppermute | solution.py:28
  36.3 2.7 %collective-permute-start.5 = (f32[128,1152]{1,0:T(8,128)S(1)}, f32[128,1152]{1,0:T(8,128)}, u32[]{:S(2)}, u32[]{:S(2)}) collective-permute-start(f32[128,1152]{1,0:T(8,128)S(1)} %constant_dynamic-update-slice_fusion.refs_0_.after_ref), channel_id=1, source_target_pairs={{0,192},{4,196},{8,200},{12,204},{16,208},{20,212},{24,216},{28,22... | collective-permute-start | bytes 1769480 | tf_op jit(solution)/shard_map/ppermute | solution.py:28
  39.0 0.1 collective-permute-start.7
  39.1 2.6 %collective-permute-start.8 = (f32[64,1152]{1,0:T(8,128)S(1)}, f32[64,1152]{1,0:T(8,128)S(1)}, u32[]{:S(2)}, u32[]{:S(2)}) collective-permute-start(f32[64,1152]{1,0:T(8,128)S(1)} %pad_maximum_fusion), channel_id=1, source_target_pairs={{0,56},{4,60},{8,0},{12,4},{16,8},{20,12},{24,16},{28,20},{32,24},... | collective-permute-start | bytes 884744 | tf_op jit(solution)/shard_map/ppermute | solution.py:28
  41.8 0.1 pad_maximum_fusion.2
  41.8 5.9 %collective-permute-done.6.refs_3_.refs_0_ = f32[128,1152]{1,0:T(8,128)S(1)} collective-permute-done((f32[128,1152]{1,0:T(8,128)S(1)}, f32[128,1152]{1,0:T(8,128)S(1)}, u32[]{:S(2)}, u32[]{:S(2)}) %collective-permute-start.6) | collective-permute-done | bytes 589856 | tf_op jit(solution)/shard_map/ppermute | solution.py:28
  47.7 1.5 %collective-permute-start.9 = (f32[128,1152]{1,0:T(8,128)S(1)}, f32[128,1152]{1,0:T(8,128)S(1)}, u32[]{:S(2)}, u32[]{:S(2)}) collective-permute-start(f32[128,1152]{1,0:T(8,128)S(1)} %collective-permute-done.6.refs_3_.refs_0_), channel_id=1, source_target_pairs={{0,64},{4,68},{8,72},{12,76},{16,80},{20,84},{24,88},{28,92},{32,9... | collective-permute-start | bytes 1769480 | tf_op jit(solution)/shard_map/ppermute | solution.py:28
  49.2 0.1 shard_map.125
  49.3 0.1 collective-permute-start.11
  49.4 1.6 %collective-permute-done.4.refs_1_ = f32[128,1152]{1,0:T(8,128)} collective-permute-done((f32[128,1152]{1,0:T(8,128)S(1)}, f32[128,1152]{1,0:T(8,128)}, u32[]{:S(2)}, u32[]{:S(2)}) %collective-permute-start.4) | collective-permute-done | bytes 589856 | tf_op jit(solution)/shard_map/ppermute | solution.py:28
  50.9 1.1 %collective-permute-start.12 = (f32[64,1152]{1,0:T(8,128)S(1)}, f32[64,1152]{1,0:T(8,128)S(1)}, u32[]{:S(2)}, u32[]{:S(2)}) collective-permute-start(f32[64,1152]{1,0:T(8,128)S(1)} %shard_map.125), channel_id=1, source_target_pairs={{0,56},{4,60},{8,0},{12,4},{16,8},{20,12},{24,16},{28,20},{32,24},... | collective-permute-start | bytes 884744 | tf_op jit(solution)/shard_map/ppermute | solution.py:28
  52.1 0.1 fusion.17
  52.1 0.1 concatenate.27
  52.2 0.1 copy.16.index_ref
  52.4 5.5 %shard_map.124 = (bf16[1024,768]{1,0:T(8,128)(2,1)S(1)}, bf16[1024,768]{1,0:T(8,128)(2,1)S(1)}) custom-call(f32[8,1024]{1,0:T(8,128)S(1)} %select_maximum_fusion.weight_ref, f32[1024,768]{1,0:T(8,128)} %lt_ref.3, f32[128,1152]{1,0:T(8,128)S(1)} %constant_dynamic-update-slice_fusion.refs_0_.after_ref), custom_call_target="tpu_custom_call" | custom-call | flops 6291456 | bytes 6291456 | tf_op jit(solution)/shard_map/pallas_call | solution.py:189
  58.0 3.8 %shard_map.123.carry_ref = f32[512,1152]{1,0:T(8,128)S(1)} custom-call(s32[512,1]{1,0:T(8,128)S(1)} %copy.16.index_ref, f32[128,1152]{1,0:T(8,128)S(1)} %constant_dynamic-update-slice_fusion.refs_0_.after_ref, f32[128,1152]{1,0:T(8,128)} %collective-permute-done.4.refs_1_, f32[128,1152]{1,0:T(8,128)} %collective-permute-done.5.refs_2_, ...), custom_call_target="tpu_custom_call" | custom-call | flops 1509949440 | bytes 2951168 | tf_op jit(solution)/shard_map/pallas_call | solution.py:276
  61.8 0.6 collective-permute-done.10.refs_1_
  62.5 0.8 collective-permute-done.9.refs_0_
  63.2 2.6 %shard_map.126 = (f32[128,1024]{1,0:T(8,128)S(1)}, f32[256,1024]{1,0:T(8,128)S(1)}, f32[256,128]{1,0:T(8,128)S(1)}, bf16[256,1024]{1,0:T(8,128)(2,1)S(1)}, bf16[...) custom-call(s32[512,1]{1,0:T(8,128)S(1)} %copy.16.index_ref, f32[8,1024]{1,0:T(8,128)S(1)} %select_maximum_fusion.weight_ref, ...), custom_call_target="tpu_custom_call" | custom-call | flops 1711276032 | bytes 10455040 | tf_op jit(solution)/shard_map/pallas_call | solution.py:276
  65.9 2.7 %collective-permute-start.13 = (f32[128,1024]{1,0:T(8,128)S(1)}, f32[128,1024]{1,0:T(8,128)S(1)}, u32[]{:S(2)}, u32[]{:S(2)}) collective-permute-start(f32[128,1024]{1,0:T(8,128)S(1)} %get-tuple-element.24), channel_id=1, source_target_pairs={{0,1},{1,0},{2,3},{3,2},{4,5},{5,4},{6,7},{7,6},{8,9},{9,8},{10,11... | collective-permute-start | bytes 1572872 | tf_op jit(solution)/shard_map/ppermute | solution.py:309
  68.6 0.1 fusion.13
  68.7 1.2 %shard_map.128.keep_ref = f32[128,1024]{1,0:T(8,128)S(1)} custom-call(f32[128,1024]{1,0:T(8,128)S(1)} %get-tuple-element.21.taken_ref, bf16[1024,768]{1,0:T(8,128)(2,1)S(1)} %get-tuple-element.17.lt_big_ref, bf16[1024,768]{1,0:T(8,128)(2,1)S(1)} %get-tuple-element.18.lt_small_ref, bf16[256,1024]{1,0:T(8,128)(2,1)S(1)} %get-tuple-element.22.big_ref, ...), custom_call_target="tpu_custom_call" | custom-call | flops 805306368 | bytes 8912896 | tf_op jit(solution)/shard_map/pallas_call | solution.py:276
  69.9 0.2 collective-permute-done.13.got_ref
  70.1 0.1 shard_map.129
  70.2 1.5 %collective-permute-start.14 = (f32[64,1024]{1,0:T(8,128)S(1)}, f32[64,1024]{1,0:T(8,128)S(1)}, u32[]{:S(2)}, u32[]{:S(2)}) collective-permute-start(f32[64,1024]{1,0:T(8,128)S(1)} %get-tuple-element.26), channel_id=1, source_target_pairs={{0,2},{1,3},{2,0},{3,1},{4,6},{5,7},{6,4},{7,5},{8,10},{9,11},{10,... | collective-permute-start | bytes 786440 | tf_op jit(solution)/shard_map/ppermute | solution.py:312
  71.7 0.1 pad_add_fusion.quarter_ref
  71.8 0.0 copy-start
  71.8 2.0 %shard_map.127.update_ref = f32[256,768]{1,0:T(8,128)S(1)} custom-call(s32[4]{0:T(128)S(1)} %pad_add_fusion.quarter_ref, f32[256,1024]{1,0:T(8,128)S(1)} %get-tuple-element.20.second_ref, bf16[1024,768]{1,0:T(8,128)(2,1)S(1)} %get-tuple-element.17.lt_big_ref, bf16[1024,768]{1,0:T(8,128)(2,1)S(1)} %get-tuple-element.18.lt_small_ref), custom_call_target="tpu_custom_call" | custom-call | flops 1207959552 | bytes 7340048 | tf_op jit(solution)/shard_map/pallas_call | solution.py:276
  73.8 4.0 %collective-permute-done.14.away_ref = f32[64,1024]{1,0:T(8,128)S(1)} collective-permute-done((f32[64,1024]{1,0:T(8,128)S(1)}, f32[64,1024]{1,0:T(8,128)S(1)}, u32[]{:S(2)}, u32[]{:S(2)}) %collective-permute-start.14) | collective-permute-done | bytes 262176 | tf_op jit(solution)/shard_map/ppermute | solution.py:312
  77.8 1.5 %shard_map.130 = (f32[64,768]{1,0:T(8,128)}, f32[128,768]{1,0:T(8,128)S(1)}, f32[128,768]{1,0:T(8,128)S(1)}) custom-call(s32[4]{0:T(128)S(1)} %pad_add_fusion.quarter_ref, f32[8,128]{1,0:T(8,128)S(1)} %select_maximum_fusion.4.weight_ref, f32[64,768]{1,0:T(8,128)S(1)} %copy-done, f32[256,128]{1,0:T(8,128)S(1)} %get-tuple-element.19.entries_ref, ...), custom_call_target="tpu_custom_call" | custom-call | flops 75497472 | bytes 1642512 | tf_op jit(solution)/shard_map/pallas_call | solution.py:276
  79.3 1.2 %collective-permute-start.15 = (f32[128,768]{1,0:T(8,128)S(1)}, f32[128,768]{1,0:T(8,128)S(1)}, u32[]{:S(2)}, u32[]{:S(2)}) collective-permute-start(f32[128,768]{1,0:T(8,128)S(1)} %get-tuple-element.29), channel_id=1, source_target_pairs={{0,1},{1,0},{2,3},{3,2},{4,5},{5,4},{6,7},{7,6},{8,9},{9,8},{10,11... | collective-permute-start | bytes 1179656 | tf_op jit(solution)/shard_map/ppermute | solution.py:309
  80.5 1.3 %collective-permute-done.15.got_ref = f32[128,768]{1,0:T(8,128)S(1)} collective-permute-done((f32[128,768]{1,0:T(8,128)S(1)}, f32[128,768]{1,0:T(8,128)S(1)}, u32[]{:S(2)}, u32[]{:S(2)}) %collective-permute-start.15) | collective-permute-done | bytes 393248 | tf_op jit(solution)/shard_map/ppermute | solution.py:309
  81.8 0.1 shard_map.131
  81.9 1.5 %collective-permute-start.16 = (f32[64,768]{1,0:T(8,128)S(1)}, f32[64,768]{1,0:T(8,128)S(1)}, u32[]{:S(2)}, u32[]{:S(2)}) collective-permute-start(f32[64,768]{1,0:T(8,128)S(1)} %get-tuple-element.31), channel_id=1, source_target_pairs={{0,2},{1,3},{2,0},{3,1},{4,6},{5,7},{6,4},{7,5},{8,10},{9,11},{10,... | collective-permute-start | bytes 589832 | tf_op jit(solution)/shard_map/ppermute | solution.py:312
  83.3 0.1 fusion.14
  83.4 4.6 %collective-permute-done.16.away_ref = f32[64,768]{1,0:T(8,128)S(1)} collective-permute-done((f32[64,768]{1,0:T(8,128)S(1)}, f32[64,768]{1,0:T(8,128)S(1)}, u32[]{:S(2)}, u32[]{:S(2)}) %collective-permute-start.16) | collective-permute-done | bytes 196640 | tf_op jit(solution)/shard_map/ppermute | solution.py:312
  88.1 0.9 shard_map.132
  (51 shorter events, 0.3 us)
Async XLA Ops:
  0.6 13.9 %copy-start.9 = (s32[64]{0:T(128)S(1)}, s32[64]{0:T(128)}, u32[]{:S(2)}) copy-start(s32[64]{0:T(128)} %constant.136.clone) | copy-start | bytes 772
  0.6 13.5 %copy-start.2 = (s32[2,256]{1,0:T(2,128)S(1)}, s32[2,256]{1,0:T(2,128)}, u32[]{:S(2)}) copy-start(s32[2,256]{1,0:T(2,128)} %pivots_hbm.1) | copy-start | bytes 6148
  0.7 13.8 %copy-start.3 = (f32[1024]{0:T(1024)S(1)}, f32[1024]{0:T(1024)}, u32[]{:S(2)}) copy-start(f32[1024]{0:T(1024)} %param.13) | copy-start | bytes 12292
  0.7 13.8 %copy-start.4 = (s32[1024]{0:T(1024)S(1)}, s32[1024]{0:T(1024)}, u32[]{:S(2)}) copy-start(s32[1024]{0:T(1024)} %param.14) | copy-start | bytes 12292
  0.7 48.5 %copy-start.6 = (s32[2,64]{1,0:T(2,128)S(1)}, s32[2,64]{1,0:T(2,128)}, u32[]{:S(2)}) copy-start(s32[2,64]{1,0:T(2,128)} %param.20) | copy-start | bytes 1540
  0.7 48.5 %copy-start.7 = (f32[2,64]{1,0:T(2,128)S(1)}, f32[2,64]{1,0:T(2,128)}, u32[]{:S(2)}) copy-start(f32[2,64]{1,0:T(2,128)} %param.19) | copy-start | bytes 1540
  6.3 46.1 %copy-start.5 = (f32[1024]{0:T(1024)S(1)}, f32[1024]{0:T(1024)}, u32[]{:S(2)}) copy-start(f32[1024]{0:T(1024)} %param.12) | copy-start | bytes 12292
  6.3 9.7 %collective-permute-start = (f32[16,1152]{1,0:T(8,128)S(1)}, f32[16,1152]{1,0:T(8,128)S(1)}, u32[]{:S(2)}, u32[]{:S(2)}) collective-permute-start(f32[16,1152]{1,0:T(8,128)S(1)} %shard_map.122), channel_id=1, source_target_pairs={{0,32},{4,36},{8,40},{12,44},{16,48},{20,52},{24,56},{28,60},{32,0... | collective-permute-start | bytes 221192 | tf_op jit(solution)/shard_map/ppermute | solution.py:28
  16.0 11.5 %collective-permute-start.1 = (f32[32,1152]{1,0:T(8,128)S(1)}, f32[32,1152]{1,0:T(8,128)S(1)}, u32[]{:S(2)}, u32[]{:S(2)}) collective-permute-start(f32[32,1152]{1,0:T(8,128)S(1)} %pad_maximum_fusion.1), channel_id=1, source_target_pairs={{0,136},{4,140},{8,144},{12,148},{16,152},{20,156},{24,160},{28,16... | collective-permute-start | bytes 442376 | tf_op jit(solution)/shard_map/ppermute | solution.py:28
  19.3 8.2 %collective-permute-start.2 = (f32[32,1152]{1,0:T(8,128)S(1)}, f32[32,1152]{1,0:T(8,128)S(1)}, u32[]{:S(2)}, u32[]{:S(2)}) collective-permute-start(f32[32,1152]{1,0:T(8,128)S(1)} %pad_maximum_fusion.1), channel_id=1, source_target_pairs={{0,184},{4,188},{8,128},{12,132},{16,136},{20,140},{24,144},{28,14... | collective-permute-start | bytes 442376 | tf_op jit(solution)/shard_map/ppermute | solution.py:28
  23.5 9.3 %collective-permute-start.3 = (f32[32,1152]{1,0:T(8,128)S(1)}, f32[32,1152]{1,0:T(8,128)S(1)}, u32[]{:S(2)}, u32[]{:S(2)}) collective-permute-start(f32[32,1152]{1,0:T(8,128)S(1)} %pad_maximum_fusion.1), channel_id=1, source_target_pairs={{0,16},{4,20},{8,24},{12,28},{16,32},{20,36},{24,40},{28,44},{32,4... | collective-permute-start | bytes 442376 | tf_op jit(solution)/shard_map/ppermute | solution.py:28
  32.8 14.9 %collective-permute-start.6 = (f32[128,1152]{1,0:T(8,128)S(1)}, f32[128,1152]{1,0:T(8,128)S(1)}, u32[]{:S(2)}, u32[]{:S(2)}) collective-permute-start(f32[128,1152]{1,0:T(8,128)S(1)} %constant_dynamic-update-slice_fusion.refs_0_.after_ref), channel_id=1, source_target_pairs={{0,4},{4,0},{8,12},{12,8},{16,20},{20,16},{24,28},{28,24},{32,36},... | collective-permute-start | bytes 1769480 | tf_op jit(solution)/shard_map/ppermute | solution.py:28
  36.3 14.7 %collective-permute-start.4 = (f32[128,1152]{1,0:T(8,128)S(1)}, f32[128,1152]{1,0:T(8,128)}, u32[]{:S(2)}, u32[]{:S(2)}) collective-permute-start(f32[128,1152]{1,0:T(8,128)S(1)} %constant_dynamic-update-slice_fusion.refs_0_.after_ref), channel_id=1, source_target_pairs={{0,64},{4,68},{8,72},{12,76},{16,80},{20,84},{24,88},{28,92},{32,9... | collective-permute-start | bytes 1769480 | tf_op jit(solution)/shard_map/ppermute | solution.py:28
  36.3 21.7 %collective-permute-start.5 = (f32[128,1152]{1,0:T(8,128)S(1)}, f32[128,1152]{1,0:T(8,128)}, u32[]{:S(2)}, u32[]{:S(2)}) collective-permute-start(f32[128,1152]{1,0:T(8,128)S(1)} %constant_dynamic-update-slice_fusion.refs_0_.after_ref), channel_id=1, source_target_pairs={{0,192},{4,196},{8,200},{12,204},{16,208},{20,212},{24,216},{28,22... | collective-permute-start | bytes 1769480 | tf_op jit(solution)/shard_map/ppermute | solution.py:28
  39.0 8.7 %collective-permute-start.7 = (f32[64,1152]{1,0:T(8,128)S(1)}, f32[64,1152]{1,0:T(8,128)S(1)}, u32[]{:S(2)}, u32[]{:S(2)}) collective-permute-start(f32[64,1152]{1,0:T(8,128)S(1)} %pad_maximum_fusion), channel_id=1, source_target_pairs={{0,8},{4,12},{8,16},{12,20},{16,24},{20,28},{24,32},{28,36},{32,40... | collective-permute-start | bytes 884744 | tf_op jit(solution)/shard_map/ppermute | solution.py:28
  39.1 10.1 %collective-permute-start.8 = (f32[64,1152]{1,0:T(8,128)S(1)}, f32[64,1152]{1,0:T(8,128)S(1)}, u32[]{:S(2)}, u32[]{:S(2)}) collective-permute-start(f32[64,1152]{1,0:T(8,128)S(1)} %pad_maximum_fusion), channel_id=1, source_target_pairs={{0,56},{4,60},{8,0},{12,4},{16,8},{20,12},{24,16},{28,20},{32,24},... | collective-permute-start | bytes 884744 | tf_op jit(solution)/shard_map/ppermute | solution.py:28
  47.7 14.8 %collective-permute-start.10 = (f32[128,1152]{1,0:T(8,128)S(1)}, f32[128,1152]{1,0:T(8,128)S(1)}, u32[]{:S(2)}, u32[]{:S(2)}) collective-permute-start(f32[128,1152]{1,0:T(8,128)S(1)} %collective-permute-done.6.refs_3_.refs_0_), channel_id=1, source_target_pairs={{0,192},{4,196},{8,200},{12,204},{16,208},{20,212},{24,216},{28,22... | collective-permute-start | bytes 1769480 | tf_op jit(solution)/shard_map/ppermute | solution.py:28
  47.7 1.7 %copy-start.10 = (f32[64,1152]{1,0:T(8,128)}, f32[64,1152]{1,0:T(8,128)S(1)}, u32[]{:S(2)}) copy-start(f32[64,1152]{1,0:T(8,128)S(1)} %collective-permute-done.7.refs_4_) | copy-start | bytes 884740
  47.7 15.5 %collective-permute-start.9 = (f32[128,1152]{1,0:T(8,128)S(1)}, f32[128,1152]{1,0:T(8,128)S(1)}, u32[]{:S(2)}, u32[]{:S(2)}) collective-permute-start(f32[128,1152]{1,0:T(8,128)S(1)} %collective-permute-done.6.refs_3_.refs_0_), channel_id=1, source_target_pairs={{0,64},{4,68},{8,72},{12,76},{16,80},{20,84},{24,88},{28,92},{32,9... | collective-permute-start | bytes 1769480 | tf_op jit(solution)/shard_map/ppermute | solution.py:28
  49.3 2.9 %copy-start.11 = (f32[64,1152]{1,0:T(8,128)}, f32[64,1152]{1,0:T(8,128)S(1)}, u32[]{:S(2)}) copy-start(f32[64,1152]{1,0:T(8,128)S(1)} %collective-permute-done.8.refs_5_) | copy-start | bytes 884740
  49.3 12.5 %collective-permute-start.11 = (f32[64,1152]{1,0:T(8,128)S(1)}, f32[64,1152]{1,0:T(8,128)S(1)}, u32[]{:S(2)}, u32[]{:S(2)}) collective-permute-start(f32[64,1152]{1,0:T(8,128)S(1)} %shard_map.125), channel_id=1, source_target_pairs={{0,8},{4,12},{8,16},{12,20},{16,24},{20,28},{24,32},{28,36},{32,40... | collective-permute-start | bytes 884744 | tf_op jit(solution)/shard_map/ppermute | solution.py:28
  50.9 10.9 %collective-permute-start.12 = (f32[64,1152]{1,0:T(8,128)S(1)}, f32[64,1152]{1,0:T(8,128)S(1)}, u32[]{:S(2)}, u32[]{:S(2)}) collective-permute-start(f32[64,1152]{1,0:T(8,128)S(1)} %shard_map.125), channel_id=1, source_target_pairs={{0,56},{4,60},{8,0},{12,4},{16,8},{20,12},{24,16},{28,20},{32,24},... | collective-permute-start | bytes 884744 | tf_op jit(solution)/shard_map/ppermute | solution.py:28
  63.2 5.4 %copy-start.8 = (f32[2,64]{1,0:T(2,128)S(1)}, f32[2,64]{1,0:T(2,128)}, u32[]{:S(2)}) copy-start(f32[2,64]{1,0:T(2,128)} %param.18) | copy-start | bytes 1540
  65.9 4.3 %collective-permute-start.13 = (f32[128,1024]{1,0:T(8,128)S(1)}, f32[128,1024]{1,0:T(8,128)S(1)}, u32[]{:S(2)}, u32[]{:S(2)}) collective-permute-start(f32[128,1024]{1,0:T(8,128)S(1)} %get-tuple-element.24), channel_id=1, source_target_pairs={{0,1},{1,0},{2,3},{3,2},{4,5},{5,4},{6,7},{7,6},{8,9},{9,8},{10,11... | collective-permute-start | bytes 1572872 | tf_op jit(solution)/shard_map/ppermute | solution.py:309
  70.2 7.6 %collective-permute-start.14 = (f32[64,1024]{1,0:T(8,128)S(1)}, f32[64,1024]{1,0:T(8,128)S(1)}, u32[]{:S(2)}, u32[]{:S(2)}) collective-permute-start(f32[64,1024]{1,0:T(8,128)S(1)} %get-tuple-element.26), channel_id=1, source_target_pairs={{0,2},{1,3},{2,0},{3,1},{4,6},{5,7},{6,4},{7,5},{8,10},{9,11},{10,... | collective-permute-start | bytes 786440 | tf_op jit(solution)/shard_map/ppermute | solution.py:312
  71.8 6.0 %copy-start = (f32[64,768]{1,0:T(8,128)S(1)}, f32[64,768]{1,0:T(8,128)}, u32[]{:S(2)}) copy-start(f32[64,768]{1,0:T(8,128)} %a_ref.2) | copy-start | bytes 589828
  73.8 14.3 %copy-start.1 = (f32[64,768]{1,0:T(8,128)S(1)}, f32[64,768]{1,0:T(8,128)}, u32[]{:S(2)}) copy-start(f32[64,768]{1,0:T(8,128)} %a_ref.3) | copy-start | bytes 589828
  79.3 2.6 %collective-permute-start.15 = (f32[128,768]{1,0:T(8,128)S(1)}, f32[128,768]{1,0:T(8,128)S(1)}, u32[]{:S(2)}, u32[]{:S(2)}) collective-permute-start(f32[128,768]{1,0:T(8,128)S(1)} %get-tuple-element.29), channel_id=1, source_target_pairs={{0,1},{1,0},{2,3},{3,2},{4,5},{5,4},{6,7},{7,6},{8,9},{9,8},{10,11... | collective-permute-start | bytes 1179656 | tf_op jit(solution)/shard_map/ppermute | solution.py:309
  81.9 6.2 %collective-permute-start.16 = (f32[64,768]{1,0:T(8,128)S(1)}, f32[64,768]{1,0:T(8,128)S(1)}, u32[]{:S(2)}, u32[]{:S(2)}) collective-permute-start(f32[64,768]{1,0:T(8,128)S(1)} %get-tuple-element.31), channel_id=1, source_target_pairs={{0,2},{1,3},{2,0},{3,1},{4,6},{5,7},{6,4},{7,5},{8,10},{9,11},{10,... | collective-permute-start | bytes 589832 | tf_op jit(solution)/shard_map/ppermute | solution.py:312

commit v12 on v11

--- a/solution.py
+++ b/solution.py
@@ -170,7 +170,7 @@
             pltpu.VMEM((k_local, width), jnp.float32),
             pltpu.VMEM(pivots.shape, jnp.int32),
             pltpu.VMEM((blocks, width), jnp.float32),
-            pltpu.SemaphoreType.DMA((8,)),
+            pltpu.SemaphoreType.DMA((2,)),
             pltpu.SemaphoreType.DMA((2,)),
         ],
         compiler_params=pltpu.CompilerParams(vmem_limit_bytes=20 * 2**20),
@@ -183,12 +183,12 @@
 
 def coupled_parts(weights, prior_lt, following):
     k_local, width = prior_lt.shape
-    depth = k_local // 8
+    depth = k_local // 2
     block = pl.BlockSpec((depth, width), lambda i: (i, 0))
     shape = jax.ShapeDtypeStruct((k_local, width), jnp.bfloat16)
     return pl.pallas_call(
         couple_kernel,
-        grid=(8,),
+        grid=(2,),
         in_specs=[
             pl.BlockSpec((8, depth), lambda i: (0, i)),
             block,

time: 89.2 us -> 87.3 us (0.979)
  Pallas kernels: 23.3 us -> 19.3 us
  waiting for transfers between devices: 29.6 us -> 32.3 us
    ppermute x13, waiting for transfers between devices: 19.4 us -> 21.6 us  [moved(): got = lax.ppermute(block, 'wide', shift(*step))]
    pallas_call x1, Pallas kernels: 5.54 us -> 3.32 us  [coupled_parts(): pl.pallas_call(couple_kernel, grid=(2,), in_specs=[pl.BlockSpec((8, depth...]
    pallas_call x1, Pallas kernels: 5.55 us -> 3.79 us  [tile_slots(): pl.pallas_call(slots_kernel, in_specs=[pl.BlockSpec(memory_space=pltpu.SM...]
  transfers between devices with their start and end apart: 17 -> 17, of which waited for: 11 -> 11; matrix products, arithmetic and copies ran while one was open for 1% -> 1% of each run, Pallas kernels for 14% -> 12%
where the time goes in v12:
time: 87.3 us; the launch traced here: 87.2 us
  starting transfers between devices  33.3 us (38%)
  waiting for transfers between devices  32.3 us (37%)
  Pallas kernels  19.3 us (22%)
  between operations  1.05 us (1%)
    ppermute x13, starting transfers between devices, moved(): got = lax.ppermute(block, 'wide', shift(*step))  26.9 us
    ppermute x13, waiting for transfers between devices, moved(): got = lax.ppermute(block, 'wide', shift(*step))  21.6 us
    pallas_call x8, Pallas kernels, local_call(): pl.pallas_call(kernel, in_specs=specs, out_specs=jax.tree.map(lambda _: v...  12.1 us
    ppermute x2, waiting for transfers between devices, hop_sum(): return (rest, lax.ppermute(away, 'narrow', CHIP))  9.16 us
    ppermute x2, starting transfers between devices, hop_sum(): got = lax.ppermute(send, 'narrow', CORE)  3.93 us
    pallas_call x1, Pallas kernels, tile_slots(): pl.pallas_call(slots_kernel, in_specs=[pl.BlockSpec(memory_space=pltpu.SM...  3.79 us
    pallas_call x1, Pallas kernels, coupled_parts(): pl.pallas_call(couple_kernel, grid=(2,), in_specs=[pl.BlockSpec((8, depth...  3.32 us
    ppermute x2, starting transfers between devices, hop_sum(): return (rest, lax.ppermute(away, 'narrow', CHIP))  2.45 us
  transfers between devices with their start and end apart: 17, of which 11 were waited for; matrix products, arithmetic and copies ran while one was open for 1% of the time, Pallas kernels for 12%

profile of v12, /device:TPU:1, one launch (start us, length us, event | category | flops | bytes accessed | tf_op | source)
XLA Modules:
  0.0 87.2 jit_solution(2093060296769098887)
XLA Ops:
  0.6 0.0 copy-start.9
  0.7 3.8 %shard_map.122 = f32[16,1152]{1,0:T(8,128)S(1)} custom-call(s32[1]{0:T(128)} %bitcast.10.low_ref, s32[2,256]{1,0:T(2,128)} %pivots_hbm.1, f32[64,768]{1,0:T(8,128)} %a_ref.2, f32[1024,768]{1,0:T(8,128)} %lt_ref.3), custom_call_target="tpu_custom_call" | custom-call | tf_op jit(solution)/shard_map/pallas_call | solution.py:159
  4.5 0.0 copy-start.5
  4.5 7.8 %collective-permute-start = (f32[16,1152]{1,0:T(8,128)S(1)}, f32[16,1152]{1,0:T(8,128)S(1)}, u32[]{:S(2)}, u32[]{:S(2)}) collective-permute-start(f32[16,1152]{1,0:T(8,128)S(1)} %shard_map.122), channel_id=1, source_target_pairs={{0,32},{4,36},{8,40},{12,44},{16,48},{20,52},{24,56},{28,60},{32,0... | collective-permute-start | bytes 221192 | tf_op jit(solution)/shard_map/ppermute | solution.py:28
  12.5 0.2 convert_reduce_fusion
  12.8 0.1 select_reduce_fusion
  12.9 1.3 %collective-permute-done = f32[16,1152]{1,0:T(8,128)S(1)} collective-permute-done((f32[16,1152]{1,0:T(8,128)S(1)}, f32[16,1152]{1,0:T(8,128)S(1)}, u32[]{:S(2)}, u32[]{:S(2)}) %collective-permute-start) | collective-permute-done | bytes 73760 | tf_op jit(solution)/shard_map/ppermute | solution.py:28
  14.2 3.3 %collective-permute-start.1 = (f32[32,1152]{1,0:T(8,128)S(1)}, f32[32,1152]{1,0:T(8,128)S(1)}, u32[]{:S(2)}, u32[]{:S(2)}) collective-permute-start(f32[32,1152]{1,0:T(8,128)S(1)} %pad_maximum_fusion.1), channel_id=1, source_target_pairs={{0,136},{4,140},{8,144},{12,148},{16,152},{20,156},{24,160},{28,16... | collective-permute-start | bytes 442376 | tf_op jit(solution)/shard_map/ppermute | solution.py:28
  17.5 4.2 %collective-permute-start.2 = (f32[32,1152]{1,0:T(8,128)S(1)}, f32[32,1152]{1,0:T(8,128)S(1)}, u32[]{:S(2)}, u32[]{:S(2)}) collective-permute-start(f32[32,1152]{1,0:T(8,128)S(1)} %pad_maximum_fusion.1), channel_id=1, source_target_pairs={{0,184},{4,188},{8,128},{12,132},{16,136},{20,140},{24,144},{28,14... | collective-permute-start | bytes 442376 | tf_op jit(solution)/shard_map/ppermute | solution.py:28
  21.8 3.9 %collective-permute-done.1 = f32[32,1152]{1,0:T(8,128)S(1)} collective-permute-done((f32[32,1152]{1,0:T(8,128)S(1)}, f32[32,1152]{1,0:T(8,128)S(1)}, u32[]{:S(2)}, u32[]{:S(2)}) %collective-permute-start.1) | collective-permute-done | bytes 147488 | tf_op jit(solution)/shard_map/ppermute | solution.py:28
  25.7 5.3 %collective-permute-done.3 = f32[32,1152]{1,0:T(8,128)S(1)} collective-permute-done((f32[32,1152]{1,0:T(8,128)S(1)}, f32[32,1152]{1,0:T(8,128)S(1)}, u32[]{:S(2)}, u32[]{:S(2)}) %collective-permute-start.3) | collective-permute-done | bytes 147488 | tf_op jit(solution)/shard_map/ppermute | solution.py:28
  31.1 3.4 %collective-permute-start.6 = (f32[128,1152]{1,0:T(8,128)S(1)}, f32[128,1152]{1,0:T(8,128)S(1)}, u32[]{:S(2)}, u32[]{:S(2)}) collective-permute-start(f32[128,1152]{1,0:T(8,128)S(1)} %constant_dynamic-update-slice_fusion.refs_0_.after_ref), channel_id=1, source_target_pairs={{0,4},{4,0},{8,12},{12,8},{16,20},{20,16},{24,28},{28,24},{32,36},... | collective-permute-start | bytes 1769480 | tf_op jit(solution)/shard_map/ppermute | solution.py:28
  34.5 2.7 %collective-permute-start.5 = (f32[128,1152]{1,0:T(8,128)S(1)}, f32[128,1152]{1,0:T(8,128)}, u32[]{:S(2)}, u32[]{:S(2)}) collective-permute-start(f32[128,1152]{1,0:T(8,128)S(1)} %constant_dynamic-update-slice_fusion.refs_0_.after_ref), channel_id=1, source_target_pairs={{0,192},{4,196},{8,200},{12,204},{16,208},{20,212},{24,216},{28,22... | collective-permute-start | bytes 1769480 | tf_op jit(solution)/shard_map/ppermute | solution.py:28
  37.2 0.1 collective-permute-start.7
  37.4 2.6 %collective-permute-start.8 = (f32[64,1152]{1,0:T(8,128)S(1)}, f32[64,1152]{1,0:T(8,128)S(1)}, u32[]{:S(2)}, u32[]{:S(2)}) collective-permute-start(f32[64,1152]{1,0:T(8,128)S(1)} %pad_maximum_fusion), channel_id=1, source_target_pairs={{0,56},{4,60},{8,0},{12,4},{16,8},{20,12},{24,16},{28,20},{32,24},... | collective-permute-start | bytes 884744 | tf_op jit(solution)/shard_map/ppermute | solution.py:28
  40.0 0.1 pad_maximum_fusion.2
  40.1 5.9 %collective-permute-done.6.refs_3_.refs_0_ = f32[128,1152]{1,0:T(8,128)S(1)} collective-permute-done((f32[128,1152]{1,0:T(8,128)S(1)}, f32[128,1152]{1,0:T(8,128)S(1)}, u32[]{:S(2)}, u32[]{:S(2)}) %collective-permute-start.6) | collective-permute-done | bytes 589856 | tf_op jit(solution)/shard_map/ppermute | solution.py:28
  46.0 1.5 %collective-permute-start.9 = (f32[128,1152]{1,0:T(8,128)S(1)}, f32[128,1152]{1,0:T(8,128)S(1)}, u32[]{:S(2)}, u32[]{:S(2)}) collective-permute-start(f32[128,1152]{1,0:T(8,128)S(1)} %collective-permute-done.6.refs_3_.refs_0_), channel_id=1, source_target_pairs={{0,64},{4,68},{8,72},{12,76},{16,80},{20,84},{24,88},{28,92},{32,9... | collective-permute-start | bytes 1769480 | tf_op jit(solution)/shard_map/ppermute | solution.py:28
  47.4 0.1 shard_map.125
  47.5 0.1 collective-permute-start.11
  47.6 1.6 %collective-permute-done.4.refs_1_ = f32[128,1152]{1,0:T(8,128)} collective-permute-done((f32[128,1152]{1,0:T(8,128)S(1)}, f32[128,1152]{1,0:T(8,128)}, u32[]{:S(2)}, u32[]{:S(2)}) %collective-permute-start.4) | collective-permute-done | bytes 589856 | tf_op jit(solution)/shard_map/ppermute | solution.py:28
  49.2 1.1 %collective-permute-start.12 = (f32[64,1152]{1,0:T(8,128)S(1)}, f32[64,1152]{1,0:T(8,128)S(1)}, u32[]{:S(2)}, u32[]{:S(2)}) collective-permute-start(f32[64,1152]{1,0:T(8,128)S(1)} %shard_map.125), channel_id=1, source_target_pairs={{0,56},{4,60},{8,0},{12,4},{16,8},{20,12},{24,16},{28,20},{32,24},... | collective-permute-start | bytes 884744 | tf_op jit(solution)/shard_map/ppermute | solution.py:28
  50.3 0.1 fusion.17
  50.4 0.1 concatenate.27
  50.5 0.1 copy.16.index_ref
  50.7 3.3 %shard_map.124 = (bf16[1024,768]{1,0:T(8,128)(2,1)S(1)}, bf16[1024,768]{1,0:T(8,128)(2,1)S(1)}) custom-call(f32[8,1024]{1,0:T(8,128)S(1)} %select_maximum_fusion.weight_ref, f32[1024,768]{1,0:T(8,128)} %lt_ref.3, f32[128,1152]{1,0:T(8,128)S(1)} %constant_dynamic-update-slice_fusion.refs_0_.after_ref), custom_call_target="tpu_custom_call" | custom-call | flops 6291456 | bytes 6291456 | tf_op jit(solution)/shard_map/pallas_call | solution.py:189
  54.0 3.8 %shard_map.123.carry_ref = f32[512,1152]{1,0:T(8,128)S(1)} custom-call(s32[512,1]{1,0:T(8,128)S(1)} %copy.16.index_ref, f32[128,1152]{1,0:T(8,128)S(1)} %constant_dynamic-update-slice_fusion.refs_0_.after_ref, f32[128,1152]{1,0:T(8,128)} %collective-permute-done.4.refs_1_, f32[128,1152]{1,0:T(8,128)} %collective-permute-done.5.refs_2_, ...), custom_call_target="tpu_custom_call" | custom-call | flops 1509949440 | bytes 2951168 | tf_op jit(solution)/shard_map/pallas_call | solution.py:276
  57.8 2.9 %collective-permute-done.10.refs_1_ = f32[128,1152]{1,0:T(8,128)S(1)} collective-permute-done((f32[128,1152]{1,0:T(8,128)S(1)}, f32[128,1152]{1,0:T(8,128)S(1)}, u32[]{:S(2)}, u32[]{:S(2)}) %collective-permute-start.10) | collective-permute-done | bytes 589856 | tf_op jit(solution)/shard_map/ppermute | solution.py:28
  60.7 0.8 collective-permute-done.9.refs_0_
  61.5 2.6 %shard_map.126 = (f32[128,1024]{1,0:T(8,128)S(1)}, f32[256,1024]{1,0:T(8,128)S(1)}, f32[256,128]{1,0:T(8,128)S(1)}, bf16[256,1024]{1,0:T(8,128)(2,1)S(1)}, bf16[...) custom-call(s32[512,1]{1,0:T(8,128)S(1)} %copy.16.index_ref, f32[8,1024]{1,0:T(8,128)S(1)} %select_maximum_fusion.weight_ref, ...), custom_call_target="tpu_custom_call" | custom-call | flops 1711276032 | bytes 10455040 | tf_op jit(solution)/shard_map/pallas_call | solution.py:276
  64.1 2.7 %collective-permute-start.13 = (f32[128,1024]{1,0:T(8,128)S(1)}, f32[128,1024]{1,0:T(8,128)S(1)}, u32[]{:S(2)}, u32[]{:S(2)}) collective-permute-start(f32[128,1024]{1,0:T(8,128)S(1)} %get-tuple-element.24), channel_id=1, source_target_pairs={{0,1},{1,0},{2,3},{3,2},{4,5},{5,4},{6,7},{7,6},{8,9},{9,8},{10,11... | collective-permute-start | bytes 1572872 | tf_op jit(solution)/shard_map/ppermute | solution.py:309
  66.8 0.1 fusion.13
  66.9 1.2 %shard_map.128.keep_ref = f32[128,1024]{1,0:T(8,128)S(1)} custom-call(f32[128,1024]{1,0:T(8,128)S(1)} %get-tuple-element.21.taken_ref, bf16[1024,768]{1,0:T(8,128)(2,1)S(1)} %get-tuple-element.17.lt_big_ref, bf16[1024,768]{1,0:T(8,128)(2,1)S(1)} %get-tuple-element.18.lt_small_ref, bf16[256,1024]{1,0:T(8,128)(2,1)S(1)} %get-tuple-element.22.big_ref, ...), custom_call_target="tpu_custom_call" | custom-call | flops 805306368 | bytes 8912896 | tf_op jit(solution)/shard_map/pallas_call | solution.py:276
  68.2 0.2 collective-permute-done.13.got_ref
  68.4 0.1 shard_map.129
  68.4 1.2 %collective-permute-start.14 = (f32[64,1024]{1,0:T(8,128)S(1)}, f32[64,1024]{1,0:T(8,128)S(1)}, u32[]{:S(2)}, u32[]{:S(2)}) collective-permute-start(f32[64,1024]{1,0:T(8,128)S(1)} %get-tuple-element.26), channel_id=1, source_target_pairs={{0,2},{1,3},{2,0},{3,1},{4,6},{5,7},{6,4},{7,5},{8,10},{9,11},{10,... | collective-permute-start | bytes 786440 | tf_op jit(solution)/shard_map/ppermute | solution.py:312
  69.7 0.1 pad_add_fusion.quarter_ref
  69.8 0.0 copy-start
  69.8 2.0 %shard_map.127.update_ref = f32[256,768]{1,0:T(8,128)S(1)} custom-call(s32[4]{0:T(128)S(1)} %pad_add_fusion.quarter_ref, f32[256,1024]{1,0:T(8,128)S(1)} %get-tuple-element.20.second_ref, bf16[1024,768]{1,0:T(8,128)(2,1)S(1)} %get-tuple-element.17.lt_big_ref, bf16[1024,768]{1,0:T(8,128)(2,1)S(1)} %get-tuple-element.18.lt_small_ref), custom_call_target="tpu_custom_call" | custom-call | flops 1207959552 | bytes 7340048 | tf_op jit(solution)/shard_map/pallas_call | solution.py:276
  71.8 4.3 %collective-permute-done.14.away_ref = f32[64,1024]{1,0:T(8,128)S(1)} collective-permute-done((f32[64,1024]{1,0:T(8,128)S(1)}, f32[64,1024]{1,0:T(8,128)S(1)}, u32[]{:S(2)}, u32[]{:S(2)}) %collective-permute-start.14) | collective-permute-done | bytes 262176 | tf_op jit(solution)/shard_map/ppermute | solution.py:312
  76.0 1.5 %shard_map.130 = (f32[64,768]{1,0:T(8,128)}, f32[128,768]{1,0:T(8,128)S(1)}, f32[128,768]{1,0:T(8,128)S(1)}) custom-call(s32[4]{0:T(128)S(1)} %pad_add_fusion.quarter_ref, f32[8,128]{1,0:T(8,128)S(1)} %select_maximum_fusion.4.weight_ref, f32[64,768]{1,0:T(8,128)S(1)} %copy-done, f32[256,128]{1,0:T(8,128)S(1)} %get-tuple-element.19.entries_ref, ...), custom_call_target="tpu_custom_call" | custom-call | flops 75497472 | bytes 1642512 | tf_op jit(solution)/shard_map/pallas_call | solution.py:276
  77.5 1.2 %collective-permute-start.15 = (f32[128,768]{1,0:T(8,128)S(1)}, f32[128,768]{1,0:T(8,128)S(1)}, u32[]{:S(2)}, u32[]{:S(2)}) collective-permute-start(f32[128,768]{1,0:T(8,128)S(1)} %get-tuple-element.29), channel_id=1, source_target_pairs={{0,1},{1,0},{2,3},{3,2},{4,5},{5,4},{6,7},{7,6},{8,9},{9,8},{10,11... | collective-permute-start | bytes 1179656 | tf_op jit(solution)/shard_map/ppermute | solution.py:309
  78.7 1.3 %collective-permute-done.15.got_ref = f32[128,768]{1,0:T(8,128)S(1)} collective-permute-done((f32[128,768]{1,0:T(8,128)S(1)}, f32[128,768]{1,0:T(8,128)S(1)}, u32[]{:S(2)}, u32[]{:S(2)}) %collective-permute-start.15) | collective-permute-done | bytes 393248 | tf_op jit(solution)/shard_map/ppermute | solution.py:309
  80.0 0.1 shard_map.131
  80.1 1.2 %collective-permute-start.16 = (f32[64,768]{1,0:T(8,128)S(1)}, f32[64,768]{1,0:T(8,128)S(1)}, u32[]{:S(2)}, u32[]{:S(2)}) collective-permute-start(f32[64,768]{1,0:T(8,128)S(1)} %get-tuple-element.31), channel_id=1, source_target_pairs={{0,2},{1,3},{2,0},{3,1},{4,6},{5,7},{6,4},{7,5},{8,10},{9,11},{10,... | collective-permute-start | bytes 589832 | tf_op jit(solution)/shard_map/ppermute | solution.py:312
  81.3 0.1 fusion.14
  81.4 4.9 %collective-permute-done.16.away_ref = f32[64,768]{1,0:T(8,128)S(1)} collective-permute-done((f32[64,768]{1,0:T(8,128)S(1)}, f32[64,768]{1,0:T(8,128)S(1)}, u32[]{:S(2)}, u32[]{:S(2)}) %collective-permute-start.16) | collective-permute-done | bytes 196640 | tf_op jit(solution)/shard_map/ppermute | solution.py:312
  86.3 0.9 %shard_map.132 = f32[64,768]{1,0:T(8,128)} custom-call(f32[8,128]{1,0:T(8,128)S(1)} %select_maximum_fusion.2.weight_ref, f32[64,768]{1,0:T(8,128)S(1)} %copy-done.1, f32[64,768]{1,0:T(8,128)S(1)} %get-tuple-element.30.rest_ref, f32[64,768]{1,0:T(8,128)S(1)} %collective-permute-done.16.away_ref), custom_call_target="tpu_custom_call" | custom-call | flops 393216 | bytes 593920 | tf_op jit(solution)/shard_map/pallas_call | solution.py:276
  (51 shorter events, 0.3 us)
Async XLA Ops:
  0.6 12.1 %copy-start.9 = (s32[64]{0:T(128)S(1)}, s32[64]{0:T(128)}, u32[]{:S(2)}) copy-start(s32[64]{0:T(128)} %constant.136.clone) | copy-start | bytes 772
  0.6 11.7 %copy-start.2 = (s32[2,256]{1,0:T(2,128)S(1)}, s32[2,256]{1,0:T(2,128)}, u32[]{:S(2)}) copy-start(s32[2,256]{1,0:T(2,128)} %pivots_hbm.1) | copy-start | bytes 6148
  0.7 12.1 %copy-start.3 = (f32[1024]{0:T(1024)S(1)}, f32[1024]{0:T(1024)}, u32[]{:S(2)}) copy-start(f32[1024]{0:T(1024)} %param.13) | copy-start | bytes 12292
  0.7 12.1 %copy-start.4 = (s32[1024]{0:T(1024)S(1)}, s32[1024]{0:T(1024)}, u32[]{:S(2)}) copy-start(s32[1024]{0:T(1024)} %param.14) | copy-start | bytes 12292
  0.7 46.7 %copy-start.6 = (s32[2,64]{1,0:T(2,128)S(1)}, s32[2,64]{1,0:T(2,128)}, u32[]{:S(2)}) copy-start(s32[2,64]{1,0:T(2,128)} %param.20) | copy-start | bytes 1540
  0.7 46.7 %copy-start.7 = (f32[2,64]{1,0:T(2,128)S(1)}, f32[2,64]{1,0:T(2,128)}, u32[]{:S(2)}) copy-start(f32[2,64]{1,0:T(2,128)} %param.19) | copy-start | bytes 1540
  4.5 46.1 %copy-start.5 = (f32[1024]{0:T(1024)S(1)}, f32[1024]{0:T(1024)}, u32[]{:S(2)}) copy-start(f32[1024]{0:T(1024)} %param.12) | copy-start | bytes 12292
  4.5 9.7 %collective-permute-start = (f32[16,1152]{1,0:T(8,128)S(1)}, f32[16,1152]{1,0:T(8,128)S(1)}, u32[]{:S(2)}, u32[]{:S(2)}) collective-permute-start(f32[16,1152]{1,0:T(8,128)S(1)} %shard_map.122), channel_id=1, source_target_pairs={{0,32},{4,36},{8,40},{12,44},{16,48},{20,52},{24,56},{28,60},{32,0... | collective-permute-start | bytes 221192 | tf_op jit(solution)/shard_map/ppermute | solution.py:28
  14.2 11.5 %collective-permute-start.1 = (f32[32,1152]{1,0:T(8,128)S(1)}, f32[32,1152]{1,0:T(8,128)S(1)}, u32[]{:S(2)}, u32[]{:S(2)}) collective-permute-start(f32[32,1152]{1,0:T(8,128)S(1)} %pad_maximum_fusion.1), channel_id=1, source_target_pairs={{0,136},{4,140},{8,144},{12,148},{16,152},{20,156},{24,160},{28,16... | collective-permute-start | bytes 442376 | tf_op jit(solution)/shard_map/ppermute | solution.py:28
  17.5 8.2 %collective-permute-start.2 = (f32[32,1152]{1,0:T(8,128)S(1)}, f32[32,1152]{1,0:T(8,128)S(1)}, u32[]{:S(2)}, u32[]{:S(2)}) collective-permute-start(f32[32,1152]{1,0:T(8,128)S(1)} %pad_maximum_fusion.1), channel_id=1, source_target_pairs={{0,184},{4,188},{8,128},{12,132},{16,136},{20,140},{24,144},{28,14... | collective-permute-start | bytes 442376 | tf_op jit(solution)/shard_map/ppermute | solution.py:28
  21.8 9.3 %collective-permute-start.3 = (f32[32,1152]{1,0:T(8,128)S(1)}, f32[32,1152]{1,0:T(8,128)S(1)}, u32[]{:S(2)}, u32[]{:S(2)}) collective-permute-start(f32[32,1152]{1,0:T(8,128)S(1)} %pad_maximum_fusion.1), channel_id=1, source_target_pairs={{0,16},{4,20},{8,24},{12,28},{16,32},{20,36},{24,40},{28,44},{32,4... | collective-permute-start | bytes 442376 | tf_op jit(solution)/shard_map/ppermute | solution.py:28
  31.1 14.9 %collective-permute-start.6 = (f32[128,1152]{1,0:T(8,128)S(1)}, f32[128,1152]{1,0:T(8,128)S(1)}, u32[]{:S(2)}, u32[]{:S(2)}) collective-permute-start(f32[128,1152]{1,0:T(8,128)S(1)} %constant_dynamic-update-slice_fusion.refs_0_.after_ref), channel_id=1, source_target_pairs={{0,4},{4,0},{8,12},{12,8},{16,20},{20,16},{24,28},{28,24},{32,36},... | collective-permute-start | bytes 1769480 | tf_op jit(solution)/shard_map/ppermute | solution.py:28
  34.5 14.7 %collective-permute-start.4 = (f32[128,1152]{1,0:T(8,128)S(1)}, f32[128,1152]{1,0:T(8,128)}, u32[]{:S(2)}, u32[]{:S(2)}) collective-permute-start(f32[128,1152]{1,0:T(8,128)S(1)} %constant_dynamic-update-slice_fusion.refs_0_.after_ref), channel_id=1, source_target_pairs={{0,64},{4,68},{8,72},{12,76},{16,80},{20,84},{24,88},{28,92},{32,9... | collective-permute-start | bytes 1769480 | tf_op jit(solution)/shard_map/ppermute | solution.py:28
  34.5 19.4 %collective-permute-start.5 = (f32[128,1152]{1,0:T(8,128)S(1)}, f32[128,1152]{1,0:T(8,128)}, u32[]{:S(2)}, u32[]{:S(2)}) collective-permute-start(f32[128,1152]{1,0:T(8,128)S(1)} %constant_dynamic-update-slice_fusion.refs_0_.after_ref), channel_id=1, source_target_pairs={{0,192},{4,196},{8,200},{12,204},{16,208},{20,212},{24,216},{28,22... | collective-permute-start | bytes 1769480 | tf_op jit(solution)/shard_map/ppermute | solution.py:28
  37.2 8.7 %collective-permute-start.7 = (f32[64,1152]{1,0:T(8,128)S(1)}, f32[64,1152]{1,0:T(8,128)S(1)}, u32[]{:S(2)}, u32[]{:S(2)}) collective-permute-start(f32[64,1152]{1,0:T(8,128)S(1)} %pad_maximum_fusion), channel_id=1, source_target_pairs={{0,8},{4,12},{8,16},{12,20},{16,24},{20,28},{24,32},{28,36},{32,40... | collective-permute-start | bytes 884744 | tf_op jit(solution)/shard_map/ppermute | solution.py:28
  37.4 10.1 %collective-permute-start.8 = (f32[64,1152]{1,0:T(8,128)S(1)}, f32[64,1152]{1,0:T(8,128)S(1)}, u32[]{:S(2)}, u32[]{:S(2)}) collective-permute-start(f32[64,1152]{1,0:T(8,128)S(1)} %pad_maximum_fusion), channel_id=1, source_target_pairs={{0,56},{4,60},{8,0},{12,4},{16,8},{20,12},{24,16},{28,20},{32,24},... | collective-permute-start | bytes 884744 | tf_op jit(solution)/shard_map/ppermute | solution.py:28
  45.9 14.8 %collective-permute-start.10 = (f32[128,1152]{1,0:T(8,128)S(1)}, f32[128,1152]{1,0:T(8,128)S(1)}, u32[]{:S(2)}, u32[]{:S(2)}) collective-permute-start(f32[128,1152]{1,0:T(8,128)S(1)} %collective-permute-done.6.refs_3_.refs_0_), channel_id=1, source_target_pairs={{0,192},{4,196},{8,200},{12,204},{16,208},{20,212},{24,216},{28,22... | collective-permute-start | bytes 1769480 | tf_op jit(solution)/shard_map/ppermute | solution.py:28
  46.0 1.7 %copy-start.10 = (f32[64,1152]{1,0:T(8,128)}, f32[64,1152]{1,0:T(8,128)S(1)}, u32[]{:S(2)}) copy-start(f32[64,1152]{1,0:T(8,128)S(1)} %collective-permute-done.7.refs_4_) | copy-start | bytes 884740
  46.0 15.5 %collective-permute-start.9 = (f32[128,1152]{1,0:T(8,128)S(1)}, f32[128,1152]{1,0:T(8,128)S(1)}, u32[]{:S(2)}, u32[]{:S(2)}) collective-permute-start(f32[128,1152]{1,0:T(8,128)S(1)} %collective-permute-done.6.refs_3_.refs_0_), channel_id=1, source_target_pairs={{0,64},{4,68},{8,72},{12,76},{16,80},{20,84},{24,88},{28,92},{32,9... | collective-permute-start | bytes 1769480 | tf_op jit(solution)/shard_map/ppermute | solution.py:28
  47.5 2.9 %copy-start.11 = (f32[64,1152]{1,0:T(8,128)}, f32[64,1152]{1,0:T(8,128)S(1)}, u32[]{:S(2)}) copy-start(f32[64,1152]{1,0:T(8,128)S(1)} %collective-permute-done.8.refs_5_) | copy-start | bytes 884740
  47.5 10.3 %collective-permute-start.11 = (f32[64,1152]{1,0:T(8,128)S(1)}, f32[64,1152]{1,0:T(8,128)S(1)}, u32[]{:S(2)}, u32[]{:S(2)}) collective-permute-start(f32[64,1152]{1,0:T(8,128)S(1)} %shard_map.125), channel_id=1, source_target_pairs={{0,8},{4,12},{8,16},{12,20},{16,24},{20,28},{24,32},{28,36},{32,40... | collective-permute-start | bytes 884744 | tf_op jit(solution)/shard_map/ppermute | solution.py:28
  49.2 8.6 %collective-permute-start.12 = (f32[64,1152]{1,0:T(8,128)S(1)}, f32[64,1152]{1,0:T(8,128)S(1)}, u32[]{:S(2)}, u32[]{:S(2)}) collective-permute-start(f32[64,1152]{1,0:T(8,128)S(1)} %shard_map.125), channel_id=1, source_target_pairs={{0,56},{4,60},{8,0},{12,4},{16,8},{20,12},{24,16},{28,20},{32,24},... | collective-permute-start | bytes 884744 | tf_op jit(solution)/shard_map/ppermute | solution.py:28
  61.5 5.4 %copy-start.8 = (f32[2,64]{1,0:T(2,128)S(1)}, f32[2,64]{1,0:T(2,128)}, u32[]{:S(2)}) copy-start(f32[2,64]{1,0:T(2,128)} %param.18) | copy-start | bytes 1540
  64.1 4.3 %collective-permute-start.13 = (f32[128,1024]{1,0:T(8,128)S(1)}, f32[128,1024]{1,0:T(8,128)S(1)}, u32[]{:S(2)}, u32[]{:S(2)}) collective-permute-start(f32[128,1024]{1,0:T(8,128)S(1)} %get-tuple-element.24), channel_id=1, source_target_pairs={{0,1},{1,0},{2,3},{3,2},{4,5},{5,4},{6,7},{7,6},{8,9},{9,8},{10,11... | collective-permute-start | bytes 1572872 | tf_op jit(solution)/shard_map/ppermute | solution.py:309
  68.4 7.6 %collective-permute-start.14 = (f32[64,1024]{1,0:T(8,128)S(1)}, f32[64,1024]{1,0:T(8,128)S(1)}, u32[]{:S(2)}, u32[]{:S(2)}) collective-permute-start(f32[64,1024]{1,0:T(8,128)S(1)} %get-tuple-element.26), channel_id=1, source_target_pairs={{0,2},{1,3},{2,0},{3,1},{4,6},{5,7},{6,4},{7,5},{8,10},{9,11},{10,... | collective-permute-start | bytes 786440 | tf_op jit(solution)/shard_map/ppermute | solution.py:312
  69.8 6.3 %copy-start = (f32[64,768]{1,0:T(8,128)S(1)}, f32[64,768]{1,0:T(8,128)}, u32[]{:S(2)}) copy-start(f32[64,768]{1,0:T(8,128)} %a_ref.2) | copy-start | bytes 589828
  71.8 14.5 %copy-start.1 = (f32[64,768]{1,0:T(8,128)S(1)}, f32[64,768]{1,0:T(8,128)}, u32[]{:S(2)}) copy-start(f32[64,768]{1,0:T(8,128)} %a_ref.3) | copy-start | bytes 589828
  77.5 2.6 %collective-permute-start.15 = (f32[128,768]{1,0:T(8,128)S(1)}, f32[128,768]{1,0:T(8,128)S(1)}, u32[]{:S(2)}, u32[]{:S(2)}) collective-permute-start(f32[128,768]{1,0:T(8,128)S(1)} %get-tuple-element.29), channel_id=1, source_target_pairs={{0,1},{1,0},{2,3},{3,2},{4,5},{5,4},{6,7},{7,6},{8,9},{9,8},{10,11... | collective-permute-start | bytes 1179656 | tf_op jit(solution)/shard_map/ppermute | solution.py:309
  80.1 6.2 %collective-permute-start.16 = (f32[64,768]{1,0:T(8,128)S(1)}, f32[64,768]{1,0:T(8,128)S(1)}, u32[]{:S(2)}, u32[]{:S(2)}) collective-permute-start(f32[64,768]{1,0:T(8,128)S(1)} %get-tuple-element.31), channel_id=1, source_target_pairs={{0,2},{1,3},{2,0},{3,1},{4,6},{5,7},{6,4},{7,5},{8,10},{9,11},{10,... | collective-permute-start | bytes 589832 | tf_op jit(solution)/shard_map/ppermute | solution.py:312
